TPU v7x, 128 devices: a whole 4x4x4 slice. The times are simulated.
128 devices in a mesh: rows: 16 (over y, z), cols: 8 (over x, core).
Axes of the slice: x: 4, y: 4, z: 4, core: 2. Of those that a mesh axis runs over, the one named last changes fastest.
Arguments:
- coefficients: float32 [4, 2048, 4, 256], P(None, 'rows'), may hold values from -0.03 to 0.09
- support: int32 [4, 2048, 4], P(None, 'rows'), may hold values from 0 to 23, all different within a row
- primal: float32 [24, 256, 256], P('cols'), may hold values from -0.5 to 9, as said below
- dual_inverse: float32 [24, 256, 256], P('cols'), may hold values from -0.5 to 9, as said below
- block_sizes: int32 [24], P('cols'), may hold values from 64 to 256, as said below
- damping: float32 [4, 2048], P(None, 'rows'), may hold values from 0.5 to 2
- right_sides: float32 [4, 32, 2048], P(None, 'cols', 'rows'), may hold values from -6 to 6
Outputs:
- updated: float32 [4, 2048, 8192], P(None, 'rows', 'cols')
- panel_factor: float32 [4, 2048, 128], P(None, 'rows')
- solved: float32 [4, 32, 2048], P(None, 'cols', 'rows')
Inputs may be any that keep to these rules, and one draw needn't show every extreme that they name: `primal`: each block is symmetric positive definite. `dual_inverse`: each block is symmetric positive definite. `block_sizes`: some block has order 256.
All inputs are finite; a program needn't handle non-finite values.
Results may differ from a plain program's by a relative error of at most 0.00015.
Values sent between devices are 32-bit elements; how exact they have to be, the bound alone decides.
No kernel may reach another device: no remote copies, remote signals or barrier semaphores. Data moves between devices by JAX's collectives and lax.ppermute only.
A program may use at most 192 MiB of HBM per device.

v0:
```python
import jax
import jax.numpy as jnp
from jax import lax
from jax.sharding import PartitionSpec as P

BS = 256
NBL = 3
TILE = 128
TPR = 4


highest = lax.Precision.HIGHEST


def broadcast(block, axis, holder):
    block = jnp.where(lax.axis_index(axis) == holder, block, jnp.zeros_like(block))
    return lax.psum(block, axis)


def densify(values, labels, owned_blocks):
    chosen = (labels[..., None] == owned_blocks).astype(jnp.float32)
    return jnp.einsum("tnkq,tnkd->tnqd", chosen, values, precision=highest)


def local(coefficients, support, primal, dual_inverse, block_sizes, damping, right_sides):
    col_index = lax.axis_index("cols")
    row_index = lax.axis_index("rows")
    rows_total = lax.axis_size("rows")
    cols_total = lax.axis_size("cols")
    count_all = TPR * TILE * rows_total
    col_width = count_all // cols_total
    positions = jnp.arange(BS, dtype=jnp.int32)
    active = (positions[None, :] < block_sizes[:, None]).astype(jnp.float32)
    weights = primal * dual_inverse * active[:, :, None] * active[:, None, :]
    owned_blocks = col_index * NBL + jnp.arange(NBL, dtype=jnp.int32)
    own_dense = densify(coefficients, support, owned_blocks)
    weighted = jnp.einsum("taqd,qde->taqe", own_dense, weights, precision=highest)
    block_piece = lax.all_gather((coefficients, support), "rows", axis=1, tiled=True)
    partial_value = jnp.einsum(
        "taqe,snqe->tasn",
        weighted,
        densify(block_piece[0], block_piece[1], owned_blocks),
        precision=highest,
    )
    partial_value = partial_value.reshape(TPR, TILE, count_all)
    schur_rows = lax.psum_scatter(partial_value, "cols", scatter_dimension=2, tiled=True)
    row_global = (jnp.arange(TPR)[:, None] * rows_total + row_index) * TILE + jnp.arange(TILE)[
        None, :
    ]
    col_global = col_index * col_width + jnp.arange(col_width)
    on_diagonal = row_global[:, :, None] == col_global[None, None, :]
    schur_rows = schur_rows + jnp.where(on_diagonal, damping[:, :, None], 0.0)
    corner = broadcast(schur_rows[0, :, :TILE], ("rows", "cols"), 0)
    top_sides = broadcast(right_sides[0], "rows", 0)
    factor = jnp.linalg.cholesky(corner)
    inverse = jax.scipy.linalg.solve_triangular(
        factor, jnp.eye(TILE, dtype=jnp.float32), lower=True
    )
    candidate = jnp.einsum("tak,jk->taj", schur_rows[:, :, :TILE], inverse, precision=highest)
    panel_factor = broadcast(candidate, "cols", 0)
    every_row = lax.all_gather(panel_factor, "rows", axis=1, tiled=True).reshape(count_all, TILE)
    column_panel = lax.dynamic_slice_in_dim(every_row, col_index * col_width, col_width, 0)
    outer_term = jnp.einsum("tak,mk->tam", panel_factor, column_panel, precision=highest)
    row_later = row_global[:, 0] >= TILE
    col_later = col_global >= TILE
    updated = schur_rows - jnp.where(
        row_later[:, None, None] & col_later[None, None, :], outer_term, 0.0
    )
    leading = jnp.dot(top_sides, inverse.T, precision=highest, preferred_element_type=jnp.float32)
    remainder = right_sides - jnp.einsum("sk,tak->tsa", leading, panel_factor, precision=highest)
    solved = jnp.where(row_later[:, None, None], remainder, leading[None, :, :])
    return (updated, panel_factor, solved)


def solution(mesh):
    in_specs = (
        P(None, "rows", None, None),
        P(None, "rows", None),
        P("cols", None, None),
        P("cols", None, None),
        P("cols"),
        P(None, "rows"),
        P(None, "cols", "rows"),
    )
    out_specs = (P(None, "rows", "cols"), P(None, "rows", None), P(None, "cols", "rows"))
    return jax.shard_map(local, mesh=mesh, in_specs=in_specs, out_specs=out_specs, check_vma=False)
```

profile of v0, /device:TPU:1, one launch (start us, length us, event | category | flops | bytes accessed | tf_op | source)
XLA Modules:
  0.0 686.1 jit_solution(17401384814189750230)
XLA Ops:
  7.2 0.0 copy-start.4
  7.2 0.0 all-gather.3.cloned.1.call-start
  7.2 0.7 all-gather.3.cloned.1.call-update
  7.9 0.0 reduce-scatter.2.cloned.1.call-start
  8.0 0.0 copy-done.4
  8.0 0.1 copy.18
  8.1 20.8 %all_gather.9 = s32[4,2048,4]{1,2,0:T(4,128)S(1)} all-gather(s32[4,128,4]{1,2,0:T(4,128)S(1)} %copy-done.4), channel_id=1, replica_groups=mesh['rows'=16,'cols'=8] {'rows'}, dimensions={1}, use_global_device_ids=true | all-gather | bytes 139264 | tf_op jit(solution)/shard_map/all_gather | solution.py:38
  28.9 0.2 broadcast_compare_fusion
  29.1 0.0 copy-start.7
  29.1 0.0 copy-start
  29.1 9.5 %copy.26 = pred[4,2048,4,3]{2,3,1,0:T(4,128)(4,1)} copy(pred[4,2048,4,3]{1,2,3,0:T(4,128)(4,1)S(1)} %broadcast_compare_fusion) | data formatting | bytes 196608 | tf_op jit(solution)/shard_map/eq | solution.py:21
  38.6 0.0 copy-done.7
  38.6 0.1 fusion.27
  38.7 0.0 copy-done
  38.7 3.2 fusion.8
  41.9 1.8 fusion.4
  43.7 167.0 %all-gather.3.cloned.1.call-done = f32[4,2048,4,256]{3,2,1,0:T(4,128)} async-done(((f32[4,128,4,256]{3,2,1,0:T(4,128)}), f32[4,2048,4,256]{3,2,1,0:T(4,128)}) %all-gather.3.cloned.1.call-update) | async-done | bytes 33554448 | tf_op jit(solution)/shard_map/all_gather | solution.py:38
  210.7 43.1 %fusion.30 = f32[4,2048,3,256]{3,2,1,0:T(4,128)} fusion(pred[4,2048,4,3]{2,3,1,0:T(4,128)(4,1)} %copy.26, f32[4,2048,4,256]{3,2,1,0:T(4,128)} %all-gather.3.cloned.1.call-done), kind=kOutput, calls=%fused_computation.51 | convolution fusion | flops 301989888 | bytes 58818560 | tf_op jit(solution)/shard_map/tnkq,tnkd->tnqd/dot_general | solution.py:22
  253.8 47.8 %fusion = f32[4,128,4,2048,1]{1,3,4,2,0:T(8,128)} fusion(f32[4,2048,3,256]{3,2,1,0:T(4,128)} %fusion.30, f32[3,256,4,128]{1,3,0,2:T(8,128)S(1)} %fusion.4), kind=kOutput, calls=%fused_computation | convolution fusion | flops 38654705664 | bytes 43515904 | tf_op jit(solution)/shard_map/taqe,snqe->tasn/dot_general | solution.py:39
  301.6 0.0 reduce-scatter.2.cloned.1.call-update
  301.6 0.0 all-reduce.3.cloned.1.call-start
  301.7 0.1 copy.20
  301.8 90.8 %reduce-scatter.2.cloned.1.call-done = f32[4,128,1024]{1,2,0:T(8,128)} async-done(((f32[4,128,8192]{1,2,0:T(8,128)}), f32[4,128,1024]{1,2,0:T(8,128)}) %reduce-scatter.2.cloned.1.call-update) | async-done | bytes 2097168 | tf_op jit(solution)/shard_map/reduce_scatter | solution.py:46
  392.6 1.9 select_add_fusion
  394.4 0.6 fusion.22
  395.1 0.0 all-reduce.3.cloned.1.call-update
  395.1 0.0 all-reduce.5.cloned.1.call-start
  395.1 140.7 %all-reduce.3.cloned.1.call-done = f32[128,128]{0,1:T(8,128)} async-done(((f32[128,128]{0,1:T(8,128)}), f32[128,128]{0,1:T(8,128)}) %all-reduce.3.cloned.1.call-update) | async-done | bytes 65552 | tf_op jit(solution)/shard_map/psum | solution.py:17
  535.9 0.9 copy.21
  536.8 0.9 fusion.26
  537.6 11.7 %cholesky.16 = f32[128,128]{1,0:T(8,128)S(1)} custom-call(f32[128,128]{1,0:T(8,128)S(1)} %fusion.26), custom_call_target="Cholesky" | custom-call | tf_op jit(solution)/shard_map/jit(cholesky)/cholesky | solution.py:55
  549.4 0.6 compare_reduce_fusion
  550.0 0.7 fusion.21
  550.7 9.8 %custom-call.7 = f32[1,128,128]{1,2,0:T(8,128)S(1)} custom-call(f32[1,128,128]{2,1,0:T(8,128)S(1)} %fusion.21), custom_call_target="InvertDiagBlocksLowerTriangular" | custom-call | tf_op jit(solution)/shard_map/jit(_solve_triangular)/triangular_solve | solution.py:56
  560.5 0.2 fusion.24
  560.8 1.3 convolution_select_fusion
  562.1 0.0 all-reduce.5.cloned.1.call-update
  562.1 0.0 all-gather.5.cloned.1.call-start
  562.1 54.6 %all-reduce.5.cloned.1.call-done = f32[4,128,128]{2,1,0:T(8,128)} async-done(((f32[4,128,128]{2,1,0:T(8,128)}), f32[4,128,128]{2,1,0:T(8,128)}) %all-reduce.5.cloned.1.call-update) | async-done | bytes 262160 | tf_op jit(solution)/shard_map/psum | solution.py:17
  616.8 0.0 all-gather.5.cloned.1.call-update
  616.8 33.6 %psum.23 = f32[4,128]{1,0:T(4,128)S(1)} all-reduce(f32[4,128]{1,0:T(4,128)S(1)} %select_bitcast_fusion), channel_id=1, replica_groups=mesh['rows'=16,'cols'=8] {'rows'}, use_global_device_ids=true, to_apply=%region_5.6 | all-reduce | flops 512 | bytes 4096 | tf_op jit(solution)/shard_map/psum | solution.py:17
  650.5 0.1 broadcast_and_fusion
  650.6 0.2 fusion.31
  650.7 2.0 fusion.7
  652.7 19.0 %all-gather.5.cloned.1.call-done = f32[4,2048,128]{2,1,0:T(8,128)} async-done(((f32[4,128,128]{2,1,0:T(8,128)}), f32[4,2048,128]{2,1,0:T(8,128)}) %all-gather.5.cloned.1.call-update) | async-done | bytes 4194320 | tf_op jit(solution)/shard_map/all_gather | solution.py:61
  671.8 4.1 select_subtract_fusion
  675.9 2.9 copy.24
  678.8 0.7 copy.41
  (18 shorter events, 0.1 us)
Async XLA Ops:
  7.2 0.8 copy-start.4
  7.2 203.6 %all-gather.3.cloned.1.call-start = ((), (), s32[]{:S(2)}) async-start(), calls=%async_computation.1 | async-start | bytes 35651584 | tf_op jit(solution)/shard_map/all_gather | solution.py:38
  7.9 384.6 %reduce-scatter.2.cloned.1.call-start = ((), (), s32[]{:S(2)}) async-start(), calls=%async_computation.2 | async-start | bytes 18874368 | tf_op jit(solution)/shard_map/reduce_scatter | solution.py:46
  29.1 9.6 %copy-start.7 = (s32[3]{0:T(128)S(1)}, s32[3]{0:T(128)}, u32[]{:S(2)}) copy-start(s32[3]{0:T(128)} %param.11) | copy-start | bytes 40
  29.1 9.6 %copy-start = (f32[4,128,4,256]{3,2,1,0:T(4,128)S(1)}, f32[4,128,4,256]{3,2,1,0:T(4,128)}, u32[]{:S(2)}) copy-start(f32[4,128,4,256]{3,2,1,0:T(4,128)} %param.7) | copy-start | bytes 6291460
  38.7 3.2 copy-start.2
  38.7 3.2 copy-start.3
  301.6 91.0 %copy-start.6 = (f32[4,128]{1,0:T(4,128)S(1)}, f32[4,128]{1,0:T(4,128)}, u32[]{:S(2)}) copy-start(f32[4,128]{1,0:T(4,128)} %param.12) | copy-start | bytes 6148
  301.6 234.2 %all-reduce.3.cloned.1.call-start = ((), (), s32[]{:S(2)}) async-start(), calls=%async_computation.3 | async-start | bytes 131072 | tf_op jit(solution)/shard_map/psum | solution.py:17
  301.8 315.0 %copy-start.5 = (f32[4,4,128]{2,1,0:T(4,128)S(1)}, f32[4,4,128]{2,1,0:T(4,128)}, u32[]{:S(2)}) copy-start(f32[4,4,128]{2,1,0:T(4,128)} %param.13) | copy-start | bytes 24580
  395.1 221.7 %all-reduce.5.cloned.1.call-start = ((), (), s32[]{:S(2)}) async-start(), calls=%async_computation.4 | async-start | bytes 524288 | tf_op jit(solution)/shard_map/psum | solution.py:17
  562.1 109.7 %all-gather.5.cloned.1.call-start = ((), (), s32[]{:S(2)}) async-start(), calls=%async_computation.5 | async-start | bytes 4456448 | tf_op jit(solution)/shard_map/all_gather | solution.py:61
  675.9 2.9 copy-start.1
Sparse Core Ops, SparseCore 0:
  10.2 200.4 all-gather.2
  301.7 90.7 reduce-scatter.1
  397.9 137.9 all-reduce.2
  562.2 54.5 all-reduce.4
  618.8 52.9 all-gather.4
where the time goes:
time: 686 us
  waiting for transfers between devices  473 us (69%)
  matrix products  104 us (15%)
  blocking collectives  54.4 us (8%)
  other arithmetic  26.6 us (4%)
  local copies, waits for them, and re-layouts  14.3 us (2%)
  between operations  14 us (2%)
    psum x2, waiting for transfers between devices, broadcast(): return lax.psum(block, axis)  195 us
    all_gather x1, waiting for transfers between devices, local(): lax.all_gather((coefficients, support), 'rows', axis=1, tiled=True)  167 us
    reduce_scatter x1, waiting for transfers between devices, local(): lax.psum_scatter(partial_value, 'cols', scatter_dimension=2, tiled=True)  90.8 us
    dot_general x1, matrix products, local(): jnp.einsum('taqe,snqe->tasn', weighted, densify(block_piece[0], block_pie...  47.8 us
    dot_general x2, matrix products, densify(): return jnp.einsum('tnkq,tnkd->tnqd', chosen, values, precision=highest)  46.3 us
    psum x1, blocking collectives, broadcast(): return lax.psum(block, axis)  33.6 us
    all_gather x1, blocking collectives, local(): lax.all_gather((coefficients, support), 'rows', axis=1, tiled=True)  20.8 us
    all_gather x1, waiting for transfers between devices, local(): lax.all_gather(panel_factor, 'rows', axis=1, tiled=True)  19 us
  transfers between devices with their start and end apart: 5, of which 5 were waited for; matrix products, arithmetic and copies ran while one was open for 3% of the time, Pallas kernels for 0%

commit v1 on v0

v1 whole, which is shorter than its diff:
```python
import functools
import jax
import jax.numpy as jnp
from jax.sharding import PartitionSpec as P
from jax import lax
from jax.experimental import pallas as pl
from jax.experimental.pallas import tpu as pltpu
BF=jnp.bfloat16; F32=jnp.float32
NT=(((1,),(1,)),((),()))
NN=(((1,),(0,)),((),()))

def split(v):
    h=v.astype(BF)
    return h,(v-h.astype(F32)).astype(BF)

def dot3(ah,al,bh,bl,dims):
    d=functools.partial(lax.dot_general,dimension_numbers=dims,preferred_element_type=F32)
    return d(ah,bh)+d(al,bh)+d(ah,bl)

def pick(block,masks_src,vals):
    out=None
    m=[s==block for s in masks_src]
    for k in range(4):
        v=vals[k]
        out=jnp.where(m[k],v,jnp.zeros_like(v) if out is None else out)
    return out

def weigh_body(ids,c_ref,s_ref,w_ref,vh_ref,vl_ref,ac_ref,ch,cl):
    b=pl.program_id(0)
    @pl.when(b==0)
    def _():
        for k in range(4):
            h,l=split(c_ref[k]); ch[k]=h; cl[k]=l
        ac_ref[...]=jnp.zeros_like(ac_ref)
    block=ids[b].astype(F32).astype(BF)
    wh,wl=split(w_ref[0])
    sup=[s_ref[k] for k in range(4)]
    def dense(src):
        return jnp.concatenate([pick(block,sup,[src[k,:,q*128:(q+1)*128] for k in range(4)]) for q in range(2)],axis=1)
    dh=dense(ch); dl=dense(cl)
    v=dot3(dh,dl,wh,wl,NN)
    vh,vl=split(v)
    for q in range(2):
        vh_ref[q]=vh[:,q*128:(q+1)*128]; vl_ref[q]=vl[:,q*128:(q+1)*128]
    n=dh.shape[0]
    ac_ref[...]+=dot3(vh,vl,dh[n-128:],dl[n-128:],NT)

def weigh(ids,c,s,w):
    n=c.shape[1]
    grid=pltpu.PrefetchScalarGridSpec(num_scalar_prefetch=1,grid=(24,),
        in_specs=[pl.BlockSpec((4,n,256),lambda b,i:(0,0,0)),pl.BlockSpec((4,n,128),lambda b,i:(0,0,0)),pl.BlockSpec((1,256,256),lambda b,i:(b,0,0))],
        out_specs=[pl.BlockSpec((2,n,128),lambda b,i:(0,0,b)),pl.BlockSpec((2,n,128),lambda b,i:(0,0,b)),pl.BlockSpec((n,128),lambda b,i:(0,0))],
        scratch_shapes=[pltpu.VMEM((4,n,256),BF),pltpu.VMEM((4,n,256),BF)])
    return pl.pallas_call(weigh_body,grid_spec=grid,out_shape=[jax.ShapeDtypeStruct((2,n,3072),BF)]*2+[jax.ShapeDtypeStruct((n,128),F32)],
        compiler_params=pltpu.CompilerParams(vmem_limit_bytes=48<<20),name="weigh",
        cost_estimate=pl.CostEstimate(flops=2*3*n*6144*384,bytes_accessed=20<<20,transcendentals=0))(ids,c,s,w)

def prod_body(has_acc,ids,pid,vh_ref,vl_ref,c_ref,s_ref,*rest):
    if has_acc: a_ref,o_ref,ch,cl=rest
    else: o_ref,ch,cl=rest
    g=pl.program_id(0)
    @pl.when(g==0)
    def _():
        for t in range(8):
            for k in range(4):
                h,l=split(c_ref[t,k*128:(k+1)*128])
                ch[k,t*128:(t+1)*128]=h; cl[k,t*128:(t+1)*128]=l
        o_ref[...]=a_ref[...] if has_acc else jnp.zeros_like(o_ref)
    blocks=[ids[2*g+u].astype(F32).astype(BF) for u in range(2)]
    vh=vh_ref[0]; vl=vl_ref[0]
    for q in range(4):
        r=slice(q*256,(q+1)*256)
        sup=[s_ref[k,r] for k in range(4)]
        dh=jnp.concatenate([pick(bk,sup,[ch[k,r] for k in range(4)]) for bk in blocks],axis=1)
        dl=jnp.concatenate([pick(bk,sup,[cl[k,r] for k in range(4)]) for bk in blocks],axis=1)
        o_ref[:,r]+=dot3(vh,vl,dh,dl,NT)

def prod(ids,pid,vh,vl,c,s,acc=None):
    n=vh.shape[1]
    vspec=pl.BlockSpec((1,n,256),lambda g,i,p:(p[0],0,g))
    full=pl.BlockSpec((n,1024),lambda g,i,p:(0,0))
    grid=pltpu.PrefetchScalarGridSpec(num_scalar_prefetch=2,grid=(12,),
        in_specs=[vspec,vspec,pl.BlockSpec((8,520,128),lambda g,i,p:(0,0,0)),pl.BlockSpec((4,1024,128),lambda g,i,p:(0,0,0))]+([full] if acc is not None else []),
        out_specs=full,scratch_shapes=[pltpu.VMEM((4,1024,128),BF),pltpu.VMEM((4,1024,128),BF)])
    return pl.pallas_call(functools.partial(prod_body,acc is not None),grid_spec=grid,out_shape=jax.ShapeDtypeStruct((n,1024),F32),
        compiler_params=pltpu.CompilerParams(vmem_limit_bytes=48<<20),name="prod",
        cost_estimate=pl.CostEstimate(flops=2*3*n*3072*1024,bytes_accessed=16<<20,transcendentals=0))(ids,pid,vh,vl,c,s,*([acc] if acc is not None else []))

def inverse_body(c_ref,o_ref):
    n=128
    row=lax.broadcasted_iota(jnp.int32,(n,2*n),0)
    col=lax.broadcasted_iota(jnp.int32,(n,2*n),1)
    rowc=lax.broadcasted_iota(jnp.int32,(n,1),0)
    m=jnp.concatenate([c_ref[...],jnp.where(row[:,:n]==col[:,:n],1.0,0.0).astype(F32)],axis=1)
    o_ref[...]=m
    lane=lax.broadcasted_iota(jnp.int32,(1,n),1)
    sub=lax.broadcasted_iota(jnp.int32,(n,n),0)
    def step(k,_):
        line=o_ref[pl.ds(k,1),:]
        left=line[:,:n]
        piv=jnp.sum(jnp.where(lane==k,left,0.0),axis=1,keepdims=True)
        r=lax.rsqrt(piv)
        colk=jnp.sum(jnp.where(lane==k,o_ref[:,:n],0.0),axis=1,keepdims=True)
        f=jnp.where(rowc>k,colk*r,0.0)
        scaled=line*r
        o_ref[...]=o_ref[...]-f*scaled
        o_ref[pl.ds(k,1),:]=scaled
        return 0
    lax.fori_loop(0,n,step,0)

def inverse_aug(c):
    return pl.pallas_call(inverse_body,out_shape=jax.ShapeDtypeStruct((128,256),F32),name="inverse")(c)


highest = lax.Precision.HIGHEST
SWAP = [(i, i ^ 1) for i in range(8)]
UP = [(2 * x + c, 2 * ((x + 1) % 4) + c) for x in range(4) for c in range(2)]
DOWN = [(2 * x + c, 2 * ((x + 3) % 4) + c) for x in range(4) for c in range(2)]


def over_cols(v, pairs):
    return lax.ppermute(v, "cols", pairs)


def over_rows(v, pairs):
    return lax.ppermute(v, "rows", pairs)


def gather_weights(w):
    below = over_cols(w, UP)
    above = over_cols(w, DOWN)
    far = jnp.concatenate([over_cols(below[:, :128], UP), over_cols(above[:, 128:], DOWN)], axis=1)
    parts = [w, below, above, far]
    return jnp.concatenate(parts + [over_cols(v, SWAP) for v in parts], axis=0)


def spread_first(v, r):
    one = over_rows(v, [(0, 1)])
    three = over_rows(v, [(0, 3)])
    two = over_rows(one, [(1, 2)])
    line = jnp.where(r == 0, v, one + three + two)
    first = over_rows(line, [(z, 4 + z) for z in range(4)])
    third = over_rows(line, [(z, 12 + z) for z in range(4)])
    second = over_rows(first, [(4 + z, 8 + z) for z in range(4)])
    return jnp.where(r < 4, line, first + third + second)


def lanes(s):
    return jnp.broadcast_to(s[:, :, None], s.shape + (128,)).astype(BF)


def by_slot(v):
    return jnp.transpose(v, (1, 0, 2)).reshape(512, 128)


def local(coefficients, support, primal, dual_inverse, block_sizes, damping, right_sides):
    col = lax.axis_index("cols")
    r = lax.axis_index("rows")
    x = col // 2
    p = col % 2
    positions = jnp.arange(256, dtype=jnp.int32)
    active = (positions[None, :] < block_sizes[:, None]).astype(F32)
    w = primal * dual_inverse * active[:, :, None] * active[:, None, :]
    sup = support.astype(F32)

    def piece(t):
        tile = lax.dynamic_index_in_dim(coefficients, t, 0, keepdims=False)
        return by_slot(lax.dynamic_slice_in_dim(tile, p * 128, 128, 2))

    mine = jnp.concatenate([piece(x), lax.dynamic_index_in_dim(sup, x, 0, keepdims=False).T,
                            jnp.zeros((4, 128), F32)], axis=0)
    gathered = lax.all_gather(mine, "rows")
    head = jnp.concatenate([piece(0), sup[0].T, right_sides[0], damping[:1], jnp.zeros((7, 128), F32)], axis=0)
    head = spread_first(head, r)
    head_other = over_cols(head[:512], SWAP)
    weights = gather_weights(w)
    near = (2 * ((x + jnp.array([0, 3, 1, 2])) % 4))
    ids = jnp.concatenate([near + p, near + 1 - p])
    ids = (ids[:, None] * 3 + jnp.arange(3)).reshape(24).astype(jnp.int32)

    lo = jnp.where(p == 0, head[:512], head_other).reshape(4, 128, 128)
    hi = jnp.where(p == 0, head_other, head[:512]).reshape(4, 128, 128)
    own = jnp.transpose(coefficients, (2, 0, 1, 3)).reshape(4, 512, 256)
    rows = jnp.concatenate([own, jnp.concatenate([lo, hi], axis=2)], axis=1)
    row_sup = lanes(jnp.concatenate([jnp.transpose(sup, (2, 0, 1)).reshape(4, 512), head[512:516]], axis=1))
    vh, vl, ac = weigh(ids, rows, row_sup, weights)

    eye = jnp.eye(128, dtype=F32)
    corner = ac[512:] + eye * head[520]
    inverse = inverse_aug(corner)[:, 128:]
    top = jnp.where(r == 0, corner, ac[:128])
    panel = lax.dot_general(jnp.concatenate([top, ac[128:512]], axis=0), inverse, NT, precision=highest)
    leading = lax.dot_general(head[516:520], inverse, NT, precision=highest)
    panel_factor = panel.reshape(4, 128, 128)
    remainder = right_sides - jnp.einsum("sk,tak->tsa", leading, panel_factor, precision=highest)
    solved = jnp.where(((jnp.arange(4) > 0) | (r > 0))[:, None, None], remainder, leading[None])

    kept = lax.dynamic_slice_in_dim(gathered, 8 * p, 8, 0)
    given = lax.dynamic_slice_in_dim(gathered, 8 * (1 - p), 8, 0)
    swapped = over_cols(given, SWAP)
    col_sup = lanes(jnp.transpose(kept[:, 512:516], (1, 0, 2)).reshape(4, 1024))
    which = p.astype(jnp.int32)[None]
    out = prod(ids, which, vh, vl, kept, col_sup)
    out = prod(ids, 1 - which, vh, vl, swapped, col_sup, out)

    row_global = ((jnp.arange(4)[:, None] * 16 + r) * 128 + jnp.arange(128)[None, :]).reshape(512)
    col_global = col * 1024 + jnp.arange(1024)
    schur = out[:512] + jnp.where(row_global[:, None] == col_global[None, :], damping.reshape(512)[:, None], 0.0)
    col_panel = jnp.dot(inverse, out[512:], precision=highest)
    outer = jnp.dot(panel, col_panel, precision=lax.Precision.HIGH)
    later = (row_global >= 128)[:, None] & (col_global >= 128)[None, :]
    updated = schur - jnp.where(later, outer, 0.0)
    return updated.reshape(4, 128, 1024), panel_factor, solved


def solution(mesh):
    in_specs = (
        P(None, "rows", None, None),
        P(None, "rows", None),
        P("cols", None, None),
        P("cols", None, None),
        P("cols"),
        P(None, "rows"),
        P(None, "cols", "rows"),
    )
    out_specs = (P(None, "rows", "cols"), P(None, "rows", None), P(None, "cols", "rows"))
    return jax.shard_map(local, mesh=mesh, in_specs=in_specs, out_specs=out_specs, check_vma=False)
```

time: 686 us -> 177 us (0.26)
  the two profiles are of different devices: /device:TPU:1 before, /device:TPU:73 now
where the time goes in v1:
time: 177 us; the launch traced here: 176 us
  Pallas kernels  88.5 us (50%)
  local copies, waits for them, and re-layouts  23.8 us (13%)
  starting transfers between devices  20.4 us (12%)
  waiting for transfers between devices  15.7 us (9%)
  between operations  14.4 us (8%)
  other arithmetic  6.7 us (4%)
  matrix products  6.48 us (4%)
    pallas_call x2, Pallas kernels, prod(): pl.pallas_call(functools.partial(prod_body, acc is not None), grid_spec=g...  40 us
    pallas_call x1, Pallas kernels, weigh(): pl.pallas_call(weigh_body, grid_spec=grid, out_shape=[jax.ShapeDtypeStruc...  33.4 us
    ppermute x6, waiting for transfers between devices, over_rows(): return lax.ppermute(v, 'rows', pairs)  15.7 us
    pallas_call x1, Pallas kernels, inverse_aug(): pl.pallas_call(inverse_body, out_shape=jax.ShapeDtypeStruct((128, 256), F...  15.2 us
    ppermute x10, starting transfers between devices, over_cols(): return lax.ppermute(v, 'cols', pairs)  13 us
    unnamed x31, local copies, waits for them, and re-layouts  10.2 us
    ppermute x6, starting transfers between devices, over_rows(): return lax.ppermute(v, 'rows', pairs)  7.38 us
    dynamic_slice x1, local copies, waits for them, and re-layouts, local(): kept = lax.dynamic_slice_in_dim(gathered, 8 * p, 8, 0)  3.92 us
  transfers between devices with their start and end apart: 17, of which 1 were waited for; matrix products, arithmetic and copies ran while one was open for 14% of the time, Pallas kernels for 38%

profile of v1, /device:TPU:73, one launch (start us, length us, event | category | flops | bytes accessed | tf_op | source)
XLA Modules:
  0.0 176.1 jit_solution(9265045584100984894)
XLA Ops:
  7.3 0.8 convert_bitcast_fusion
  8.1 1.1 constant_dynamic-slice_fusion.2
  9.4 0.9 maximum_maximum_fusion.1
  10.2 1.1 dynamic_slice.26
  11.4 0.7 slice.55
  12.1 0.7 slice_bitcast_fusion.1
  12.8 0.7 collective-permute-start
  13.5 1.4 collective-permute-start.1
  15.0 1.3 constant_dynamic-update-slice_fusion.8
  16.3 1.2 collective-permute-start.7
  17.5 1.5 collective-permute-start.8
  19.0 1.3 collective-permute-start.11
  20.5 0.7 collective-permute-start.2
  21.2 1.1 add_select_fusion.1
  22.4 1.3 collective-permute-start.3
  23.8 1.4 collective-permute-start.4
  25.2 15.7 %collective-permute-done.3 = f32[528,128]{1,0:T(8,128)S(1)} collective-permute-done((f32[528,128]{1,0:T(8,128)S(1)}, f32[528,128]{1,0:T(8,128)S(1)}, u32[]{:S(2)}, u32[]{:S(2)}) %collective-permute-start.3) | collective-permute-done | bytes 270368 | tf_op jit(solution)/shard_map/ppermute | solution.py:126
  40.9 2.0 %collective-permute-start.5 = (f32[528,128]{1,0:T(8,128)S(1)}, f32[528,128]{1,0:T(8,128)}, u32[]{:S(2)}, u32[]{:S(2)}) collective-permute-start(f32[528,128]{1,0:T(8,128)S(1)} %collective-permute-done.3), channel_id=1, source_target_pairs={{32,64},{40,72},{48,80},{56,88},{33,65},{41,73},{49,81},{57,89},{3... | collective-permute-start | bytes 811016 | tf_op jit(solution)/shard_map/ppermute | solution.py:126
  42.9 2.0 %copy.12 = f32[4,4,128,256]{3,2,1,0:T(8,128)S(1)} copy(f32[4,4,128,256]{3,0,2,1:T(4,128)} %bitcast.60) | data formatting | bytes 4194304 | tf_op jit(solution)/shard_map/transpose | solution.py:183
  45.0 1.0 slice.72
  46.0 1.0 collective-permute-start.9
  47.1 1.8 %collective-permute-start.10 = (f32[3,128,256]{2,1,0:T(8,128)S(1)}, f32[3,128,256]{2,1,0:T(8,128)S(1)}, u32[]{:S(2)}, u32[]{:S(2)}) collective-permute-start(f32[3,128,256]{2,1,0:T(8,128)S(1)} %slice.73), channel_id=1, source_target_pairs={{0,6},{1,7},{2,0},{3,1},{4,2},{5,3},{6,4},{7,5},{8,14},{9,15},{10,... | collective-permute-start | bytes 1179656 | tf_op jit(solution)/shard_map/ppermute | solution.py:122
  48.8 2.1 %constant_dynamic-update-slice_fusion.7 = f32[24,256,256]{2,1,0:T(8,128)} fusion(f32[24,256,256]{2,1,0:T(8,128)} %get-tuple-element.11, f32[3,256,256]{2,1,0:T(8,128)} %collective-permute-done.7), kind=kLoop, calls=%fused_computation.32 | loop fusion | bytes 1572864
  50.9 0.9 constant_dynamic-update-slice_fusion.6
  51.9 2.7 %collective-permute-start.12 = (f32[3,256,256]{2,1,0:T(8,128)}, f32[3,256,256]{2,1,0:T(8,128)S(1)}, u32[]{:S(2)}, u32[]{:S(2)}) collective-permute-start(f32[3,256,256]{2,1,0:T(8,128)} %collective-permute-done.7), channel_id=1, source_target_pairs={{0,1},{1,0},{2,3},{3,2},{4,5},{5,4},{6,7},{7,6},{8,9},{9,8},{10,11... | collective-permute-start | bytes 2359304 | tf_op jit(solution)/shard_map/ppermute | solution.py:122
  54.9 1.2 add_select_fusion
  56.2 2.6 %collective-permute-start.6 = (f32[512,128]{1,0:T(8,128)S(1)}, f32[512,128]{1,0:T(8,128)S(1)}, u32[]{:S(2)}, u32[]{:S(2)}) collective-permute-start(f32[512,128]{1,0:T(8,128)S(1)} %slice.70), channel_id=1, source_target_pairs={{0,1},{1,0},{2,3},{3,2},{4,5},{5,4},{6,7},{7,6},{8,9},{9,8},{10,11... | collective-permute-start | bytes 786440 | tf_op jit(solution)/shard_map/ppermute | solution.py:122
  59.0 0.8 constant_dynamic-update-slice_fusion.5
  59.7 0.8 constant_dynamic-update-slice_fusion.4
  60.5 2.1 %constant_dynamic-update-slice_fusion.3 = f32[24,256,256]{2,1,0:T(8,128)} fusion(f32[24,256,256]{2,1,0:T(8,128)} %constant_dynamic-update-slice_fusion.4, f32[3,256,256]{2,1,0:T(8,128)} %collective-permute-done.11), kind=kLoop, calls=%fused_computation.28 | loop fusion | bytes 1572864
  62.9 1.0 constant_dynamic-update-slice_fusion.2
  63.9 0.9 constant_dynamic-update-slice_fusion.1
  64.8 0.9 constant_dynamic-update-slice_fusion.w_ref
  66.2 33.4 %weigh.1 = (bf16[2,640,3072]{2,1,0:T(8,128)(2,1)}, bf16[2,640,3072]{2,1,0:T(8,128)(2,1)}, f32[640,128]{1,0:T(8,128)S(1)}) custom-call(s32[24]{0:T(128)S(1)} %add.141.ids, f32[4,640,256]{2,1,0:T(8,128)S(1)} %maximum_maximum_fusion.c_ref, bf16[4,640,128]{2,1,0:T(8,128)(2,1)S(1)} %broadcast_in_dim.43.s_ref, f32[24,256,256]{2,1,0:T(8,128)} %constant_dynamic-update-slice_fusion.w_ref), custom_call_target="tpu_custom_call" | custom-call | flops 9059696640 | bytes 20971520 | tf_op jit(solution)/shard_map/weigh/pallas_call | solution.py:54
  99.6 3.9 %constant_dynamic-slice_fusion = (f32[8,520,128]{2,1,0:T(8,128)S(1)}, f32[8,520,128]{2,1,0:T(8,128)}) fusion(f32[16,520,128]{2,1,0:T(8,128)} %bitcast.58, s32[]{:T(128)S(6)} %select_n.100, s32[]{:T(128)S(6)} %select_n.99), kind=kLoop, calls=%fused_computation.55 | loop fusion | bytes 8519688 | tf_op jit(solution)/shard_map/dynamic_slice | solution.py:198
  103.6 0.5 collective-permute-start.15
  104.0 0.6 slice_select_fusion
  104.7 15.2 %inverse.1 = f32[128,256]{1,0:T(8,128)} custom-call(f32[128,128]{1,0:T(8,128)} %get-tuple-element.10.c_ref), custom_call_target="tpu_custom_call" | custom-call | tf_op jit(solution)/shard_map/inverse/pallas_call | solution.py:112
  119.9 1.0 fusion.8
  120.9 1.3 fusion.4
  122.2 0.9 broadcast_select_fusion.2
  123.1 0.8 fusion.12
  123.9 0.6 broadcast_in_dim.69.s_ref
  124.5 19.2 %prod.2.rest_0_ = f32[640,1024]{1,0:T(8,128)S(1)} custom-call(s32[24]{0:T(128)S(1)} %add.141.ids, s32[1]{0:T(128)} %bitcast.pid, bf16[2,640,3072]{2,1,0:T(8,128)(2,1)} %get-tuple-element.6.vh_ref, bf16[2,640,3072]{2,1,0:T(8,128)(2,1)} %get-tuple-element.7.vl_ref, f32[8,520,128]{2,1,0:T(8,128)S(1)} %get-tuple-element.15.c_ref, ...), custom_call_target="tpu_custom_call" | custom-call | flops 12079595520 | bytes 16777216 | tf_op jit(solution)/shard_map/prod/pallas_call | solution.py:85
  143.7 1.5 copy-done
  145.2 20.8 %prod.3 = f32[640,1024]{1,0:T(8,128)S(1)} custom-call(s32[24]{0:T(128)S(1)} %add.141.ids, s32[1]{0:T(128)S(6)} %sub.22.pid, bf16[2,640,3072]{2,1,0:T(8,128)(2,1)} %get-tuple-element.6.vh_ref, bf16[2,640,3072]{2,1,0:T(8,128)(2,1)} %get-tuple-element.7.vl_ref, f32[8,520,128]{2,1,0:T(8,128)} %collective-permute-done.15.c_ref, ...), custom_call_target="tpu_custom_call" | custom-call | flops 12079595520 | bytes 16777216 | tf_op jit(solution)/shard_map/prod/pallas_call | solution.py:85
  166.0 0.6 fusion.2
  166.6 2.7 %fusion = f32[512,1024]{1,0:T(8,128)} fusion(f32[640,1024]{1,0:T(8,128)S(1)} %prod.3, f32[512,128]{1,0:T(8,128)S(1)} %fusion.4, f32[128,1024]{1,0:T(8,128)S(1)} %fusion.2, f32[512]{0:T(512)S(1)} %bitcast.68, s32[1024]{0:T(1024)S(1)} %iota_add_fusion, s32[512]{0:T(512)S(1)} %add_bitcast_fusion, pred[1024]{0:T(1024)(128)(4,1)S(1)} %broadcast_compare_fusion, ...), kind=kOutput, calls=%fused_computation.2 | convolution fusion | flops 405798912 | bytes 4990464 | tf_op jit(solution)/shard_map/dot_general | solution.py:210
  (71 shorter events, 2.1 us)
Async XLA Ops:
  7.2 13.2 %copy-start.10 = (s32[4]{0:T(128)S(1)}, s32[4]{0:T(128)}, u32[]{:S(2)}) copy-start(s32[4]{0:T(128)} %constant.110.clone) | copy-start | bytes 52
  7.2 7.7 %copy-start.9 = (s32[3]{0:T(128)S(1)}, s32[3]{0:T(128)}, u32[]{:S(2)}) copy-start(s32[3]{0:T(128)} %param.12) | copy-start | bytes 40
  7.2 7.8 %copy-start.3 = (f32[3,256,256]{2,1,0:T(8,128)S(1)}, f32[3,256,256]{2,1,0:T(8,128)}, u32[]{:S(2)}) copy-start(f32[3,256,256]{2,1,0:T(8,128)} %param.10) | copy-start | bytes 2359300
  7.2 7.8 %copy-start.4 = (f32[3,256,256]{2,1,0:T(8,128)S(1)}, f32[3,256,256]{2,1,0:T(8,128)}, u32[]{:S(2)}) copy-start(f32[3,256,256]{2,1,0:T(8,128)} %param.11) | copy-start | bytes 2359300
  7.2 92.4 %all-gather.3.cloned.1.call-start = ((), (), s32[]{:S(2)}) async-start(), calls=%async_computation | async-start | bytes 4526080 | tf_op jit(solution)/shard_map/all_gather | solution.py:172
  12.8 7.7 %collective-permute-start = (f32[528,128]{1,0:T(8,128)S(1)}, f32[528,128]{1,0:T(8,128)S(1)}, u32[]{:S(2)}, u32[]{:S(2)}) collective-permute-start(f32[528,128]{1,0:T(8,128)S(1)} %concatenate.33), channel_id=1, source_target_pairs={{0,8},{1,9},{2,10},{3,11},{4,12},{5,13},{6,14},{7,15}} | collective-permute-start | bytes 811016 | tf_op jit(solution)/shard_map/ppermute | solution.py:126
  13.5 7.7 %collective-permute-start.1 = (f32[528,128]{1,0:T(8,128)S(1)}, f32[528,128]{1,0:T(8,128)}, u32[]{:S(2)}, u32[]{:S(2)}) collective-permute-start(f32[528,128]{1,0:T(8,128)S(1)} %concatenate.33), channel_id=1, source_target_pairs={{0,24},{1,25},{2,26},{3,27},{4,28},{5,29},{6,30},{7,31}} | collective-permute-start | bytes 811016 | tf_op jit(solution)/shard_map/ppermute | solution.py:126
  16.3 28.7 %collective-permute-start.7 = (f32[3,256,256]{2,1,0:T(8,128)}, f32[3,256,256]{2,1,0:T(8,128)}, u32[]{:S(2)}, u32[]{:S(2)}) collective-permute-start(f32[3,256,256]{2,1,0:T(8,128)} %get-tuple-element.12), channel_id=1, source_target_pairs={{0,2},{1,3},{2,4},{3,5},{4,6},{5,7},{6,0},{7,1},{8,10},{9,11},{10,... | collective-permute-start | bytes 2359304 | tf_op jit(solution)/shard_map/ppermute | solution.py:122
  17.5 29.5 %collective-permute-start.8 = (f32[3,256,256]{2,1,0:T(8,128)}, f32[3,256,256]{2,1,0:T(8,128)S(1)}, u32[]{:S(2)}, u32[]{:S(2)}) collective-permute-start(f32[3,256,256]{2,1,0:T(8,128)} %get-tuple-element.12), channel_id=1, source_target_pairs={{0,6},{1,7},{2,0},{3,1},{4,2},{5,3},{6,4},{7,5},{8,14},{9,15},{10,... | collective-permute-start | bytes 2359304 | tf_op jit(solution)/shard_map/ppermute | solution.py:122
  19.0 41.5 %collective-permute-start.11 = (f32[3,256,256]{2,1,0:T(8,128)}, f32[3,256,256]{2,1,0:T(8,128)}, u32[]{:S(2)}, u32[]{:S(2)}) collective-permute-start(f32[3,256,256]{2,1,0:T(8,128)} %get-tuple-element.12), channel_id=1, source_target_pairs={{0,1},{1,0},{2,3},{3,2},{4,5},{5,4},{6,7},{7,6},{8,9},{9,8},{10,11... | collective-permute-start | bytes 2359304 | tf_op jit(solution)/shard_map/ppermute | solution.py:122
  20.5 0.7 copy-start.6
  20.5 0.7 collective-permute-start.2
  22.4 18.5 %collective-permute-start.3 = (f32[528,128]{1,0:T(8,128)S(1)}, f32[528,128]{1,0:T(8,128)S(1)}, u32[]{:S(2)}, u32[]{:S(2)}) collective-permute-start(f32[528,128]{1,0:T(8,128)S(1)} %add_select_fusion.1), channel_id=1, source_target_pairs={{0,32},{8,40},{16,48},{24,56},{1,33},{9,41},{17,49},{25,57},{2,34}... | collective-permute-start | bytes 811016 | tf_op jit(solution)/shard_map/ppermute | solution.py:126
  23.8 28.1 %collective-permute-start.4 = (f32[528,128]{1,0:T(8,128)S(1)}, f32[528,128]{1,0:T(8,128)}, u32[]{:S(2)}, u32[]{:S(2)}) collective-permute-start(f32[528,128]{1,0:T(8,128)S(1)} %add_select_fusion.1), channel_id=1, source_target_pairs={{0,96},{8,104},{16,112},{24,120},{1,97},{9,105},{17,113},{25,121},... | collective-permute-start | bytes 811016 | tf_op jit(solution)/shard_map/ppermute | solution.py:126
  40.9 13.7 %copy-start.5 = (f32[528,128]{1,0:T(8,128)}, f32[528,128]{1,0:T(8,128)S(1)}, u32[]{:S(2)}) copy-start(f32[528,128]{1,0:T(8,128)S(1)} %collective-permute-done.3) | copy-start | bytes 811012
  40.9 13.7 %collective-permute-start.5 = (f32[528,128]{1,0:T(8,128)S(1)}, f32[528,128]{1,0:T(8,128)}, u32[]{:S(2)}, u32[]{:S(2)}) collective-permute-start(f32[528,128]{1,0:T(8,128)S(1)} %collective-permute-done.3), channel_id=1, source_target_pairs={{32,64},{40,72},{48,80},{56,88},{33,65},{41,73},{49,81},{57,89},{3... | collective-permute-start | bytes 811016 | tf_op jit(solution)/shard_map/ppermute | solution.py:126
  46.0 10.2 %collective-permute-start.9 = (f32[3,128,256]{2,1,0:T(8,128)S(1)}, f32[3,128,256]{2,1,0:T(8,128)S(1)}, u32[]{:S(2)}, u32[]{:S(2)}) collective-permute-start(f32[3,128,256]{2,1,0:T(8,128)S(1)} %slice.72), channel_id=1, source_target_pairs={{0,2},{1,3},{2,4},{3,5},{4,6},{5,7},{6,0},{7,1},{8,10},{9,11},{10,... | collective-permute-start | bytes 1179656 | tf_op jit(solution)/shard_map/ppermute | solution.py:122
  47.1 11.8 %collective-permute-start.10 = (f32[3,128,256]{2,1,0:T(8,128)S(1)}, f32[3,128,256]{2,1,0:T(8,128)S(1)}, u32[]{:S(2)}, u32[]{:S(2)}) collective-permute-start(f32[3,128,256]{2,1,0:T(8,128)S(1)} %slice.73), channel_id=1, source_target_pairs={{0,6},{1,7},{2,0},{3,1},{4,2},{5,3},{6,4},{7,5},{8,14},{9,15},{10,... | collective-permute-start | bytes 1179656 | tf_op jit(solution)/shard_map/ppermute | solution.py:122
  51.9 11.0 %collective-permute-start.12 = (f32[3,256,256]{2,1,0:T(8,128)}, f32[3,256,256]{2,1,0:T(8,128)S(1)}, u32[]{:S(2)}, u32[]{:S(2)}) collective-permute-start(f32[3,256,256]{2,1,0:T(8,128)} %collective-permute-done.7), channel_id=1, source_target_pairs={{0,1},{1,0},{2,3},{3,2},{4,5},{5,4},{6,7},{7,6},{8,9},{9,8},{10,11... | collective-permute-start | bytes 2359304 | tf_op jit(solution)/shard_map/ppermute | solution.py:122
  54.6 9.3 %collective-permute-start.13 = (f32[3,256,256]{2,1,0:T(8,128)S(1)}, f32[3,256,256]{2,1,0:T(8,128)S(1)}, u32[]{:S(2)}, u32[]{:S(2)}) collective-permute-start(f32[3,256,256]{2,1,0:T(8,128)S(1)} %collective-permute-done.8), channel_id=1, source_target_pairs={{0,1},{1,0},{2,3},{3,2},{4,5},{5,4},{6,7},{7,6},{8,9},{9,8},{10,11... | collective-permute-start | bytes 2359304 | tf_op jit(solution)/shard_map/ppermute | solution.py:122
  56.2 6.4 %collective-permute-start.6 = (f32[512,128]{1,0:T(8,128)S(1)}, f32[512,128]{1,0:T(8,128)S(1)}, u32[]{:S(2)}, u32[]{:S(2)}) collective-permute-start(f32[512,128]{1,0:T(8,128)S(1)} %slice.70), channel_id=1, source_target_pairs={{0,1},{1,0},{2,3},{3,2},{4,5},{5,4},{6,7},{7,6},{8,9},{9,8},{10,11... | collective-permute-start | bytes 786440 | tf_op jit(solution)/shard_map/ppermute | solution.py:122
  58.9 6.0 %collective-permute-start.14 = (f32[3,256,256]{2,1,0:T(8,128)S(1)}, f32[3,256,256]{2,1,0:T(8,128)S(1)}, u32[]{:S(2)}, u32[]{:S(2)}) collective-permute-start(f32[3,256,256]{2,1,0:T(8,128)S(1)} %pad_maximum_fusion), channel_id=1, source_target_pairs={{0,1},{1,0},{2,3},{3,2},{4,5},{5,4},{6,7},{7,6},{8,9},{9,8},{10,11... | collective-permute-start | bytes 2359304 | tf_op jit(solution)/shard_map/ppermute | solution.py:122
  99.6 22.6 %copy-start.7 = (f32[4,4,128]{2,1,0:T(4,128)S(1)}, f32[4,4,128]{2,1,0:T(4,128)}, u32[]{:S(2)}) copy-start(f32[4,4,128]{2,1,0:T(4,128)} %param.14) | copy-start | bytes 24580
  103.6 41.6 %collective-permute-start.15 = (f32[8,520,128]{2,1,0:T(8,128)}, f32[8,520,128]{2,1,0:T(8,128)}, u32[]{:S(2)}, u32[]{:S(2)}) collective-permute-start(f32[8,520,128]{2,1,0:T(8,128)} %get-tuple-element.16), channel_id=1, source_target_pairs={{0,1},{1,0},{2,3},{3,2},{4,5},{5,4},{6,7},{7,6},{8,9},{9,8},{10,11... | collective-permute-start | bytes 6389768 | tf_op jit(solution)/shard_map/ppermute | solution.py:122
  122.2 44.4 %copy-start.1 = (f32[512,128]{1,0:T(8,128)}, f32[512,128]{1,0:T(8,128)S(1)}, u32[]{:S(2)}) copy-start(f32[512,128]{1,0:T(8,128)S(1)} %fusion.4) | copy-start | bytes 786436
  143.7 1.5 copy-start
  145.2 20.8 %copy-start.2 = (f32[128,256]{1,0:T(8,128)S(1)}, f32[128,256]{1,0:T(8,128)}, u32[]{:S(2)}) copy-start(f32[128,256]{1,0:T(8,128)} %inverse.1) | copy-start | bytes 393220
  145.2 21.4 %copy-start.8 = (f32[4,128]{1,0:T(4,128)S(1)}, f32[4,128]{1,0:T(4,128)}, u32[]{:S(2)}) copy-start(f32[4,128]{1,0:T(4,128)} %param.13) | copy-start | bytes 6148
Sparse Core Ops, SparseCore 0:
  10.3 55.2 all-gather.2

commit v2 on v0

v2 whole, which is shorter than its diff:
```python
import functools
import jax
import jax.numpy as jnp
from jax import lax
from jax.experimental import pallas as pl
from jax.experimental.pallas import tpu as pltpu
from jax.sharding import PartitionSpec as P

BF = jnp.bfloat16
F32 = jnp.float32
NT = (((1,), (1,)), ((), ()))
NN = (((1,), (0,)), ((), ()))
VMEM = 56 << 20
highest = lax.Precision.HIGHEST


def split(v):
    h = v.astype(BF)
    return h, (v - h.astype(F32)).astype(BF)


def product(ah, al, bh, bl, dims):
    side = dims[0][1][0]
    left = jnp.concatenate([ah, al, ah], axis=1)
    right = jnp.concatenate([bh, bh, bl], axis=side)
    return lax.dot_general(left, right, dims, preferred_element_type=F32)


def choose(masks, values):
    out = jnp.zeros_like(values[0])
    for m, v in zip(masks, values):
        out = jnp.where(m, v, out)
    return out


def label(ids, i):
    return ids[i].astype(F32).astype(BF)


def dense_rows(block, sup, src):
    m = [s == block for s in sup]
    return jnp.concatenate([choose(m, [src[k, :, q * 128:(q + 1) * 128] for k in range(4)]) for q in range(2)], axis=1)


def corner_body(ids, c_ref, s_ref, w_ref, o_ref):
    parts = [split(c_ref[k]) for k in range(4)]
    high = jnp.stack([h for h, _ in parts])
    low = jnp.stack([l for _, l in parts])
    sup = [s_ref[k] for k in range(4)]
    total = jnp.zeros((128, 128), F32)
    for u in range(3):
        block = label(ids, u)
        dh, dl = dense_rows(block, sup, high), dense_rows(block, sup, low)
        wh, wl = split(w_ref[u])
        vh, vl = split(product(dh, dl, wh, wl, NN))
        total = total + product(vh, vl, dh, dl, NT)
    o_ref[...] = total


def corner_part(ids, c, s, w):
    grid = pltpu.PrefetchScalarGridSpec(
        num_scalar_prefetch=1, grid=(1,),
        in_specs=[pl.BlockSpec((4, 128, 256), lambda g, i: (0, 0, 0)), pl.BlockSpec((4, 128, 128), lambda g, i: (0, 0, 0)),
                  pl.BlockSpec((3, 256, 256), lambda g, i: (0, 0, 0))],
        out_specs=pl.BlockSpec((128, 128), lambda g, i: (0, 0)))
    return pl.pallas_call(corner_body, grid_spec=grid, out_shape=jax.ShapeDtypeStruct((128, 128), F32),
                          compiler_params=pltpu.CompilerParams(vmem_limit_bytes=VMEM), name="corner",
                          cost_estimate=pl.CostEstimate(flops=2 * 3 * 128 * 768 * 384, bytes_accessed=2 << 20, transcendentals=0))(ids, c, s, w)


def weigh_body(ids, c_ref, s_ref, *rest):
    w_refs, (vh_ref, vl_ref, a_ref, ch, cl, wh, wl) = rest[:10], rest[10:]
    g = pl.program_id(0)

    @pl.when(g == 0)
    def _():
        for k in range(4):
            ch[k], cl[k] = split(c_ref[k])
        a_ref[...] = jnp.zeros_like(a_ref)

    for i in range(8):
        @pl.when(g == i)
        def _(i=i):
            base = 5 * (i // 4)
            if i % 4 < 3:
                wh[...], wl[...] = split(w_refs[base + i % 4][...])
            else:
                wh[:, :128], wl[:, :128] = split(w_refs[base + 3][...])
                wh[:, 128:], wl[:, 128:] = split(w_refs[base + 4][...])

    sup = [s_ref[k] for k in range(4)]
    n = vh_ref.shape[1]
    kept = []
    for u in range(3):
        block = label(ids, 3 * g + u)
        dh, dl = dense_rows(block, sup, ch), dense_rows(block, sup, cl)
        vh, vl = split(product(dh[:n], dl[:n], wh[u], wl[u], NN))
        for q in range(2):
            vh_ref[q, :, u * 128:(u + 1) * 128] = vh[:, q * 128:(q + 1) * 128]
            vl_ref[q, :, u * 128:(u + 1) * 128] = vl[:, q * 128:(q + 1) * 128]
        kept.append((vh, vl, dh[n:], dl[n:]))
    vh, vl, dh, dl = [jnp.concatenate(list(v), axis=1) for v in zip(*kept)]
    a_ref[...] += product(vh, vl, dh, dl, NT)


def weigh(ids, c, s, parts):
    m = c.shape[1]
    n = m - 128
    whole = lambda v: pl.BlockSpec(v.shape, lambda g, i: (0,) * v.ndim)
    grid = pltpu.PrefetchScalarGridSpec(
        num_scalar_prefetch=1, grid=(8,),
        in_specs=[whole(c), whole(s)] + [whole(v) for v in parts],
        out_specs=[pl.BlockSpec((2, n, 384), lambda g, i: (0, 0, g))] * 2 + [pl.BlockSpec((n, 128), lambda g, i: (0, 0))],
        scratch_shapes=[pltpu.VMEM((4, m, 256), BF)] * 2 + [pltpu.VMEM((3, 256, 256), BF)] * 2)
    return pl.pallas_call(weigh_body, grid_spec=grid,
                          out_shape=[jax.ShapeDtypeStruct((2, n, 3072), BF)] * 2 + [jax.ShapeDtypeStruct((n, 128), F32)],
                          compiler_params=pltpu.CompilerParams(vmem_limit_bytes=VMEM), name="weigh",
                          cost_estimate=pl.CostEstimate(flops=2 * 3 * n * 6144 * 384, bytes_accessed=20 << 20, transcendentals=0))(ids, c, s, *parts)


def block_body(has_sum, ids, which, vh_ref, vl_ref, c_ref, s_ref, *rest):
    if has_sum:
        a_ref, o_ref, ch, cl = rest
    else:
        o_ref, ch, cl = rest
    g = pl.program_id(0)

    @pl.when(g == 0)
    def _():
        for t in range(8):
            for k in range(4):
                ch[k, :, t * 128:(t + 1) * 128], cl[k, :, t * 128:(t + 1) * 128] = split(c_ref[t, k * 128:(k + 1) * 128])
        o_ref[...] = a_ref[...] if has_sum else jnp.zeros_like(o_ref)

    vh, vl = vh_ref[0], vl_ref[0]
    for q in range(2):
        r = slice(q * 512, (q + 1) * 512)
        sup = [s_ref[k:k + 1, r] for k in range(4)]
        highs, lows = [], []
        for u in range(6):
            block = label(ids, 6 * g + u)
            m = [jnp.broadcast_to(s, (128, 512)).astype(BF) == block for s in sup]
            highs.append(choose(m, [ch[k, :, r] for k in range(4)]))
            lows.append(choose(m, [cl[k, :, r] for k in range(4)]))
        o_ref[:, r] += product(vh, vl, jnp.concatenate(highs, axis=0), jnp.concatenate(lows, axis=0), NN)


def block_product(ids, which, vh, vl, c, s, start=None):
    n = vh.shape[1]
    side = pl.BlockSpec((1, n, 768), lambda g, i, w: (w[0], 0, g))
    full = pl.BlockSpec((n, 1024), lambda g, i, w: (0, 0))
    extra = [] if start is None else [start]
    grid = pltpu.PrefetchScalarGridSpec(
        num_scalar_prefetch=2, grid=(4,),
        in_specs=[side, side, pl.BlockSpec((8, 520, 128), lambda g, i, w: (0, 0, 0)),
                  pl.BlockSpec((8, 1024), lambda g, i, w: (0, 0))] + [full] * len(extra),
        out_specs=full, scratch_shapes=[pltpu.VMEM((4, 128, 1024), BF)] * 2)
    return pl.pallas_call(functools.partial(block_body, start is not None), grid_spec=grid,
                          out_shape=jax.ShapeDtypeStruct((n, 1024), F32),
                          compiler_params=pltpu.CompilerParams(vmem_limit_bytes=VMEM), name="block",
                          cost_estimate=pl.CostEstimate(flops=2 * 3 * n * 3072 * 1024, bytes_accessed=16 << 20, transcendentals=0))(ids, which, vh, vl, c, s, *extra)


def inverse_body(c_ref, o_ref):
    n = 128
    row = lax.broadcasted_iota(jnp.int32, (n, n), 0)
    col = lax.broadcasted_iota(jnp.int32, (n, n), 1)
    below = lax.broadcasted_iota(jnp.int32, (n, 1), 0)
    lane = lax.broadcasted_iota(jnp.int32, (1, n), 1)
    o_ref[...] = jnp.concatenate([c_ref[...], jnp.where(row == col, 1.0, 0.0).astype(F32)], axis=1)

    def step(k, _):
        line = o_ref[pl.ds(k, 1), :]
        pivot = jnp.sum(jnp.where(lane == k, line[:, :n], 0.0), axis=1, keepdims=True)
        scale = lax.rsqrt(pivot)
        column = jnp.sum(jnp.where(lane == k, o_ref[:, :n], 0.0), axis=1, keepdims=True)
        factor = jnp.where(below > k, column * scale, 0.0)
        scaled = line * scale
        o_ref[...] = o_ref[...] - factor * scaled
        o_ref[pl.ds(k, 1), :] = scaled
        return 0

    lax.fori_loop(0, n, step, 0)


def inverse_of(c):
    return pl.pallas_call(inverse_body, out_shape=jax.ShapeDtypeStruct((128, 256), F32), name="inverse",
                          cost_estimate=pl.CostEstimate(flops=2 * 3 * 512 * 3072 * 1024, bytes_accessed=1 << 20, transcendentals=0))(c)


def finish_body(where, place, s_ref, p_ref, q_ref, d_ref, o_ref):
    g = pl.program_id(0)
    r, col = where[0], where[1]
    row = lax.broadcasted_iota(jnp.int32, (128, 128), 0)
    lane = lax.broadcasted_iota(jnp.int32, (128, 128), 1)
    qh, ql = split(q_ref[0])
    across = col * 8 + g
    for t in range(4):
        ph, plo = split(p_ref[t])
        down = t * 16 + r
        outer = product(ph, plo, qh, ql, NT)
        diagonal = jnp.where((row == lane) & (down == across), jnp.broadcast_to(d_ref[t:t + 1], (128, 128)), 0.0)
        o_ref[t] = s_ref[t] + diagonal - jnp.where((down > 0) & (across > 0), outer, 0.0)


def finish(where, place, s, p, q, d):
    grid = pltpu.PrefetchScalarGridSpec(
        num_scalar_prefetch=2, grid=(8,),
        in_specs=[pl.BlockSpec((4, 128, 128), lambda g, w, i: (0, 0, g)), pl.BlockSpec((4, 128, 128), lambda g, w, i: (0, 0, 0)),
                  pl.BlockSpec((1, 128, 128), lambda g, w, i: (i[g], 0, 0)), pl.BlockSpec((4, 128), lambda g, w, i: (0, 0))],
        out_specs=pl.BlockSpec((4, 128, 128), lambda g, w, i: (0, 0, g)))
    return pl.pallas_call(finish_body, grid_spec=grid, out_shape=jax.ShapeDtypeStruct((4, 128, 1024), F32),
                          compiler_params=pltpu.CompilerParams(vmem_limit_bytes=VMEM), name="finish",
                          cost_estimate=pl.CostEstimate(flops=2 * 3 * 512 * 128 * 1024, bytes_accessed=5 << 20, transcendentals=0))(where, place, s, p, q, d)


def chips(step):
    return [(2 * x + c, 2 * step(x) + c) for x in range(4) for c in range(2)]


SWAP = [(i, i ^ 1) for i in range(8)]
UP = chips(lambda x: (x + 1) % 4)
DOWN = chips(lambda x: (x + 3) % 4)
PAIR = chips(lambda x: x ^ 1)
FAR = chips(lambda x: x ^ 2)
ALONG_Z = [[(4 * y + z, 4 * y + (z + d) % 4) for y in range(4) for z in range(4)] for d in (1, 3, 2)]
ALONG_Y = [[(4 * y + z, 4 * ((y + d) % 4) + z) for y in range(4) for z in range(4)] for d in (1, 3, 2)]


def over_cols(v, pairs):
    return lax.ppermute(v, "cols", pairs)


def over_rows(v, pairs):
    return lax.ppermute(v, "rows", pairs)


def gather_weights(w):
    below = over_cols(w, UP)
    above = over_cols(w, DOWN)
    parts = [w, below, above, over_cols(below[:, :128], UP), over_cols(above[:, 128:], DOWN)]
    return parts + [over_cols(v, SWAP) for v in parts]


def spread_first(v, r):
    one = over_rows(v, [(0, 1)])
    three = over_rows(v, [(0, 3)])
    two = over_rows(one, [(1, 2)])
    line = jnp.where(r == 0, v, one + three + two)
    first = over_rows(line, [(z, 4 + z) for z in range(4)])
    third = over_rows(line, [(z, 12 + z) for z in range(4)])
    second = over_rows(first, [(4 + z, 8 + z) for z in range(4)])
    return jnp.where(r < 4, line, first + third + second)


def gather_plane(v):
    line = jnp.stack([v] + [over_rows(v, s) for s in ALONG_Z])
    return jnp.concatenate([line] + [over_rows(line, s) for s in ALONG_Y])


def lanes(s):
    return jnp.broadcast_to(s[:, :, None], s.shape + (128,)).astype(BF)


def local(coefficients, support, primal, dual_inverse, block_sizes, damping, right_sides):
    col = lax.axis_index("cols")
    r = lax.axis_index("rows")
    x = col // 2
    p = col % 2
    positions = jnp.arange(256, dtype=jnp.int32)
    active = (positions[None, :] < block_sizes[:, None]).astype(F32)
    w = primal * dual_inverse * active[:, :, None] * active[:, None, :]
    weights = gather_weights(w)
    sup = support.astype(F32)

    def piece(t):
        tile = lax.dynamic_index_in_dim(coefficients, t, 0, keepdims=False)
        return lax.dynamic_slice_in_dim(tile, p * 128, 128, 2)

    mine = jnp.concatenate([jnp.transpose(piece(x), (1, 2, 0)).reshape(512, 128),
                            lax.dynamic_index_in_dim(sup, x, 0, keepdims=False).T, jnp.zeros((4, 128), F32)], axis=0)
    gathered = lax.all_gather(mine, "rows")
    near = 2 * ((x + jnp.array([0, 3, 1, 2])) % 4)
    ids = jnp.concatenate([near + p, near + 1 - p])
    ids = (ids[:, None] * 3 + jnp.arange(3)).reshape(24).astype(jnp.int32)

    own = jnp.transpose(coefficients, (2, 0, 1, 3)).reshape(4, 512, 256)
    own_sup = jnp.transpose(sup, (2, 0, 1)).reshape(4, 512)
    corner = corner_part(ids, own[:, :128], lanes(own_sup[:, :128]), w)
    for pairs in (SWAP, PAIR, FAR):
        corner = corner + over_cols(corner, pairs)
    corner = corner + jnp.eye(128, dtype=F32) * damping[0]
    both = spread_first(inverse_of(corner)[:, 128:], r)
    inverse = both

    head = jnp.concatenate([jnp.transpose(piece(0), (1, 0, 2)).reshape(512, 128), sup[0].T, right_sides[0],
                            damping[:1], jnp.zeros((7, 128), F32)], axis=0)
    head = spread_first(head, r)
    head_other = over_cols(head[:512], SWAP)
    lo = jnp.where(p == 0, head[:512], head_other).reshape(4, 128, 128)
    hi = jnp.where(p == 0, head_other, head[:512]).reshape(4, 128, 128)
    rows = jnp.concatenate([own, jnp.concatenate([lo, hi], axis=2)], axis=1)
    row_sup = lanes(jnp.concatenate([own_sup, head[512:516]], axis=1))
    vh, vl, first = weigh(ids, rows, row_sup, weights)

    shift = jnp.where(r == 0, damping[0], 0.0) * jnp.eye(128, dtype=F32)
    first = first.at[:128].add(shift)
    panel_factor = lax.dot_general(first, inverse, NT, precision=highest).reshape(4, 128, 128)
    every = gather_plane(lax.dynamic_index_in_dim(panel_factor, x, 0, keepdims=False))
    leading = lax.dot_general(head[516:520], inverse, NT, precision=highest)
    remainder = right_sides - jnp.einsum("sk,tak->tsa", leading, panel_factor, precision=highest)
    solved = jnp.where(((jnp.arange(4) > 0) | (r > 0))[:, None, None], remainder, leading[None])

    kept = lax.dynamic_slice_in_dim(gathered, 8 * p, 8, 0)
    given = lax.dynamic_slice_in_dim(gathered, 8 * (1 - p), 8, 0)
    swapped = over_cols(given, SWAP)
    col_sup = jnp.pad(jnp.transpose(kept[:, 512:516], (1, 0, 2)).reshape(4, 1024), ((0, 4), (0, 0)))
    which = p.astype(jnp.int32)[None]
    out = block_product(ids, which, vh, vl, kept, col_sup)
    out = block_product(ids, 1 - which, vh, vl, swapped, col_sup, out)

    order = jnp.array([0, 2, 3, 1])
    tiles = 8 * p + jnp.arange(8)
    place = order[(tiles // 4 - r // 4) % 4] * 4 + order[(tiles % 4 - r % 4) % 4]
    updated = finish(jnp.stack([r, col]).astype(jnp.int32), place.astype(jnp.int32), out.reshape(4, 128, 1024), panel_factor, every, damping)
    return updated, panel_factor, solved


def solution(mesh):
    in_specs = (
        P(None, "rows", None, None),
        P(None, "rows", None),
        P("cols", None, None),
        P("cols", None, None),
        P("cols"),
        P(None, "rows"),
        P(None, "cols", "rows"),
    )
    out_specs = (P(None, "rows", "cols"), P(None, "rows", None), P(None, "cols", "rows"))
    return jax.shard_map(local, mesh=mesh, in_specs=in_specs, out_specs=out_specs, check_vma=False)
```

time: 686 us -> 204 us (0.30)
  waiting for transfers between devices: 473 us -> 27.8 us
  matrix products: 104 us -> 2.43 us
  Pallas kernels: 0 us -> 82.8 us
  blocking collectives: 54.4 us -> 0 us
  starting transfers between devices: 0.2 us -> 46.2 us
  other arithmetic: 26.6 us -> 10.6 us
    psum x2 -> x0, waiting for transfers between devices: 195 us -> none  [broadcast(): return lax.psum(block, axis)]
    all_gather x2 -> x1, waiting for transfers between devices: 186 us -> 0.01 us  [local(): gathered = lax.all_gather(mine, 'rows')]
    dot_general x7 -> x2, matrix products: 101 us -> 1.49 us  [the longest x1 1.32 us: local(): lax.dot_general(first, inverse, NT, precision=highest).reshape(4, 128, 128)]
    reduce_scatter x1 -> x0, waiting for transfers between devices: 90.8 us -> none  [local(): lax.psum_scatter(partial_value, 'cols', scatter_dimension=2, tiled=True)]
    pallas_call x0 -> x6, Pallas kernels: none -> 82.8 us  [the longest x2 32.4 us: block_product(): pl.pallas_call(functools.partial(block_body, start is not None), grid_spe...]
    ppermute x0 -> x32, starting transfers between devices: none -> 46.2 us  [the longest x18 28.5 us: over_rows(): return lax.ppermute(v, 'rows', pairs)]
    psum x1 -> x0, blocking collectives: 33.6 us -> none  [broadcast(): return lax.psum(block, axis)]
    ppermute x0 -> x32, waiting for transfers between devices: none -> 27.8 us  [the longest x14 16 us: over_cols(): return lax.ppermute(v, 'cols', pairs)]
  transfers between devices with their start and end apart: 5 -> 33, of which waited for: 5 -> 8; matrix products, arithmetic and copies ran while one was open for 3% -> 14% of each run, Pallas kernels for 0% -> 29%
where the time goes in v2:
time: 204 us; the launch traced here: 203 us
  Pallas kernels  82.8 us (41%)
  starting transfers between devices  46.2 us (23%)
  waiting for transfers between devices  27.8 us (14%)
  local copies, waits for them, and re-layouts  17.9 us (9%)
  between operations  14.6 us (7%)
  other arithmetic  10.6 us (5%)
  matrix products  2.43 us (1%)
    pallas_call x2, Pallas kernels, block_product(): pl.pallas_call(functools.partial(block_body, start is not None), grid_spe...  32.4 us
    ppermute x18, starting transfers between devices, over_rows(): return lax.ppermute(v, 'rows', pairs)  28.5 us
    pallas_call x1, Pallas kernels, weigh(): pl.pallas_call(weigh_body, grid_spec=grid, out_shape=[jax.ShapeDtypeStruc...  24.2 us
    ppermute x14, starting transfers between devices, over_cols(): return lax.ppermute(v, 'cols', pairs)  17.7 us
    ppermute x14, waiting for transfers between devices, over_cols(): return lax.ppermute(v, 'cols', pairs)  16 us
    pallas_call x1, Pallas kernels, inverse_of(): pl.pallas_call(inverse_body, out_shape=jax.ShapeDtypeStruct((128, 256), F...  15.2 us
    ppermute x18, waiting for transfers between devices, over_rows(): return lax.ppermute(v, 'rows', pairs)  11.8 us
    pallas_call x1, Pallas kernels, finish(): pl.pallas_call(finish_body, grid_spec=grid, out_shape=jax.ShapeDtypeStruc...  7.54 us
  transfers between devices with their start and end apart: 33, of which 8 were waited for; matrix products, arithmetic and copies ran while one was open for 14% of the time, Pallas kernels for 29%

profile of v2, /device:TPU:1, one launch (start us, length us, event | category | flops | bytes accessed | tf_op | source)
XLA Modules:
  0.0 202.5 jit_solution(7137341271863853638)
XLA Ops:
  8.0 1.1 constant_dynamic-slice_fusion.3
  9.4 0.8 maximum_maximum_fusion.1
  11.1 4.4 %collective-permute-start = (f32[528,128]{1,0:T(8,128)S(1)}, f32[528,128]{1,0:T(8,128)S(1)}, u32[]{:S(2)}, u32[]{:S(2)}) collective-permute-start(f32[528,128]{1,0:T(8,128)S(1)} %concatenate.30), channel_id=1, source_target_pairs={{0,8},{1,9},{2,10},{3,11},{4,12},{5,13},{6,14},{7,15}} | collective-permute-start | bytes 811016 | tf_op jit(solution)/shard_map/ppermute | solution.py:235
  15.5 2.8 %collective-permute-start.1 = (f32[528,128]{1,0:T(8,128)S(1)}, f32[528,128]{1,0:T(8,128)S(1)}, u32[]{:S(2)}, u32[]{:S(2)}) collective-permute-start(f32[528,128]{1,0:T(8,128)S(1)} %concatenate.30), channel_id=1, source_target_pairs={{0,24},{1,25},{2,26},{3,27},{4,28},{5,29},{6,30},{7,31}} | collective-permute-start | bytes 811016 | tf_op jit(solution)/shard_map/ppermute | solution.py:235
  18.4 1.1 multiply_multiply_fusion.rest_0_.w_ref
  19.5 1.2 collective-permute-start.7
  20.7 1.5 collective-permute-start.8
  22.9 2.1 %copy.16 = f32[4,4,128,256]{3,2,1,0:T(8,128)S(1)} copy(f32[4,4,128,256]{3,0,2,1:T(4,128)} %bitcast.73) | data formatting | bytes 4194304 | tf_op jit(solution)/shard_map/transpose | solution.py:287
  25.0 0.9 slice.84.c_ref
  26.7 3.5 %corner.1 = f32[128,128]{1,0:T(8,128)} custom-call(s32[24]{0:T(128)} %add.218.ids, f32[4,128,256]{2,1,0:T(8,128)} %slice.84.c_ref, bf16[4,128,128]{2,1,0:T(8,128)(2,1)} %broadcast_in_dim.35.s_ref, f32[3,256,256]{2,1,0:T(8,128)} %multiply_multiply_fusion.rest_0_.w_ref), custom_call_target="tpu_custom_call" | custom-call | flops 226492416 | bytes 2097152 | tf_op jit(solution)/shard_map/corner/pallas_call | solution.py:66
  30.2 1.6 collective-permute-start.17
  31.8 1.1 collective-permute-done.17
  32.9 0.9 add.228
  33.9 6.3 %collective-permute-done.18 = f32[128,128]{1,0:T(8,128)S(1)} collective-permute-done((f32[128,128]{1,0:T(8,128)S(1)}, f32[128,128]{1,0:T(8,128)S(1)}, u32[]{:S(2)}, u32[]{:S(2)}) %collective-permute-start.18) | collective-permute-done | bytes 65568 | tf_op jit(solution)/shard_map/ppermute | solution.py:231
  40.1 2.5 %collective-permute-start.19 = (f32[128,128]{1,0:T(8,128)S(1)}, f32[128,128]{1,0:T(8,128)S(1)}, u32[]{:S(2)}, u32[]{:S(2)}) collective-permute-start(f32[128,128]{1,0:T(8,128)S(1)} %add.229), channel_id=1, source_target_pairs={{0,4},{1,5},{2,6},{3,7},{4,0},{5,1},{6,2},{7,3},{8,12},{9,13},{10,... | collective-permute-start | bytes 196616 | tf_op jit(solution)/shard_map/ppermute | solution.py:231
  44.0 0.9 collective-permute-done.19
  46.1 15.2 %inverse.1 = f32[128,256]{1,0:T(8,128)} custom-call(f32[128,128]{1,0:T(8,128)} %select_add_fusion.c_ref), custom_call_target="tpu_custom_call" | custom-call | flops 9663676416 | bytes 1048576 | tf_op jit(solution)/shard_map/inverse/pallas_call | solution.py:187
  61.3 1.5 slice.86
  62.8 1.7 collective-permute-start.20
  65.1 1.0 collective-permute-done.20
  66.2 1.3 collective-permute-start.21
  68.2 1.3 collective-permute-start.3
  69.6 0.9 add_select_fusion.3
  70.4 1.3 collective-permute-start.23
  71.7 1.3 collective-permute-start.24
  74.3 1.3 collective-permute-start.4
  76.9 1.0 slice.82
  78.0 4.8 %collective-permute-start.11 = (f32[3,256,256]{2,1,0:T(8,128)}, f32[3,256,256]{2,1,0:T(8,128)S(1)}, u32[]{:S(2)}, u32[]{:S(2)}) collective-permute-start(f32[3,256,256]{2,1,0:T(8,128)} %multiply_multiply_fusion.rest_0_.w_ref), channel_id=1, source_target_pairs={{0,1},{1,0},{2,3},{3,2},{4,5},{5,4},{6,7},{7,6},{8,9},{9,8},{10,11... | collective-permute-start | bytes 2359304 | tf_op jit(solution)/shard_map/ppermute | solution.py:231
  82.8 1.0 slice.83
  83.8 2.7 %collective-permute-start.10 = (f32[3,128,256]{2,1,0:T(8,128)S(1)}, f32[3,128,256]{2,1,0:T(8,128)S(1)}, u32[]{:S(2)}, u32[]{:S(2)}) collective-permute-start(f32[3,128,256]{2,1,0:T(8,128)S(1)} %slice.83), channel_id=1, source_target_pairs={{0,6},{1,7},{2,0},{3,1},{4,2},{5,3},{6,4},{7,5},{8,14},{9,15},{10,... | collective-permute-start | bytes 1179656 | tf_op jit(solution)/shard_map/ppermute | solution.py:231
  87.4 7.2 %collective-permute-done.9.rest_3_ = f32[3,128,256]{2,1,0:T(8,128)S(1)} collective-permute-done((f32[3,128,256]{2,1,0:T(8,128)S(1)}, f32[3,128,256]{2,1,0:T(8,128)S(1)}, u32[]{:S(2)}, u32[]{:S(2)}) %collective-permute-start.9) | collective-permute-done | bytes 393248 | tf_op jit(solution)/shard_map/ppermute | solution.py:231
  94.6 0.9 collective-permute-start.6
  97.1 1.7 maximum_maximum_fusion.c_ref
  98.9 1.6 broadcast_in_dim.26.s_ref
  100.6 24.2 %weigh.1 = (bf16[2,512,3072]{2,1,0:T(8,128)(2,1)}, bf16[2,512,3072]{2,1,0:T(8,128)(2,1)}, f32[512,128]{1,0:T(8,128)}) custom-call(s32[24]{0:T(128)} %add.218.ids, f32[4,640,256]{2,1,0:T(8,128)} %maximum_maximum_fusion.c_ref, bf16[4,640,128]{2,1,0:T(8,128)(2,1)} %broadcast_in_dim.26.s_ref, f32[3,256,256]{2,1,0:T(8,128)} %multiply_multiply_fusion.rest_0_.w_ref, ...), custom_call_target="tpu_custom_call" | custom-call | flops 7247757312 | bytes 20971520 | tf_op jit(solution)/shard_map/weigh/pallas_call | solution.py:115
  124.9 1.5 add_dynamic-update-slice_fusion
  126.3 1.3 fusion.16
  127.7 2.0 %collective-permute-start.26 = (f32[128,128]{1,0:T(8,128)S(1)}, f32[128,128]{1,0:T(8,128)S(1)}, u32[]{:S(2)}, u32[]{:S(2)}) collective-permute-start(f32[128,128]{1,0:T(8,128)S(1)} %bitcast.83), channel_id=1, source_target_pairs={{0,8},{8,16},{16,24},{24,0},{32,40},{40,48},{48,56},{56,32},{64,72... | collective-permute-start | bytes 196616 | tf_op jit(solution)/shard_map/ppermute | solution.py:235
  130.6 2.9 %collective-permute-start.28 = (f32[128,128]{1,0:T(8,128)S(1)}, f32[128,128]{1,0:T(8,128)S(1)}, u32[]{:S(2)}, u32[]{:S(2)}) collective-permute-start(f32[128,128]{1,0:T(8,128)S(1)} %bitcast.85), channel_id=1, source_target_pairs={{0,16},{8,24},{16,0},{24,8},{32,48},{40,56},{48,32},{56,40},{64,80... | collective-permute-start | bytes 196616 | tf_op jit(solution)/shard_map/ppermute | solution.py:235
  133.5 0.9 broadcast_select_fusion.2
  134.4 3.9 %constant_dynamic-slice_fusion.1 = (f32[8,520,128]{2,1,0:T(8,128)}, f32[8,520,128]{2,1,0:T(8,128)S(1)}) fusion(f32[16,520,128]{2,1,0:T(8,128)} %bitcast.71, s32[]{:T(128)S(6)} %select_n.191, s32[]{:T(128)S(6)} %select_n.190), kind=kLoop, calls=%fused_computation.49 | loop fusion | bytes 8519688 | tf_op jit(solution)/shard_map/dynamic_slice | solution.py:314
  138.3 1.0 collective-permute-start.16
  139.3 2.8 %collective-permute-start.29 = (f32[4,128,128]{2,1,0:T(8,128)S(1)}, f32[4,128,128]{2,1,0:T(8,128)S(1)}, u32[]{:S(2)}, u32[]{:S(2)}) collective-permute-start(f32[4,128,128]{2,1,0:T(8,128)S(1)} %pad_maximum_fusion), channel_id=1, source_target_pairs={{0,32},{8,40},{16,48},{24,56},{32,64},{40,72},{48,80},{56,88},{64,... | collective-permute-start | bytes 786440 | tf_op jit(solution)/shard_map/ppermute | solution.py:235
  142.1 1.9 collective-permute-start.31
  144.0 10.1 %collective-permute-done.29 = f32[4,128,128]{2,1,0:T(8,128)S(1)} collective-permute-done((f32[4,128,128]{2,1,0:T(8,128)S(1)}, f32[4,128,128]{2,1,0:T(8,128)S(1)}, u32[]{:S(2)}, u32[]{:S(2)}) %collective-permute-start.29) | collective-permute-done | bytes 262176 | tf_op jit(solution)/shard_map/ppermute | solution.py:235
  155.7 15.9 %block.2.rest_0_ = f32[512,1024]{1,0:T(8,128)} custom-call(s32[24]{0:T(128)} %add.218.ids, s32[1]{0:T(128)} %bitcast.4.which, bf16[2,512,3072]{2,1,0:T(8,128)(2,1)} %get-tuple-element.18.vh_ref, bf16[2,512,3072]{2,1,0:T(8,128)(2,1)} %get-tuple-element.19.vl_ref, f32[8,520,128]{2,1,0:T(8,128)} %get-tuple-element.25.c_ref, f32[8,1024]{1,0:T(8,128)} %pad.6.s_ref), custom_call_target="tpu_custom_call" | custom-call | flops 9663676416 | bytes 16777216 | tf_op jit(solution)/shard_map/block/pallas_call | solution.py:158
  171.6 16.5 %block.3 = f32[512,1024]{1,0:T(8,128)} custom-call(s32[24]{0:T(128)} %add.218.ids, s32[1]{0:T(128)S(6)} %sub.58.which, bf16[2,512,3072]{2,1,0:T(8,128)(2,1)} %get-tuple-element.18.vh_ref, bf16[2,512,3072]{2,1,0:T(8,128)(2,1)} %get-tuple-element.19.vl_ref, f32[8,520,128]{2,1,0:T(8,128)} %collective-permute-done.16.c_ref, f32[8,1024]{1,0:T(8,128)} %pad.6.s_ref, ...), custom_call_target="tpu_custom_call" | custom-call | flops 9663676416 | bytes 16777216 | tf_op jit(solution)/shard_map/block/pallas_call | solution.py:158
  188.1 7.5 %finish.1 = f32[4,128,1024]{2,1,0:T(8,128)} custom-call(s32[2]{0:T(128)} %pad_add_fusion.where, s32[8]{0:T(128)} %multiply_add_fusion.place, f32[4,128,1024]{2,1,0:T(8,128)} %bitcast.78, f32[4,128,128]{2,1,0:T(8,128)} %bitcast.76, f32[16,128,128]{2,1,0:T(8,128)} %copy-done.2, f32[4,128]{1,0:T(4,128)} %d_ref.1), custom_call_target="tpu_custom_call" | custom-call | flops 402653184 | bytes 5242880 | tf_op jit(solution)/shard_map/finish/pallas_call | solution.py:212
  (120 shorter events, 15.1 us)
Async XLA Ops:
  7.2 3.1 %slice-start = ((f32[4,128,4,256]{3,2,1,0:T(4,128)}), f32[1,128,4,256]{3,2,1,0:T(4,128)S(1)}, s32[]{:S(2)}) async-start(f32[4,128,4,256]{3,2,1,0:T(4,128)} %param.11), calls=%async_computation.1 | async-start | bytes 1048576 | tf_op jit(solution)/shard_map/jit(dynamic_index_in_dim)/dynamic_slice | solution.py:277
  7.2 3.9 %copy-start.5 = (f32[4,4,128]{2,1,0:T(4,128)S(1)}, f32[4,4,128]{2,1,0:T(4,128)}, u32[]{:S(2)}) copy-start(f32[4,4,128]{2,1,0:T(4,128)} %param.17) | copy-start | bytes 24580
  7.2 127.3 %all-gather.3.cloned.1.call-start = ((), (), s32[]{:S(2)}) async-start(), calls=%async_computation | async-start | bytes 4526080 | tf_op jit(solution)/shard_map/all_gather | solution.py:282
  9.1 9.2 %copy-start.6 = (s32[3]{0:T(128)S(1)}, s32[3]{0:T(128)}, u32[]{:S(2)}) copy-start(s32[3]{0:T(128)} %param.15) | copy-start | bytes 40
  9.2 9.3 %copy-start.3 = (f32[3,256,256]{2,1,0:T(8,128)S(1)}, f32[3,256,256]{2,1,0:T(8,128)}, u32[]{:S(2)}) copy-start(f32[3,256,256]{2,1,0:T(8,128)} %param.13) | copy-start | bytes 2359300
  9.2 9.2 %copy-start.4 = (f32[3,256,256]{2,1,0:T(8,128)S(1)}, f32[3,256,256]{2,1,0:T(8,128)}, u32[]{:S(2)}) copy-start(f32[3,256,256]{2,1,0:T(8,128)} %param.14) | copy-start | bytes 2359300
  10.3 11.9 %copy-start.7 = (s32[4]{0:T(128)S(1)}, s32[4]{0:T(128)}, u32[]{:S(2)}) copy-start(s32[4]{0:T(128)} %constant.180.clone) | copy-start | bytes 52
  11.1 34.3 %collective-permute-start = (f32[528,128]{1,0:T(8,128)S(1)}, f32[528,128]{1,0:T(8,128)S(1)}, u32[]{:S(2)}, u32[]{:S(2)}) collective-permute-start(f32[528,128]{1,0:T(8,128)S(1)} %concatenate.30), channel_id=1, source_target_pairs={{0,8},{1,9},{2,10},{3,11},{4,12},{5,13},{6,14},{7,15}} | collective-permute-start | bytes 811016 | tf_op jit(solution)/shard_map/ppermute | solution.py:235
  15.5 51.9 %collective-permute-start.1 = (f32[528,128]{1,0:T(8,128)S(1)}, f32[528,128]{1,0:T(8,128)S(1)}, u32[]{:S(2)}, u32[]{:S(2)}) collective-permute-start(f32[528,128]{1,0:T(8,128)S(1)} %concatenate.30), channel_id=1, source_target_pairs={{0,24},{1,25},{2,26},{3,27},{4,28},{5,29},{6,30},{7,31}} | collective-permute-start | bytes 811016 | tf_op jit(solution)/shard_map/ppermute | solution.py:235
  19.5 54.8 %collective-permute-start.7 = (f32[3,256,256]{2,1,0:T(8,128)}, f32[3,256,256]{2,1,0:T(8,128)}, u32[]{:S(2)}, u32[]{:S(2)}) collective-permute-start(f32[3,256,256]{2,1,0:T(8,128)} %multiply_multiply_fusion.rest_0_.w_ref), channel_id=1, source_target_pairs={{0,2},{1,3},{2,4},{3,5},{4,6},{5,7},{6,0},{7,1},{8,10},{9,11},{10,... | collective-permute-start | bytes 2359304 | tf_op jit(solution)/shard_map/ppermute | solution.py:231
  20.7 62.1 %collective-permute-start.8 = (f32[3,256,256]{2,1,0:T(8,128)}, f32[3,256,256]{2,1,0:T(8,128)}, u32[]{:S(2)}, u32[]{:S(2)}) collective-permute-start(f32[3,256,256]{2,1,0:T(8,128)} %multiply_multiply_fusion.rest_0_.w_ref), channel_id=1, source_target_pairs={{0,6},{1,7},{2,0},{3,1},{4,2},{5,3},{6,4},{7,5},{8,14},{9,15},{10,... | collective-permute-start | bytes 2359304 | tf_op jit(solution)/shard_map/ppermute | solution.py:231
  25.0 17.6 %copy-start = (s32[4]{0:T(128)S(1)}, s32[4]{0:T(128)}, u32[]{:S(2)}) copy-start(s32[4]{0:T(128)} %constant.181.clone) | copy-start | bytes 52
  30.2 2.7 %collective-permute-start.17 = (f32[128,128]{1,0:T(8,128)}, f32[128,128]{1,0:T(8,128)S(1)}, u32[]{:S(2)}, u32[]{:S(2)}) collective-permute-start(f32[128,128]{1,0:T(8,128)} %corner.1), channel_id=1, source_target_pairs={{0,1},{1,0},{2,3},{3,2},{4,5},{5,4},{6,7},{7,6},{8,9},{9,8},{10,11... | collective-permute-start | bytes 196616 | tf_op jit(solution)/shard_map/ppermute | solution.py:231
  33.8 6.4 %collective-permute-start.18 = (f32[128,128]{1,0:T(8,128)S(1)}, f32[128,128]{1,0:T(8,128)S(1)}, u32[]{:S(2)}, u32[]{:S(2)}) collective-permute-start(f32[128,128]{1,0:T(8,128)S(1)} %add.228), channel_id=1, source_target_pairs={{0,2},{1,3},{2,0},{3,1},{4,6},{5,7},{6,4},{7,5},{8,10},{9,11},{10,... | collective-permute-start | bytes 196616 | tf_op jit(solution)/shard_map/ppermute | solution.py:231
  40.1 4.7 %collective-permute-start.19 = (f32[128,128]{1,0:T(8,128)S(1)}, f32[128,128]{1,0:T(8,128)S(1)}, u32[]{:S(2)}, u32[]{:S(2)}) collective-permute-start(f32[128,128]{1,0:T(8,128)S(1)} %add.229), channel_id=1, source_target_pairs={{0,4},{1,5},{2,6},{3,7},{4,0},{5,1},{6,2},{7,3},{8,12},{9,13},{10,... | collective-permute-start | bytes 196616 | tf_op jit(solution)/shard_map/ppermute | solution.py:231
  45.5 22.7 %collective-permute-start.2 = (f32[528,128]{1,0:T(8,128)S(1)}, f32[528,128]{1,0:T(8,128)S(1)}, u32[]{:S(2)}, u32[]{:S(2)}) collective-permute-start(f32[528,128]{1,0:T(8,128)S(1)} %collective-permute-done), channel_id=1, source_target_pairs={{8,16},{9,17},{10,18},{11,19},{12,20},{13,21},{14,22},{15,23}} | collective-permute-start | bytes 811016 | tf_op jit(solution)/shard_map/ppermute | solution.py:235
  62.8 3.4 %collective-permute-start.20 = (f32[128,128]{1,0:T(8,128)}, f32[128,128]{1,0:T(8,128)S(1)}, u32[]{:S(2)}, u32[]{:S(2)}) collective-permute-start(f32[128,128]{1,0:T(8,128)} %slice.86), channel_id=1, source_target_pairs={{0,8},{1,9},{2,10},{3,11},{4,12},{5,13},{6,14},{7,15}} | collective-permute-start | bytes 196616 | tf_op jit(solution)/shard_map/ppermute | solution.py:235
  66.2 3.4 %collective-permute-start.21 = (f32[128,128]{1,0:T(8,128)}, f32[128,128]{1,0:T(8,128)S(1)}, u32[]{:S(2)}, u32[]{:S(2)}) collective-permute-start(f32[128,128]{1,0:T(8,128)} %slice.86), channel_id=1, source_target_pairs={{0,24},{1,25},{2,26},{3,27},{4,28},{5,29},{6,30},{7,31}} | collective-permute-start | bytes 196616 | tf_op jit(solution)/shard_map/ppermute | solution.py:235
  67.5 2.1 %collective-permute-start.22 = (f32[128,128]{1,0:T(8,128)S(1)}, f32[128,128]{1,0:T(8,128)S(1)}, u32[]{:S(2)}, u32[]{:S(2)}) collective-permute-start(f32[128,128]{1,0:T(8,128)S(1)} %collective-permute-done.20), channel_id=1, source_target_pairs={{8,16},{9,17},{10,18},{11,19},{12,20},{13,21},{14,22},{15,23}} | collective-permute-start | bytes 196616 | tf_op jit(solution)/shard_map/ppermute | solution.py:235
  68.2 7.4 %collective-permute-start.3 = (f32[528,128]{1,0:T(8,128)S(1)}, f32[528,128]{1,0:T(8,128)S(1)}, u32[]{:S(2)}, u32[]{:S(2)}) collective-permute-start(f32[528,128]{1,0:T(8,128)S(1)} %add_select_fusion.1), channel_id=1, source_target_pairs={{0,32},{8,40},{16,48},{24,56},{1,33},{9,41},{17,49},{25,57},{2,34}... | collective-permute-start | bytes 811016 | tf_op jit(solution)/shard_map/ppermute | solution.py:235
  70.4 3.2 %collective-permute-start.23 = (f32[128,128]{1,0:T(8,128)S(1)}, f32[128,128]{1,0:T(8,128)S(1)}, u32[]{:S(2)}, u32[]{:S(2)}) collective-permute-start(f32[128,128]{1,0:T(8,128)S(1)} %add_select_fusion.3), channel_id=1, source_target_pairs={{0,32},{8,40},{16,48},{24,56},{1,33},{9,41},{17,49},{25,57},{2,34}... | collective-permute-start | bytes 196616 | tf_op jit(solution)/shard_map/ppermute | solution.py:235
  71.7 6.2 %collective-permute-start.24 = (f32[128,128]{1,0:T(8,128)S(1)}, f32[128,128]{1,0:T(8,128)S(1)}, u32[]{:S(2)}, u32[]{:S(2)}) collective-permute-start(f32[128,128]{1,0:T(8,128)S(1)} %add_select_fusion.3), channel_id=1, source_target_pairs={{0,96},{8,104},{16,112},{24,120},{1,97},{9,105},{17,113},{25,121},... | collective-permute-start | bytes 196616 | tf_op jit(solution)/shard_map/ppermute | solution.py:235
  73.6 9.1 %collective-permute-start.25 = (f32[128,128]{1,0:T(8,128)S(1)}, f32[128,128]{1,0:T(8,128)S(1)}, u32[]{:S(2)}, u32[]{:S(2)}) collective-permute-start(f32[128,128]{1,0:T(8,128)S(1)} %collective-permute-done.23), channel_id=1, source_target_pairs={{32,64},{40,72},{48,80},{56,88},{33,65},{41,73},{49,81},{57,89},{3... | collective-permute-start | bytes 196616 | tf_op jit(solution)/shard_map/ppermute | solution.py:235
  74.3 12.3 %collective-permute-start.4 = (f32[528,128]{1,0:T(8,128)S(1)}, f32[528,128]{1,0:T(8,128)S(1)}, u32[]{:S(2)}, u32[]{:S(2)}) collective-permute-start(f32[528,128]{1,0:T(8,128)S(1)} %add_select_fusion.1), channel_id=1, source_target_pairs={{0,96},{8,104},{16,112},{24,120},{1,97},{9,105},{17,113},{25,121},... | collective-permute-start | bytes 811016 | tf_op jit(solution)/shard_map/ppermute | solution.py:235
  75.6 11.6 %collective-permute-start.5 = (f32[528,128]{1,0:T(8,128)S(1)}, f32[528,128]{1,0:T(8,128)S(1)}, u32[]{:S(2)}, u32[]{:S(2)}) collective-permute-start(f32[528,128]{1,0:T(8,128)S(1)} %collective-permute-done.3), channel_id=1, source_target_pairs={{32,64},{40,72},{48,80},{56,88},{33,65},{41,73},{49,81},{57,89},{3... | collective-permute-start | bytes 811016 | tf_op jit(solution)/shard_map/ppermute | solution.py:235
  78.0 20.8 %collective-permute-start.11 = (f32[3,256,256]{2,1,0:T(8,128)}, f32[3,256,256]{2,1,0:T(8,128)S(1)}, u32[]{:S(2)}, u32[]{:S(2)}) collective-permute-start(f32[3,256,256]{2,1,0:T(8,128)} %multiply_multiply_fusion.rest_0_.w_ref), channel_id=1, source_target_pairs={{0,1},{1,0},{2,3},{3,2},{4,5},{5,4},{6,7},{7,6},{8,9},{9,8},{10,11... | collective-permute-start | bytes 2359304 | tf_op jit(solution)/shard_map/ppermute | solution.py:231
  82.8 11.9 %collective-permute-start.9 = (f32[3,128,256]{2,1,0:T(8,128)S(1)}, f32[3,128,256]{2,1,0:T(8,128)S(1)}, u32[]{:S(2)}, u32[]{:S(2)}) collective-permute-start(f32[3,128,256]{2,1,0:T(8,128)S(1)} %slice.82), channel_id=1, source_target_pairs={{0,2},{1,3},{2,4},{3,5},{4,6},{5,7},{6,0},{7,1},{8,10},{9,11},{10,... | collective-permute-start | bytes 1179656 | tf_op jit(solution)/shard_map/ppermute | solution.py:231
  83.8 11.9 %collective-permute-start.10 = (f32[3,128,256]{2,1,0:T(8,128)S(1)}, f32[3,128,256]{2,1,0:T(8,128)S(1)}, u32[]{:S(2)}, u32[]{:S(2)}) collective-permute-start(f32[3,128,256]{2,1,0:T(8,128)S(1)} %slice.83), channel_id=1, source_target_pairs={{0,6},{1,7},{2,0},{3,1},{4,2},{5,3},{6,4},{7,5},{8,14},{9,15},{10,... | collective-permute-start | bytes 1179656 | tf_op jit(solution)/shard_map/ppermute | solution.py:231
  86.6 12.3 %collective-permute-start.12 = (f32[3,256,256]{2,1,0:T(8,128)}, f32[3,256,256]{2,1,0:T(8,128)S(1)}, u32[]{:S(2)}, u32[]{:S(2)}) collective-permute-start(f32[3,256,256]{2,1,0:T(8,128)} %collective-permute-done.7.rest_1_), channel_id=1, source_target_pairs={{0,1},{1,0},{2,3},{3,2},{4,5},{5,4},{6,7},{7,6},{8,9},{9,8},{10,11... | collective-permute-start | bytes 2359304 | tf_op jit(solution)/shard_map/ppermute | solution.py:231
  87.2 11.7 %collective-permute-start.13 = (f32[3,256,256]{2,1,0:T(8,128)}, f32[3,256,256]{2,1,0:T(8,128)S(1)}, u32[]{:S(2)}, u32[]{:S(2)}) collective-permute-start(f32[3,256,256]{2,1,0:T(8,128)} %collective-permute-done.8.rest_2_), channel_id=1, source_target_pairs={{0,1},{1,0},{2,3},{3,2},{4,5},{5,4},{6,7},{7,6},{8,9},{9,8},{10,11... | collective-permute-start | bytes 2359304 | tf_op jit(solution)/shard_map/ppermute | solution.py:231
  94.6 4.2 %copy-start.11 = (f32[3,128,256]{2,1,0:T(8,128)}, f32[3,128,256]{2,1,0:T(8,128)S(1)}, u32[]{:S(2)}) copy-start(f32[3,128,256]{2,1,0:T(8,128)S(1)} %collective-permute-done.9.rest_3_) | copy-start | bytes 1179652
  94.6 2.0 %collective-permute-start.6 = (f32[512,128]{1,0:T(8,128)S(1)}, f32[512,128]{1,0:T(8,128)S(1)}, u32[]{:S(2)}, u32[]{:S(2)}) collective-permute-start(f32[512,128]{1,0:T(8,128)S(1)} %slice.80), channel_id=1, source_target_pairs={{0,1},{1,0},{2,3},{3,2},{4,5},{5,4},{6,7},{7,6},{8,9},{9,8},{10,11... | collective-permute-start | bytes 786440 | tf_op jit(solution)/shard_map/ppermute | solution.py:231
  95.7 3.1 %copy-start.12 = (f32[3,128,256]{2,1,0:T(8,128)}, f32[3,128,256]{2,1,0:T(8,128)S(1)}, u32[]{:S(2)}) copy-start(f32[3,128,256]{2,1,0:T(8,128)S(1)} %collective-permute-done.10.rest_4_) | copy-start | bytes 1179652
  95.7 3.1 %collective-permute-start.14 = (f32[3,128,256]{2,1,0:T(8,128)S(1)}, f32[3,128,256]{2,1,0:T(8,128)S(1)}, u32[]{:S(2)}, u32[]{:S(2)}) collective-permute-start(f32[3,128,256]{2,1,0:T(8,128)S(1)} %collective-permute-done.9.rest_3_), channel_id=1, source_target_pairs={{0,1},{1,0},{2,3},{3,2},{4,5},{5,4},{6,7},{7,6},{8,9},{9,8},{10,11... | collective-permute-start | bytes 1179656 | tf_op jit(solution)/shard_map/ppermute | solution.py:231
  96.7 2.2 %collective-permute-start.15 = (f32[3,128,256]{2,1,0:T(8,128)S(1)}, f32[3,128,256]{2,1,0:T(8,128)S(1)}, u32[]{:S(2)}, u32[]{:S(2)}) collective-permute-start(f32[3,128,256]{2,1,0:T(8,128)S(1)} %collective-permute-done.10.rest_4_), channel_id=1, source_target_pairs={{0,1},{1,0},{2,3},{3,2},{4,5},{5,4},{6,7},{7,6},{8,9},{9,8},{10,11... | collective-permute-start | bytes 1179656 | tf_op jit(solution)/shard_map/ppermute | solution.py:231
  98.8 1.7 copy-start.8
  98.8 1.7 copy-start.13
  98.8 1.7 copy-start.14
  98.9 1.8 copy-start.10
  127.7 10.6 %copy-start.1 = (f32[512,128]{1,0:T(8,128)}, f32[512,128]{1,0:T(8,128)S(1)}, u32[]{:S(2)}) copy-start(f32[512,128]{1,0:T(8,128)S(1)} %fusion.16) | copy-start | bytes 786436
  127.7 11.6 %collective-permute-start.26 = (f32[128,128]{1,0:T(8,128)S(1)}, f32[128,128]{1,0:T(8,128)S(1)}, u32[]{:S(2)}, u32[]{:S(2)}) collective-permute-start(f32[128,128]{1,0:T(8,128)S(1)} %bitcast.83), channel_id=1, source_target_pairs={{0,8},{8,16},{16,24},{24,0},{32,40},{40,48},{48,56},{56,32},{64,72... | collective-permute-start | bytes 196616 | tf_op jit(solution)/shard_map/ppermute | solution.py:235
  129.7 9.6 %collective-permute-start.27 = (f32[128,128]{1,0:T(8,128)S(1)}, f32[128,128]{1,0:T(8,128)S(1)}, u32[]{:S(2)}, u32[]{:S(2)}) collective-permute-start(f32[128,128]{1,0:T(8,128)S(1)} %bitcast.84), channel_id=1, source_target_pairs={{0,24},{8,0},{16,8},{24,16},{32,56},{40,32},{48,40},{56,48},{64,88... | collective-permute-start | bytes 196616 | tf_op jit(solution)/shard_map/ppermute | solution.py:235
  130.6 8.8 %collective-permute-start.28 = (f32[128,128]{1,0:T(8,128)S(1)}, f32[128,128]{1,0:T(8,128)S(1)}, u32[]{:S(2)}, u32[]{:S(2)}) collective-permute-start(f32[128,128]{1,0:T(8,128)S(1)} %bitcast.85), channel_id=1, source_target_pairs={{0,16},{8,24},{16,0},{24,8},{32,48},{40,56},{48,32},{56,40},{64,80... | collective-permute-start | bytes 196616 | tf_op jit(solution)/shard_map/ppermute | solution.py:235
  138.3 33.3 %collective-permute-start.16 = (f32[8,520,128]{2,1,0:T(8,128)S(1)}, f32[8,520,128]{2,1,0:T(8,128)}, u32[]{:S(2)}, u32[]{:S(2)}) collective-permute-start(f32[8,520,128]{2,1,0:T(8,128)S(1)} %get-tuple-element.26), channel_id=1, source_target_pairs={{0,1},{1,0},{2,3},{3,2},{4,5},{5,4},{6,7},{7,6},{8,9},{9,8},{10,11... | collective-permute-start | bytes 6389768 | tf_op jit(solution)/shard_map/ppermute | solution.py:231
  139.3 14.8 %collective-permute-start.29 = (f32[4,128,128]{2,1,0:T(8,128)S(1)}, f32[4,128,128]{2,1,0:T(8,128)S(1)}, u32[]{:S(2)}, u32[]{:S(2)}) collective-permute-start(f32[4,128,128]{2,1,0:T(8,128)S(1)} %pad_maximum_fusion), channel_id=1, source_target_pairs={{0,32},{8,40},{16,48},{24,56},{32,64},{40,72},{48,80},{56,88},{64,... | collective-permute-start | bytes 786440 | tf_op jit(solution)/shard_map/ppermute | solution.py:235
  142.1 12.1 %collective-permute-start.30 = (f32[4,128,128]{2,1,0:T(8,128)S(1)}, f32[4,128,128]{2,1,0:T(8,128)S(1)}, u32[]{:S(2)}, u32[]{:S(2)}) collective-permute-start(f32[4,128,128]{2,1,0:T(8,128)S(1)} %pad_maximum_fusion), channel_id=1, source_target_pairs={{0,96},{8,104},{16,112},{24,120},{32,0},{40,8},{48,16},{56,24},{64... | collective-permute-start | bytes 786440 | tf_op jit(solution)/shard_map/ppermute | solution.py:235
  142.1 12.1 %collective-permute-start.31 = (f32[4,128,128]{2,1,0:T(8,128)S(1)}, f32[4,128,128]{2,1,0:T(8,128)S(1)}, u32[]{:S(2)}, u32[]{:S(2)}) collective-permute-start(f32[4,128,128]{2,1,0:T(8,128)S(1)} %pad_maximum_fusion), channel_id=1, source_target_pairs={{0,64},{8,72},{16,80},{24,88},{32,96},{40,104},{48,112},{56,120},{... | collective-permute-start | bytes 786440 | tf_op jit(solution)/shard_map/ppermute | solution.py:235
  154.3 17.3 %copy-start.2 = (f32[16,128,128]{2,1,0:T(8,128)}, f32[16,128,128]{2,1,0:T(8,128)S(1)}, u32[]{:S(2)}) copy-start(f32[16,128,128]{2,1,0:T(8,128)S(1)} %constant_dynamic-update-slice_fusion.q_ref) | copy-start | bytes 3145732
  (1 other events, 1.6 us)
Sparse Core Ops, SparseCore 0:
  10.4 55.2 all-gather.2

commit v3 on v0

v3 whole, which is shorter than its diff:
```python
import functools
import jax
import jax.numpy as jnp
from jax import lax
from jax.experimental import pallas as pl
from jax.experimental.pallas import tpu as pltpu
from jax.sharding import PartitionSpec as P

BF = jnp.bfloat16
F32 = jnp.float32
NT = (((1,), (1,)), ((), ()))
NN = (((1,), (0,)), ((), ()))
VMEM = 56 << 20
highest = lax.Precision.HIGHEST


def split(v):
    h = v.astype(BF)
    return h, (v - h.astype(F32)).astype(BF)


def product(ah, al, bh, bl, dims):
    side = dims[0][1][0]
    left = jnp.concatenate([ah, al, ah], axis=1)
    right = jnp.concatenate([bh, bh, bl], axis=side)
    return lax.dot_general(left, right, dims, preferred_element_type=F32)


def choose(masks, values):
    out = jnp.zeros_like(values[0])
    for m, v in zip(masks, values):
        out = jnp.where(m, v, out)
    return out


def label(ids, i):
    return ids[i].astype(F32).astype(BF)


def partial_body(ids, c_ref, s_ref, w_ref, v_ref, o_ref):
    total = jnp.zeros((128, 128), F32)
    for u in range(3):
        block = ids[u].astype(F32)
        wh, wl = split(w_ref[u])
        m = [s_ref[k] == block for k in range(4)]
        d = jnp.concatenate([choose(m, [c_ref[k, :, q * 128:(q + 1) * 128] for k in range(4)]) for q in range(2)], axis=1)
        dh, dl = split(d)
        v = product(dh, dl, wh, wl, NN)
        vh, vl = split(v[:128])
        total = total + product(vh, vl, dh[:128], dl[:128], NT)
        for q in range(2):
            for t in range(4):
                part = v[t * 128:(t + 1) * 128, q * 128:(q + 1) * 128]
                for k in range(4):
                    before = jnp.zeros_like(part) if u == 0 else v_ref[q, t, k]
                    v_ref[q, t, k] = jnp.where(m[k][t * 128:(t + 1) * 128], part, before)
    o_ref[...] = total


def partial(ids, c, s, w):
    whole = lambda shape: pl.BlockSpec(shape, lambda g, i: (0,) * len(shape))
    shapes = [(2, 4, 4, 128, 128), (128, 128)]
    grid = pltpu.PrefetchScalarGridSpec(num_scalar_prefetch=1, grid=(1,), in_specs=[whole(c.shape), whole(s.shape), whole(w.shape)],
                                        out_specs=[whole(v) for v in shapes])
    return pl.pallas_call(partial_body, grid_spec=grid, out_shape=[jax.ShapeDtypeStruct(v, F32) for v in shapes],
                          compiler_params=pltpu.CompilerParams(vmem_limit_bytes=VMEM), name="partial",
                          cost_estimate=pl.CostEstimate(flops=2 * 3 * 512 * 768 * 256, bytes_accessed=6 << 20, transcendentals=0))(ids, c, s, w)


def fill_rows(v_ref, high, low):
    for t in range(4):
        for k in range(4):
            high[k, t * 128:(t + 1) * 128], low[k, t * 128:(t + 1) * 128] = split(v_ref[t, k])


def gather_blocks(ids, base, sup, high, low, axis):
    highs, lows = [], []
    for u in range(6):
        block = label(ids, base + u)
        m = [s == block for s in sup]
        highs.append(choose(m, [high(k) for k in range(4)]))
        lows.append(choose(m, [low(k) for k in range(4)]))
    return jnp.concatenate(highs, axis=axis), jnp.concatenate(lows, axis=axis)


def lead_body(ids, v0_ref, v1_ref, s_ref, d_ref, z_ref, i_ref, h_ref, p_ref, vh, vl, dh, dl, total):
    g = pl.program_id(0)

    @pl.when(g == 0)
    def _():
        for j, ref in enumerate((v0_ref, v1_ref)):
            fill_rows(ref, vh.at[j], vl.at[j])
            for k in range(4):
                dh[j, k], dl[j, k] = split(d_ref[j, k])
        total[...] = jnp.zeros_like(total)

    sup = [s_ref[k] for k in range(4)]
    first = [z_ref[k] for k in range(4)]
    for j in range(2):
        ah, al = gather_blocks(ids, 6 * g, sup, lambda k: vh[j, k], lambda k: vl[j, k], 1)
        bh, bl = gather_blocks(ids, 6 * g, first, lambda k: dh[j, k], lambda k: dl[j, k], 1)
        total[...] += product(ah, al, bh, bl, NT)

    @pl.when(g == 3)
    def _():
        ih, il = split(i_ref[...])
        total[:128] += h_ref[...]
        ah, al = split(total[...])
        p_ref[...] = product(ah, al, ih, il, NT)


def lead(ids, v0, v1, s, d, z, inverse, shift):
    whole = lambda v: pl.BlockSpec(v.shape, lambda g, i: (0,) * v.ndim)
    args = [v0, v1, s, d, z, inverse, shift]
    grid = pltpu.PrefetchScalarGridSpec(
        num_scalar_prefetch=1, grid=(4,), in_specs=[whole(v) for v in args], out_specs=pl.BlockSpec((512, 128), lambda g, i: (0, 0)),
        scratch_shapes=[pltpu.VMEM((2, 4, 512, 128), BF)] * 2 + [pltpu.VMEM((2, 4, 128, 128), BF)] * 2 + [pltpu.VMEM((512, 128), F32)])
    return pl.pallas_call(lead_body, grid_spec=grid, out_shape=jax.ShapeDtypeStruct((512, 128), F32),
                          compiler_params=pltpu.CompilerParams(vmem_limit_bytes=VMEM), name="lead",
                          cost_estimate=pl.CostEstimate(flops=2 * 3 * 512 * 6144 * 128, bytes_accessed=6 << 20, transcendentals=0))(ids, *args)


def block_body(has_sum, ids, v_ref, r_ref, c_ref, s_ref, *rest):
    if has_sum:
        a_ref, o_ref, vh, vl, ch, cl = rest
    else:
        o_ref, vh, vl, ch, cl = rest
    g = pl.program_id(0)

    @pl.when(g == 0)
    def _():
        fill_rows(v_ref, vh, vl)
        for t in range(8):
            for k in range(4):
                ch[k, :, t * 128:(t + 1) * 128], cl[k, :, t * 128:(t + 1) * 128] = split(c_ref[t, k * 128:(k + 1) * 128])
        o_ref[...] = a_ref[...] if has_sum else jnp.zeros_like(o_ref)

    rows = [r_ref[k] for k in range(4)]
    ah, al = gather_blocks(ids, 6 * g, rows, lambda k: vh[k], lambda k: vl[k], 1)
    for q in range(2):
        r = slice(q * 512, (q + 1) * 512)
        sup = [jnp.broadcast_to(s_ref[k:k + 1, r], (128, 512)).astype(BF) for k in range(4)]
        bh, bl = gather_blocks(ids, 6 * g, sup, lambda k: ch[k, :, r], lambda k: cl[k, :, r], 0)
        o_ref[:, r] += product(ah, al, bh, bl, NN)


def block_product(ids, v, r, c, s, start=None):
    whole = lambda u: pl.BlockSpec(u.shape, lambda g, i: (0,) * u.ndim)
    args = [v, r, c, s] + ([] if start is None else [start])
    grid = pltpu.PrefetchScalarGridSpec(
        num_scalar_prefetch=1, grid=(4,), in_specs=[whole(u) for u in args], out_specs=pl.BlockSpec((512, 1024), lambda g, i: (0, 0)),
        scratch_shapes=[pltpu.VMEM((4, 512, 128), BF)] * 2 + [pltpu.VMEM((4, 128, 1024), BF)] * 2)
    return pl.pallas_call(functools.partial(block_body, start is not None), grid_spec=grid,
                          out_shape=jax.ShapeDtypeStruct((512, 1024), F32),
                          compiler_params=pltpu.CompilerParams(vmem_limit_bytes=VMEM), name="block",
                          cost_estimate=pl.CostEstimate(flops=2 * 3 * 512 * 3072 * 1024, bytes_accessed=10 << 20, transcendentals=0))(ids, *args)


def inverse_body(c_ref, o_ref):
    n = 128
    row = lax.broadcasted_iota(jnp.int32, (n, n), 0)
    col = lax.broadcasted_iota(jnp.int32, (n, n), 1)
    below = lax.broadcasted_iota(jnp.int32, (n, 1), 0)
    lane = lax.broadcasted_iota(jnp.int32, (1, n), 1)
    o_ref[...] = jnp.concatenate([c_ref[...], jnp.where(row == col, 1.0, 0.0).astype(F32)], axis=1)

    def at(v, k):
        return jnp.sum(jnp.where(lane == k, v, 0.0), axis=1, keepdims=True)

    def step(i, _):
        k = 2 * i
        line0 = o_ref[pl.ds(k, 1), :]
        line1 = o_ref[pl.ds(k + 1, 1), :]
        left = o_ref[:, :n]
        a, b, c = at(line0[:, :n], k), at(line0[:, :n], k + 1), at(line1[:, :n], k + 1)
        col0, col1 = at(left, k), at(left, k + 1)
        s0 = lax.rsqrt(a)
        b = b * s0
        s1 = lax.rsqrt(c - b * b)
        line0 = line0 * s0
        line1 = (line1 - b * line0) * s1
        f0 = jnp.where(below > k + 1, col0 * s0, 0.0)
        f1 = jnp.where(below > k + 1, (col1 - f0 * b) * s1, 0.0)
        o_ref[...] = o_ref[...] - f0 * line0 - f1 * line1
        o_ref[pl.ds(k, 1), :] = line0
        o_ref[pl.ds(k + 1, 1), :] = line1
        return 0

    lax.fori_loop(0, n // 2, step, 0)


def inverse_of(c):
    return pl.pallas_call(inverse_body, out_shape=jax.ShapeDtypeStruct((128, 256), F32), name="inverse",
                          cost_estimate=pl.CostEstimate(flops=2 * 3 * 512 * 3072 * 768, bytes_accessed=1 << 20, transcendentals=0))(c)


def finish_body(where, s_ref, p_ref, q_ref, d_ref, o_ref):
    g = pl.program_id(0)
    r, col = where[0], where[1]
    row = lax.broadcasted_iota(jnp.int32, (128, 128), 0)
    lane = lax.broadcasted_iota(jnp.int32, (128, 128), 1)
    for j in range(2):
        qh, ql = split(q_ref[j])
        across = col * 8 + 2 * g + j
        span = slice(j * 128, (j + 1) * 128)
        for t in range(4):
            ph, plo = split(p_ref[t])
            down = t * 16 + r
            outer = product(ph, plo, qh, ql, NT)
            diagonal = jnp.where((row == lane) & (down == across), jnp.broadcast_to(d_ref[t:t + 1], (128, 128)), 0.0)
            o_ref[t, :, span] = s_ref[t, :, span] + diagonal - jnp.where((down > 0) & (across > 0), outer, 0.0)


def finish(where, s, p, q, d):
    grid = pltpu.PrefetchScalarGridSpec(
        num_scalar_prefetch=1, grid=(4,),
        in_specs=[pl.BlockSpec((4, 128, 256), lambda g, w: (0, 0, g)), pl.BlockSpec((4, 128, 128), lambda g, w: (0, 0, 0)),
                  pl.BlockSpec((2, 128, 128), lambda g, w: (w[2] * 4 + g, 0, 0)), pl.BlockSpec((4, 128), lambda g, w: (0, 0))],
        out_specs=pl.BlockSpec((4, 128, 256), lambda g, w: (0, 0, g)))
    return pl.pallas_call(finish_body, grid_spec=grid, out_shape=jax.ShapeDtypeStruct((4, 128, 1024), F32),
                          compiler_params=pltpu.CompilerParams(vmem_limit_bytes=VMEM), name="finish",
                          cost_estimate=pl.CostEstimate(flops=2 * 3 * 512 * 128 * 1024, bytes_accessed=5 << 20, transcendentals=0))(where, s, p, q, d)


SWAP = [(i, i ^ 1) for i in range(8)]
CHIPS = [[0, 2, 4, 6], [1, 3, 5, 7]]


def swap(v):
    return lax.ppermute(v, "cols", SWAP)


def exchange(v, axis, groups=None):
    return lax.all_to_all(v, axis, 0, 0, axis_index_groups=groups, tiled=True)


def repeat(v, n):
    return jnp.broadcast_to(v[None], (n,) + v.shape)


def lanes(s):
    return jnp.broadcast_to(s[:, :, None], s.shape + (128,))


def local(coefficients, support, primal, dual_inverse, block_sizes, damping, right_sides):
    col = lax.axis_index("cols")
    r = lax.axis_index("rows")
    x = col // 2
    p = col % 2
    sup = support.astype(F32)
    tile = lax.dynamic_index_in_dim(coefficients, x, 0, keepdims=False)
    tile = lax.dynamic_slice_in_dim(tile, p * 128, 128, 2)
    mine = jnp.concatenate([jnp.transpose(tile, (1, 2, 0)).reshape(512, 128),
                            lax.dynamic_index_in_dim(sup, x, 0, keepdims=False).T, jnp.zeros((4, 128), F32)], axis=0)
    gathered = lax.all_gather(mine, "rows")

    positions = jnp.arange(256, dtype=jnp.int32)
    active = (positions[None, :] < block_sizes[:, None]).astype(F32)
    w = primal * dual_inverse * active[:, :, None] * active[:, None, :]
    ids = jnp.arange(24, dtype=jnp.int32)
    owned = (col * 3 + jnp.arange(3)).astype(jnp.int32)
    own = jnp.transpose(coefficients, (2, 0, 1, 3)).reshape(4, 512, 256)
    own_sup = lanes(jnp.transpose(sup, (2, 0, 1)).reshape(4, 512))
    part, corner = partial(owned, own, own_sup, w)
    eye = jnp.eye(128, dtype=F32)

    half = lax.dynamic_index_in_dim(part, p, 0, keepdims=False)
    half = half + swap(lax.dynamic_index_in_dim(part, 1 - p, 0, keepdims=False))
    corner = jnp.sum(exchange(repeat(corner, 8), "cols").reshape(8, 128, 128), axis=0) + eye * damping[0]
    tile_sum = jnp.sum(exchange(half, "cols", CHIPS), axis=0)
    v_own = exchange(repeat(tile_sum, 4), "cols", CHIPS)
    v_other = swap(v_own)
    inverse = exchange(repeat(inverse_of(corner)[:, 128:], 16), "rows")[0]

    head = lax.dynamic_slice_in_dim(lax.dynamic_index_in_dim(coefficients[0], x, 1, keepdims=False), p * 128, 128, 1)
    head = jnp.concatenate([head, sup[0].T, right_sides[0], damping[:1], jnp.zeros((7, 128), F32)], axis=0)
    head = exchange(repeat(head, 16), "rows")[0]
    first = exchange(repeat(head[:128], 8), "cols").reshape(4, 2, 128, 128)
    first = jnp.stack([jnp.where(p == 0, first[:, 0], first[:, 1]), jnp.where(p == 0, first[:, 1], first[:, 0])])
    first_sup = lanes(head[128:132]).astype(BF)
    row_sup = own_sup.astype(BF)
    shift = jnp.where(r == 0, damping[0], 0.0) * eye
    panel_factor = lead(ids, v_own, v_other, row_sup, first, first_sup, inverse, shift).reshape(4, 128, 128)
    every = exchange(repeat(lax.dynamic_index_in_dim(panel_factor, x, 0, keepdims=False), 16), "rows")
    leading = lax.dot_general(head[132:136], inverse, NT, precision=highest)
    remainder = right_sides - jnp.einsum("sk,tak->tsa", leading, panel_factor, precision=highest)
    solved = jnp.where(((jnp.arange(4) > 0) | (r > 0))[:, None, None], remainder, leading[None])

    kept = lax.dynamic_slice_in_dim(gathered, 8 * p, 8, 0)
    swapped = swap(lax.dynamic_slice_in_dim(gathered, 8 * (1 - p), 8, 0))
    col_sup = jnp.pad(jnp.transpose(kept[:, 512:516], (1, 0, 2)).reshape(4, 1024), ((0, 4), (0, 0)))
    out = block_product(ids, v_own, row_sup, kept, col_sup)
    out = block_product(ids, v_other, row_sup, swapped, col_sup, out)
    updated = finish(jnp.stack([r, col, p]).astype(jnp.int32), out.reshape(4, 128, 1024), panel_factor, every, damping)
    return updated, panel_factor, solved


def solution(mesh):
    in_specs = (
        P(None, "rows", None, None),
        P(None, "rows", None),
        P("cols", None, None),
        P("cols", None, None),
        P("cols"),
        P(None, "rows"),
        P(None, "cols", "rows"),
    )
    out_specs = (P(None, "rows", "cols"), P(None, "rows", None), P(None, "cols", "rows"))
    return jax.shard_map(local, mesh=mesh, in_specs=in_specs, out_specs=out_specs, check_vma=False)
```

time: 686 us -> 218 us (0.32)
  waiting for transfers between devices: 473 us -> 48.7 us
  matrix products: 104 us -> 1.96 us
  Pallas kernels: 0 us -> 70.1 us
  blocking collectives: 54.4 us -> 0 us
  starting transfers between devices: 0.2 us -> 41.7 us
  other arithmetic: 26.6 us -> 9.17 us
  local copies, waits for them, and re-layouts: 14.3 us -> 30.6 us
    psum x2 -> x0, waiting for transfers between devices: 195 us -> none  [broadcast(): return lax.psum(block, axis)]
    all_gather x2 -> x1, waiting for transfers between devices: 186 us -> 0.01 us  [local(): gathered = lax.all_gather(mine, 'rows')]
    dot_general x7 -> x1, matrix products: 101 us -> 1.01 us  [local(): leading = lax.dot_general(head[132:136], inverse, NT, precision=highest)]
    reduce_scatter x1 -> x0, waiting for transfers between devices: 90.8 us -> none  [local(): lax.psum_scatter(partial_value, 'cols', scatter_dimension=2, tiled=True)]
    pallas_call x0 -> x6, Pallas kernels: none -> 70.1 us  [the longest x2 35.1 us: block_product(): pl.pallas_call(functools.partial(block_body, start is not None), grid_spe...]
    all_to_all x0 -> x7, waiting for transfers between devices: none -> 48.7 us  [exchange(): return lax.all_to_all(v, axis, 0, 0, axis_index_groups=groups, tiled=True)]
    all_to_all x0 -> x7, starting transfers between devices: none -> 37.4 us  [exchange(): return lax.all_to_all(v, axis, 0, 0, axis_index_groups=groups, tiled=True)]
    psum x1 -> x0, blocking collectives: 33.6 us -> none  [broadcast(): return lax.psum(block, axis)]
  transfers between devices with their start and end apart: 5 -> 11, of which waited for: 5 -> 6; matrix products, arithmetic and copies ran while one was open for 3% -> 17% of each run, Pallas kernels for 0% -> 30%
where the time goes in v3:
time: 218 us; the launch traced here: 217 us
  Pallas kernels  70.1 us (32%)
  waiting for transfers between devices  48.7 us (22%)
  starting transfers between devices  41.7 us (19%)
  local copies, waits for them, and re-layouts  30.6 us (14%)
  between operations  14.2 us (7%)
  other arithmetic  9.17 us (4%)
    all_to_all x7, waiting for transfers between devices, exchange(): return lax.all_to_all(v, axis, 0, 0, axis_index_groups=groups, tiled=True)  48.7 us
    all_to_all x7, starting transfers between devices, exchange(): return lax.all_to_all(v, axis, 0, 0, axis_index_groups=groups, tiled=True)  37.4 us
    pallas_call x2, Pallas kernels, block_product(): pl.pallas_call(functools.partial(block_body, start is not None), grid_spe...  35.1 us
    pallas_call x1, Pallas kernels, lead(): pl.pallas_call(lead_body, grid_spec=grid, out_shape=jax.ShapeDtypeStruct(...  14.4 us
    pallas_call x1, Pallas kernels, inverse_of(): pl.pallas_call(inverse_body, out_shape=jax.ShapeDtypeStruct((128, 256), F...  9.55 us
    broadcast_in_dim x8, local copies, waits for them, and re-layouts, repeat(): return jnp.broadcast_to(v[None], (n,) + v.shape)  8.72 us
    pallas_call x1, Pallas kernels, partial(): pl.pallas_call(partial_body, grid_spec=grid, out_shape=[jax.ShapeDtypeStr...  5.64 us
    pallas_call x1, Pallas kernels, finish(): pl.pallas_call(finish_body, grid_spec=grid, out_shape=jax.ShapeDtypeStruc...  5.47 us
  transfers between devices with their start and end apart: 11, of which 6 were waited for; matrix products, arithmetic and copies ran while one was open for 17% of the time, Pallas kernels for 30%

profile of v3, /device:TPU:1, one launch (start us, length us, event | category | flops | bytes accessed | tf_op | source)
XLA Modules:
  0.0 216.6 jit_solution(196302791841368106)
XLA Ops:
  7.2 0.7 fusion.9
  7.9 1.1 constant_dynamic-slice_fusion.4
  9.3 0.9 maximum_maximum_fusion
  10.2 3.4 %copy.20 = f32[4,4,128,256]{3,2,1,0:T(8,128)} copy(f32[4,4,128,256]{3,0,2,1:T(4,128)} %bitcast.84) | data formatting | bytes 4194304 | tf_op jit(solution)/shard_map/transpose | solution.py:262
  14.3 1.1 multiply_multiply_fusion.w_ref
  15.4 1.3 broadcast_in_dim.43.s_ref
  16.7 5.6 %partial.1 = (f32[2,4,4,128,128]{4,3,2,1,0:T(8,128)}, f32[128,128]{1,0:T(8,128)}) custom-call(s32[3]{0:T(128)} %iota_add_fusion.ids, f32[4,512,256]{2,1,0:T(8,128)} %bitcast.81, f32[4,512,128]{2,1,0:T(8,128)} %broadcast_in_dim.43.s_ref, f32[3,256,256]{2,1,0:T(8,128)} %multiply_multiply_fusion.w_ref), custom_call_target="tpu_custom_call" | custom-call | flops 603979776 | bytes 6291456 | tf_op jit(solution)/shard_map/partial/pallas_call | solution.py:65
  22.4 2.5 %dynamic-slice_bitcast_fusion = f32[4,4,128,128]{3,2,1,0:T(8,128)} fusion(f32[2,4,4,128,128]{4,3,2,1,0:T(8,128)} %get-tuple-element.5, s32[]{:T(128)S(6)} %select_n.89), kind=kLoop, calls=%fused_computation.4 | loop fusion | bytes 2097156 | tf_op jit(solution)/shard_map/jit(dynamic_index_in_dim)/squeeze | solution.py:268
  24.8 1.5 collective-permute-start
  26.3 1.7 broadcast_in_dim.98
  28.0 4.5 %all-to-all-start.4 = ((f32[8,128,128]{2,1,0:T(8,128)}), f32[8,128,128]{2,1,0:T(8,128)S(1)}, u32[]{:S(2)}, u32[]{:S(2)}) async-start(f32[8,128,128]{2,1,0:T(8,128)} %broadcast_in_dim.98), calls=%async_computation.4 | async-start | bytes 1048576 | tf_op jit(solution)/shard_map/all_to_all | solution.py:234
  32.5 2.3 %bitcast_add_fusion = f32[4,4,128,128]{3,2,1,0:T(8,128)} fusion(f32[4,4,128,128]{3,2,1,0:T(8,128)} %collective-permute-done, f32[2,4,4,128,128]{4,3,2,1,0:T(8,128)S(1)} %copy-done.1, s32[]{:T(128)S(6)} %select_n.88), kind=kLoop, calls=%fused_computation.3 | loop fusion | flops 262144 | bytes 3145732 | tf_op jit(solution)/shard_map/add | solution.py:268
  34.9 7.1 %all-to-all-done.4 = f32[8,128,128]{2,1,0:T(8,128)S(1)} async-done(((f32[8,128,128]{2,1,0:T(8,128)}), f32[8,128,128]{2,1,0:T(8,128)S(1)}, u32[]{:S(2)}, u32[]{:S(2)}) %all-to-all-start.4) | async-done | bytes 524320 | tf_op jit(solution)/shard_map/all_to_all | solution.py:234
  42.0 3.5 %all-to-all-start = ((f32[4,4,128,128]{3,2,1,0:T(8,128)}), f32[4,4,128,128]{3,2,1,0:T(8,128)S(1)}, u32[]{:S(2)}, u32[]{:S(2)}) async-start(f32[4,4,128,128]{3,2,1,0:T(8,128)} %bitcast_add_fusion), calls=%async_computation | async-start | bytes 2097152 | tf_op jit(solution)/shard_map/all_to_all | solution.py:234
  45.5 1.1 slice.51
  46.8 0.7 fusion.8
  47.6 12.1 %all-to-all-done = f32[4,4,128,128]{3,2,1,0:T(8,128)S(1)} async-done(((f32[4,4,128,128]{3,2,1,0:T(8,128)}), f32[4,4,128,128]{3,2,1,0:T(8,128)S(1)}, u32[]{:S(2)}, u32[]{:S(2)}) %all-to-all-start) | async-done | bytes 1048608 | tf_op jit(solution)/shard_map/all_to_all | solution.py:234
  59.7 1.1 broadcast_in_dim.94
  60.8 7.9 %all-to-all-start.2 = ((f32[16,144,128]{2,1,0:T(8,128)}), f32[16,144,128]{2,1,0:T(8,128)}, u32[]{:S(2)}, u32[]{:S(2)}) async-start(f32[16,144,128]{2,1,0:T(8,128)} %broadcast_in_dim.94), calls=%async_computation.2 | async-start | bytes 2359296 | tf_op jit(solution)/shard_map/all_to_all | solution.py:234
  68.8 16.2 %all-to-all-done.2 = f32[16,144,128]{2,1,0:T(8,128)} async-done(((f32[16,144,128]{2,1,0:T(8,128)}), f32[16,144,128]{2,1,0:T(8,128)}, u32[]{:S(2)}, u32[]{:S(2)}) %all-to-all-start.2) | async-done | bytes 1179680 | tf_op jit(solution)/shard_map/all_to_all | solution.py:234
  85.0 1.1 broadcast_in_dim.44
  86.1 4.3 %all-to-all-start.1 = ((f32[4,4,128,128]{3,2,1,0:T(8,128)}), f32[4,4,128,128]{3,2,1,0:T(8,128)}, u32[]{:S(2)}, u32[]{:S(2)}) async-start(f32[4,4,128,128]{3,2,1,0:T(8,128)} %broadcast_in_dim.44), calls=%async_computation.1 | async-start | bytes 2097152 | tf_op jit(solution)/shard_map/all_to_all | solution.py:234
  91.0 9.6 %inverse.1 = f32[128,256]{1,0:T(8,128)} custom-call(f32[128,128]{1,0:T(8,128)} %select_add_fusion.c_ref), custom_call_target="tpu_custom_call" | custom-call | flops 7247757312 | bytes 1048576 | tf_op jit(solution)/shard_map/inverse/pallas_call | solution.py:193
  100.5 0.8 slice.68
  101.8 1.1 broadcast_in_dim.99
  102.9 6.5 %all-to-all-start.5 = ((f32[16,128,128]{2,1,0:T(8,128)}), f32[16,128,128]{2,1,0:T(8,128)S(1)}, u32[]{:S(2)}, u32[]{:S(2)}) async-start(f32[16,128,128]{2,1,0:T(8,128)} %broadcast_in_dim.99), calls=%async_computation.5 | async-start | bytes 2097152 | tf_op jit(solution)/shard_map/all_to_all | solution.py:234
  110.6 0.8 slice_bitcast_fusion.3
  111.5 2.7 %collective-permute-start.1 = (f32[4,4,128,128]{3,2,1,0:T(8,128)}, f32[4,4,128,128]{3,2,1,0:T(8,128)}, u32[]{:S(2)}, u32[]{:S(2)}) collective-permute-start(f32[4,4,128,128]{3,2,1,0:T(8,128)} %all-to-all-done.1.v_ref.v0_ref), channel_id=1, source_target_pairs={{0,1},{1,0},{2,3},{3,2},{4,5},{5,4},{6,7},{7,6},{8,9},{9,8},{10,11... | collective-permute-start | bytes 3145736 | tf_op jit(solution)/shard_map/ppermute | solution.py:230
  114.1 0.7 fusion.7
  114.8 9.0 %all-to-all-done.5 = f32[16,128,128]{2,1,0:T(8,128)S(1)} async-done(((f32[16,128,128]{2,1,0:T(8,128)}), f32[16,128,128]{2,1,0:T(8,128)S(1)}, u32[]{:S(2)}, u32[]{:S(2)}) %all-to-all-start.5) | async-done | bytes 1048608 | tf_op jit(solution)/shard_map/all_to_all | solution.py:234
  123.8 0.9 broadcast_in_dim.96
  124.7 7.0 %all-to-all-start.3 = ((f32[8,128,128]{2,1,0:T(8,128)}), f32[8,128,128]{2,1,0:T(8,128)S(1)}, u32[]{:S(2)}, u32[]{:S(2)}) async-start(f32[8,128,128]{2,1,0:T(8,128)} %broadcast_in_dim.96), calls=%async_computation.3 | async-start | bytes 1048576 | tf_op jit(solution)/shard_map/all_to_all | solution.py:234
  132.3 3.9 %constant_dynamic-slice_fusion.1 = (f32[8,520,128]{2,1,0:T(8,128)}, f32[8,520,128]{2,1,0:T(8,128)S(1)}) fusion(f32[16,520,128]{2,1,0:T(8,128)} %bitcast.82, s32[]{:T(128)S(6)} %select_n.96, s32[]{:T(128)S(6)} %select_n.95), kind=kLoop, calls=%fused_computation.22 | loop fusion | bytes 8519688 | tf_op jit(solution)/shard_map/dynamic_slice | solution.py:289
  136.4 1.0 fusion.5
  137.4 3.8 %all-to-all-done.3 = f32[8,128,128]{2,1,0:T(8,128)S(1)} async-done(((f32[8,128,128]{2,1,0:T(8,128)}), f32[8,128,128]{2,1,0:T(8,128)S(1)}, u32[]{:S(2)}, u32[]{:S(2)}) %all-to-all-start.3) | async-done | bytes 524320 | tf_op jit(solution)/shard_map/all_to_all | solution.py:234
  141.3 0.8 pad_maximum_fusion.d_ref
  142.1 0.8 broadcast_in_dim.97.z_ref
  142.9 1.1 broadcast_in_dim.45.r_ref.s_ref
  144.5 14.4 %lead.1 = f32[512,128]{1,0:T(8,128)} custom-call(s32[24]{0:T(128)} %iota.43.ids, f32[4,4,128,128]{3,2,1,0:T(8,128)} %all-to-all-done.1.v_ref.v0_ref, f32[4,4,128,128]{3,2,1,0:T(8,128)} %collective-permute-done.1.v_ref.v1_ref, bf16[4,512,128]{2,1,0:T(8,128)(2,1)} %broadcast_in_dim.45.r_ref.s_ref, f32[2,4,128,128]{3,2,1,0:T(8,128)} %pad_maximum_fusion.d_ref, ...), custom_call_target="tpu_custom_call" | custom-call | flops 2415919104 | bytes 6291456 | tf_op jit(solution)/shard_map/lead/pallas_call | solution.py:118
  158.9 0.9 dynamic-slice_bitcast_fusion.1
  159.8 1.1 broadcast_in_dim.102
  160.9 3.8 %all-to-all-start.6 = ((f32[16,128,128]{2,1,0:T(8,128)}), f32[16,128,128]{2,1,0:T(8,128)S(1)}, u32[]{:S(2)}, u32[]{:S(2)}) async-start(f32[16,128,128]{2,1,0:T(8,128)} %broadcast_in_dim.102), calls=%async_computation.6 | async-start | bytes 2097152 | tf_op jit(solution)/shard_map/all_to_all | solution.py:234
  164.8 0.9 fusion.1
  165.7 0.8 dynamic-slice_bitcast_fusion.2
  167.6 17.2 %block.2.rest_0_ = f32[512,1024]{1,0:T(8,128)} custom-call(s32[24]{0:T(128)} %iota.42.ids, f32[4,4,128,128]{3,2,1,0:T(8,128)} %all-to-all-done.1.v_ref.v0_ref, bf16[4,512,128]{2,1,0:T(8,128)(2,1)} %broadcast_in_dim.45.r_ref.s_ref, f32[8,520,128]{2,1,0:T(8,128)} %get-tuple-element.7.c_ref, f32[8,1024]{1,0:T(8,128)} %pad.4.s_ref), custom_call_target="tpu_custom_call" | custom-call | flops 9663676416 | bytes 10485760 | tf_op jit(solution)/shard_map/block/pallas_call | solution.py:153
  185.4 17.9 %block.3 = f32[512,1024]{1,0:T(8,128)} custom-call(s32[24]{0:T(128)} %iota.40.ids, f32[4,4,128,128]{3,2,1,0:T(8,128)} %collective-permute-done.1.v_ref.v1_ref, bf16[4,512,128]{2,1,0:T(8,128)(2,1)} %broadcast_in_dim.45.r_ref.s_ref, f32[8,520,128]{2,1,0:T(8,128)} %collective-permute-done.2.c_ref, f32[8,1024]{1,0:T(8,128)} %pad.4.s_ref, f32[512,1024]{1,0:T(8,128)} %block.2.rest_0_), custom_call_target="tpu_custom_call" | custom-call | flops 9663676416 | bytes 10485760 | tf_op jit(solution)/shard_map/block/pallas_call | solution.py:153
  203.3 1.0 copy-done
  204.2 5.5 %finish.1 = f32[4,128,1024]{2,1,0:T(8,128)} custom-call(s32[3]{0:T(128)} %pad_add_fusion.where, f32[4,128,1024]{2,1,0:T(8,128)} %bitcast.85, f32[4,128,128]{2,1,0:T(8,128)} %bitcast.88, f32[16,128,128]{2,1,0:T(8,128)} %copy-done, f32[4,128]{1,0:T(4,128)} %d_ref.1), custom_call_target="tpu_custom_call" | custom-call | flops 402653184 | bytes 5242880 | tf_op jit(solution)/shard_map/finish/pallas_call | solution.py:220
  (46 shorter events, 6.6 us)
Async XLA Ops:
  7.2 125.2 %all-gather.3.cloned.1.call-start = ((), (), s32[]{:S(2)}) async-start(), calls=%async_computation.7 | async-start | bytes 4526080 | tf_op jit(solution)/shard_map/all_gather | solution.py:255
  10.2 4.0 %copy-start.7 = (s32[3]{0:T(128)S(1)}, s32[3]{0:T(128)}, u32[]{:S(2)}) copy-start(s32[3]{0:T(128)} %param.11) | copy-start | bytes 40
  10.2 4.1 %copy-start.4 = (f32[3,256,256]{2,1,0:T(8,128)S(1)}, f32[3,256,256]{2,1,0:T(8,128)}, u32[]{:S(2)}) copy-start(f32[3,256,256]{2,1,0:T(8,128)} %param.9) | copy-start | bytes 2359300
  10.2 4.1 %copy-start.5 = (f32[3,256,256]{2,1,0:T(8,128)S(1)}, f32[3,256,256]{2,1,0:T(8,128)}, u32[]{:S(2)}) copy-start(f32[3,256,256]{2,1,0:T(8,128)} %param.10) | copy-start | bytes 2359300
  22.3 10.2 %copy-start.1 = (f32[2,4,4,128,128]{4,3,2,1,0:T(8,128)S(1)}, f32[2,4,4,128,128]{4,3,2,1,0:T(8,128)}, u32[]{:S(2)}) copy-start(f32[2,4,4,128,128]{4,3,2,1,0:T(8,128)} %get-tuple-element.5) | copy-start | bytes 6291460
  24.8 7.7 %collective-permute-start = (f32[4,4,128,128]{3,2,1,0:T(8,128)}, f32[4,4,128,128]{3,2,1,0:T(8,128)}, u32[]{:S(2)}, u32[]{:S(2)}) collective-permute-start(f32[4,4,128,128]{3,2,1,0:T(8,128)} %dynamic-slice_bitcast_fusion), channel_id=1, source_target_pairs={{0,1},{1,0},{2,3},{3,2},{4,5},{5,4},{6,7},{7,6},{8,9},{9,8},{10,11... | collective-permute-start | bytes 3145736 | tf_op jit(solution)/shard_map/ppermute | solution.py:230
  28.0 14.0 %all-to-all-start.4 = ((f32[8,128,128]{2,1,0:T(8,128)}), f32[8,128,128]{2,1,0:T(8,128)S(1)}, u32[]{:S(2)}, u32[]{:S(2)}) async-start(f32[8,128,128]{2,1,0:T(8,128)} %broadcast_in_dim.98), calls=%async_computation.4 | async-start | bytes 1048576 | tf_op jit(solution)/shard_map/all_to_all | solution.py:234
  34.9 12.7 %copy-start.6 = (f32[4,4,128]{2,1,0:T(4,128)S(1)}, f32[4,4,128]{2,1,0:T(4,128)}, u32[]{:S(2)}) copy-start(f32[4,4,128]{2,1,0:T(4,128)} %param.13) | copy-start | bytes 24580
  42.0 17.7 %all-to-all-start = ((f32[4,4,128,128]{3,2,1,0:T(8,128)}), f32[4,4,128,128]{3,2,1,0:T(8,128)S(1)}, u32[]{:S(2)}, u32[]{:S(2)}) async-start(f32[4,4,128,128]{3,2,1,0:T(8,128)} %bitcast_add_fusion), calls=%async_computation | async-start | bytes 2097152 | tf_op jit(solution)/shard_map/all_to_all | solution.py:234
  60.8 24.2 %all-to-all-start.2 = ((f32[16,144,128]{2,1,0:T(8,128)}), f32[16,144,128]{2,1,0:T(8,128)}, u32[]{:S(2)}, u32[]{:S(2)}) async-start(f32[16,144,128]{2,1,0:T(8,128)} %broadcast_in_dim.94), calls=%async_computation.2 | async-start | bytes 2359296 | tf_op jit(solution)/shard_map/all_to_all | solution.py:234
  86.1 15.7 %all-to-all-start.1 = ((f32[4,4,128,128]{3,2,1,0:T(8,128)}), f32[4,4,128,128]{3,2,1,0:T(8,128)}, u32[]{:S(2)}, u32[]{:S(2)}) async-start(f32[4,4,128,128]{3,2,1,0:T(8,128)} %broadcast_in_dim.44), calls=%async_computation.1 | async-start | bytes 2097152 | tf_op jit(solution)/shard_map/all_to_all | solution.py:234
  102.9 20.9 %all-to-all-start.5 = ((f32[16,128,128]{2,1,0:T(8,128)}), f32[16,128,128]{2,1,0:T(8,128)S(1)}, u32[]{:S(2)}, u32[]{:S(2)}) async-start(f32[16,128,128]{2,1,0:T(8,128)} %broadcast_in_dim.99), calls=%async_computation.5 | async-start | bytes 2097152 | tf_op jit(solution)/shard_map/all_to_all | solution.py:234
  111.5 30.6 %collective-permute-start.1 = (f32[4,4,128,128]{3,2,1,0:T(8,128)}, f32[4,4,128,128]{3,2,1,0:T(8,128)}, u32[]{:S(2)}, u32[]{:S(2)}) collective-permute-start(f32[4,4,128,128]{3,2,1,0:T(8,128)} %all-to-all-done.1.v_ref.v0_ref), channel_id=1, source_target_pairs={{0,1},{1,0},{2,3},{3,2},{4,5},{5,4},{6,7},{7,6},{8,9},{9,8},{10,11... | collective-permute-start | bytes 3145736 | tf_op jit(solution)/shard_map/ppermute | solution.py:230
  123.8 8.5 %copy-start.2 = (f32[16,128,128]{2,1,0:T(8,128)}, f32[16,128,128]{2,1,0:T(8,128)S(1)}, u32[]{:S(2)}) copy-start(f32[16,128,128]{2,1,0:T(8,128)S(1)} %all-to-all-done.5) | copy-start | bytes 3145732
  124.7 16.5 %all-to-all-start.3 = ((f32[8,128,128]{2,1,0:T(8,128)}), f32[8,128,128]{2,1,0:T(8,128)S(1)}, u32[]{:S(2)}, u32[]{:S(2)}) async-start(f32[8,128,128]{2,1,0:T(8,128)} %broadcast_in_dim.96), calls=%async_computation.3 | async-start | bytes 1048576 | tf_op jit(solution)/shard_map/all_to_all | solution.py:234
  136.3 48.6 %collective-permute-start.2 = (f32[8,520,128]{2,1,0:T(8,128)S(1)}, f32[8,520,128]{2,1,0:T(8,128)}, u32[]{:S(2)}, u32[]{:S(2)}) collective-permute-start(f32[8,520,128]{2,1,0:T(8,128)S(1)} %get-tuple-element.8), channel_id=1, source_target_pairs={{0,1},{1,0},{2,3},{3,2},{4,5},{5,4},{6,7},{7,6},{8,9},{9,8},{10,11... | collective-permute-start | bytes 6389768 | tf_op jit(solution)/shard_map/ppermute | solution.py:230
  158.9 5.9 %copy-start.3 = (f32[512,128]{1,0:T(8,128)S(1)}, f32[512,128]{1,0:T(8,128)}, u32[]{:S(2)}) copy-start(f32[512,128]{1,0:T(8,128)} %lead.1) | copy-start | bytes 786436
  160.9 42.3 %all-to-all-start.6 = ((f32[16,128,128]{2,1,0:T(8,128)}), f32[16,128,128]{2,1,0:T(8,128)S(1)}, u32[]{:S(2)}, u32[]{:S(2)}) async-start(f32[16,128,128]{2,1,0:T(8,128)} %broadcast_in_dim.102), calls=%async_computation.6 | async-start | bytes 2097152 | tf_op jit(solution)/shard_map/all_to_all | solution.py:234
  203.3 1.0 copy-start
Sparse Core Ops, SparseCore 0:
  10.3 55.2 all-gather.2

commit v4 on v3

v4 whole, which is shorter than its diff:
```python
import functools
import jax
import jax.numpy as jnp
from jax import lax
from jax.experimental import pallas as pl
from jax.experimental.pallas import tpu as pltpu
from jax.sharding import PartitionSpec as P

BF = jnp.bfloat16
F32 = jnp.float32
NT = (((1,), (1,)), ((), ()))
NN = (((1,), (0,)), ((), ()))
VMEM = 56 << 20
highest = lax.Precision.HIGHEST


def split(v):
    h = v.astype(BF)
    return h, (v - h.astype(F32)).astype(BF)


def product(ah, al, bh, bl, dims):
    side = dims[0][1][0]
    left = jnp.concatenate([ah, al, ah], axis=1)
    right = jnp.concatenate([bh, bh, bl], axis=side)
    return lax.dot_general(left, right, dims, preferred_element_type=F32)


def choose(masks, values):
    out = jnp.zeros_like(values[0])
    for m, v in zip(masks, values):
        out = jnp.where(m, v, out)
    return out


def partial_body(info, c_ref, s_ref, w_ref, v_ref, g_ref):
    p = info[2]
    mine = pl.ds(pl.multiple_of(p * 128, 128), 128)
    other = pl.ds(pl.multiple_of((1 - p) * 128, 128), 128)
    total = jnp.zeros((128, 128), F32)
    for u in range(3):
        block = (info[1] * 3 + u).astype(F32)
        w = jnp.concatenate([w_ref[u, :, mine], w_ref[u, :, other]], axis=1)
        wh, wl = split(w)
        m = [s_ref[k] == block for k in range(4)]
        d = jnp.concatenate([choose(m, [c_ref[k, :, q * 128:(q + 1) * 128] for k in range(4)]) for q in range(2)], axis=1)
        dh, dl = split(d)
        v = product(dh, dl, wh, wl, NN)
        vh, vl = split(v[:128])
        top = [z[:128] for z in m]
        e = jnp.concatenate([choose(top, [c_ref[k, :128, h] for k in range(4)]) for h in (mine, other)], axis=1)
        eh, el = split(e)
        total = total + product(vh, vl, eh, el, NT)
        for ref, q in ((v_ref, 0), (g_ref, 1)):
            for t in range(4):
                part = v[t * 128:(t + 1) * 128, q * 128:(q + 1) * 128]
                for k in range(4):
                    before = jnp.zeros_like(part) if u == 0 else ref[t, k]
                    ref[t, k] = jnp.where(m[k][t * 128:(t + 1) * 128], part, before)
    for ref in (v_ref, g_ref):
        for t in range(4):
            ref[t, 4] = total


def whole(v):
    return pl.BlockSpec(v.shape, lambda g, i: (0,) * v.ndim)


def partial(info, c, s, w):
    out = jax.ShapeDtypeStruct((4, 5, 128, 128), F32)
    grid = pltpu.PrefetchScalarGridSpec(num_scalar_prefetch=1, grid=(1,), in_specs=[whole(c), whole(s), whole(w)],
                                        out_specs=[pl.BlockSpec((4, 5, 128, 128), lambda g, i: (0, 0, 0, 0))] * 2)
    return pl.pallas_call(partial_body, grid_spec=grid, out_shape=[out, out],
                          compiler_params=pltpu.CompilerParams(vmem_limit_bytes=VMEM), name="partial",
                          cost_estimate=pl.CostEstimate(flops=2 * 3 * 512 * 768 * 256, bytes_accessed=6 << 20, transcendentals=0))(info, c, s, w)


def gather_blocks(base, sup, high, low, axis):
    highs, lows = [], []
    for u in range(6):
        block = (base + u).astype(F32).astype(BF)
        m = [s == block for s in sup]
        highs.append(choose(m, [high(k) for k in range(4)]))
        lows.append(choose(m, [low(k) for k in range(4)]))
    return jnp.concatenate(highs, axis=axis), jnp.concatenate(lows, axis=axis)


def column_labels(rows, n):
    return jnp.broadcast_to(jnp.concatenate(rows, axis=1), (128, n)).astype(BF)


def lead_body(info, v0_ref, v1_ref, s_ref, d0_ref, d1_ref, a_ref, vh, vl, dh, dl):
    g = pl.program_id(0)
    x = info[3]

    @pl.when(g == 0)
    def _():
        for j, (v_ref, d_ref) in enumerate(((v0_ref, d0_ref), (v1_ref, d1_ref))):
            for k in range(4):
                vh[j, k], vl[j, k] = split(v_ref[x, k])
                dh[j, k], dl[j, k] = split(d_ref[k * 128:(k + 1) * 128])
        a_ref[...] = jnp.zeros_like(a_ref)

    here = pl.ds(pl.multiple_of(x * 128, 128), 128)
    sup = [s_ref[k, here].astype(BF) for k in range(4)]
    first = [column_labels([d0_ref[512 + k:513 + k]], 128) for k in range(4)]
    for j in range(2):
        ah, al = gather_blocks(6 * g, sup, lambda k: vh[j, k], lambda k: vl[j, k], 1)
        bh, bl = gather_blocks(6 * g, first, lambda k: dh[j, k], lambda k: dl[j, k], 0)
        a_ref[...] += product(ah, al, bh, bl, NN)


def lead(info, v0, v1, s, d0, d1):
    args = [v0, v1, s, d0, d1]
    grid = pltpu.PrefetchScalarGridSpec(
        num_scalar_prefetch=1, grid=(4,), in_specs=[whole(v) for v in args], out_specs=pl.BlockSpec((128, 128), lambda g, i: (0, 0)),
        scratch_shapes=[pltpu.VMEM((2, 4, 128, 128), BF)] * 4)
    return pl.pallas_call(lead_body, grid_spec=grid, out_shape=jax.ShapeDtypeStruct((128, 128), F32),
                          compiler_params=pltpu.CompilerParams(vmem_limit_bytes=VMEM), name="lead",
                          cost_estimate=pl.CostEstimate(flops=2 * 3 * 128 * 6144 * 128, bytes_accessed=6 << 20, transcendentals=0))(info, *args)


def block_body(has_sum, info, v_ref, r_ref, c_ref, z_ref, d_ref, *rest):
    if has_sum:
        s_ref, b_ref, o_ref, a_ref, vh, vl, ch, cl = rest
    else:
        o_ref, a_ref, vh, vl, ch, cl = rest
    g = pl.program_id(0)

    @pl.when(g == 0)
    def _():
        for k in range(4):
            for t in range(4):
                vh[k, t * 128:(t + 1) * 128], vl[k, t * 128:(t + 1) * 128] = split(v_ref[t, k])
            for t in range(8):
                ch[k, :, t * 128:(t + 1) * 128], cl[k, :, t * 128:(t + 1) * 128] = split(c_ref[t, k * 128:(k + 1) * 128])
            ch[k, :, 1024:], cl[k, :, 1024:] = split(d_ref[k * 128:(k + 1) * 128])
        o_ref[...] = s_ref[...] if has_sum else jnp.zeros_like(o_ref)
        a_ref[...] = b_ref[...] if has_sum else jnp.zeros_like(a_ref)

    rows = [r_ref[k].astype(BF) for k in range(4)]
    ah, al = gather_blocks(6 * g, rows, lambda k: vh[k], lambda k: vl[k], 1)
    for q in range(3):
        n = 512 if q < 2 else 128
        r = slice(q * 512, q * 512 + n)
        if q < 2:
            sup = [column_labels([c_ref[4 * q + t, 512 + k:513 + k] for t in range(4)], n) for k in range(4)]
        else:
            sup = [column_labels([z_ref[512 + k:513 + k]], n) for k in range(4)]
        bh, bl = gather_blocks(6 * g, sup, lambda k: ch[k, :, r], lambda k: cl[k, :, r], 0)
        value = product(ah, al, bh, bl, NN)
        if q < 2:
            o_ref[:, r] += value
        else:
            a_ref[...] += value


def block_product(info, v, r, c, pick, z, d, start=None):
    args = [v, r, c, z, d] + ([] if start is None else list(start))
    specs = [whole(u) for u in args]
    specs[2] = pl.BlockSpec((8, 520, 128), pick)
    shapes = [(512, 1024), (512, 128)]
    grid = pltpu.PrefetchScalarGridSpec(
        num_scalar_prefetch=1, grid=(4,), in_specs=specs, out_specs=[pl.BlockSpec(u, lambda g, i: (0, 0)) for u in shapes],
        scratch_shapes=[pltpu.VMEM((4, 512, 128), BF)] * 2 + [pltpu.VMEM((4, 128, 1152), BF)] * 2)
    return pl.pallas_call(functools.partial(block_body, start is not None), grid_spec=grid,
                          out_shape=[jax.ShapeDtypeStruct(u, F32) for u in shapes],
                          compiler_params=pltpu.CompilerParams(vmem_limit_bytes=VMEM), name="block",
                          cost_estimate=pl.CostEstimate(flops=2 * 3 * 512 * 3072 * 1152, bytes_accessed=10 << 20, transcendentals=0))(info, *args)


def inverse_body(c_ref, o_ref):
    n = 128
    row = lax.broadcasted_iota(jnp.int32, (n, n), 0)
    col = lax.broadcasted_iota(jnp.int32, (n, n), 1)
    below = lax.broadcasted_iota(jnp.int32, (n, 1), 0)
    lane = lax.broadcasted_iota(jnp.int32, (1, n), 1)
    o_ref[...] = jnp.concatenate([c_ref[...], jnp.where(row == col, 1.0, 0.0).astype(F32)], axis=1)

    def at(v, k):
        return jnp.sum(jnp.where(lane == k, v, 0.0), axis=1, keepdims=True)

    def step(i, _):
        k = 2 * i
        line0 = o_ref[pl.ds(k, 1), :]
        line1 = o_ref[pl.ds(k + 1, 1), :]
        left = o_ref[:, :n]
        a, b, c = at(line0[:, :n], k), at(line0[:, :n], k + 1), at(line1[:, :n], k + 1)
        col0, col1 = at(left, k), at(left, k + 1)
        s0 = lax.rsqrt(a)
        b = b * s0
        s1 = lax.rsqrt(c - b * b)
        line0 = line0 * s0
        line1 = (line1 - b * line0) * s1
        f0 = jnp.where(below > k + 1, col0 * s0, 0.0)
        f1 = jnp.where(below > k + 1, (col1 - f0 * b) * s1, 0.0)
        o_ref[...] = o_ref[...] - f0 * line0 - f1 * line1
        o_ref[pl.ds(k, 1), :] = line0
        o_ref[pl.ds(k + 1, 1), :] = line1
        return 0

    lax.fori_loop(0, n // 2, step, 0)


def inverse_of(c):
    return pl.pallas_call(inverse_body, out_shape=jax.ShapeDtypeStruct((128, 256), F32), name="inverse",
                          cost_estimate=pl.CostEstimate(flops=2 * 3 * 512 * 3072 * 768, bytes_accessed=1 << 20, transcendentals=0))(c)


def finish_body(where, s_ref, p_ref, q_ref, d_ref, o_ref):
    g = pl.program_id(0)
    r, col = where[0], where[1]
    row = lax.broadcasted_iota(jnp.int32, (128, 128), 0)
    lane = lax.broadcasted_iota(jnp.int32, (128, 128), 1)
    for j in range(2):
        qh, ql = split(q_ref[j])
        across = col * 8 + 2 * g + j
        span = slice(j * 128, (j + 1) * 128)
        for t in range(4):
            ph, plo = split(p_ref[t])
            down = t * 16 + r
            outer = product(ph, plo, qh, ql, NT)
            diagonal = jnp.where((row == lane) & (down == across), jnp.broadcast_to(d_ref[t:t + 1], (128, 128)), 0.0)
            o_ref[t, :, span] = s_ref[t, :, span] + diagonal - jnp.where((down > 0) & (across > 0), outer, 0.0)


def finish(where, s, p, q, d):
    grid = pltpu.PrefetchScalarGridSpec(
        num_scalar_prefetch=1, grid=(4,),
        in_specs=[pl.BlockSpec((4, 128, 256), lambda g, w: (0, 0, g)), pl.BlockSpec((4, 128, 128), lambda g, w: (0, 0, 0)),
                  pl.BlockSpec((2, 128, 128), lambda g, w: (g, 0, 0)), pl.BlockSpec((4, 128), lambda g, w: (0, 0))],
        out_specs=pl.BlockSpec((4, 128, 256), lambda g, w: (0, 0, g)))
    return pl.pallas_call(finish_body, grid_spec=grid, out_shape=jax.ShapeDtypeStruct((4, 128, 1024), F32),
                          compiler_params=pltpu.CompilerParams(vmem_limit_bytes=VMEM), name="finish",
                          cost_estimate=pl.CostEstimate(flops=2 * 3 * 512 * 128 * 1024, bytes_accessed=5 << 20, transcendentals=0))(where, s, p, q, d)


SWAP = [(i, i ^ 1) for i in range(8)]
CHIPS = [[0, 2, 4, 6], [1, 3, 5, 7]]


def swap(v):
    return lax.ppermute(v, "cols", SWAP)


def exchange(v, axis, groups=None):
    return lax.all_to_all(v, axis, 0, 0, axis_index_groups=groups, tiled=True)


def repeat(v, n):
    return jnp.broadcast_to(v[None], (n,) + v.shape)


def lanes(s):
    return jnp.broadcast_to(s[:, :, None], s.shape + (128,))


def over_rows(v, pairs):
    return lax.ppermute(v, "rows", pairs)


def spread_first(v, r):
    one = over_rows(v, [(0, 1)])
    three = over_rows(v, [(0, 3)])
    two = over_rows(one, [(1, 2)])
    line = jnp.where(r == 0, v, one + three + two)
    first = over_rows(line, [(z, 4 + z) for z in range(4)])
    third = over_rows(line, [(z, 12 + z) for z in range(4)])
    second = over_rows(first, [(4 + z, 8 + z) for z in range(4)])
    return jnp.where(r < 4, line, first + third + second)


def local(coefficients, support, primal, dual_inverse, block_sizes, damping, right_sides):
    col = lax.axis_index("cols")
    r = lax.axis_index("rows")
    x = col // 2
    p = col % 2
    info = jnp.stack([r, col, p, x]).astype(jnp.int32)
    sup = support.astype(F32)

    def message(t, extra):
        tile = lax.dynamic_index_in_dim(coefficients, t, 0, keepdims=False)
        tile = lax.dynamic_slice_in_dim(tile, p * 128, 128, 2)
        return jnp.concatenate([jnp.transpose(tile, (1, 2, 0)).reshape(512, 128),
                                lax.dynamic_index_in_dim(sup, t, 0, keepdims=False).T, extra], axis=0)

    gathered = lax.all_gather(message(x, jnp.zeros((4, 128), F32)), "rows")

    positions = jnp.arange(256, dtype=jnp.int32)
    active = (positions[None, :] < block_sizes[:, None]).astype(F32)
    w = primal * dual_inverse * active[:, :, None] * active[:, None, :]
    own = jnp.transpose(coefficients, (2, 0, 1, 3)).reshape(4, 512, 256)
    own_sup = lanes(jnp.transpose(sup, (2, 0, 1)).reshape(4, 512))
    kept, given = partial(info, own, own_sup, w)
    half = kept + swap(given)
    total = jnp.sum(exchange(half, "cols", CHIPS), axis=0)
    v_own = exchange(repeat(total[:4], 4), "cols", CHIPS)
    v_other = swap(v_own)
    eye = jnp.eye(128, dtype=F32)
    inverse = inverse_of(total[4] + eye * damping[0])[:, 128:]

    head = spread_first(message(0, right_sides[0]), r)
    head_other = swap(head[:512])
    tile = lead(info, v_own, v_other, own_sup, head, head_other)
    every = exchange(repeat(jnp.concatenate([tile, inverse], axis=0), 16), "rows")

    swapped = swap(lax.dynamic_slice_in_dim(gathered, 8 * (1 - p), 8, 0))
    start = block_product(info, v_own, own_sup, gathered, lambda g, i: (i[2], 0, 0), head, head)
    out, first = block_product(info, v_other, own_sup, swapped, lambda g, i: (0, 0, 0), head, head_other, start)

    every, out, first = lax.optimization_barrier((every, out, first))
    inverse = every[0, 128:]
    tiles = lax.dynamic_slice(every, (8 * p, 0, 0), (8, 128, 128)).reshape(1024, 128)
    col_panel = lax.dot_general(tiles, inverse, NT, precision=highest).reshape(8, 128, 128)
    first = first.at[:128].add(jnp.where(r == 0, damping[0], 0.0) * eye)
    panel_factor = lax.dot_general(first, inverse, NT, precision=highest).reshape(4, 128, 128)
    leading = lax.dot_general(head[516:520], inverse, NT, precision=highest)
    remainder = right_sides - jnp.einsum("sk,tak->tsa", leading, panel_factor, precision=highest)
    solved = jnp.where(((jnp.arange(4) > 0) | (r > 0))[:, None, None], remainder, leading[None])
    updated = finish(info, out.reshape(4, 128, 1024), panel_factor, col_panel, damping)
    return updated, panel_factor, solved


def solution(mesh):
    in_specs = (
        P(None, "rows", None, None),
        P(None, "rows", None),
        P("cols", None, None),
        P("cols", None, None),
        P("cols"),
        P(None, "rows"),
        P(None, "cols", "rows"),
    )
    out_specs = (P(None, "rows", "cols"), P(None, "rows", None), P(None, "cols", "rows"))
    return jax.shard_map(local, mesh=mesh, in_specs=in_specs, out_specs=out_specs, check_vma=False)
```

time: 218 us -> 165 us (0.76)
  waiting for transfers between devices: 48.7 us -> 17.9 us
  local copies, waits for them, and re-layouts: 30.6 us -> 15 us
  Pallas kernels: 70.1 us -> 64.4 us
  starting transfers between devices: 41.7 us -> 36.6 us
  matrix products: 1.96 us -> 5.2 us
    all_to_all x7 -> x3, waiting for transfers between devices: 48.7 us -> 7.73 us  [exchange(): return lax.all_to_all(v, axis, 0, 0, axis_index_groups=groups, tiled=True)]
    all_to_all x7 -> x3, starting transfers between devices: 37.4 us -> 18.4 us  [exchange(): return lax.all_to_all(v, axis, 0, 0, axis_index_groups=groups, tiled=True)]
    ppermute x0 -> x6, starting transfers between devices: none -> 13.7 us  [over_rows(): return lax.ppermute(v, 'rows', pairs)]
    pallas_call x1, Pallas kernels: 14.4 us -> 5.89 us  [lead(): pl.pallas_call(lead_body, grid_spec=grid, out_shape=jax.ShapeDtypeStruct(...]
    ppermute x0 -> x6, waiting for transfers between devices: none -> 7.27 us  [over_rows(): return lax.ppermute(v, 'rows', pairs)]
    broadcast_in_dim x8 -> x2, local copies, waits for them, and re-layouts: 8.72 us -> 2.65 us  [repeat(): return jnp.broadcast_to(v[None], (n,) + v.shape)]
    dot_general x1 -> x3, matrix products: 1.01 us -> 4.26 us  [the longest x1 2.03 us: local(): lax.dot_general(first, inverse, NT, precision=highest).reshape(4, 128, 128)]
    squeeze x3 -> x1, local copies, waits for them, and re-layouts: 3.11 us -> 0.01 us  [local(): head = spread_first(message(0, right_sides[0]), r)]
  transfers between devices with their start and end apart: 11 -> 14, of which waited for: 6 -> 5; matrix products, arithmetic and copies ran while one was open for 17% -> 12% of each run, Pallas kernels for 30% -> 36%
where the time goes in v4:
time: 165 us; the launch traced here: 164 us
  Pallas kernels  64.4 us (39%)
  starting transfers between devices  36.6 us (22%)
  waiting for transfers between devices  17.9 us (11%)
  local copies, waits for them, and re-layouts  15 us (9%)
  between operations  14.3 us (9%)
  other arithmetic  10.8 us (7%)
  matrix products  5.2 us (3%)
    pallas_call x2, Pallas kernels, block_product(): pl.pallas_call(functools.partial(block_body, start is not None), grid_spe...  37.3 us
    all_to_all x3, starting transfers between devices, exchange(): return lax.all_to_all(v, axis, 0, 0, axis_index_groups=groups, tiled=True)  18.4 us
    ppermute x6, starting transfers between devices, over_rows(): return lax.ppermute(v, 'rows', pairs)  13.7 us
    pallas_call x1, Pallas kernels, inverse_of(): pl.pallas_call(inverse_body, out_shape=jax.ShapeDtypeStruct((128, 256), F...  9.55 us
    all_to_all x3, waiting for transfers between devices, exchange(): return lax.all_to_all(v, axis, 0, 0, axis_index_groups=groups, tiled=True)  7.73 us
    ppermute x6, waiting for transfers between devices, over_rows(): return lax.ppermute(v, 'rows', pairs)  7.27 us
    pallas_call x1, Pallas kernels, partial(): pl.pallas_call(partial_body, grid_spec=grid, out_shape=[out, out], compil...  6.02 us
    pallas_call x1, Pallas kernels, lead(): pl.pallas_call(lead_body, grid_spec=grid, out_shape=jax.ShapeDtypeStruct(...  5.89 us
  transfers between devices with their start and end apart: 14, of which 5 were waited for; matrix products, arithmetic and copies ran while one was open for 12% of the time, Pallas kernels for 36%

profile of v4, /device:TPU:1, one launch (start us, length us, event | category | flops | bytes accessed | tf_op | source)
XLA Modules:
  0.0 164.2 jit_solution(12117971472962695330)
XLA Ops:
  7.2 0.7 fusion.19
  7.9 1.1 constant_dynamic-slice_fusion.1
  9.3 0.8 maximum_maximum_fusion
  10.2 3.4 %copy.15 = f32[4,4,128,256]{3,2,1,0:T(8,128)} copy(f32[4,4,128,256]{3,0,2,1:T(4,128)} %bitcast.65) | data formatting | bytes 4194304 | tf_op jit(solution)/shard_map/transpose | solution.py:292
  13.7 0.6 pad_add_fusion.info.where
  14.3 1.1 multiply_multiply_fusion.w_ref
  15.4 1.3 broadcast_in_dim.25.s_ref.r_ref
  16.7 6.0 %partial.1 = (f32[4,5,128,128]{3,2,1,0:T(8,128)}, f32[4,5,128,128]{3,2,1,0:T(8,128)}) custom-call(s32[4]{0:T(128)} %pad_add_fusion.info.where, f32[4,512,256]{2,1,0:T(8,128)} %bitcast.64, f32[4,512,128]{2,1,0:T(8,128)} %broadcast_in_dim.25.s_ref.r_ref, f32[3,256,256]{2,1,0:T(8,128)} %multiply_multiply_fusion.w_ref), custom_call_target="tpu_custom_call" | custom-call | flops 603979776 | bytes 6291456 | tf_op jit(solution)/shard_map/partial/pallas_call | solution.py:73
  22.7 1.5 collective-permute-start
  24.2 2.9 %collective-permute-done = f32[4,5,128,128]{3,2,1,0:T(8,128)S(1)} collective-permute-done((f32[4,5,128,128]{3,2,1,0:T(8,128)}, f32[4,5,128,128]{3,2,1,0:T(8,128)S(1)}, u32[]{:S(2)}, u32[]{:S(2)}) %collective-permute-start) | collective-permute-done | bytes 1310752 | tf_op jit(solution)/shard_map/ppermute | solution.py:243
  27.1 2.6 %add.55 = f32[4,5,128,128]{3,2,1,0:T(8,128)} add(f32[4,5,128,128]{3,2,1,0:T(8,128)} %get-tuple-element.24, f32[4,5,128,128]{3,2,1,0:T(8,128)S(1)} %collective-permute-done) | non-fusion elementwise | flops 327680 | bytes 3932160 | tf_op jit(solution)/shard_map/add | solution.py:295
  29.7 4.2 %all-to-all-start = ((f32[4,5,128,128]{3,2,1,0:T(8,128)}), f32[4,5,128,128]{3,2,1,0:T(8,128)S(1)}, u32[]{:S(2)}, u32[]{:S(2)}) async-start(f32[4,5,128,128]{3,2,1,0:T(8,128)} %add.55), calls=%async_computation | async-start | bytes 2621440 | tf_op jit(solution)/shard_map/all_to_all | solution.py:247
  33.9 1.1 dynamic_slice.30
  35.0 0.1 copy.23
  35.2 3.5 %collective-permute-start.2 = (f32[520,128]{1,0:T(8,128)S(1)}, f32[520,128]{1,0:T(8,128)S(1)}, u32[]{:S(2)}, u32[]{:S(2)}) collective-permute-start(f32[520,128]{1,0:T(8,128)S(1)} %pad_maximum_fusion), channel_id=1, source_target_pairs={{0,8},{1,9},{2,10},{3,11},{4,12},{5,13},{6,14},{7,15}} | collective-permute-start | bytes 798728 | tf_op jit(solution)/shard_map/ppermute | solution.py:259
  38.8 2.8 %collective-permute-start.3 = (f32[520,128]{1,0:T(8,128)S(1)}, f32[520,128]{1,0:T(8,128)S(1)}, u32[]{:S(2)}, u32[]{:S(2)}) collective-permute-start(f32[520,128]{1,0:T(8,128)S(1)} %pad_maximum_fusion), channel_id=1, source_target_pairs={{0,24},{1,25},{2,26},{3,27},{4,28},{5,29},{6,30},{7,31}} | collective-permute-start | bytes 798728 | tf_op jit(solution)/shard_map/ppermute | solution.py:259
  41.6 2.2 %collective-permute-done.2 = f32[520,128]{1,0:T(8,128)S(1)} collective-permute-done((f32[520,128]{1,0:T(8,128)S(1)}, f32[520,128]{1,0:T(8,128)S(1)}, u32[]{:S(2)}, u32[]{:S(2)}) %collective-permute-start.2) | collective-permute-done | bytes 266272 | tf_op jit(solution)/shard_map/ppermute | solution.py:259
  43.8 0.7 collective-permute-start.4
  44.5 6.7 %all-to-all-done = f32[4,5,128,128]{3,2,1,0:T(8,128)S(1)} async-done(((f32[4,5,128,128]{3,2,1,0:T(8,128)}), f32[4,5,128,128]{3,2,1,0:T(8,128)S(1)}, u32[]{:S(2)}, u32[]{:S(2)}) %all-to-all-start) | async-done | bytes 1310752 | tf_op jit(solution)/shard_map/all_to_all | solution.py:247
  51.3 1.1 broadcast_in_dim.26
  52.4 3.5 %all-to-all-start.1 = ((f32[4,4,128,128]{3,2,1,0:T(8,128)}), f32[4,4,128,128]{3,2,1,0:T(8,128)S(1)}, u32[]{:S(2)}, u32[]{:S(2)}) async-start(f32[4,4,128,128]{3,2,1,0:T(8,128)} %broadcast_in_dim.26), calls=%async_computation.1 | async-start | bytes 2097152 | tf_op jit(solution)/shard_map/all_to_all | solution.py:247
  56.1 3.2 %collective-permute-start.5 = (f32[520,128]{1,0:T(8,128)S(1)}, f32[520,128]{1,0:T(8,128)S(1)}, u32[]{:S(2)}, u32[]{:S(2)}) collective-permute-start(f32[520,128]{1,0:T(8,128)S(1)} %add_select_fusion.1), channel_id=1, source_target_pairs={{0,32},{8,40},{16,48},{24,56},{1,33},{9,41},{17,49},{25,57},{2,34}... | collective-permute-start | bytes 798728 | tf_op jit(solution)/shard_map/ppermute | solution.py:259
  59.3 0.7 fusion.18
  60.0 2.1 %collective-permute-start.6 = (f32[520,128]{1,0:T(8,128)S(1)}, f32[520,128]{1,0:T(8,128)S(1)}, u32[]{:S(2)}, u32[]{:S(2)}) collective-permute-start(f32[520,128]{1,0:T(8,128)S(1)} %add_select_fusion.1), channel_id=1, source_target_pairs={{0,96},{8,104},{16,112},{24,120},{1,97},{9,105},{17,113},{25,121},... | collective-permute-start | bytes 798728 | tf_op jit(solution)/shard_map/ppermute | solution.py:259
  62.1 5.0 %collective-permute-done.5 = f32[520,128]{1,0:T(8,128)S(1)} collective-permute-done((f32[520,128]{1,0:T(8,128)S(1)}, f32[520,128]{1,0:T(8,128)S(1)}, u32[]{:S(2)}, u32[]{:S(2)}) %collective-permute-start.5) | collective-permute-done | bytes 266272 | tf_op jit(solution)/shard_map/ppermute | solution.py:259
  67.2 1.4 collective-permute-start.7
  68.5 1.0 all-to-all-done.1.v0_ref.v_ref
  69.5 2.4 %collective-permute-start.1 = (f32[4,4,128,128]{3,2,1,0:T(8,128)S(1)}, f32[4,4,128,128]{3,2,1,0:T(8,128)S(1)}, u32[]{:S(2)}, u32[]{:S(2)}) collective-permute-start(f32[4,4,128,128]{3,2,1,0:T(8,128)S(1)} %all-to-all-done.1.v0_ref.v_ref), channel_id=1, source_target_pairs={{0,1},{1,0},{2,3},{3,2},{4,5},{5,4},{6,7},{7,6},{8,9},{9,8},{10,11... | collective-permute-start | bytes 3145736 | tf_op jit(solution)/shard_map/ppermute | solution.py:243
  72.0 3.2 %constant_dynamic-slice_fusion = f32[8,520,128]{2,1,0:T(8,128)} fusion(f32[16,520,128]{2,1,0:T(8,128)} %bitcast.69, s32[]{:T(128)S(6)} %select_n.72), kind=kLoop, calls=%fused_computation.32 | loop fusion | bytes 4259844 | tf_op jit(solution)/shard_map/dynamic_slice | solution.py:307
  75.1 0.4 collective-permute-start.9
  75.5 1.0 add_select_fusion.d0_ref.z_ref.d_ref
  76.6 0.2 collective-permute-start.8
  76.8 0.6 fusion.3.c_ref
  77.4 9.6 %inverse.1 = f32[128,256]{1,0:T(8,128)} custom-call(f32[128,128]{1,0:T(8,128)} %fusion.3.c_ref), custom_call_target="tpu_custom_call" | custom-call | flops 7247757312 | bytes 1048576 | tf_op jit(solution)/shard_map/inverse/pallas_call | solution.py:206
  87.0 0.7 copy-done.6
  87.7 1.0 copy-done.3
  88.7 5.9 %lead.1 = f32[128,128]{1,0:T(8,128)} custom-call(s32[4]{0:T(128)} %pad_add_fusion.info.where, f32[4,4,128,128]{3,2,1,0:T(8,128)} %copy-done, f32[4,4,128,128]{3,2,1,0:T(8,128)} %copy-done.3, f32[4,512,128]{2,1,0:T(8,128)} %broadcast_in_dim.25.s_ref.r_ref, f32[520,128]{1,0:T(8,128)} %copy-done.1, f32[512,128]{1,0:T(8,128)} %copy-done.6), custom_call_target="tpu_custom_call" | custom-call | flops 603979776 | bytes 6291456 | tf_op jit(solution)/shard_map/lead/pallas_call | solution.py:118
  94.6 0.8 pad_maximum_fusion.1
  95.5 1.6 broadcast_in_dim.52
  97.0 10.6 %all-to-all-start.2 = ((f32[16,256,128]{2,1,0:T(8,128)}), f32[16,256,128]{2,1,0:T(8,128)S(1)}, u32[]{:S(2)}, u32[]{:S(2)}) async-start(f32[16,256,128]{2,1,0:T(8,128)} %broadcast_in_dim.52), calls=%async_computation.2 | async-start | bytes 4194304 | tf_op jit(solution)/shard_map/all_to_all | solution.py:247
  107.7 18.3 %block.2 = (f32[512,1024]{1,0:T(8,128)}, f32[512,128]{1,0:T(8,128)}) custom-call(s32[4]{0:T(128)} %pad_add_fusion.info.where, f32[4,4,128,128]{3,2,1,0:T(8,128)} %copy-done, f32[4,512,128]{2,1,0:T(8,128)} %broadcast_in_dim.25.s_ref.r_ref, f32[16,520,128]{2,1,0:T(8,128)} %bitcast.70, f32[520,128]{1,0:T(8,128)} %copy-done.1, f32[520,128]{1,0:T(8,128)} %copy-done.1), custom_call_target="tpu_custom_call" | custom-call | flops 10871635968 | bytes 10485760 | tf_op jit(solution)/shard_map/block/pallas_call | solution.py:166
  126.0 19.0 %block.3 = (f32[512,1024]{1,0:T(8,128)}, f32[512,128]{1,0:T(8,128)}) custom-call(s32[4]{0:T(128)} %pad_add_fusion.info.where, f32[4,4,128,128]{3,2,1,0:T(8,128)} %copy-done.3, f32[4,512,128]{2,1,0:T(8,128)} %broadcast_in_dim.25.s_ref.r_ref, f32[8,520,128]{2,1,0:T(8,128)} %collective-permute-done.9.c_ref, f32[520,128]{1,0:T(8,128)} %copy-done.1, ...), custom_call_target="tpu_custom_call" | custom-call | flops 10871635968 | bytes 10485760 | tf_op jit(solution)/shard_map/block/pallas_call | solution.py:166
  145.0 0.8 fusion.7
  145.9 1.5 add_dynamic-update-slice_fusion
  147.4 2.0 %fusion.5.p_ref = f32[4,128,128]{2,1,0:T(8,128)} fusion(f32[4,128,128]{2,1,0:T(8,128)} %bitcast.72, f32[16,256,128]{2,1,0:T(8,128)S(1)} %all-to-all-done.2), kind=kOutput, calls=%fused_computation.13 | convolution fusion | flops 100663296 | bytes 589824 | tf_op jit(solution)/shard_map/dot_general | solution.py:316
  149.4 1.4 fusion.1.q_ref
  150.8 5.6 %finish.1 = f32[4,128,1024]{2,1,0:T(8,128)} custom-call(s32[4]{0:T(128)} %pad_add_fusion.info.where, f32[4,128,1024]{2,1,0:T(8,128)} %bitcast.68, f32[4,128,128]{2,1,0:T(8,128)} %fusion.5.p_ref, f32[8,128,128]{2,1,0:T(8,128)} %fusion.1.q_ref, f32[4,128]{1,0:T(4,128)} %d_ref.1), custom_call_target="tpu_custom_call" | custom-call | flops 402653184 | bytes 5242880 | tf_op jit(solution)/shard_map/finish/pallas_call | solution.py:233
  156.4 0.9 broadcast_select_fusion
  (42 shorter events, 0.7 us)
Async XLA Ops:
  7.2 64.8 %all-gather.3.cloned.1.call-start = ((), (), s32[]{:S(2)}) async-start(), calls=%async_computation.3 | async-start | bytes 4526080 | tf_op jit(solution)/shard_map/all_gather | solution.py:287
  10.2 4.0 %copy-start.8 = (s32[3]{0:T(128)S(1)}, s32[3]{0:T(128)}, u32[]{:S(2)}) copy-start(s32[3]{0:T(128)} %param.13) | copy-start | bytes 40
  10.2 4.1 %copy-start.4 = (f32[3,256,256]{2,1,0:T(8,128)S(1)}, f32[3,256,256]{2,1,0:T(8,128)}, u32[]{:S(2)}) copy-start(f32[3,256,256]{2,1,0:T(8,128)} %param.11) | copy-start | bytes 2359300
  10.2 4.1 %copy-start.5 = (f32[3,256,256]{2,1,0:T(8,128)S(1)}, f32[3,256,256]{2,1,0:T(8,128)}, u32[]{:S(2)}) copy-start(f32[3,256,256]{2,1,0:T(8,128)} %param.12) | copy-start | bytes 2359300
  22.7 4.4 %collective-permute-start = (f32[4,5,128,128]{3,2,1,0:T(8,128)}, f32[4,5,128,128]{3,2,1,0:T(8,128)S(1)}, u32[]{:S(2)}, u32[]{:S(2)}) collective-permute-start(f32[4,5,128,128]{3,2,1,0:T(8,128)} %get-tuple-element.25), channel_id=1, source_target_pairs={{0,1},{1,0},{2,3},{3,2},{4,5},{5,4},{6,7},{7,6},{8,9},{9,8},{10,11... | collective-permute-start | bytes 3932168 | tf_op jit(solution)/shard_map/ppermute | solution.py:243
  29.7 5.5 %copy-start.7 = (f32[4,4,128]{2,1,0:T(4,128)S(1)}, f32[4,4,128]{2,1,0:T(4,128)}, u32[]{:S(2)}) copy-start(f32[4,4,128]{2,1,0:T(4,128)} %param.15) | copy-start | bytes 24580
  29.7 21.6 %all-to-all-start = ((f32[4,5,128,128]{3,2,1,0:T(8,128)}), f32[4,5,128,128]{3,2,1,0:T(8,128)S(1)}, u32[]{:S(2)}, u32[]{:S(2)}) async-start(f32[4,5,128,128]{3,2,1,0:T(8,128)} %add.55), calls=%async_computation | async-start | bytes 2621440 | tf_op jit(solution)/shard_map/all_to_all | solution.py:247
  35.2 8.6 %collective-permute-start.2 = (f32[520,128]{1,0:T(8,128)S(1)}, f32[520,128]{1,0:T(8,128)S(1)}, u32[]{:S(2)}, u32[]{:S(2)}) collective-permute-start(f32[520,128]{1,0:T(8,128)S(1)} %pad_maximum_fusion), channel_id=1, source_target_pairs={{0,8},{1,9},{2,10},{3,11},{4,12},{5,13},{6,14},{7,15}} | collective-permute-start | bytes 798728 | tf_op jit(solution)/shard_map/ppermute | solution.py:259
  38.8 17.2 %collective-permute-start.3 = (f32[520,128]{1,0:T(8,128)S(1)}, f32[520,128]{1,0:T(8,128)S(1)}, u32[]{:S(2)}, u32[]{:S(2)}) collective-permute-start(f32[520,128]{1,0:T(8,128)S(1)} %pad_maximum_fusion), channel_id=1, source_target_pairs={{0,24},{1,25},{2,26},{3,27},{4,28},{5,29},{6,30},{7,31}} | collective-permute-start | bytes 798728 | tf_op jit(solution)/shard_map/ppermute | solution.py:259
  43.8 12.1 %collective-permute-start.4 = (f32[520,128]{1,0:T(8,128)S(1)}, f32[520,128]{1,0:T(8,128)S(1)}, u32[]{:S(2)}, u32[]{:S(2)}) collective-permute-start(f32[520,128]{1,0:T(8,128)S(1)} %collective-permute-done.2), channel_id=1, source_target_pairs={{8,16},{9,17},{10,18},{11,19},{12,20},{13,21},{14,22},{15,23}} | collective-permute-start | bytes 798728 | tf_op jit(solution)/shard_map/ppermute | solution.py:259
  52.4 17.1 %all-to-all-start.1 = ((f32[4,4,128,128]{3,2,1,0:T(8,128)}), f32[4,4,128,128]{3,2,1,0:T(8,128)S(1)}, u32[]{:S(2)}, u32[]{:S(2)}) async-start(f32[4,4,128,128]{3,2,1,0:T(8,128)} %broadcast_in_dim.26), calls=%async_computation.1 | async-start | bytes 2097152 | tf_op jit(solution)/shard_map/all_to_all | solution.py:247
  56.1 11.1 %collective-permute-start.5 = (f32[520,128]{1,0:T(8,128)S(1)}, f32[520,128]{1,0:T(8,128)S(1)}, u32[]{:S(2)}, u32[]{:S(2)}) collective-permute-start(f32[520,128]{1,0:T(8,128)S(1)} %add_select_fusion.1), channel_id=1, source_target_pairs={{0,32},{8,40},{16,48},{24,56},{1,33},{9,41},{17,49},{25,57},{2,34}... | collective-permute-start | bytes 798728 | tf_op jit(solution)/shard_map/ppermute | solution.py:259
  60.0 15.5 %collective-permute-start.6 = (f32[520,128]{1,0:T(8,128)S(1)}, f32[520,128]{1,0:T(8,128)S(1)}, u32[]{:S(2)}, u32[]{:S(2)}) collective-permute-start(f32[520,128]{1,0:T(8,128)S(1)} %add_select_fusion.1), channel_id=1, source_target_pairs={{0,96},{8,104},{16,112},{24,120},{1,97},{9,105},{17,113},{25,121},... | collective-permute-start | bytes 798728 | tf_op jit(solution)/shard_map/ppermute | solution.py:259
  67.2 8.4 %collective-permute-start.7 = (f32[520,128]{1,0:T(8,128)S(1)}, f32[520,128]{1,0:T(8,128)}, u32[]{:S(2)}, u32[]{:S(2)}) collective-permute-start(f32[520,128]{1,0:T(8,128)S(1)} %collective-permute-done.5), channel_id=1, source_target_pairs={{32,64},{40,72},{48,80},{56,88},{33,65},{41,73},{49,81},{57,89},{3... | collective-permute-start | bytes 798728 | tf_op jit(solution)/shard_map/ppermute | solution.py:259
  69.5 5.6 %copy-start = (f32[4,4,128,128]{3,2,1,0:T(8,128)}, f32[4,4,128,128]{3,2,1,0:T(8,128)S(1)}, u32[]{:S(2)}) copy-start(f32[4,4,128,128]{3,2,1,0:T(8,128)S(1)} %all-to-all-done.1.v0_ref.v_ref) | copy-start | bytes 3145732
  69.5 17.5 %collective-permute-start.1 = (f32[4,4,128,128]{3,2,1,0:T(8,128)S(1)}, f32[4,4,128,128]{3,2,1,0:T(8,128)S(1)}, u32[]{:S(2)}, u32[]{:S(2)}) collective-permute-start(f32[4,4,128,128]{3,2,1,0:T(8,128)S(1)} %all-to-all-done.1.v0_ref.v_ref), channel_id=1, source_target_pairs={{0,1},{1,0},{2,3},{3,2},{4,5},{5,4},{6,7},{7,6},{8,9},{9,8},{10,11... | collective-permute-start | bytes 3145736 | tf_op jit(solution)/shard_map/ppermute | solution.py:243
  75.1 50.9 %collective-permute-start.9 = (f32[8,520,128]{2,1,0:T(8,128)}, f32[8,520,128]{2,1,0:T(8,128)}, u32[]{:S(2)}, u32[]{:S(2)}) collective-permute-start(f32[8,520,128]{2,1,0:T(8,128)} %constant_dynamic-slice_fusion), channel_id=1, source_target_pairs={{0,1},{1,0},{2,3},{3,2},{4,5},{5,4},{6,7},{7,6},{8,9},{9,8},{10,11... | collective-permute-start | bytes 6389768 | tf_op jit(solution)/shard_map/ppermute | solution.py:243
  76.6 10.4 %copy-start.1 = (f32[520,128]{1,0:T(8,128)}, f32[520,128]{1,0:T(8,128)S(1)}, u32[]{:S(2)}) copy-start(f32[520,128]{1,0:T(8,128)S(1)} %add_select_fusion.d0_ref.z_ref.d_ref) | copy-start | bytes 798724
  76.6 10.4 %collective-permute-start.8 = (f32[512,128]{1,0:T(8,128)S(1)}, f32[512,128]{1,0:T(8,128)S(1)}, u32[]{:S(2)}, u32[]{:S(2)}) collective-permute-start(f32[512,128]{1,0:T(8,128)S(1)} %slice.56), channel_id=1, source_target_pairs={{0,1},{1,0},{2,3},{3,2},{4,5},{5,4},{6,7},{7,6},{8,9},{9,8},{10,11... | collective-permute-start | bytes 786440 | tf_op jit(solution)/shard_map/ppermute | solution.py:243
  87.0 7.6 %slice-start = ((f32[128,256]{1,0:T(8,128)}), f32[128,128]{1,0:T(8,128)S(1)}, s32[]{:S(2)}) async-start(f32[128,256]{1,0:T(8,128)} %inverse.1), calls=%async_computation.4 | async-start | bytes 131072 | tf_op jit(solution)/shard_map/slice | solution.py:300
  87.0 0.7 copy-start.6
  87.7 1.0 copy-start.3
  97.0 48.0 %all-to-all-start.2 = ((f32[16,256,128]{2,1,0:T(8,128)}), f32[16,256,128]{2,1,0:T(8,128)S(1)}, u32[]{:S(2)}, u32[]{:S(2)}) async-start(f32[16,256,128]{2,1,0:T(8,128)} %broadcast_in_dim.52), calls=%async_computation.2 | async-start | bytes 4194304 | tf_op jit(solution)/shard_map/all_to_all | solution.py:247
  150.8 5.6 %copy-start.2 = (f32[4,128,128]{2,1,0:T(8,128)S(1)}, f32[4,128,128]{2,1,0:T(8,128)}, u32[]{:S(2)}) copy-start(f32[4,128,128]{2,1,0:T(8,128)} %fusion.5.p_ref) | copy-start | bytes 786436
Sparse Core Ops, SparseCore 0:
  10.3 55.2 all-gather.2

commit v5 on v4

--- a/solution.py
+++ b/solution.py
@@ -11,7 +11,6 @@
 NT = (((1,), (1,)), ((), ()))
 NN = (((1,), (0,)), ((), ()))
 VMEM = 56 << 20
-highest = lax.Precision.HIGHEST
 
 
 def split(v):
@@ -42,7 +41,7 @@
         block = (info[1] * 3 + u).astype(F32)
         w = jnp.concatenate([w_ref[u, :, mine], w_ref[u, :, other]], axis=1)
         wh, wl = split(w)
-        m = [s_ref[k] == block for k in range(4)]
+        m = [jnp.broadcast_to(s_ref[:, k:k + 1], (512, 128)) == block for k in range(4)]
         d = jnp.concatenate([choose(m, [c_ref[k, :, q * 128:(q + 1) * 128] for k in range(4)]) for q in range(2)], axis=1)
         dh, dl = split(d)
         v = product(dh, dl, wh, wl, NN)
@@ -89,7 +88,7 @@
     return jnp.broadcast_to(jnp.concatenate(rows, axis=1), (128, n)).astype(BF)
 
 
-def lead_body(info, v0_ref, v1_ref, s_ref, d0_ref, d1_ref, a_ref, vh, vl, dh, dl):
+def lead_body(info, v0_ref, v1_ref, s_ref, d0_ref, d1_ref, a_ref, vh, vl, dh, dl, rs):
     g = pl.program_id(0)
     x = info[3]
 
@@ -99,10 +98,12 @@
             for k in range(4):
                 vh[j, k], vl[j, k] = split(v_ref[x, k])
                 dh[j, k], dl[j, k] = split(d_ref[k * 128:(k + 1) * 128])
+        here = pl.ds(pl.multiple_of(x * 128, 128), 128)
+        for k in range(4):
+            rs[k] = jnp.broadcast_to(s_ref[here, k:k + 1], (128, 128)).astype(BF)
         a_ref[...] = jnp.zeros_like(a_ref)
 
-    here = pl.ds(pl.multiple_of(x * 128, 128), 128)
-    sup = [s_ref[k, here].astype(BF) for k in range(4)]
+    sup = [rs[k] for k in range(4)]
     first = [column_labels([d0_ref[512 + k:513 + k]], 128) for k in range(4)]
     for j in range(2):
         ah, al = gather_blocks(6 * g, sup, lambda k: vh[j, k], lambda k: vl[j, k], 1)
@@ -114,31 +115,32 @@
     args = [v0, v1, s, d0, d1]
     grid = pltpu.PrefetchScalarGridSpec(
         num_scalar_prefetch=1, grid=(4,), in_specs=[whole(v) for v in args], out_specs=pl.BlockSpec((128, 128), lambda g, i: (0, 0)),
-        scratch_shapes=[pltpu.VMEM((2, 4, 128, 128), BF)] * 4)
+        scratch_shapes=[pltpu.VMEM((2, 4, 128, 128), BF)] * 4 + [pltpu.VMEM((4, 128, 128), BF)])
     return pl.pallas_call(lead_body, grid_spec=grid, out_shape=jax.ShapeDtypeStruct((128, 128), F32),
                           compiler_params=pltpu.CompilerParams(vmem_limit_bytes=VMEM), name="lead",
                           cost_estimate=pl.CostEstimate(flops=2 * 3 * 128 * 6144 * 128, bytes_accessed=6 << 20, transcendentals=0))(info, *args)
 
 
-def block_body(has_sum, info, v_ref, r_ref, c_ref, z_ref, d_ref, *rest):
-    if has_sum:
-        s_ref, b_ref, o_ref, a_ref, vh, vl, ch, cl = rest
+def block_body(last, info, v_ref, r_ref, c_ref, z_ref, d_ref, *rest):
+    if last:
+        s_ref, b_ref, e_ref, h_ref, y_ref, o_ref, p_ref, x_ref, vh, vl, ch, cl, rs, total = rest
     else:
-        o_ref, a_ref, vh, vl, ch, cl = rest
+        o_ref, total, vh, vl, ch, cl, rs = rest
     g = pl.program_id(0)
 
     @pl.when(g == 0)
     def _():
         for k in range(4):
+            rs[k] = jnp.broadcast_to(r_ref[:, k:k + 1], (512, 128)).astype(BF)
             for t in range(4):
                 vh[k, t * 128:(t + 1) * 128], vl[k, t * 128:(t + 1) * 128] = split(v_ref[t, k])
             for t in range(8):
                 ch[k, :, t * 128:(t + 1) * 128], cl[k, :, t * 128:(t + 1) * 128] = split(c_ref[t, k * 128:(k + 1) * 128])
             ch[k, :, 1024:], cl[k, :, 1024:] = split(d_ref[k * 128:(k + 1) * 128])
-        o_ref[...] = s_ref[...] if has_sum else jnp.zeros_like(o_ref)
-        a_ref[...] = b_ref[...] if has_sum else jnp.zeros_like(a_ref)
-
-    rows = [r_ref[k].astype(BF) for k in range(4)]
+        o_ref[...] = s_ref[...] if last else jnp.zeros_like(o_ref)
+        total[...] = b_ref[...] if last else jnp.zeros_like(total)
+
+    rows = [rs[k] for k in range(4)]
     ah, al = gather_blocks(6 * g, rows, lambda k: vh[k], lambda k: vl[k], 1)
     for q in range(3):
         n = 512 if q < 2 else 128
@@ -152,18 +154,52 @@
         if q < 2:
             o_ref[:, r] += value
         else:
-            a_ref[...] += value
-
-
-def block_product(info, v, r, c, pick, z, d, start=None):
-    args = [v, r, c, z, d] + ([] if start is None else list(start))
+            total[...] += value
+
+    if last:
+        @pl.when(g == 3)
+        def _():
+            row, col, p = info[0], info[1], info[2]
+            same = lax.broadcasted_iota(jnp.int32, (128, 128), 0) == lax.broadcasted_iota(jnp.int32, (128, 128), 1)
+            ih, il = split(e_ref[8 * (1 - p)])
+            total[:128] += jnp.where(same & (row == 0), jnp.broadcast_to(h_ref[:1], (128, 128)), 0.0)
+            th, tl = split(total[...])
+            panel = product(th, tl, ih, il, NT)
+            p_ref[...] = panel
+            ph, plo = split(panel)
+            zh, zl = split(z_ref[512:520])
+            sides = product(zh, zl, ih, il, NT)
+            xh, xl = split(sides)
+            for t in range(4):
+                tile = slice(t * 128, (t + 1) * 128)
+                taken = product(xh, xl, ph[tile], plo[tile], NT)
+                x_ref[t] = jnp.where(t * 16 + row > 0, y_ref[t] - taken[4:], sides[4:])
+            for j in range(8):
+                span = slice(j * 128, (j + 1) * 128)
+                eh, el = split(e_ref[8 * p + j])
+                qh, ql = split(product(eh, el, ih, il, NT))
+                outer = product(ph, plo, qh, ql, NT)
+                across = col * 8 + j
+                for t in range(4):
+                    tile = slice(t * 128, (t + 1) * 128)
+                    down = t * 16 + row
+                    diagonal = jnp.where(same & (down == across), jnp.broadcast_to(h_ref[t:t + 1], (128, 128)), 0.0)
+                    o_ref[tile, span] += diagonal - jnp.where((down > 0) & (across > 0), outer[tile], 0.0)
+
+
+def block_product(info, v, r, c, pick, z, d, tail=None):
+    last = tail is not None
+    args = [v, r, c, z, d] + (list(tail) if last else [])
     specs = [whole(u) for u in args]
     specs[2] = pl.BlockSpec((8, 520, 128), pick)
-    shapes = [(512, 1024), (512, 128)]
+    shapes = [(512, 1024), (512, 128)] + ([(4, 4, 128)] if last else [])
+    outs = [pl.BlockSpec((512, 1024), lambda g, i: (0, 0)), pl.BlockSpec((512, 128), lambda g, i: (0, 0)),
+            pl.BlockSpec((4, 4, 128), lambda g, i: (0, 0, 0))]
     grid = pltpu.PrefetchScalarGridSpec(
-        num_scalar_prefetch=1, grid=(4,), in_specs=specs, out_specs=[pl.BlockSpec(u, lambda g, i: (0, 0)) for u in shapes],
-        scratch_shapes=[pltpu.VMEM((4, 512, 128), BF)] * 2 + [pltpu.VMEM((4, 128, 1152), BF)] * 2)
-    return pl.pallas_call(functools.partial(block_body, start is not None), grid_spec=grid,
+        num_scalar_prefetch=1, grid=(4,), in_specs=specs, out_specs=outs[:len(shapes)],
+        scratch_shapes=[pltpu.VMEM((4, 512, 128), BF)] * 2 + [pltpu.VMEM((4, 128, 1152), BF)] * 2
+        + [pltpu.VMEM((4, 512, 128), BF)] + ([pltpu.VMEM((512, 128), F32)] if last else []))
+    return pl.pallas_call(functools.partial(block_body, last), grid_spec=grid,
                           out_shape=[jax.ShapeDtypeStruct(u, F32) for u in shapes],
                           compiler_params=pltpu.CompilerParams(vmem_limit_bytes=VMEM), name="block",
                           cost_estimate=pl.CostEstimate(flops=2 * 3 * 512 * 3072 * 1152, bytes_accessed=10 << 20, transcendentals=0))(info, *args)
@@ -207,34 +243,6 @@
                           cost_estimate=pl.CostEstimate(flops=2 * 3 * 512 * 3072 * 768, bytes_accessed=1 << 20, transcendentals=0))(c)
 
 
-def finish_body(where, s_ref, p_ref, q_ref, d_ref, o_ref):
-    g = pl.program_id(0)
-    r, col = where[0], where[1]
-    row = lax.broadcasted_iota(jnp.int32, (128, 128), 0)
-    lane = lax.broadcasted_iota(jnp.int32, (128, 128), 1)
-    for j in range(2):
-        qh, ql = split(q_ref[j])
-        across = col * 8 + 2 * g + j
-        span = slice(j * 128, (j + 1) * 128)
-        for t in range(4):
-            ph, plo = split(p_ref[t])
-            down = t * 16 + r
-            outer = product(ph, plo, qh, ql, NT)
-            diagonal = jnp.where((row == lane) & (down == across), jnp.broadcast_to(d_ref[t:t + 1], (128, 128)), 0.0)
-            o_ref[t, :, span] = s_ref[t, :, span] + diagonal - jnp.where((down > 0) & (across > 0), outer, 0.0)
-
-
-def finish(where, s, p, q, d):
-    grid = pltpu.PrefetchScalarGridSpec(
-        num_scalar_prefetch=1, grid=(4,),
-        in_specs=[pl.BlockSpec((4, 128, 256), lambda g, w: (0, 0, g)), pl.BlockSpec((4, 128, 128), lambda g, w: (0, 0, 0)),
-                  pl.BlockSpec((2, 128, 128), lambda g, w: (g, 0, 0)), pl.BlockSpec((4, 128), lambda g, w: (0, 0))],
-        out_specs=pl.BlockSpec((4, 128, 256), lambda g, w: (0, 0, g)))
-    return pl.pallas_call(finish_body, grid_spec=grid, out_shape=jax.ShapeDtypeStruct((4, 128, 1024), F32),
-                          compiler_params=pltpu.CompilerParams(vmem_limit_bytes=VMEM), name="finish",
-                          cost_estimate=pl.CostEstimate(flops=2 * 3 * 512 * 128 * 1024, bytes_accessed=5 << 20, transcendentals=0))(where, s, p, q, d)
-
-
 SWAP = [(i, i ^ 1) for i in range(8)]
 CHIPS = [[0, 2, 4, 6], [1, 3, 5, 7]]
 
@@ -251,23 +259,8 @@
     return jnp.broadcast_to(v[None], (n,) + v.shape)
 
 
-def lanes(s):
-    return jnp.broadcast_to(s[:, :, None], s.shape + (128,))
-
-
 def over_rows(v, pairs):
     return lax.ppermute(v, "rows", pairs)
-
-
-def spread_first(v, r):
-    one = over_rows(v, [(0, 1)])
-    three = over_rows(v, [(0, 3)])
-    two = over_rows(one, [(1, 2)])
-    line = jnp.where(r == 0, v, one + three + two)
-    first = over_rows(line, [(z, 4 + z) for z in range(4)])
-    third = over_rows(line, [(z, 12 + z) for z in range(4)])
-    second = over_rows(first, [(4 + z, 8 + z) for z in range(4)])
-    return jnp.where(r < 4, line, first + third + second)
 
 
 def local(coefficients, support, primal, dual_inverse, block_sizes, damping, right_sides):
@@ -290,35 +283,40 @@
     active = (positions[None, :] < block_sizes[:, None]).astype(F32)
     w = primal * dual_inverse * active[:, :, None] * active[:, None, :]
     own = jnp.transpose(coefficients, (2, 0, 1, 3)).reshape(4, 512, 256)
-    own_sup = lanes(jnp.transpose(sup, (2, 0, 1)).reshape(4, 512))
+    own_sup = sup.reshape(512, 4)
+    eye = jnp.eye(128, dtype=F32)
+
+    head = jnp.where(r == 0, message(0, right_sides[0]), 0.0)
+    head_next = over_rows(head, [(0, 2)])
     kept, given = partial(info, own, own_sup, w)
+    head_next, kept, given = lax.optimization_barrier((head_next, kept, given))
+    head = head + head_next
+    head_next = over_rows(head, [(0, 1), (2, 3)])
     half = kept + swap(given)
-    total = jnp.sum(exchange(half, "cols", CHIPS), axis=0)
+    head_next, half = lax.optimization_barrier((head_next, half))
+    head = head + head_next
+    head_next = over_rows(head, [(z, 8 + z) for z in range(4)])
+    terms = exchange(half, "cols", CHIPS)
+    head_next, terms = lax.optimization_barrier((head_next, terms))
+    head = head + head_next
+    head_next = over_rows(head, [(y + z, y + 4 + z) for y in (0, 8) for z in range(4)])
+    total = jnp.sum(terms, axis=0)
     v_own = exchange(repeat(total[:4], 4), "cols", CHIPS)
+    inverse = inverse_of(total[4] + eye * damping[0])
+    head_next, v_own, inverse, gathered = lax.optimization_barrier((head_next, v_own, inverse, gathered))
     v_other = swap(v_own)
-    eye = jnp.eye(128, dtype=F32)
-    inverse = inverse_of(total[4] + eye * damping[0])[:, 128:]
-
-    head = spread_first(message(0, right_sides[0]), r)
+    head = head + head_next
+    inverse = inverse[:, 128:]
     head_other = swap(head[:512])
     tile = lead(info, v_own, v_other, own_sup, head, head_other)
-    every = exchange(repeat(jnp.concatenate([tile, inverse], axis=0), 16), "rows")
-
-    swapped = swap(lax.dynamic_slice_in_dim(gathered, 8 * (1 - p), 8, 0))
+    sent = jnp.where((r == 0) & (p == 1), inverse, jnp.where((r == 8) & (p == 0), over_rows(inverse, [(0, 8)]), tile))
+    every = exchange(repeat(sent, 16), "rows")
+
+    swapped = swap(gathered)
     start = block_product(info, v_own, own_sup, gathered, lambda g, i: (i[2], 0, 0), head, head)
-    out, first = block_product(info, v_other, own_sup, swapped, lambda g, i: (0, 0, 0), head, head_other, start)
-
-    every, out, first = lax.optimization_barrier((every, out, first))
-    inverse = every[0, 128:]
-    tiles = lax.dynamic_slice(every, (8 * p, 0, 0), (8, 128, 128)).reshape(1024, 128)
-    col_panel = lax.dot_general(tiles, inverse, NT, precision=highest).reshape(8, 128, 128)
-    first = first.at[:128].add(jnp.where(r == 0, damping[0], 0.0) * eye)
-    panel_factor = lax.dot_general(first, inverse, NT, precision=highest).reshape(4, 128, 128)
-    leading = lax.dot_general(head[516:520], inverse, NT, precision=highest)
-    remainder = right_sides - jnp.einsum("sk,tak->tsa", leading, panel_factor, precision=highest)
-    solved = jnp.where(((jnp.arange(4) > 0) | (r > 0))[:, None, None], remainder, leading[None])
-    updated = finish(info, out.reshape(4, 128, 1024), panel_factor, col_panel, damping)
-    return updated, panel_factor, solved
+    updated, panel, solved = block_product(info, v_other, own_sup, swapped, lambda g, i: (i[2], 0, 0), head, head_other,
+                                           list(start) + [every, damping, right_sides])
+    return updated.reshape(4, 128, 1024), panel.reshape(4, 128, 128), solved
 
 
 def solution(mesh):

time: 165 us -> 160 us (0.970)
  waiting for transfers between devices: 17.9 us -> 29.1 us
  starting transfers between devices: 36.6 us -> 27.4 us
  matrix products: 5.2 us -> 0 us
  Pallas kernels: 64.4 us -> 69.2 us
  local copies, waits for them, and re-layouts: 15 us -> 11.3 us
  other arithmetic: 10.8 us -> 7.79 us
    all_to_all x3, starting transfers between devices: 18.4 us -> 11.6 us  [exchange(): return lax.all_to_all(v, axis, 0, 0, axis_index_groups=groups, tiled=True)]
    ppermute x6 -> x5, waiting for transfers between devices: 7.27 us -> 12.6 us  [over_rows(): return lax.ppermute(v, 'rows', pairs)]
    dot_general x4 -> x0, matrix products: 5.2 us -> none  [the longest x1 2.03 us: local(): lax.dot_general(first, inverse, NT, precision=highest).reshape(4, 128, 128)]
    ppermute x4, waiting for transfers between devices: 2.88 us -> 7.33 us  [swap(): return lax.ppermute(v, 'cols', SWAP)]
    pallas_call x3 -> x2, Pallas kernels: 42.9 us -> 46.2 us  [block_product(): pl.pallas_call(functools.partial(block_body, last), grid_spec=grid, out_s...]
    dynamic_slice x1 -> x0, local copies, waits for them, and re-layouts: 3.16 us -> none  [local(): swapped = swap(lax.dynamic_slice_in_dim(gathered, 8 * (1 - p), 8, 0))]
    ppermute x6 -> x5, starting transfers between devices: 13.7 us -> 11.5 us  [over_rows(): return lax.ppermute(v, 'rows', pairs)]
    transpose x1, local copies, waits for them, and re-layouts: 3.43 us -> 1.7 us  [local(): own = jnp.transpose(coefficients, (2, 0, 1, 3)).reshape(4, 512, 256)]
  transfers between devices with their start and end apart: 14 -> 13, of which waited for: 5 -> 6; matrix products, arithmetic and copies ran while one was open for 12% -> 8% of each run, Pallas kernels for 36% -> 28%
where the time goes in v5:
time: 160 us; the launch traced here: 159 us
  Pallas kernels  69.2 us (43%)
  waiting for transfers between devices  29.1 us (18%)
  starting transfers between devices  27.4 us (17%)
  between operations  14.3 us (9%)
  local copies, waits for them, and re-layouts  11.3 us (7%)
  other arithmetic  7.79 us (5%)
    pallas_call x2, Pallas kernels, block_product(): pl.pallas_call(functools.partial(block_body, last), grid_spec=grid, out_s...  46.2 us
    ppermute x5, waiting for transfers between devices, over_rows(): return lax.ppermute(v, 'rows', pairs)  12.6 us
    all_to_all x3, starting transfers between devices, exchange(): return lax.all_to_all(v, axis, 0, 0, axis_index_groups=groups, tiled=True)  11.6 us
    ppermute x5, starting transfers between devices, over_rows(): return lax.ppermute(v, 'rows', pairs)  11.5 us
    pallas_call x1, Pallas kernels, inverse_of(): pl.pallas_call(inverse_body, out_shape=jax.ShapeDtypeStruct((128, 256), F...  9.55 us
    all_to_all x3, waiting for transfers between devices, exchange(): return lax.all_to_all(v, axis, 0, 0, axis_index_groups=groups, tiled=True)  9.15 us
    ppermute x4, waiting for transfers between devices, swap(): return lax.ppermute(v, 'cols', SWAP)  7.33 us
    pallas_call x1, Pallas kernels, lead(): pl.pallas_call(lead_body, grid_spec=grid, out_shape=jax.ShapeDtypeStruct(...  7.04 us
  transfers between devices with their start and end apart: 13, of which 6 were waited for; matrix products, arithmetic and copies ran while one was open for 8% of the time, Pallas kernels for 28%

profile of v5, /device:TPU:1, one launch (start us, length us, event | category | flops | bytes accessed | tf_op | source)
XLA Modules:
  0.0 159.1 jit_solution(8570738495932825461)
XLA Ops:
  7.2 0.0 all-gather.3.cloned.1.call-start
  7.3 0.7 convert_bitcast_fusion
  8.0 1.1 constant_dynamic-slice_fusion
  9.2 0.1 copy.32
  9.3 0.1 pad.2.clone
  9.4 0.9 maximum_maximum_fusion
  10.3 0.1 constant_dynamic-slice_fusion.1
  10.4 0.1 copy.31
  10.5 0.7 slice_bitcast_fusion.2
  11.2 6.3 %collective-permute-start = (f32[520,128]{1,0:T(8,128)S(1)}, f32[520,128]{1,0:T(8,128)S(1)}, u32[]{:S(2)}, u32[]{:S(2)}) collective-permute-start(f32[520,128]{1,0:T(8,128)S(1)} %maximum_select_fusion), channel_id=1, source_target_pairs={{0,16},{1,17},{2,18},{3,19},{4,20},{5,21},{6,22},{7,23}} | collective-permute-start | bytes 798728 | tf_op jit(solution)/shard_map/ppermute | solution.py:263
  17.6 0.9 copy.22.s_ref.r_ref
  18.5 1.7 %copy.21 = f32[4,4,128,256]{3,2,1,0:T(8,128)} copy(f32[4,4,128,256]{3,0,2,1:T(4,128)S(1)} %bitcast.40) | data formatting | bytes 4194304 | tf_op jit(solution)/shard_map/transpose | solution.py:285
  20.2 0.7 pad_add_fusion.info
  20.8 0.1 fusion.1
  20.9 1.1 multiply_multiply_fusion.w_ref
  22.0 6.4 %partial.1 = (f32[4,5,128,128]{3,2,1,0:T(8,128)}, f32[4,5,128,128]{3,2,1,0:T(8,128)}) custom-call(s32[4]{0:T(128)} %pad_add_fusion.info, f32[4,512,256]{2,1,0:T(8,128)} %bitcast.39, f32[512,4]{1,0:T(8,128)} %copy.22.s_ref.r_ref, f32[3,256,256]{2,1,0:T(8,128)} %multiply_multiply_fusion.w_ref), custom_call_target="tpu_custom_call" | custom-call | flops 603979776 | bytes 6291456 | tf_op jit(solution)/shard_map/partial/pallas_call | solution.py:72
  28.4 1.0 collective-permute-start.2
  29.4 1.3 collective-permute-start.1
  30.7 1.5 collective-permute-done.2
  32.3 2.6 %add.44 = f32[4,5,128,128]{3,2,1,0:T(8,128)} add(f32[4,5,128,128]{3,2,1,0:T(8,128)} %get-tuple-element.24, f32[4,5,128,128]{3,2,1,0:T(8,128)S(1)} %collective-permute-done.2) | non-fusion elementwise | flops 327680 | bytes 3932160 | tf_op jit(solution)/shard_map/add | solution.py:295
  34.9 3.5 %collective-permute-done.1 = f32[520,128]{1,0:T(8,128)S(1)} collective-permute-done((f32[520,128]{1,0:T(8,128)S(1)}, f32[520,128]{1,0:T(8,128)S(1)}, u32[]{:S(2)}, u32[]{:S(2)}) %collective-permute-start.1) | collective-permute-done | bytes 266272 | tf_op jit(solution)/shard_map/ppermute | solution.py:263
  38.4 3.8 %all-to-all-start = ((f32[4,5,128,128]{3,2,1,0:T(8,128)}), f32[4,5,128,128]{3,2,1,0:T(8,128)S(1)}, u32[]{:S(2)}, u32[]{:S(2)}) async-start(f32[4,5,128,128]{3,2,1,0:T(8,128)} %add.44), calls=%async_computation | async-start | bytes 2621440 | tf_op jit(solution)/shard_map/all_to_all | solution.py:255
  42.2 1.3 collective-permute-start.3
  43.6 0.7 slice_bitcast_fusion.3
  44.2 9.1 %collective-permute-done.3 = f32[520,128]{1,0:T(8,128)S(1)} collective-permute-done((f32[520,128]{1,0:T(8,128)S(1)}, f32[520,128]{1,0:T(8,128)S(1)}, u32[]{:S(2)}, u32[]{:S(2)}) %collective-permute-start.3) | collective-permute-done | bytes 266272 | tf_op jit(solution)/shard_map/ppermute | solution.py:263
  53.3 6.0 %all-to-all-done = f32[4,5,128,128]{3,2,1,0:T(8,128)S(1)} async-done(((f32[4,5,128,128]{3,2,1,0:T(8,128)}), f32[4,5,128,128]{3,2,1,0:T(8,128)S(1)}, u32[]{:S(2)}, u32[]{:S(2)}) %all-to-all-start) | async-done | bytes 1310752 | tf_op jit(solution)/shard_map/all_to_all | solution.py:255
  59.3 1.3 collective-permute-start.4
  60.7 0.1 reduce_sum.9
  60.8 1.1 broadcast_in_dim.11
  61.9 3.5 %all-to-all-start.1 = ((f32[4,4,128,128]{3,2,1,0:T(8,128)}), f32[4,4,128,128]{3,2,1,0:T(8,128)S(1)}, u32[]{:S(2)}, u32[]{:S(2)}) async-start(f32[4,4,128,128]{3,2,1,0:T(8,128)} %broadcast_in_dim.11), calls=%async_computation.1 | async-start | bytes 2097152 | tf_op jit(solution)/shard_map/all_to_all | solution.py:255
  65.4 0.6 fusion.c_ref
  66.0 9.6 %inverse.1 = f32[128,256]{1,0:T(8,128)} custom-call(f32[128,128]{1,0:T(8,128)} %fusion.c_ref), custom_call_target="tpu_custom_call" | custom-call | flops 7247757312 | bytes 1048576 | tf_op jit(solution)/shard_map/inverse/pallas_call | solution.py:242
  75.6 3.1 %all-to-all-done.1.v_ref.v0_ref = f32[4,4,128,128]{3,2,1,0:T(8,128)S(1)} async-done(((f32[4,4,128,128]{3,2,1,0:T(8,128)}), f32[4,4,128,128]{3,2,1,0:T(8,128)S(1)}, u32[]{:S(2)}, u32[]{:S(2)}) %all-to-all-start.1) | async-done | bytes 1048608 | tf_op jit(solution)/shard_map/all_to_all | solution.py:255
  78.7 2.7 %collective-permute-start.6 = (f32[16,520,128]{2,1,0:T(8,128)}, f32[16,520,128]{2,1,0:T(8,128)}, u32[]{:S(2)}, u32[]{:S(2)}) collective-permute-start(f32[16,520,128]{2,1,0:T(8,128)} %bitcast.43), channel_id=1, source_target_pairs={{0,1},{1,0},{2,3},{3,2},{4,5},{5,4},{6,7},{7,6},{8,9},{9,8},{10,11... | collective-permute-start | bytes 12779528 | tf_op jit(solution)/shard_map/ppermute | solution.py:251
  81.4 0.1 collective-permute-start.5
  81.6 0.5 collective-permute-start.7
  82.1 0.8 slice.25
  82.9 1.3 collective-permute-start.8
  84.2 5.8 %collective-permute-done.7.d1_ref.d_ref = f32[512,128]{1,0:T(8,128)S(1)} collective-permute-done((f32[512,128]{1,0:T(8,128)S(1)}, f32[512,128]{1,0:T(8,128)S(1)}, u32[]{:S(2)}, u32[]{:S(2)}) %collective-permute-start.7) | collective-permute-done | bytes 262176 | tf_op jit(solution)/shard_map/ppermute | solution.py:251
  90.1 0.7 copy-done.7
  90.7 1.0 copy-done.3
  91.7 7.0 %lead.1 = f32[128,128]{1,0:T(8,128)} custom-call(s32[4]{0:T(128)} %pad_add_fusion.info, f32[4,4,128,128]{3,2,1,0:T(8,128)} %copy-done, f32[4,4,128,128]{3,2,1,0:T(8,128)} %copy-done.3, f32[512,4]{1,0:T(8,128)} %copy.22.s_ref.r_ref, f32[520,128]{1,0:T(8,128)} %copy-done.2, f32[512,128]{1,0:T(8,128)} %copy-done.7), custom_call_target="tpu_custom_call" | custom-call | flops 603979776 | bytes 6291456 | tf_op jit(solution)/shard_map/lead/pallas_call | solution.py:119
  98.8 0.9 select_select_fusion
  99.6 1.1 broadcast_in_dim.13
  100.7 4.3 %all-to-all-start.2 = ((f32[16,128,128]{2,1,0:T(8,128)}), f32[16,128,128]{2,1,0:T(8,128)S(1)}, u32[]{:S(2)}, u32[]{:S(2)}) async-start(f32[16,128,128]{2,1,0:T(8,128)} %broadcast_in_dim.13), calls=%async_computation.2 | async-start | bytes 2097152 | tf_op jit(solution)/shard_map/all_to_all | solution.py:255
  105.0 21.0 %block.2 = (f32[512,1024]{1,0:T(8,128)}, f32[512,128]{1,0:T(8,128)}) custom-call(s32[4]{0:T(128)} %pad_add_fusion.info, f32[4,4,128,128]{3,2,1,0:T(8,128)} %copy-done, f32[512,4]{1,0:T(8,128)} %copy.22.s_ref.r_ref, f32[16,520,128]{2,1,0:T(8,128)} %bitcast.44, f32[520,128]{1,0:T(8,128)} %copy-done.2, f32[520,128]{1,0:T(8,128)} %copy-done.2), custom_call_target="tpu_custom_call" | custom-call | flops 10871635968 | bytes 10485760 | tf_op jit(solution)/shard_map/block/pallas_call | solution.py:202
  126.0 1.0 copy-done.4
  127.0 25.2 %block.3 = (f32[512,1024]{1,0:T(8,128)}, f32[512,128]{1,0:T(8,128)}, f32[4,4,128]{2,1,0:T(4,128)}) custom-call(s32[4]{0:T(128)} %pad_add_fusion.info, f32[4,4,128,128]{3,2,1,0:T(8,128)} %copy-done.3, f32[512,4]{1,0:T(8,128)} %copy.22.s_ref.r_ref, f32[16,520,128]{2,1,0:T(8,128)} %collective-permute-done.6.c_ref, f32[520,128]{1,0:T(8,128)} %copy-done.2, ...), custom_call_target="tpu_custom_call" | custom-call | flops 10871635968 | bytes 10485760 | tf_op jit(solution)/shard_map/block/pallas_call | solution.py:202
  (36 shorter events, 0.3 us)
Async XLA Ops:
  7.2 3.2 %slice-start = ((f32[4,128,4,256]{3,2,1,0:T(4,128)}), f32[1,128,4,256]{3,2,1,0:T(4,128)S(1)}, s32[]{:S(2)}) async-start(f32[4,128,4,256]{3,2,1,0:T(4,128)} %param.7), calls=%async_computation.4 | async-start | bytes 1048576 | tf_op jit(solution)/shard_map/jit(dynamic_index_in_dim)/dynamic_slice | solution.py:275
  7.2 71.6 %all-gather.3.cloned.1.call-start = ((), (), s32[]{:S(2)}) async-start(), calls=%async_computation.3 | async-start | bytes 4526080 | tf_op jit(solution)/shard_map/all_gather | solution.py:280
  9.2 9.3 %copy-start.1 = (f32[4,128,4,256]{3,2,1,0:T(4,128)S(1)}, f32[4,128,4,256]{3,2,1,0:T(4,128)}, u32[]{:S(2)}) copy-start(f32[4,128,4,256]{3,2,1,0:T(4,128)} %param.7) | copy-start | bytes 6291460
  11.2 17.2 %collective-permute-start = (f32[520,128]{1,0:T(8,128)S(1)}, f32[520,128]{1,0:T(8,128)S(1)}, u32[]{:S(2)}, u32[]{:S(2)}) collective-permute-start(f32[520,128]{1,0:T(8,128)S(1)} %maximum_select_fusion), channel_id=1, source_target_pairs={{0,16},{1,17},{2,18},{3,19},{4,20},{5,21},{6,22},{7,23}} | collective-permute-start | bytes 798728 | tf_op jit(solution)/shard_map/ppermute | solution.py:263
  18.5 2.4 %copy-start.9 = (s32[3]{0:T(128)S(1)}, s32[3]{0:T(128)}, u32[]{:S(2)}) copy-start(s32[3]{0:T(128)} %param.11) | copy-start | bytes 40
  18.5 2.4 %copy-start.5 = (f32[3,256,256]{2,1,0:T(8,128)S(1)}, f32[3,256,256]{2,1,0:T(8,128)}, u32[]{:S(2)}) copy-start(f32[3,256,256]{2,1,0:T(8,128)} %param.9) | copy-start | bytes 2359300
  18.5 2.4 %copy-start.6 = (f32[3,256,256]{2,1,0:T(8,128)S(1)}, f32[3,256,256]{2,1,0:T(8,128)}, u32[]{:S(2)}) copy-start(f32[3,256,256]{2,1,0:T(8,128)} %param.10) | copy-start | bytes 2359300
  28.4 3.9 %collective-permute-start.2 = (f32[4,5,128,128]{3,2,1,0:T(8,128)}, f32[4,5,128,128]{3,2,1,0:T(8,128)S(1)}, u32[]{:S(2)}, u32[]{:S(2)}) collective-permute-start(f32[4,5,128,128]{3,2,1,0:T(8,128)} %get-tuple-element.25), channel_id=1, source_target_pairs={{0,1},{1,0},{2,3},{3,2},{4,5},{5,4},{6,7},{7,6},{8,9},{9,8},{10,11... | collective-permute-start | bytes 3932168 | tf_op jit(solution)/shard_map/ppermute | solution.py:251
  29.4 9.0 %collective-permute-start.1 = (f32[520,128]{1,0:T(8,128)S(1)}, f32[520,128]{1,0:T(8,128)S(1)}, u32[]{:S(2)}, u32[]{:S(2)}) collective-permute-start(f32[520,128]{1,0:T(8,128)S(1)} %add.43), channel_id=1, source_target_pairs={{0,8},{16,24},{1,9},{17,25},{2,10},{18,26},{3,11},{19,27},{4,12},{... | collective-permute-start | bytes 798728 | tf_op jit(solution)/shard_map/ppermute | solution.py:263
  38.4 20.9 %all-to-all-start = ((f32[4,5,128,128]{3,2,1,0:T(8,128)}), f32[4,5,128,128]{3,2,1,0:T(8,128)S(1)}, u32[]{:S(2)}, u32[]{:S(2)}) async-start(f32[4,5,128,128]{3,2,1,0:T(8,128)} %add.44), calls=%async_computation | async-start | bytes 2621440 | tf_op jit(solution)/shard_map/all_to_all | solution.py:255
  42.2 11.1 %collective-permute-start.3 = (f32[520,128]{1,0:T(8,128)S(1)}, f32[520,128]{1,0:T(8,128)S(1)}, u32[]{:S(2)}, u32[]{:S(2)}) collective-permute-start(f32[520,128]{1,0:T(8,128)S(1)} %add.45), channel_id=1, source_target_pairs={{0,64},{8,72},{16,80},{24,88},{1,65},{9,73},{17,81},{25,89},{2,66}... | collective-permute-start | bytes 798728 | tf_op jit(solution)/shard_map/ppermute | solution.py:263
  59.3 16.2 %collective-permute-start.4 = (f32[520,128]{1,0:T(8,128)S(1)}, f32[520,128]{1,0:T(8,128)S(1)}, u32[]{:S(2)}, u32[]{:S(2)}) collective-permute-start(f32[520,128]{1,0:T(8,128)S(1)} %add.46), channel_id=1, source_target_pairs={{0,32},{8,40},{16,48},{24,56},{64,96},{72,104},{80,112},{88,120},{... | collective-permute-start | bytes 798728 | tf_op jit(solution)/shard_map/ppermute | solution.py:263
  61.9 16.9 %all-to-all-start.1 = ((f32[4,4,128,128]{3,2,1,0:T(8,128)}), f32[4,4,128,128]{3,2,1,0:T(8,128)S(1)}, u32[]{:S(2)}, u32[]{:S(2)}) async-start(f32[4,4,128,128]{3,2,1,0:T(8,128)} %broadcast_in_dim.11), calls=%async_computation.1 | async-start | bytes 2097152 | tf_op jit(solution)/shard_map/all_to_all | solution.py:255
  78.7 11.3 %copy-start = (f32[4,4,128,128]{3,2,1,0:T(8,128)}, f32[4,4,128,128]{3,2,1,0:T(8,128)S(1)}, u32[]{:S(2)}) copy-start(f32[4,4,128,128]{3,2,1,0:T(8,128)S(1)} %all-to-all-done.1.v_ref.v0_ref) | copy-start | bytes 3145732
  78.7 20.0 %copy-start.8 = (f32[128,256]{1,0:T(8,128)S(1)}, f32[128,256]{1,0:T(8,128)}, u32[]{:S(2)}) copy-start(f32[128,256]{1,0:T(8,128)} %inverse.1) | copy-start | bytes 393220
  78.7 47.2 %collective-permute-start.6 = (f32[16,520,128]{2,1,0:T(8,128)}, f32[16,520,128]{2,1,0:T(8,128)}, u32[]{:S(2)}, u32[]{:S(2)}) collective-permute-start(f32[16,520,128]{2,1,0:T(8,128)} %bitcast.43), channel_id=1, source_target_pairs={{0,1},{1,0},{2,3},{3,2},{4,5},{5,4},{6,7},{7,6},{8,9},{9,8},{10,11... | collective-permute-start | bytes 12779528 | tf_op jit(solution)/shard_map/ppermute | solution.py:251
  81.4 8.6 %collective-permute-start.5 = (f32[4,4,128,128]{3,2,1,0:T(8,128)S(1)}, f32[4,4,128,128]{3,2,1,0:T(8,128)S(1)}, u32[]{:S(2)}, u32[]{:S(2)}) collective-permute-start(f32[4,4,128,128]{3,2,1,0:T(8,128)S(1)} %all-to-all-done.1.v_ref.v0_ref), channel_id=1, source_target_pairs={{0,1},{1,0},{2,3},{3,2},{4,5},{5,4},{6,7},{7,6},{8,9},{9,8},{10,11... | collective-permute-start | bytes 3145736 | tf_op jit(solution)/shard_map/ppermute | solution.py:251
  81.5 8.5 %copy-start.2 = (f32[520,128]{1,0:T(8,128)}, f32[520,128]{1,0:T(8,128)S(1)}, u32[]{:S(2)}) copy-start(f32[520,128]{1,0:T(8,128)S(1)} %add.49.z_ref.d_ref.d0_ref) | copy-start | bytes 798724
  81.6 8.5 %collective-permute-start.7 = (f32[512,128]{1,0:T(8,128)S(1)}, f32[512,128]{1,0:T(8,128)S(1)}, u32[]{:S(2)}, u32[]{:S(2)}) collective-permute-start(f32[512,128]{1,0:T(8,128)S(1)} %slice.28), channel_id=1, source_target_pairs={{0,1},{1,0},{2,3},{3,2},{4,5},{5,4},{6,7},{7,6},{8,9},{9,8},{10,11... | collective-permute-start | bytes 786440 | tf_op jit(solution)/shard_map/ppermute | solution.py:251
  82.9 15.8 %collective-permute-start.8 = (f32[128,128]{1,0:T(8,128)S(1)}, f32[128,128]{1,0:T(8,128)S(1)}, u32[]{:S(2)}, u32[]{:S(2)}) collective-permute-start(f32[128,128]{1,0:T(8,128)S(1)} %slice.25), channel_id=1, source_target_pairs={{0,64},{1,65},{2,66},{3,67},{4,68},{5,69},{6,70},{7,71}} | collective-permute-start | bytes 196616 | tf_op jit(solution)/shard_map/ppermute | solution.py:263
  90.0 0.7 copy-start.7
  90.7 1.0 copy-start.3
  100.7 25.2 %all-to-all-start.2 = ((f32[16,128,128]{2,1,0:T(8,128)}), f32[16,128,128]{2,1,0:T(8,128)S(1)}, u32[]{:S(2)}, u32[]{:S(2)}) async-start(f32[16,128,128]{2,1,0:T(8,128)} %broadcast_in_dim.13), calls=%async_computation.2 | async-start | bytes 2097152 | tf_op jit(solution)/shard_map/all_to_all | solution.py:255
  126.0 1.0 copy-start.4
Sparse Core Ops, SparseCore 0:
  10.4 61.5 all-gather.2

commit v6 on v5

--- a/solution.py
+++ b/solution.py
@@ -32,46 +32,64 @@
     return out
 
 
-def partial_body(info, c_ref, s_ref, w_ref, v_ref, g_ref):
+def partial_body(info, c_ref, s_ref, x_ref, y_ref, v_ref, g_ref, wh, wl, total):
+    t = pl.program_id(0)
     p = info[2]
     mine = pl.ds(pl.multiple_of(p * 128, 128), 128)
     other = pl.ds(pl.multiple_of((1 - p) * 128, 128), 128)
-    total = jnp.zeros((128, 128), F32)
+
+    @pl.when(t == 0)
+    def _():
+        row = lax.broadcasted_iota(jnp.int32, (256, 128), 0)
+        lane = lax.broadcasted_iota(jnp.int32, (256, 128), 1)
+        for u in range(3):
+            size = info[4 + u]
+            for q, (h, base) in enumerate(((mine, p * 128), (other, (1 - p) * 128))):
+                w = jnp.where((row < size) & (lane + base < size), x_ref[u, :, h] * y_ref[u, :, h], 0.0)
+                wh[u, :, q * 128:(q + 1) * 128], wl[u, :, q * 128:(q + 1) * 128] = split(w)
+
+    corner = jnp.zeros((128, 128), F32)
+    parts = [None] * 8
     for u in range(3):
         block = (info[1] * 3 + u).astype(F32)
-        w = jnp.concatenate([w_ref[u, :, mine], w_ref[u, :, other]], axis=1)
-        wh, wl = split(w)
-        m = [jnp.broadcast_to(s_ref[:, k:k + 1], (512, 128)) == block for k in range(4)]
+        m = [s_ref[k] == block for k in range(4)]
         d = jnp.concatenate([choose(m, [c_ref[k, :, q * 128:(q + 1) * 128] for k in range(4)]) for q in range(2)], axis=1)
         dh, dl = split(d)
-        v = product(dh, dl, wh, wl, NN)
-        vh, vl = split(v[:128])
-        top = [z[:128] for z in m]
-        e = jnp.concatenate([choose(top, [c_ref[k, :128, h] for k in range(4)]) for h in (mine, other)], axis=1)
+        v = product(dh, dl, wh[u], wl[u], NN)
+        vh, vl = split(v)
+        e = jnp.concatenate([choose(m, [c_ref[k, :, h] for k in range(4)]) for h in (mine, other)], axis=1)
         eh, el = split(e)
-        total = total + product(vh, vl, eh, el, NT)
-        for ref, q in ((v_ref, 0), (g_ref, 1)):
-            for t in range(4):
-                part = v[t * 128:(t + 1) * 128, q * 128:(q + 1) * 128]
-                for k in range(4):
-                    before = jnp.zeros_like(part) if u == 0 else ref[t, k]
-                    ref[t, k] = jnp.where(m[k][t * 128:(t + 1) * 128], part, before)
-    for ref in (v_ref, g_ref):
-        for t in range(4):
-            ref[t, 4] = total
+        corner = corner + product(vh, vl, eh, el, NT)
+        for q in range(2):
+            part = v[:, q * 128:(q + 1) * 128]
+            for k in range(4):
+                before = jnp.zeros_like(part) if u == 0 else parts[4 * q + k]
+                parts[4 * q + k] = jnp.where(m[k], part, before)
+
+    @pl.when(t == 0)
+    def _():
+        total[...] = corner
+
+    for q, ref in enumerate((v_ref, g_ref)):
+        for k in range(4):
+            ref[0, k] = parts[4 * q + k]
+        ref[0, 4] = total[...]
 
 
 def whole(v):
     return pl.BlockSpec(v.shape, lambda g, i: (0,) * v.ndim)
 
 
-def partial(info, c, s, w):
+def partial(info, c, s, x, y):
     out = jax.ShapeDtypeStruct((4, 5, 128, 128), F32)
-    grid = pltpu.PrefetchScalarGridSpec(num_scalar_prefetch=1, grid=(1,), in_specs=[whole(c), whole(s), whole(w)],
-                                        out_specs=[pl.BlockSpec((4, 5, 128, 128), lambda g, i: (0, 0, 0, 0))] * 2)
+    grid = pltpu.PrefetchScalarGridSpec(
+        num_scalar_prefetch=1, grid=(4,),
+        in_specs=[pl.BlockSpec((4, 128, 256), lambda t, i: (0, t, 0)), pl.BlockSpec((4, 128, 128), lambda t, i: (0, t, 0)), whole(x), whole(y)],
+        out_specs=[pl.BlockSpec((1, 5, 128, 128), lambda t, i: (t, 0, 0, 0))] * 2,
+        scratch_shapes=[pltpu.VMEM((3, 256, 256), BF)] * 2 + [pltpu.VMEM((128, 128), F32)])
     return pl.pallas_call(partial_body, grid_spec=grid, out_shape=[out, out],
                           compiler_params=pltpu.CompilerParams(vmem_limit_bytes=VMEM), name="partial",
-                          cost_estimate=pl.CostEstimate(flops=2 * 3 * 512 * 768 * 256, bytes_accessed=6 << 20, transcendentals=0))(info, c, s, w)
+                          cost_estimate=pl.CostEstimate(flops=2 * 3 * 512 * 768 * 256, bytes_accessed=8 << 20, transcendentals=0))(info, c, s, x, y)
 
 
 def gather_blocks(base, sup, high, low, axis):
@@ -88,50 +106,55 @@
     return jnp.broadcast_to(jnp.concatenate(rows, axis=1), (128, n)).astype(BF)
 
 
-def lead_body(info, v0_ref, v1_ref, s_ref, d0_ref, d1_ref, a_ref, vh, vl, dh, dl, rs):
+def lead_body(info, v0_ref, v1_ref, s_ref, d0_ref, d1_ref, f_ref, n_ref, o_ref, vh, vl, dh, dl, a_ref):
     g = pl.program_id(0)
-    x = info[3]
 
     @pl.when(g == 0)
     def _():
         for j, (v_ref, d_ref) in enumerate(((v0_ref, d0_ref), (v1_ref, d1_ref))):
             for k in range(4):
-                vh[j, k], vl[j, k] = split(v_ref[x, k])
+                vh[j, k], vl[j, k] = split(v_ref[0, k])
                 dh[j, k], dl[j, k] = split(d_ref[k * 128:(k + 1) * 128])
-        here = pl.ds(pl.multiple_of(x * 128, 128), 128)
-        for k in range(4):
-            rs[k] = jnp.broadcast_to(s_ref[here, k:k + 1], (128, 128)).astype(BF)
         a_ref[...] = jnp.zeros_like(a_ref)
 
-    sup = [rs[k] for k in range(4)]
+    sup = [s_ref[k].astype(BF) for k in range(4)]
     first = [column_labels([d0_ref[512 + k:513 + k]], 128) for k in range(4)]
     for j in range(2):
         ah, al = gather_blocks(6 * g, sup, lambda k: vh[j, k], lambda k: vl[j, k], 1)
         bh, bl = gather_blocks(6 * g, first, lambda k: dh[j, k], lambda k: dl[j, k], 0)
         a_ref[...] += product(ah, al, bh, bl, NN)
 
-
-def lead(info, v0, v1, s, d0, d1):
-    args = [v0, v1, s, d0, d1]
+    @pl.when(g == 3)
+    def _():
+        r, p = info[0], info[2]
+        sent = jnp.where((r == 0) & (p == 1), f_ref[...], jnp.where((r == 8) & (p == 0), n_ref[...], a_ref[...]))
+        for j in range(16):
+            o_ref[j] = sent
+
+
+def lead(info, v0, v1, s, d0, d1, f, n):
+    args = [v0, v1, s, d0, d1, f, n]
+    specs = [whole(v) for v in args]
+    specs[0] = specs[1] = pl.BlockSpec((1, 4, 128, 128), lambda g, i: (i[3], 0, 0, 0))
+    specs[2] = pl.BlockSpec((4, 128, 128), lambda g, i: (0, i[3], 0))
     grid = pltpu.PrefetchScalarGridSpec(
-        num_scalar_prefetch=1, grid=(4,), in_specs=[whole(v) for v in args], out_specs=pl.BlockSpec((128, 128), lambda g, i: (0, 0)),
-        scratch_shapes=[pltpu.VMEM((2, 4, 128, 128), BF)] * 4 + [pltpu.VMEM((4, 128, 128), BF)])
-    return pl.pallas_call(lead_body, grid_spec=grid, out_shape=jax.ShapeDtypeStruct((128, 128), F32),
+        num_scalar_prefetch=1, grid=(4,), in_specs=specs, out_specs=pl.BlockSpec((16, 128, 128), lambda g, i: (0, 0, 0)),
+        scratch_shapes=[pltpu.VMEM((2, 4, 128, 128), BF)] * 4 + [pltpu.VMEM((128, 128), F32)])
+    return pl.pallas_call(lead_body, grid_spec=grid, out_shape=jax.ShapeDtypeStruct((16, 128, 128), F32),
                           compiler_params=pltpu.CompilerParams(vmem_limit_bytes=VMEM), name="lead",
                           cost_estimate=pl.CostEstimate(flops=2 * 3 * 128 * 6144 * 128, bytes_accessed=6 << 20, transcendentals=0))(info, *args)
 
 
 def block_body(last, info, v_ref, r_ref, c_ref, z_ref, d_ref, *rest):
     if last:
-        s_ref, b_ref, e_ref, h_ref, y_ref, o_ref, p_ref, x_ref, vh, vl, ch, cl, rs, total = rest
+        s_ref, b_ref, e_ref, h_ref, y_ref, o_ref, p_ref, x_ref, vh, vl, ch, cl, total = rest
     else:
-        o_ref, total, vh, vl, ch, cl, rs = rest
+        o_ref, total, vh, vl, ch, cl = rest
     g = pl.program_id(0)
 
     @pl.when(g == 0)
     def _():
         for k in range(4):
-            rs[k] = jnp.broadcast_to(r_ref[:, k:k + 1], (512, 128)).astype(BF)
             for t in range(4):
                 vh[k, t * 128:(t + 1) * 128], vl[k, t * 128:(t + 1) * 128] = split(v_ref[t, k])
             for t in range(8):
@@ -140,7 +163,7 @@
         o_ref[...] = s_ref[...] if last else jnp.zeros_like(o_ref)
         total[...] = b_ref[...] if last else jnp.zeros_like(total)
 
-    rows = [rs[k] for k in range(4)]
+    rows = [r_ref[k].astype(BF) for k in range(4)]
     ah, al = gather_blocks(6 * g, rows, lambda k: vh[k], lambda k: vl[k], 1)
     for q in range(3):
         n = 512 if q < 2 else 128
@@ -198,14 +221,14 @@
     grid = pltpu.PrefetchScalarGridSpec(
         num_scalar_prefetch=1, grid=(4,), in_specs=specs, out_specs=outs[:len(shapes)],
         scratch_shapes=[pltpu.VMEM((4, 512, 128), BF)] * 2 + [pltpu.VMEM((4, 128, 1152), BF)] * 2
-        + [pltpu.VMEM((4, 512, 128), BF)] + ([pltpu.VMEM((512, 128), F32)] if last else []))
+        + ([pltpu.VMEM((512, 128), F32)] if last else []))
     return pl.pallas_call(functools.partial(block_body, last), grid_spec=grid,
                           out_shape=[jax.ShapeDtypeStruct(u, F32) for u in shapes],
                           compiler_params=pltpu.CompilerParams(vmem_limit_bytes=VMEM), name="block",
                           cost_estimate=pl.CostEstimate(flops=2 * 3 * 512 * 3072 * 1152, bytes_accessed=10 << 20, transcendentals=0))(info, *args)
 
 
-def inverse_body(c_ref, o_ref):
+def inverse_body(c_ref, i_ref, o_ref):
     n = 128
     row = lax.broadcasted_iota(jnp.int32, (n, n), 0)
     col = lax.broadcasted_iota(jnp.int32, (n, n), 1)
@@ -236,10 +259,12 @@
         return 0
 
     lax.fori_loop(0, n // 2, step, 0)
+    i_ref[...] = o_ref[:, n:]
 
 
 def inverse_of(c):
-    return pl.pallas_call(inverse_body, out_shape=jax.ShapeDtypeStruct((128, 256), F32), name="inverse",
+    return pl.pallas_call(inverse_body, out_shape=jax.ShapeDtypeStruct((128, 128), F32), name="inverse",
+                          scratch_shapes=[pltpu.VMEM((128, 256), F32)],
                           cost_estimate=pl.CostEstimate(flops=2 * 3 * 512 * 3072 * 768, bytes_accessed=1 << 20, transcendentals=0))(c)
 
 
@@ -268,7 +293,7 @@
     r = lax.axis_index("rows")
     x = col // 2
     p = col % 2
-    info = jnp.stack([r, col, p, x]).astype(jnp.int32)
+    info = jnp.concatenate([jnp.stack([r, col, p, x]).astype(jnp.int32), block_sizes])
     sup = support.astype(F32)
 
     def message(t, extra):
@@ -279,16 +304,14 @@
 
     gathered = lax.all_gather(message(x, jnp.zeros((4, 128), F32)), "rows")
 
-    positions = jnp.arange(256, dtype=jnp.int32)
-    active = (positions[None, :] < block_sizes[:, None]).astype(F32)
-    w = primal * dual_inverse * active[:, :, None] * active[:, None, :]
     own = jnp.transpose(coefficients, (2, 0, 1, 3)).reshape(4, 512, 256)
-    own_sup = sup.reshape(512, 4)
+    own_sup = jnp.transpose(sup, (2, 0, 1)).reshape(4, 512)
+    own_sup = jnp.broadcast_to(own_sup[:, :, None], (4, 512, 128))
     eye = jnp.eye(128, dtype=F32)
 
     head = jnp.where(r == 0, message(0, right_sides[0]), 0.0)
     head_next = over_rows(head, [(0, 2)])
-    kept, given = partial(info, own, own_sup, w)
+    kept, given = partial(info, own, own_sup, primal, dual_inverse)
     head_next, kept, given = lax.optimization_barrier((head_next, kept, given))
     head = head + head_next
     head_next = over_rows(head, [(0, 1), (2, 3)])
@@ -306,13 +329,12 @@
     head_next, v_own, inverse, gathered = lax.optimization_barrier((head_next, v_own, inverse, gathered))
     v_other = swap(v_own)
     head = head + head_next
-    inverse = inverse[:, 128:]
-    head_other = swap(head[:512])
-    tile = lead(info, v_own, v_other, own_sup, head, head_other)
-    sent = jnp.where((r == 0) & (p == 1), inverse, jnp.where((r == 8) & (p == 0), over_rows(inverse, [(0, 8)]), tile))
-    every = exchange(repeat(sent, 16), "rows")
-
+    head_other = swap(head)
+    second = over_rows(inverse, [(0, 8)])
+    gathered, v_other, head_other, second = lax.optimization_barrier((gathered, v_other, head_other, second))
     swapped = swap(gathered)
+    every = exchange(lead(info, v_own, v_other, own_sup, head, head_other, inverse, second), "rows")
+
     start = block_product(info, v_own, own_sup, gathered, lambda g, i: (i[2], 0, 0), head, head)
     updated, panel, solved = block_product(info, v_other, own_sup, swapped, lambda g, i: (i[2], 0, 0), head, head_other,
                                            list(start) + [every, damping, right_sides])

time: 160 us -> 148 us (0.925)
  Pallas kernels: 69.2 us -> 64 us
  waiting for transfers between devices: 29.1 us -> 24.6 us
  other arithmetic: 7.79 us -> 5.08 us
  starting transfers between devices: 27.4 us -> 30.1 us
  local copies, waits for them, and re-layouts: 11.3 us -> 8.68 us
    ppermute x4, waiting for transfers between devices: 7.33 us -> 1.53 us  [swap(): return lax.ppermute(v, 'cols', SWAP)]
    pallas_call x2, Pallas kernels: 46.2 us -> 41.1 us  [block_product(): pl.pallas_call(functools.partial(block_body, last), grid_spec=grid, out_s...]
    ppermute x5, waiting for transfers between devices: 12.6 us -> 15.5 us  [over_rows(): return lax.ppermute(v, 'rows', pairs)]
    unnamed x20 -> x16, local copies, waits for them, and re-layouts: 2.71 us -> 1 us
  transfers between devices with their start and end apart: 13 -> 13, of which waited for: 6 -> 6; matrix products, arithmetic and copies ran while one was open for 8% -> 7% of each run, Pallas kernels for 28% -> 28%
where the time goes in v6:
time: 148 us; the launch traced here: 147 us
  Pallas kernels  64 us (43%)
  starting transfers between devices  30.1 us (20%)
  waiting for transfers between devices  24.6 us (17%)
  between operations  14.3 us (10%)
  local copies, waits for them, and re-layouts  8.68 us (6%)
  other arithmetic  5.08 us (3%)
    pallas_call x2, Pallas kernels, block_product(): pl.pallas_call(functools.partial(block_body, last), grid_spec=grid, out_s...  41.1 us
    ppermute x5, waiting for transfers between devices, over_rows(): return lax.ppermute(v, 'rows', pairs)  15.5 us
    all_to_all x3, starting transfers between devices, exchange(): return lax.all_to_all(v, axis, 0, 0, axis_index_groups=groups, tiled=True)  12.4 us
    ppermute x5, starting transfers between devices, over_rows(): return lax.ppermute(v, 'rows', pairs)  12.3 us
    pallas_call x1, Pallas kernels, inverse_of(): pl.pallas_call(inverse_body, out_shape=jax.ShapeDtypeStruct((128, 128), F...  9.53 us
    pallas_call x1, Pallas kernels, partial(): pl.pallas_call(partial_body, grid_spec=grid, out_shape=[out, out], compil...  7.65 us
    all_to_all x3, waiting for transfers between devices, exchange(): return lax.all_to_all(v, axis, 0, 0, axis_index_groups=groups, tiled=True)  7.63 us
    pallas_call x1, Pallas kernels, lead(): pl.pallas_call(lead_body, grid_spec=grid, out_shape=jax.ShapeDtypeStruct(...  5.75 us
  transfers between devices with their start and end apart: 13, of which 6 were waited for; matrix products, arithmetic and copies ran while one was open for 7% of the time, Pallas kernels for 28%

profile of v6, /device:TPU:1, one launch (start us, length us, event | category | flops | bytes accessed | tf_op | source)
XLA Modules:
  0.0 146.8 jit_solution(7254565364078977400)
XLA Ops:
  7.2 0.0 slice-start
  7.2 0.0 all-gather.3.cloned.1.call-start
  7.3 0.7 convert_bitcast_fusion
  8.0 1.1 constant_dynamic-slice_fusion
  9.2 0.0 copy-start.1
  9.2 0.1 copy.24
  9.3 0.1 pad.2.clone
  9.4 0.8 maximum_maximum_fusion
  10.2 0.0 all-gather.3.cloned.1.call-update
  10.3 0.1 constant_dynamic-slice_fusion.1
  10.3 0.1 copy.23
  10.5 0.7 slice_bitcast_fusion.2
  11.2 6.3 %collective-permute-start = (f32[520,128]{1,0:T(8,128)S(1)}, f32[520,128]{1,0:T(8,128)S(1)}, u32[]{:S(2)}, u32[]{:S(2)}) collective-permute-start(f32[520,128]{1,0:T(8,128)S(1)} %maximum_select_fusion), channel_id=1, source_target_pairs={{0,16},{1,17},{2,18},{3,19},{4,20},{5,21},{6,22},{7,23}} | collective-permute-start | bytes 798728 | tf_op jit(solution)/shard_map/ppermute | solution.py:288
  17.6 0.0 copy-start.7
  17.6 1.7 %copy.17 = f32[4,4,128,256]{3,2,1,0:T(8,128)} copy(f32[4,4,128,256]{3,0,2,1:T(4,128)S(1)} %bitcast.42) | data formatting | bytes 4194304 | tf_op jit(solution)/shard_map/transpose | solution.py:307
  19.3 0.7 concatenate.9.info
  19.9 1.3 broadcast_in_dim.22.s_ref.r_ref
  21.2 7.6 %partial.1 = (f32[4,5,128,128]{3,2,1,0:T(8,128)}, f32[4,5,128,128]{3,2,1,0:T(8,128)}) custom-call(s32[7]{0:T(128)} %concatenate.9.info, f32[4,512,256]{2,1,0:T(8,128)} %bitcast.41, f32[4,512,128]{2,1,0:T(8,128)} %broadcast_in_dim.22.s_ref.r_ref, f32[3,256,256]{2,1,0:T(8,128)} %x_ref.1, f32[3,256,256]{2,1,0:T(8,128)} %y_ref.1), custom_call_target="tpu_custom_call" | custom-call | flops 603979776 | bytes 8388608 | tf_op jit(solution)/shard_map/partial/pallas_call | solution.py:90
  28.9 1.2 collective-permute-start.2
  30.1 1.3 collective-permute-start.1
  31.4 1.5 %collective-permute-done.2 = f32[4,5,128,128]{3,2,1,0:T(8,128)S(1)} collective-permute-done((f32[4,5,128,128]{3,2,1,0:T(8,128)}, f32[4,5,128,128]{3,2,1,0:T(8,128)S(1)}, u32[]{:S(2)}, u32[]{:S(2)}) %collective-permute-start.2) | collective-permute-done | bytes 1310752 | tf_op jit(solution)/shard_map/ppermute | solution.py:276
  32.9 2.6 %add.44 = f32[4,5,128,128]{3,2,1,0:T(8,128)} add(f32[4,5,128,128]{3,2,1,0:T(8,128)} %get-tuple-element.28, f32[4,5,128,128]{3,2,1,0:T(8,128)S(1)} %collective-permute-done.2) | non-fusion elementwise | flops 327680 | bytes 3932160 | tf_op jit(solution)/shard_map/add | solution.py:318
  35.5 3.3 %collective-permute-done.1 = f32[520,128]{1,0:T(8,128)S(1)} collective-permute-done((f32[520,128]{1,0:T(8,128)S(1)}, f32[520,128]{1,0:T(8,128)S(1)}, u32[]{:S(2)}, u32[]{:S(2)}) %collective-permute-start.1) | collective-permute-done | bytes 266272 | tf_op jit(solution)/shard_map/ppermute | solution.py:288
  38.8 4.0 %all-to-all-start = ((f32[4,5,128,128]{3,2,1,0:T(8,128)}), f32[4,5,128,128]{3,2,1,0:T(8,128)S(1)}, u32[]{:S(2)}, u32[]{:S(2)}) async-start(f32[4,5,128,128]{3,2,1,0:T(8,128)} %add.44), calls=%async_computation | async-start | bytes 2621440 | tf_op jit(solution)/shard_map/all_to_all | solution.py:280
  42.8 1.3 collective-permute-start.3
  44.2 0.7 slice_bitcast_fusion.3
  44.8 10.6 %collective-permute-done.3 = f32[520,128]{1,0:T(8,128)S(1)} collective-permute-done((f32[520,128]{1,0:T(8,128)S(1)}, f32[520,128]{1,0:T(8,128)S(1)}, u32[]{:S(2)}, u32[]{:S(2)}) %collective-permute-start.3) | collective-permute-done | bytes 266272 | tf_op jit(solution)/shard_map/ppermute | solution.py:288
  55.4 4.5 %all-to-all-done = f32[4,5,128,128]{3,2,1,0:T(8,128)S(1)} async-done(((f32[4,5,128,128]{3,2,1,0:T(8,128)}), f32[4,5,128,128]{3,2,1,0:T(8,128)S(1)}, u32[]{:S(2)}, u32[]{:S(2)}) %all-to-all-start) | async-done | bytes 1310752 | tf_op jit(solution)/shard_map/all_to_all | solution.py:280
  59.9 1.3 collective-permute-start.4
  61.2 0.1 reduce_sum.9
  61.4 1.1 broadcast_in_dim.23
  62.4 3.5 %all-to-all-start.1 = ((f32[4,4,128,128]{3,2,1,0:T(8,128)}), f32[4,4,128,128]{3,2,1,0:T(8,128)S(1)}, u32[]{:S(2)}, u32[]{:S(2)}) async-start(f32[4,4,128,128]{3,2,1,0:T(8,128)} %broadcast_in_dim.23), calls=%async_computation.1 | async-start | bytes 2097152 | tf_op jit(solution)/shard_map/all_to_all | solution.py:280
  66.0 0.6 fusion.c_ref
  66.6 9.5 %inverse.1.f_ref = f32[128,128]{1,0:T(8,128)} custom-call(f32[128,128]{1,0:T(8,128)} %fusion.c_ref), custom_call_target="tpu_custom_call" | custom-call | flops 7247757312 | bytes 1048576 | tf_op jit(solution)/shard_map/inverse/pallas_call | solution.py:266
  76.1 0.0 collective-permute-done.4
  76.1 3.1 %all-to-all-done.1.v_ref.v0_ref = f32[4,4,128,128]{3,2,1,0:T(8,128)S(1)} async-done(((f32[4,4,128,128]{3,2,1,0:T(8,128)}), f32[4,4,128,128]{3,2,1,0:T(8,128)S(1)}, u32[]{:S(2)}, u32[]{:S(2)}) %all-to-all-start.1) | async-done | bytes 1048608 | tf_op jit(solution)/shard_map/all_to_all | solution.py:280
  79.3 2.7 %collective-permute-start.5 = (f32[4,4,128,128]{3,2,1,0:T(8,128)S(1)}, f32[4,4,128,128]{3,2,1,0:T(8,128)S(1)}, u32[]{:S(2)}, u32[]{:S(2)}) collective-permute-start(f32[4,4,128,128]{3,2,1,0:T(8,128)S(1)} %all-to-all-done.1.v_ref.v0_ref), channel_id=1, source_target_pairs={{0,1},{1,0},{2,3},{3,2},{4,5},{5,4},{6,7},{7,6},{8,9},{9,8},{10,11... | collective-permute-start | bytes 3145736 | tf_op jit(solution)/shard_map/ppermute | solution.py:276
  82.0 0.1 collective-permute-start.6
  82.1 2.0 %collective-permute-start.7 = (f32[128,128]{1,0:T(8,128)}, f32[128,128]{1,0:T(8,128)S(1)}, u32[]{:S(2)}, u32[]{:S(2)}) collective-permute-start(f32[128,128]{1,0:T(8,128)} %inverse.1.f_ref), channel_id=1, source_target_pairs={{0,64},{1,65},{2,66},{3,67},{4,68},{5,69},{6,70},{7,71}} | collective-permute-start | bytes 196616 | tf_op jit(solution)/shard_map/ppermute | solution.py:288
  84.2 1.6 %collective-permute-done.7.n_ref = f32[128,128]{1,0:T(8,128)S(1)} collective-permute-done((f32[128,128]{1,0:T(8,128)}, f32[128,128]{1,0:T(8,128)S(1)}, u32[]{:S(2)}, u32[]{:S(2)}) %collective-permute-start.7) | collective-permute-done | bytes 65568 | tf_op jit(solution)/shard_map/ppermute | solution.py:288
  85.8 1.4 collective-permute-start.8
  87.2 5.7 %lead.1 = f32[16,128,128]{2,1,0:T(8,128)} custom-call(s32[7]{0:T(128)} %concatenate.9.info, f32[4,4,128,128]{3,2,1,0:T(8,128)} %copy-done, f32[4,4,128,128]{3,2,1,0:T(8,128)} %copy-done.3, f32[4,512,128]{2,1,0:T(8,128)} %broadcast_in_dim.22.s_ref.r_ref, f32[520,128]{1,0:T(8,128)} %copy-done.2, f32[520,128]{1,0:T(8,128)} %copy-done.5, ...), custom_call_target="tpu_custom_call" | custom-call | flops 603979776 | bytes 6291456 | tf_op jit(solution)/shard_map/lead/pallas_call | solution.py:143
  93.0 4.9 %all-to-all-start.2 = ((f32[16,128,128]{2,1,0:T(8,128)}), f32[16,128,128]{2,1,0:T(8,128)S(1)}, u32[]{:S(2)}, u32[]{:S(2)}) async-start(f32[16,128,128]{2,1,0:T(8,128)} %lead.1), calls=%async_computation.2 | async-start | bytes 2097152 | tf_op jit(solution)/shard_map/all_to_all | solution.py:280
  97.9 18.4 %block.2 = (f32[512,1024]{1,0:T(8,128)}, f32[512,128]{1,0:T(8,128)}) custom-call(s32[7]{0:T(128)} %concatenate.9.info, f32[4,4,128,128]{3,2,1,0:T(8,128)} %copy-done, f32[4,512,128]{2,1,0:T(8,128)} %broadcast_in_dim.22.s_ref.r_ref, f32[16,520,128]{2,1,0:T(8,128)} %bitcast.46, f32[520,128]{1,0:T(8,128)} %copy-done.2, f32[520,128]{1,0:T(8,128)} %copy-done.2), custom_call_target="tpu_custom_call" | custom-call | flops 10871635968 | bytes 10485760 | tf_op jit(solution)/shard_map/block/pallas_call | solution.py:225
  116.2 0.0 all-to-all-done.2.rest_2_
  116.2 0.0 collective-permute-done.8.c_ref
  116.3 1.0 copy-done.4
  117.2 22.7 %block.3 = (f32[512,1024]{1,0:T(8,128)}, f32[512,128]{1,0:T(8,128)}, f32[4,4,128]{2,1,0:T(4,128)}) custom-call(s32[7]{0:T(128)} %concatenate.9.info, f32[4,4,128,128]{3,2,1,0:T(8,128)} %copy-done.3, f32[4,512,128]{2,1,0:T(8,128)} %broadcast_in_dim.22.s_ref.r_ref, f32[16,520,128]{2,1,0:T(8,128)} %collective-permute-done.8.c_ref, f32[520,128]{1,0:T(8,128)} %copy-done.2, ...), custom_call_target="tpu_custom_call" | custom-call | flops 10871635968 | bytes 10485760 | tf_op jit(solution)/shard_map/block/pallas_call | solution.py:225
  (26 shorter events, 0.2 us)
Async XLA Ops:
  7.2 3.1 %slice-start = ((f32[4,128,4,256]{3,2,1,0:T(4,128)}), f32[1,128,4,256]{3,2,1,0:T(4,128)S(1)}, s32[]{:S(2)}) async-start(f32[4,128,4,256]{3,2,1,0:T(4,128)} %param.7), calls=%async_computation.4 | async-start | bytes 1048576 | tf_op jit(solution)/shard_map/jit(dynamic_index_in_dim)/dynamic_slice | solution.py:300
  7.2 72.1 %all-gather.3.cloned.1.call-start = ((), (), s32[]{:S(2)}) async-start(), calls=%async_computation.3 | async-start | bytes 4526080 | tf_op jit(solution)/shard_map/all_gather | solution.py:305
  9.2 8.4 %copy-start.1 = (f32[4,128,4,256]{3,2,1,0:T(4,128)S(1)}, f32[4,128,4,256]{3,2,1,0:T(4,128)}, u32[]{:S(2)}) copy-start(f32[4,128,4,256]{3,2,1,0:T(4,128)} %param.7) | copy-start | bytes 6291460
  11.2 17.7 %collective-permute-start = (f32[520,128]{1,0:T(8,128)S(1)}, f32[520,128]{1,0:T(8,128)S(1)}, u32[]{:S(2)}, u32[]{:S(2)}) collective-permute-start(f32[520,128]{1,0:T(8,128)S(1)} %maximum_select_fusion), channel_id=1, source_target_pairs={{0,16},{1,17},{2,18},{3,19},{4,20},{5,21},{6,22},{7,23}} | collective-permute-start | bytes 798728 | tf_op jit(solution)/shard_map/ppermute | solution.py:288
  17.6 1.7 %copy-start.7 = (s32[3]{0:T(128)S(1)}, s32[3]{0:T(128)}, u32[]{:S(2)}) copy-start(s32[3]{0:T(128)} %param.11) | copy-start | bytes 40
  28.9 4.0 %collective-permute-start.2 = (f32[4,5,128,128]{3,2,1,0:T(8,128)}, f32[4,5,128,128]{3,2,1,0:T(8,128)S(1)}, u32[]{:S(2)}, u32[]{:S(2)}) collective-permute-start(f32[4,5,128,128]{3,2,1,0:T(8,128)} %get-tuple-element.29), channel_id=1, source_target_pairs={{0,1},{1,0},{2,3},{3,2},{4,5},{5,4},{6,7},{7,6},{8,9},{9,8},{10,11... | collective-permute-start | bytes 3932168 | tf_op jit(solution)/shard_map/ppermute | solution.py:276
  30.1 8.7 %collective-permute-start.1 = (f32[520,128]{1,0:T(8,128)S(1)}, f32[520,128]{1,0:T(8,128)S(1)}, u32[]{:S(2)}, u32[]{:S(2)}) collective-permute-start(f32[520,128]{1,0:T(8,128)S(1)} %add.43), channel_id=1, source_target_pairs={{0,8},{16,24},{1,9},{17,25},{2,10},{18,26},{3,11},{19,27},{4,12},{... | collective-permute-start | bytes 798728 | tf_op jit(solution)/shard_map/ppermute | solution.py:288
  38.8 21.1 %all-to-all-start = ((f32[4,5,128,128]{3,2,1,0:T(8,128)}), f32[4,5,128,128]{3,2,1,0:T(8,128)S(1)}, u32[]{:S(2)}, u32[]{:S(2)}) async-start(f32[4,5,128,128]{3,2,1,0:T(8,128)} %add.44), calls=%async_computation | async-start | bytes 2621440 | tf_op jit(solution)/shard_map/all_to_all | solution.py:280
  42.8 12.6 %collective-permute-start.3 = (f32[520,128]{1,0:T(8,128)S(1)}, f32[520,128]{1,0:T(8,128)S(1)}, u32[]{:S(2)}, u32[]{:S(2)}) collective-permute-start(f32[520,128]{1,0:T(8,128)S(1)} %add.45), channel_id=1, source_target_pairs={{0,64},{8,72},{16,80},{24,88},{1,65},{9,73},{17,81},{25,89},{2,66}... | collective-permute-start | bytes 798728 | tf_op jit(solution)/shard_map/ppermute | solution.py:288
  59.9 16.2 %collective-permute-start.4 = (f32[520,128]{1,0:T(8,128)S(1)}, f32[520,128]{1,0:T(8,128)S(1)}, u32[]{:S(2)}, u32[]{:S(2)}) collective-permute-start(f32[520,128]{1,0:T(8,128)S(1)} %add.46), channel_id=1, source_target_pairs={{0,32},{8,40},{16,48},{24,56},{64,96},{72,104},{80,112},{88,120},{... | collective-permute-start | bytes 798728 | tf_op jit(solution)/shard_map/ppermute | solution.py:288
  62.4 16.8 %all-to-all-start.1 = ((f32[4,4,128,128]{3,2,1,0:T(8,128)}), f32[4,4,128,128]{3,2,1,0:T(8,128)S(1)}, u32[]{:S(2)}, u32[]{:S(2)}) async-start(f32[4,4,128,128]{3,2,1,0:T(8,128)} %broadcast_in_dim.23), calls=%async_computation.1 | async-start | bytes 2097152 | tf_op jit(solution)/shard_map/all_to_all | solution.py:280
  79.3 8.0 %copy-start = (f32[4,4,128,128]{3,2,1,0:T(8,128)}, f32[4,4,128,128]{3,2,1,0:T(8,128)S(1)}, u32[]{:S(2)}) copy-start(f32[4,4,128,128]{3,2,1,0:T(8,128)S(1)} %all-to-all-done.1.v_ref.v0_ref) | copy-start | bytes 3145732
  79.3 6.5 %collective-permute-start.5 = (f32[4,4,128,128]{3,2,1,0:T(8,128)S(1)}, f32[4,4,128,128]{3,2,1,0:T(8,128)S(1)}, u32[]{:S(2)}, u32[]{:S(2)}) collective-permute-start(f32[4,4,128,128]{3,2,1,0:T(8,128)S(1)} %all-to-all-done.1.v_ref.v0_ref), channel_id=1, source_target_pairs={{0,1},{1,0},{2,3},{3,2},{4,5},{5,4},{6,7},{7,6},{8,9},{9,8},{10,11... | collective-permute-start | bytes 3145736 | tf_op jit(solution)/shard_map/ppermute | solution.py:276
  82.0 5.2 %copy-start.2 = (f32[520,128]{1,0:T(8,128)}, f32[520,128]{1,0:T(8,128)S(1)}, u32[]{:S(2)}) copy-start(f32[520,128]{1,0:T(8,128)S(1)} %add.49.z_ref.d_ref.d0_ref) | copy-start | bytes 798724
  82.0 3.8 %collective-permute-start.6 = (f32[520,128]{1,0:T(8,128)S(1)}, f32[520,128]{1,0:T(8,128)S(1)}, u32[]{:S(2)}, u32[]{:S(2)}) collective-permute-start(f32[520,128]{1,0:T(8,128)S(1)} %add.49.z_ref.d_ref.d0_ref), channel_id=1, source_target_pairs={{0,1},{1,0},{2,3},{3,2},{4,5},{5,4},{6,7},{7,6},{8,9},{9,8},{10,11... | collective-permute-start | bytes 798728 | tf_op jit(solution)/shard_map/ppermute | solution.py:276
  82.1 3.7 %collective-permute-start.7 = (f32[128,128]{1,0:T(8,128)}, f32[128,128]{1,0:T(8,128)S(1)}, u32[]{:S(2)}, u32[]{:S(2)}) collective-permute-start(f32[128,128]{1,0:T(8,128)} %inverse.1.f_ref), channel_id=1, source_target_pairs={{0,64},{1,65},{2,66},{3,67},{4,68},{5,69},{6,70},{7,71}} | collective-permute-start | bytes 196616 | tf_op jit(solution)/shard_map/ppermute | solution.py:288
  85.8 1.4 copy-start.6
  85.8 1.4 copy-start.5
  85.8 1.4 copy-start.3
  85.8 30.4 %collective-permute-start.8 = (f32[16,520,128]{2,1,0:T(8,128)}, f32[16,520,128]{2,1,0:T(8,128)}, u32[]{:S(2)}, u32[]{:S(2)}) collective-permute-start(f32[16,520,128]{2,1,0:T(8,128)} %bitcast.45), channel_id=1, source_target_pairs={{0,1},{1,0},{2,3},{3,2},{4,5},{5,4},{6,7},{7,6},{8,9},{9,8},{10,11... | collective-permute-start | bytes 12779528 | tf_op jit(solution)/shard_map/ppermute | solution.py:276
  93.0 23.3 %all-to-all-start.2 = ((f32[16,128,128]{2,1,0:T(8,128)}), f32[16,128,128]{2,1,0:T(8,128)S(1)}, u32[]{:S(2)}, u32[]{:S(2)}) async-start(f32[16,128,128]{2,1,0:T(8,128)} %lead.1), calls=%async_computation.2 | async-start | bytes 2097152 | tf_op jit(solution)/shard_map/all_to_all | solution.py:280
  116.2 1.0 copy-start.4
Sparse Core Ops, SparseCore 0:
  10.4 62.0 all-gather.2

commit v7 on v6

--- a/solution.py
+++ b/solution.py
@@ -32,11 +32,10 @@
     return out
 
 
-def partial_body(info, c_ref, s_ref, x_ref, y_ref, v_ref, g_ref, wh, wl, total):
+def partial_body(info, c_ref, s_ref, x_ref, y_ref, z_ref, v_ref, wh, wl, total):
     t = pl.program_id(0)
-    p = info[2]
+    col, p = info[1], info[2]
     mine = pl.ds(pl.multiple_of(p * 128, 128), 128)
-    other = pl.ds(pl.multiple_of((1 - p) * 128, 128), 128)
 
     @pl.when(t == 0)
     def _():
@@ -44,52 +43,50 @@
         lane = lax.broadcasted_iota(jnp.int32, (256, 128), 1)
         for u in range(3):
             size = info[4 + u]
-            for q, (h, base) in enumerate(((mine, p * 128), (other, (1 - p) * 128))):
-                w = jnp.where((row < size) & (lane + base < size), x_ref[u, :, h] * y_ref[u, :, h], 0.0)
-                wh[u, :, q * 128:(q + 1) * 128], wl[u, :, q * 128:(q + 1) * 128] = split(w)
-
-    corner = jnp.zeros((128, 128), F32)
-    parts = [None] * 8
-    for u in range(3):
-        block = (info[1] * 3 + u).astype(F32)
+            w = jnp.where((row < size) & (lane + p * 128 < size), x_ref[u, :, mine] * y_ref[u, :, mine], 0.0)
+            wh[u], wl[u] = split(w)
+            wh[3 + u], wl[3 + u] = split(z_ref[u])
+
+    parts = [jnp.zeros((128, 128), F32)] * 4
+    masks = []
+    for u in range(6):
+        block = ((col if u < 3 else col + 1 - 2 * p) * 3 + u % 3).astype(F32)
         m = [s_ref[k] == block for k in range(4)]
+        masks.append(m)
         d = jnp.concatenate([choose(m, [c_ref[k, :, q * 128:(q + 1) * 128] for k in range(4)]) for q in range(2)], axis=1)
         dh, dl = split(d)
         v = product(dh, dl, wh[u], wl[u], NN)
-        vh, vl = split(v)
-        e = jnp.concatenate([choose(m, [c_ref[k, :, h] for k in range(4)]) for h in (mine, other)], axis=1)
-        eh, el = split(e)
-        corner = corner + product(vh, vl, eh, el, NT)
-        for q in range(2):
-            part = v[:, q * 128:(q + 1) * 128]
-            for k in range(4):
-                before = jnp.zeros_like(part) if u == 0 else parts[4 * q + k]
-                parts[4 * q + k] = jnp.where(m[k], part, before)
+        parts = [jnp.where(m[k], v, parts[k]) for k in range(4)]
+    for k in range(4):
+        v_ref[0, k] = parts[k]
 
     @pl.when(t == 0)
     def _():
-        total[...] = corner
-
-    for q, ref in enumerate((v_ref, g_ref)):
-        for k in range(4):
-            ref[0, k] = parts[4 * q + k]
-        ref[0, 4] = total[...]
+        vs, es = [], []
+        for m in masks:
+            vs.append(choose(m, parts))
+            es.append(choose(m, [c_ref[k, :, mine] for k in range(4)]))
+        vh, vl = split(jnp.concatenate(vs, axis=1))
+        eh, el = split(jnp.concatenate(es, axis=1))
+        total[...] = product(vh, vl, eh, el, NT)
+
+    v_ref[0, 4] = total[...]
 
 
 def whole(v):
     return pl.BlockSpec(v.shape, lambda g, i: (0,) * v.ndim)
 
 
-def partial(info, c, s, x, y):
+def partial(info, c, s, x, y, z):
     out = jax.ShapeDtypeStruct((4, 5, 128, 128), F32)
     grid = pltpu.PrefetchScalarGridSpec(
         num_scalar_prefetch=1, grid=(4,),
-        in_specs=[pl.BlockSpec((4, 128, 256), lambda t, i: (0, t, 0)), pl.BlockSpec((4, 128, 128), lambda t, i: (0, t, 0)), whole(x), whole(y)],
-        out_specs=[pl.BlockSpec((1, 5, 128, 128), lambda t, i: (t, 0, 0, 0))] * 2,
-        scratch_shapes=[pltpu.VMEM((3, 256, 256), BF)] * 2 + [pltpu.VMEM((128, 128), F32)])
-    return pl.pallas_call(partial_body, grid_spec=grid, out_shape=[out, out],
+        in_specs=[pl.BlockSpec((4, 128, 256), lambda t, i: (0, t, 0)), pl.BlockSpec((4, 128, 128), lambda t, i: (0, t, 0)), whole(x), whole(y), whole(z)],
+        out_specs=pl.BlockSpec((1, 5, 128, 128), lambda t, i: (t, 0, 0, 0)),
+        scratch_shapes=[pltpu.VMEM((6, 256, 128), BF)] * 2 + [pltpu.VMEM((128, 128), F32)])
+    return pl.pallas_call(partial_body, grid_spec=grid, out_shape=out,
                           compiler_params=pltpu.CompilerParams(vmem_limit_bytes=VMEM), name="partial",
-                          cost_estimate=pl.CostEstimate(flops=2 * 3 * 512 * 768 * 256, bytes_accessed=8 << 20, transcendentals=0))(info, c, s, x, y)
+                          cost_estimate=pl.CostEstimate(flops=2 * 3 * 512 * 768 * 256, bytes_accessed=8 << 20, transcendentals=0))(info, c, s, x, y, z)
 
 
 def gather_blocks(base, sup, high, low, axis):
@@ -309,14 +306,16 @@
     own_sup = jnp.broadcast_to(own_sup[:, :, None], (4, 512, 128))
     eye = jnp.eye(128, dtype=F32)
 
+    pair = [lax.dynamic_slice_in_dim(v, 128 - p * 128, 128, 2) for v in (primal, dual_inverse)]
+    places = jnp.arange(256)[None, :, None], 128 - p * 128 + jnp.arange(128)[None, None, :]
+    inside = (places[0] < block_sizes[:, None, None]) & (places[1] < block_sizes[:, None, None])
+    lent = swap(jnp.where(inside, pair[0] * pair[1], 0.0))
     head = jnp.where(r == 0, message(0, right_sides[0]), 0.0)
     head_next = over_rows(head, [(0, 2)])
-    kept, given = partial(info, own, own_sup, primal, dual_inverse)
-    head_next, kept, given = lax.optimization_barrier((head_next, kept, given))
+    half = partial(info, own, own_sup, primal, dual_inverse, lent)
+    head_next, half = lax.optimization_barrier((head_next, half))
     head = head + head_next
     head_next = over_rows(head, [(0, 1), (2, 3)])
-    half = kept + swap(given)
-    head_next, half = lax.optimization_barrier((head_next, half))
     head = head + head_next
     head_next = over_rows(head, [(z, 8 + z) for z in range(4)])
     terms = exchange(half, "cols", CHIPS)
@@ -325,7 +324,8 @@
     head_next = over_rows(head, [(y + z, y + 4 + z) for y in (0, 8) for z in range(4)])
     total = jnp.sum(terms, axis=0)
     v_own = exchange(repeat(total[:4], 4), "cols", CHIPS)
-    inverse = inverse_of(total[4] + eye * damping[0])
+    corner = total[4] + eye * jnp.where(p == 0, damping[0], 0.0)
+    inverse = inverse_of(corner + swap(corner))
     head_next, v_own, inverse, gathered = lax.optimization_barrier((head_next, v_own, inverse, gathered))
     v_other = swap(v_own)
     head = head + head_next

time: 148 us -> 150 us (1.014)
  starting transfers between devices: 30.1 us -> 34.1 us
  waiting for transfers between devices: 24.6 us -> 22.4 us
  other arithmetic: 5.08 us -> 6.8 us
    all_to_all x3, waiting for transfers between devices: 7.63 us -> 4.75 us  [exchange(): return lax.all_to_all(v, axis, 0, 0, axis_index_groups=groups, tiled=True)]
    ppermute x5, starting transfers between devices: 12.3 us -> 15.1 us  [over_rows(): return lax.ppermute(v, 'rows', pairs)]
    add x2 -> x3, other arithmetic: 3.24 us -> 0.66 us  [the longest x1 0.64 us: local(): inverse = inverse_of(corner + swap(corner))]
    ppermute x5, waiting for transfers between devices: 15.5 us -> 17.6 us  [over_rows(): return lax.ppermute(v, 'rows', pairs)]
    select_n x0 -> x1, other arithmetic: none -> 1.94 us  [local(): lent = swap(jnp.where(inside, pair[0] * pair[1], 0.0))]
    lt x0 -> x2, other arithmetic: none -> 1.6 us  [the longest x1 0.87 us: local(): places[0] < block_sizes[:, None, None]]
    ppermute x4 -> x5, waiting for transfers between devices: 1.53 us -> 0.01 us  [swap(): return lax.ppermute(v, 'cols', SWAP)]
    ppermute x4 -> x5, starting transfers between devices: 5.36 us -> 5.87 us  [swap(): return lax.ppermute(v, 'cols', SWAP)]
  transfers between devices with their start and end apart: 13 -> 14, of which waited for: 6 -> 4; matrix products, arithmetic and copies ran while one was open for 7% -> 7% of each run, Pallas kernels for 28% -> 27%
where the time goes in v7:
time: 150 us; the launch traced here: 149 us
  Pallas kernels  63.2 us (42%)
  starting transfers between devices  34.1 us (23%)
  waiting for transfers between devices  22.4 us (15%)
  between operations  14.3 us (10%)
  local copies, waits for them, and re-layouts  7.96 us (5%)
  other arithmetic  6.8 us (5%)
    pallas_call x2, Pallas kernels, block_product(): pl.pallas_call(functools.partial(block_body, last), grid_spec=grid, out_s...  41.1 us
    ppermute x5, waiting for transfers between devices, over_rows(): return lax.ppermute(v, 'rows', pairs)  17.6 us
    ppermute x5, starting transfers between devices, over_rows(): return lax.ppermute(v, 'rows', pairs)  15.1 us
    all_to_all x3, starting transfers between devices, exchange(): return lax.all_to_all(v, axis, 0, 0, axis_index_groups=groups, tiled=True)  13.1 us
    pallas_call x1, Pallas kernels, inverse_of(): pl.pallas_call(inverse_body, out_shape=jax.ShapeDtypeStruct((128, 128), F...  9.53 us
    pallas_call x1, Pallas kernels, partial(): pl.pallas_call(partial_body, grid_spec=grid, out_shape=out, compiler_para...  6.91 us
    ppermute x5, starting transfers between devices, swap(): return lax.ppermute(v, 'cols', SWAP)  5.87 us
    pallas_call x1, Pallas kernels, lead(): pl.pallas_call(lead_body, grid_spec=grid, out_shape=jax.ShapeDtypeStruct(...  5.74 us
  transfers between devices with their start and end apart: 14, of which 4 were waited for; matrix products, arithmetic and copies ran while one was open for 7% of the time, Pallas kernels for 27%

profile of v7, /device:TPU:1, one launch (start us, length us, event | category | flops | bytes accessed | tf_op | source)
XLA Modules:
  0.0 148.8 jit_solution(5927573780835248253)
XLA Ops:
  7.2 0.0 copy-start.2
  7.2 0.0 all-gather.3.cloned.1.call-start
  7.2 0.0 slice-start
  7.3 0.8 convert_bitcast_fusion
  8.1 1.1 constant_dynamic-slice_fusion
  9.2 0.1 copy.24
  9.4 0.1 pad.2.clone
  9.4 0.8 maximum_maximum_fusion
  10.3 0.0 all-gather.3.cloned.1.call-update
  10.3 0.9 iota_compare_fusion.1
  11.2 0.7 broadcast_compare_fusion
  11.9 1.9 %multiply_select_fusion = f32[3,256,128]{2,1,0:T(8,128)} fusion(f32[3,256,256]{2,1,0:T(8,128)} %y_ref.1, s32[]{:T(128)S(6)} %select_n.59, f32[3,256,256]{2,1,0:T(8,128)S(1)} %copy-done.2, pred[3,128]{1,0:T(4,128)(4,1)S(1)} %broadcast_compare_fusion, pred[3,256]{1,0:T(4,128)(4,1)S(1)} %iota_compare_fusion.1), kind=kLoop, calls=%fused_computation | loop fusion | flops 294912 | bytes 1180804 | tf_op jit(solution)/shard_map/jit(_where)/select_n | solution.py:312
  13.9 1.5 %collective-permute-start.1 = (f32[3,256,128]{2,1,0:T(8,128)}, f32[3,256,128]{2,1,0:T(8,128)S(1)}, u32[]{:S(2)}, u32[]{:S(2)}) collective-permute-start(f32[3,256,128]{2,1,0:T(8,128)} %multiply_select_fusion), channel_id=1, source_target_pairs={{0,1},{1,0},{2,3},{3,2},{4,5},{5,4},{6,7},{7,6},{8,9},{9,8},{10,11... | collective-permute-start | bytes 1179656 | tf_op jit(solution)/shard_map/ppermute | solution.py:273
  15.4 0.7 slice_bitcast_fusion.2
  16.1 0.1 copy.23
  16.3 5.6 %collective-permute-start = (f32[520,128]{1,0:T(8,128)S(1)}, f32[520,128]{1,0:T(8,128)S(1)}, u32[]{:S(2)}, u32[]{:S(2)}) collective-permute-start(f32[520,128]{1,0:T(8,128)S(1)} %maximum_select_fusion), channel_id=1, source_target_pairs={{0,16},{1,17},{2,18},{3,19},{4,20},{5,21},{6,22},{7,23}} | collective-permute-start | bytes 798728 | tf_op jit(solution)/shard_map/ppermute | solution.py:285
  21.9 0.0 copy-start.9
  21.9 1.7 %copy.17 = f32[4,4,128,256]{3,2,1,0:T(8,128)} copy(f32[4,4,128,256]{3,0,2,1:T(4,128)S(1)} %bitcast.44) | data formatting | bytes 4194304 | tf_op jit(solution)/shard_map/transpose | solution.py:304
  23.6 0.6 concatenate.9.info
  24.3 0.0 collective-permute-done.1.z_ref
  24.3 1.3 broadcast_in_dim.35.s_ref.r_ref
  25.6 6.9 %partial.1 = f32[4,5,128,128]{3,2,1,0:T(8,128)} custom-call(s32[7]{0:T(128)} %concatenate.9.info, f32[4,512,256]{2,1,0:T(8,128)} %bitcast.43, f32[4,512,128]{2,1,0:T(8,128)} %broadcast_in_dim.35.s_ref.r_ref, f32[3,256,256]{2,1,0:T(8,128)} %x_ref.1, f32[3,256,256]{2,1,0:T(8,128)} %y_ref.1, f32[3,256,128]{2,1,0:T(8,128)} %copy-done.6), custom_call_target="tpu_custom_call" | custom-call | flops 603979776 | bytes 8388608 | tf_op jit(solution)/shard_map/partial/pallas_call | solution.py:87
  32.5 0.0 collective-permute-done
  32.5 4.0 %all-to-all-start = ((f32[4,5,128,128]{3,2,1,0:T(8,128)}), f32[4,5,128,128]{3,2,1,0:T(8,128)S(1)}, u32[]{:S(2)}, u32[]{:S(2)}) async-start(f32[4,5,128,128]{3,2,1,0:T(8,128)} %partial.1), calls=%async_computation | async-start | bytes 2621440 | tf_op jit(solution)/shard_map/all_to_all | solution.py:277
  36.5 1.3 collective-permute-start.2
  37.8 5.5 %collective-permute-done.2 = f32[520,128]{1,0:T(8,128)S(1)} collective-permute-done((f32[520,128]{1,0:T(8,128)S(1)}, f32[520,128]{1,0:T(8,128)S(1)}, u32[]{:S(2)}, u32[]{:S(2)}) %collective-permute-start.2) | collective-permute-done | bytes 266272 | tf_op jit(solution)/shard_map/ppermute | solution.py:285
  43.3 1.3 collective-permute-start.3
  44.7 0.7 fusion.1
  45.4 10.5 %collective-permute-done.3 = f32[520,128]{1,0:T(8,128)S(1)} collective-permute-done((f32[520,128]{1,0:T(8,128)S(1)}, f32[520,128]{1,0:T(8,128)S(1)}, u32[]{:S(2)}, u32[]{:S(2)}) %collective-permute-start.3) | collective-permute-done | bytes 266272 | tf_op jit(solution)/shard_map/ppermute | solution.py:285
  55.9 0.0 all-to-all-done
  55.9 0.1 reduce_sum.9
  56.0 1.7 %collective-permute-start.5 = (f32[128,128]{1,0:T(8,128)S(1)}, f32[128,128]{1,0:T(8,128)S(1)}, u32[]{:S(2)}, u32[]{:S(2)}) collective-permute-start(f32[128,128]{1,0:T(8,128)S(1)} %fusion), channel_id=1, source_target_pairs={{0,1},{1,0},{2,3},{3,2},{4,5},{5,4},{6,7},{7,6},{8,9},{9,8},{10,11... | collective-permute-start | bytes 196616 | tf_op jit(solution)/shard_map/ppermute | solution.py:273
  57.8 1.3 collective-permute-start.4
  59.1 1.1 broadcast_in_dim.37
  60.2 4.2 %all-to-all-start.1 = ((f32[4,4,128,128]{3,2,1,0:T(8,128)}), f32[4,4,128,128]{3,2,1,0:T(8,128)S(1)}, u32[]{:S(2)}, u32[]{:S(2)}) async-start(f32[4,4,128,128]{3,2,1,0:T(8,128)} %broadcast_in_dim.37), calls=%async_computation.1 | async-start | bytes 2097152 | tf_op jit(solution)/shard_map/all_to_all | solution.py:277
  64.4 0.6 fusion.2.c_ref
  65.1 9.5 %inverse.1.f_ref = f32[128,128]{1,0:T(8,128)} custom-call(f32[128,128]{1,0:T(8,128)} %fusion.2.c_ref), custom_call_target="tpu_custom_call" | custom-call | flops 7247757312 | bytes 1048576 | tf_op jit(solution)/shard_map/inverse/pallas_call | solution.py:263
  74.6 4.7 %all-to-all-done.1.v_ref.v0_ref = f32[4,4,128,128]{3,2,1,0:T(8,128)S(1)} async-done(((f32[4,4,128,128]{3,2,1,0:T(8,128)}), f32[4,4,128,128]{3,2,1,0:T(8,128)S(1)}, u32[]{:S(2)}, u32[]{:S(2)}) %all-to-all-start.1) | async-done | bytes 1048608 | tf_op jit(solution)/shard_map/all_to_all | solution.py:277
  79.4 1.1 collective-permute-start.6
  80.5 0.1 collective-permute-start.7
  80.6 5.6 %collective-permute-start.8 = (f32[128,128]{1,0:T(8,128)}, f32[128,128]{1,0:T(8,128)S(1)}, u32[]{:S(2)}, u32[]{:S(2)}) collective-permute-start(f32[128,128]{1,0:T(8,128)} %inverse.1.f_ref), channel_id=1, source_target_pairs={{0,64},{1,65},{2,66},{3,67},{4,68},{5,69},{6,70},{7,71}} | collective-permute-start | bytes 196616 | tf_op jit(solution)/shard_map/ppermute | solution.py:285
  86.2 1.6 %collective-permute-done.8.n_ref = f32[128,128]{1,0:T(8,128)S(1)} collective-permute-done((f32[128,128]{1,0:T(8,128)}, f32[128,128]{1,0:T(8,128)S(1)}, u32[]{:S(2)}, u32[]{:S(2)}) %collective-permute-start.8) | collective-permute-done | bytes 65568 | tf_op jit(solution)/shard_map/ppermute | solution.py:285
  87.9 1.4 collective-permute-start.9
  89.3 5.7 %lead.1 = f32[16,128,128]{2,1,0:T(8,128)} custom-call(s32[7]{0:T(128)} %concatenate.9.info, f32[4,4,128,128]{3,2,1,0:T(8,128)} %copy-done, f32[4,4,128,128]{3,2,1,0:T(8,128)} %copy-done.4, f32[4,512,128]{2,1,0:T(8,128)} %broadcast_in_dim.35.s_ref.r_ref, f32[520,128]{1,0:T(8,128)} %copy-done.3, f32[520,128]{1,0:T(8,128)} %copy-done.7, ...), custom_call_target="tpu_custom_call" | custom-call | flops 603979776 | bytes 6291456 | tf_op jit(solution)/shard_map/lead/pallas_call | solution.py:140
  95.1 4.9 %all-to-all-start.2 = ((f32[16,128,128]{2,1,0:T(8,128)}), f32[16,128,128]{2,1,0:T(8,128)S(1)}, u32[]{:S(2)}, u32[]{:S(2)}) async-start(f32[16,128,128]{2,1,0:T(8,128)} %lead.1), calls=%async_computation.2 | async-start | bytes 2097152 | tf_op jit(solution)/shard_map/all_to_all | solution.py:277
  100.0 18.4 %block.2 = (f32[512,1024]{1,0:T(8,128)}, f32[512,128]{1,0:T(8,128)}) custom-call(s32[7]{0:T(128)} %concatenate.9.info, f32[4,4,128,128]{3,2,1,0:T(8,128)} %copy-done, f32[4,512,128]{2,1,0:T(8,128)} %broadcast_in_dim.35.s_ref.r_ref, f32[16,520,128]{2,1,0:T(8,128)} %bitcast.48, f32[520,128]{1,0:T(8,128)} %copy-done.3, f32[520,128]{1,0:T(8,128)} %copy-done.3), custom_call_target="tpu_custom_call" | custom-call | flops 10871635968 | bytes 10485760 | tf_op jit(solution)/shard_map/block/pallas_call | solution.py:222
  118.3 1.0 copy-done.5
  119.3 22.7 %block.3 = (f32[512,1024]{1,0:T(8,128)}, f32[512,128]{1,0:T(8,128)}, f32[4,4,128]{2,1,0:T(4,128)}) custom-call(s32[7]{0:T(128)} %concatenate.9.info, f32[4,4,128,128]{3,2,1,0:T(8,128)} %copy-done.4, f32[4,512,128]{2,1,0:T(8,128)} %broadcast_in_dim.35.s_ref.r_ref, f32[16,520,128]{2,1,0:T(8,128)} %collective-permute-done.9.c_ref, f32[520,128]{1,0:T(8,128)} %copy-done.3, ...), custom_call_target="tpu_custom_call" | custom-call | flops 10871635968 | bytes 10485760 | tf_op jit(solution)/shard_map/block/pallas_call | solution.py:222
  (36 shorter events, 0.3 us)
Async XLA Ops:
  7.2 4.8 %copy-start.2 = (f32[3,256,256]{2,1,0:T(8,128)S(1)}, f32[3,256,256]{2,1,0:T(8,128)}, u32[]{:S(2)}) copy-start(f32[3,256,256]{2,1,0:T(8,128)} %x_ref.1) | copy-start | bytes 2359300
  7.2 72.2 %all-gather.3.cloned.1.call-start = ((), (), s32[]{:S(2)}) async-start(), calls=%async_computation.3 | async-start | bytes 4526080 | tf_op jit(solution)/shard_map/all_gather | solution.py:302
  7.2 8.8 %slice-start = ((f32[4,128,4,256]{3,2,1,0:T(4,128)}), f32[1,128,4,256]{3,2,1,0:T(4,128)S(1)}, s32[]{:S(2)}) async-start(f32[4,128,4,256]{3,2,1,0:T(4,128)} %param.7), calls=%async_computation.4 | async-start | bytes 1048576 | tf_op jit(solution)/shard_map/jit(dynamic_index_in_dim)/dynamic_slice | solution.py:297
  10.3 11.6 %copy-start.1 = (f32[4,128,4,256]{3,2,1,0:T(4,128)S(1)}, f32[4,128,4,256]{3,2,1,0:T(4,128)}, u32[]{:S(2)}) copy-start(f32[4,128,4,256]{3,2,1,0:T(4,128)} %param.7) | copy-start | bytes 6291460
  13.9 10.4 %collective-permute-start.1 = (f32[3,256,128]{2,1,0:T(8,128)}, f32[3,256,128]{2,1,0:T(8,128)S(1)}, u32[]{:S(2)}, u32[]{:S(2)}) collective-permute-start(f32[3,256,128]{2,1,0:T(8,128)} %multiply_select_fusion), channel_id=1, source_target_pairs={{0,1},{1,0},{2,3},{3,2},{4,5},{5,4},{6,7},{7,6},{8,9},{9,8},{10,11... | collective-permute-start | bytes 1179656 | tf_op jit(solution)/shard_map/ppermute | solution.py:273
  16.3 16.2 %collective-permute-start = (f32[520,128]{1,0:T(8,128)S(1)}, f32[520,128]{1,0:T(8,128)S(1)}, u32[]{:S(2)}, u32[]{:S(2)}) collective-permute-start(f32[520,128]{1,0:T(8,128)S(1)} %maximum_select_fusion), channel_id=1, source_target_pairs={{0,16},{1,17},{2,18},{3,19},{4,20},{5,21},{6,22},{7,23}} | collective-permute-start | bytes 798728 | tf_op jit(solution)/shard_map/ppermute | solution.py:285
  21.9 1.7 %copy-start.9 = (s32[3]{0:T(128)S(1)}, s32[3]{0:T(128)}, u32[]{:S(2)}) copy-start(s32[3]{0:T(128)} %param.11) | copy-start | bytes 40
  24.3 1.3 copy-start.6
  32.5 23.4 %all-to-all-start = ((f32[4,5,128,128]{3,2,1,0:T(8,128)}), f32[4,5,128,128]{3,2,1,0:T(8,128)S(1)}, u32[]{:S(2)}, u32[]{:S(2)}) async-start(f32[4,5,128,128]{3,2,1,0:T(8,128)} %partial.1), calls=%async_computation | async-start | bytes 2621440 | tf_op jit(solution)/shard_map/all_to_all | solution.py:277
  36.5 6.8 %collective-permute-start.2 = (f32[520,128]{1,0:T(8,128)S(1)}, f32[520,128]{1,0:T(8,128)S(1)}, u32[]{:S(2)}, u32[]{:S(2)}) collective-permute-start(f32[520,128]{1,0:T(8,128)S(1)} %add.62), channel_id=1, source_target_pairs={{0,8},{16,24},{1,9},{17,25},{2,10},{18,26},{3,11},{19,27},{4,12},{... | collective-permute-start | bytes 798728 | tf_op jit(solution)/shard_map/ppermute | solution.py:285
  43.3 12.6 %collective-permute-start.3 = (f32[520,128]{1,0:T(8,128)S(1)}, f32[520,128]{1,0:T(8,128)S(1)}, u32[]{:S(2)}, u32[]{:S(2)}) collective-permute-start(f32[520,128]{1,0:T(8,128)S(1)} %add.63), channel_id=1, source_target_pairs={{0,64},{8,72},{16,80},{24,88},{1,65},{9,73},{17,81},{25,89},{2,66}... | collective-permute-start | bytes 798728 | tf_op jit(solution)/shard_map/ppermute | solution.py:285
  56.0 8.4 %collective-permute-start.5 = (f32[128,128]{1,0:T(8,128)S(1)}, f32[128,128]{1,0:T(8,128)S(1)}, u32[]{:S(2)}, u32[]{:S(2)}) collective-permute-start(f32[128,128]{1,0:T(8,128)S(1)} %fusion), channel_id=1, source_target_pairs={{0,1},{1,0},{2,3},{3,2},{4,5},{5,4},{6,7},{7,6},{8,9},{9,8},{10,11... | collective-permute-start | bytes 196616 | tf_op jit(solution)/shard_map/ppermute | solution.py:273
  57.8 16.8 %collective-permute-start.4 = (f32[520,128]{1,0:T(8,128)S(1)}, f32[520,128]{1,0:T(8,128)S(1)}, u32[]{:S(2)}, u32[]{:S(2)}) collective-permute-start(f32[520,128]{1,0:T(8,128)S(1)} %add.64), channel_id=1, source_target_pairs={{0,32},{8,40},{16,48},{24,56},{64,96},{72,104},{80,112},{88,120},{... | collective-permute-start | bytes 798728 | tf_op jit(solution)/shard_map/ppermute | solution.py:285
  60.2 19.1 %all-to-all-start.1 = ((f32[4,4,128,128]{3,2,1,0:T(8,128)}), f32[4,4,128,128]{3,2,1,0:T(8,128)S(1)}, u32[]{:S(2)}, u32[]{:S(2)}) async-start(f32[4,4,128,128]{3,2,1,0:T(8,128)} %broadcast_in_dim.37), calls=%async_computation.1 | async-start | bytes 2097152 | tf_op jit(solution)/shard_map/all_to_all | solution.py:277
  79.4 10.0 %copy-start = (f32[4,4,128,128]{3,2,1,0:T(8,128)}, f32[4,4,128,128]{3,2,1,0:T(8,128)S(1)}, u32[]{:S(2)}) copy-start(f32[4,4,128,128]{3,2,1,0:T(8,128)S(1)} %all-to-all-done.1.v_ref.v0_ref) | copy-start | bytes 3145732
  79.4 8.5 %collective-permute-start.6 = (f32[4,4,128,128]{3,2,1,0:T(8,128)S(1)}, f32[4,4,128,128]{3,2,1,0:T(8,128)S(1)}, u32[]{:S(2)}, u32[]{:S(2)}) collective-permute-start(f32[4,4,128,128]{3,2,1,0:T(8,128)S(1)} %all-to-all-done.1.v_ref.v0_ref), channel_id=1, source_target_pairs={{0,1},{1,0},{2,3},{3,2},{4,5},{5,4},{6,7},{7,6},{8,9},{9,8},{10,11... | collective-permute-start | bytes 3145736 | tf_op jit(solution)/shard_map/ppermute | solution.py:273
  80.5 8.8 %copy-start.3 = (f32[520,128]{1,0:T(8,128)}, f32[520,128]{1,0:T(8,128)S(1)}, u32[]{:S(2)}) copy-start(f32[520,128]{1,0:T(8,128)S(1)} %add.68.z_ref.d_ref.d0_ref) | copy-start | bytes 798724
  80.5 7.3 %collective-permute-start.7 = (f32[520,128]{1,0:T(8,128)S(1)}, f32[520,128]{1,0:T(8,128)S(1)}, u32[]{:S(2)}, u32[]{:S(2)}) collective-permute-start(f32[520,128]{1,0:T(8,128)S(1)} %add.68.z_ref.d_ref.d0_ref), channel_id=1, source_target_pairs={{0,1},{1,0},{2,3},{3,2},{4,5},{5,4},{6,7},{7,6},{8,9},{9,8},{10,11... | collective-permute-start | bytes 798728 | tf_op jit(solution)/shard_map/ppermute | solution.py:273
  80.6 7.2 %collective-permute-start.8 = (f32[128,128]{1,0:T(8,128)}, f32[128,128]{1,0:T(8,128)S(1)}, u32[]{:S(2)}, u32[]{:S(2)}) collective-permute-start(f32[128,128]{1,0:T(8,128)} %inverse.1.f_ref), channel_id=1, source_target_pairs={{0,64},{1,65},{2,66},{3,67},{4,68},{5,69},{6,70},{7,71}} | collective-permute-start | bytes 196616 | tf_op jit(solution)/shard_map/ppermute | solution.py:285
  87.9 1.4 copy-start.8
  87.9 1.4 copy-start.7
  87.9 1.4 copy-start.4
  87.9 30.4 %collective-permute-start.9 = (f32[16,520,128]{2,1,0:T(8,128)}, f32[16,520,128]{2,1,0:T(8,128)}, u32[]{:S(2)}, u32[]{:S(2)}) collective-permute-start(f32[16,520,128]{2,1,0:T(8,128)} %bitcast.47), channel_id=1, source_target_pairs={{0,1},{1,0},{2,3},{3,2},{4,5},{5,4},{6,7},{7,6},{8,9},{9,8},{10,11... | collective-permute-start | bytes 12779528 | tf_op jit(solution)/shard_map/ppermute | solution.py:273
  95.1 23.2 %all-to-all-start.2 = ((f32[16,128,128]{2,1,0:T(8,128)}), f32[16,128,128]{2,1,0:T(8,128)S(1)}, u32[]{:S(2)}, u32[]{:S(2)}) async-start(f32[16,128,128]{2,1,0:T(8,128)} %lead.1), calls=%async_computation.2 | async-start | bytes 2097152 | tf_op jit(solution)/shard_map/all_to_all | solution.py:277
  118.3 1.0 copy-start.5
Sparse Core Ops, SparseCore 0:
  10.4 62.7 all-gather.2

commit v8 on v7

--- a/solution.py
+++ b/solution.py
@@ -103,19 +103,19 @@
     return jnp.broadcast_to(jnp.concatenate(rows, axis=1), (128, n)).astype(BF)
 
 
-def lead_body(info, v0_ref, v1_ref, s_ref, d0_ref, d1_ref, f_ref, n_ref, o_ref, vh, vl, dh, dl, a_ref):
+def lead_body(info, v0_ref, v1_ref, s_ref, z_ref, f_ref, n_ref, o_ref, vh, vl, dh, dl, a_ref):
     g = pl.program_id(0)
 
     @pl.when(g == 0)
     def _():
-        for j, (v_ref, d_ref) in enumerate(((v0_ref, d0_ref), (v1_ref, d1_ref))):
+        for j, v_ref in enumerate((v0_ref, v1_ref)):
             for k in range(4):
-                vh[j, k], vl[j, k] = split(v_ref[0, k])
-                dh[j, k], dl[j, k] = split(d_ref[k * 128:(k + 1) * 128])
+                vh[j, k], vl[j, k] = split(v_ref[info[3], k])
+                dh[j, k], dl[j, k] = split(v_ref[k, 4])
         a_ref[...] = jnp.zeros_like(a_ref)
 
     sup = [s_ref[k].astype(BF) for k in range(4)]
-    first = [column_labels([d0_ref[512 + k:513 + k]], 128) for k in range(4)]
+    first = [column_labels([z_ref[128 + k:129 + k]], 128) for k in range(4)]
     for j in range(2):
         ah, al = gather_blocks(6 * g, sup, lambda k: vh[j, k], lambda k: vl[j, k], 1)
         bh, bl = gather_blocks(6 * g, first, lambda k: dh[j, k], lambda k: dl[j, k], 0)
@@ -129,10 +129,9 @@
             o_ref[j] = sent
 
 
-def lead(info, v0, v1, s, d0, d1, f, n):
-    args = [v0, v1, s, d0, d1, f, n]
+def lead(info, v0, v1, s, z, f, n):
+    args = [v0, v1, s, z, f, n]
     specs = [whole(v) for v in args]
-    specs[0] = specs[1] = pl.BlockSpec((1, 4, 128, 128), lambda g, i: (i[3], 0, 0, 0))
     specs[2] = pl.BlockSpec((4, 128, 128), lambda g, i: (0, i[3], 0))
     grid = pltpu.PrefetchScalarGridSpec(
         num_scalar_prefetch=1, grid=(4,), in_specs=specs, out_specs=pl.BlockSpec((16, 128, 128), lambda g, i: (0, 0, 0)),
@@ -142,7 +141,7 @@
                           cost_estimate=pl.CostEstimate(flops=2 * 3 * 128 * 6144 * 128, bytes_accessed=6 << 20, transcendentals=0))(info, *args)
 
 
-def block_body(last, info, v_ref, r_ref, c_ref, z_ref, d_ref, *rest):
+def block_body(last, info, v_ref, r_ref, c_ref, z_ref, *rest):
     if last:
         s_ref, b_ref, e_ref, h_ref, y_ref, o_ref, p_ref, x_ref, vh, vl, ch, cl, total = rest
     else:
@@ -156,7 +155,7 @@
                 vh[k, t * 128:(t + 1) * 128], vl[k, t * 128:(t + 1) * 128] = split(v_ref[t, k])
             for t in range(8):
                 ch[k, :, t * 128:(t + 1) * 128], cl[k, :, t * 128:(t + 1) * 128] = split(c_ref[t, k * 128:(k + 1) * 128])
-            ch[k, :, 1024:], cl[k, :, 1024:] = split(d_ref[k * 128:(k + 1) * 128])
+            ch[k, :, 1024:], cl[k, :, 1024:] = split(v_ref[k, 4])
         o_ref[...] = s_ref[...] if last else jnp.zeros_like(o_ref)
         total[...] = b_ref[...] if last else jnp.zeros_like(total)
 
@@ -168,7 +167,7 @@
         if q < 2:
             sup = [column_labels([c_ref[4 * q + t, 512 + k:513 + k] for t in range(4)], n) for k in range(4)]
         else:
-            sup = [column_labels([z_ref[512 + k:513 + k]], n) for k in range(4)]
+            sup = [column_labels([z_ref[128 + k:129 + k]], n) for k in range(4)]
         bh, bl = gather_blocks(6 * g, sup, lambda k: ch[k, :, r], lambda k: cl[k, :, r], 0)
         value = product(ah, al, bh, bl, NN)
         if q < 2:
@@ -187,7 +186,7 @@
             panel = product(th, tl, ih, il, NT)
             p_ref[...] = panel
             ph, plo = split(panel)
-            zh, zl = split(z_ref[512:520])
+            zh, zl = split(z_ref[128:136])
             sides = product(zh, zl, ih, il, NT)
             xh, xl = split(sides)
             for t in range(4):
@@ -207,9 +206,9 @@
                     o_ref[tile, span] += diagonal - jnp.where((down > 0) & (across > 0), outer[tile], 0.0)
 
 
-def block_product(info, v, r, c, pick, z, d, tail=None):
+def block_product(info, v, r, c, pick, z, tail=None):
     last = tail is not None
-    args = [v, r, c, z, d] + (list(tail) if last else [])
+    args = [v, r, c, z] + (list(tail) if last else [])
     specs = [whole(u) for u in args]
     specs[2] = pl.BlockSpec((8, 520, 128), pick)
     shapes = [(512, 1024), (512, 128)] + ([(4, 4, 128)] if last else [])
@@ -306,37 +305,40 @@
     own_sup = jnp.broadcast_to(own_sup[:, :, None], (4, 512, 128))
     eye = jnp.eye(128, dtype=F32)
 
-    pair = [lax.dynamic_slice_in_dim(v, 128 - p * 128, 128, 2) for v in (primal, dual_inverse)]
-    places = jnp.arange(256)[None, :, None], 128 - p * 128 + jnp.arange(128)[None, None, :]
-    inside = (places[0] < block_sizes[:, None, None]) & (places[1] < block_sizes[:, None, None])
-    lent = swap(jnp.where(inside, pair[0] * pair[1], 0.0))
-    head = jnp.where(r == 0, message(0, right_sides[0]), 0.0)
+    active = (jnp.arange(256, dtype=jnp.int32)[None, :] < block_sizes[:, None]).astype(F32)
+    away = 128 - p * 128
+    lent = lax.dynamic_slice_in_dim(primal, away, 128, 2) * lax.dynamic_slice_in_dim(dual_inverse, away, 128, 2)
+    lent = swap(lent * active[:, :, None] * lax.dynamic_slice_in_dim(active, away, 128, 1)[:, None, :])
+
+    head = lax.dynamic_slice_in_dim(lax.dynamic_index_in_dim(coefficients[0], x, 1, keepdims=False), p * 128, 128, 1)
+    head = jnp.concatenate([head.T, sup[0].T, right_sides[0]], axis=0)
+    head = jnp.where(r == 0, head, 0.0)
     head_next = over_rows(head, [(0, 2)])
+    head_next, lent = lax.optimization_barrier((head_next, lent))
+    head = head + head_next
+    head_next = over_rows(head, [(0, 1), (2, 3)])
     half = partial(info, own, own_sup, primal, dual_inverse, lent)
     head_next, half = lax.optimization_barrier((head_next, half))
     head = head + head_next
-    head_next = over_rows(head, [(0, 1), (2, 3)])
+    head_next = over_rows(head, [(z, 8 + z) for z in range(4)])
     head = head + head_next
-    head_next = over_rows(head, [(z, 8 + z) for z in range(4)])
+    head_next = over_rows(head, [(y + z, y + 4 + z) for y in (0, 8) for z in range(4)])
     terms = exchange(half, "cols", CHIPS)
     head_next, terms = lax.optimization_barrier((head_next, terms))
     head = head + head_next
-    head_next = over_rows(head, [(y + z, y + 4 + z) for y in (0, 8) for z in range(4)])
     total = jnp.sum(terms, axis=0)
-    v_own = exchange(repeat(total[:4], 4), "cols", CHIPS)
+    v_own = exchange(repeat(jnp.concatenate([total[:4], head[None, :128]], axis=0), 4), "cols", CHIPS)
     corner = total[4] + eye * jnp.where(p == 0, damping[0], 0.0)
     inverse = inverse_of(corner + swap(corner))
-    head_next, v_own, inverse, gathered = lax.optimization_barrier((head_next, v_own, inverse, gathered))
+    second = over_rows(inverse, [(0, 8)])
+    v_own, inverse, second, gathered = lax.optimization_barrier((v_own, inverse, second, gathered))
     v_other = swap(v_own)
-    head = head + head_next
-    head_other = swap(head)
-    second = over_rows(inverse, [(0, 8)])
-    gathered, v_other, head_other, second = lax.optimization_barrier((gathered, v_other, head_other, second))
+    gathered, v_other = lax.optimization_barrier((gathered, v_other))
     swapped = swap(gathered)
-    every = exchange(lead(info, v_own, v_other, own_sup, head, head_other, inverse, second), "rows")
-
-    start = block_product(info, v_own, own_sup, gathered, lambda g, i: (i[2], 0, 0), head, head)
-    updated, panel, solved = block_product(info, v_other, own_sup, swapped, lambda g, i: (i[2], 0, 0), head, head_other,
+    every = exchange(lead(info, v_own, v_other, own_sup, head, inverse, second), "rows")
+
+    start = block_product(info, v_own, own_sup, gathered, lambda g, i: (i[2], 0, 0), head)
+    updated, panel, solved = block_product(info, v_other, own_sup, swapped, lambda g, i: (i[2], 0, 0), head,
                                            list(start) + [every, damping, right_sides])
     return updated.reshape(4, 128, 1024), panel.reshape(4, 128, 128), solved
 

time: 150 us -> 150 us (level)
  starting transfers between devices: 34.1 us -> 28.2 us
  local copies, waits for them, and re-layouts: 7.96 us -> 11.5 us
  waiting for transfers between devices: 22.4 us -> 24.4 us
    ppermute x5, waiting for transfers between devices: 17.6 us -> 5.59 us  [over_rows(): return lax.ppermute(v, 'rows', pairs)]
    all_to_all x3, waiting for transfers between devices: 4.75 us -> 16.1 us  [exchange(): return lax.all_to_all(v, axis, 0, 0, axis_index_groups=groups, tiled=True)]
    ppermute x5, starting transfers between devices: 15.1 us -> 10.7 us  [over_rows(): return lax.ppermute(v, 'rows', pairs)]
    ppermute x5 -> x4, waiting for transfers between devices: 0.01 us -> 2.67 us  [swap(): return lax.ppermute(v, 'cols', SWAP)]
    select_n x2 -> x1, other arithmetic: 1.97 us -> 0.01 us  [local(): head = jnp.where(r == 0, head, 0.0)]
    mul x0 -> x1, other arithmetic: none -> 1.91 us  [local(): lent * active[:, :, None]]
    transpose x2 -> x1, local copies, waits for them, and re-layouts: 0.26 us -> 1.93 us  [message(): jnp.transpose(tile, (1, 2, 0)).reshape(512, 128)]
    lt x2 -> x0, other arithmetic: 1.6 us -> none  [the longest x1 0.87 us: local(): places[0] < block_sizes[:, None, None]]
  transfers between devices with their start and end apart: 14 -> 13, of which waited for: 4 -> 7; matrix products, arithmetic and copies ran while one was open for 7% -> 7% of each run, Pallas kernels for 27% -> 28%
where the time goes in v8:
time: 150 us; the launch traced here: 149 us
  Pallas kernels  63.8 us (43%)
  starting transfers between devices  28.2 us (19%)
  waiting for transfers between devices  24.4 us (16%)
  between operations  14.3 us (10%)
  local copies, waits for them, and re-layouts  11.5 us (8%)
  other arithmetic  6.73 us (4%)
    pallas_call x2, Pallas kernels, block_product(): pl.pallas_call(functools.partial(block_body, last), grid_spec=grid, out_s...  41.1 us
    all_to_all x3, waiting for transfers between devices, exchange(): return lax.all_to_all(v, axis, 0, 0, axis_index_groups=groups, tiled=True)  16.1 us
    all_to_all x3, starting transfers between devices, exchange(): return lax.all_to_all(v, axis, 0, 0, axis_index_groups=groups, tiled=True)  12.6 us
    ppermute x5, starting transfers between devices, over_rows(): return lax.ppermute(v, 'rows', pairs)  10.7 us
    pallas_call x1, Pallas kernels, inverse_of(): pl.pallas_call(inverse_body, out_shape=jax.ShapeDtypeStruct((128, 128), F...  9.53 us
    pallas_call x1, Pallas kernels, partial(): pl.pallas_call(partial_body, grid_spec=grid, out_shape=out, compiler_para...  6.93 us
    pallas_call x1, Pallas kernels, lead(): pl.pallas_call(lead_body, grid_spec=grid, out_shape=jax.ShapeDtypeStruct(...  6.18 us
    ppermute x5, waiting for transfers between devices, over_rows(): return lax.ppermute(v, 'rows', pairs)  5.59 us
  transfers between devices with their start and end apart: 13, of which 7 were waited for; matrix products, arithmetic and copies ran while one was open for 7% of the time, Pallas kernels for 28%

profile of v8, /device:TPU:1, one launch (start us, length us, event | category | flops | bytes accessed | tf_op | source)
XLA Modules:
  0.0 148.8 jit_solution(1023350463233303213)
XLA Ops:
  7.2 0.0 copy-start.2
  7.2 0.0 all-gather.3.cloned.1.call-start
  7.2 0.0 slice-start
  7.3 0.8 convert_bitcast_fusion
  8.1 1.9 %constant_dynamic-slice_fusion = f32[1,128,4,128]{3,2,1,0:T(4,128)} fusion(f32[4,128,4,256]{3,2,1,0:T(4,128)} %param.7, s32[]{:T(128)S(6)} %select_n.53, s32[]{:T(128)S(6)} %select_n.55), kind=kLoop, calls=%fused_computation.13 | loop fusion | bytes 524296 | tf_op jit(solution)/shard_map/dynamic_slice | solution.py:297
  9.9 1.9 %copy.20 = f32[1,128,4,128]{1,3,2,0:T(8,128)} copy(f32[1,128,4,128]{3,2,1,0:T(4,128)} %constant_dynamic-slice_fusion) | data formatting | bytes 524288 | tf_op jit(solution)/shard_map/transpose | solution.py:298
  11.9 0.1 pad.2.clone
  11.9 1.8 %maximum_maximum_fusion = f32[520,128]{1,0:T(8,128)} fusion(f32[4,128]{1,0:T(4,128)S(1)} %get-tuple-element.37, f32[512,128]{1,0:T(8,128)} %bitcast.44, f32[520]{0:T(1024)S(1)} %pad.2.clone), kind=kLoop, calls=%fused_computation.2 | loop fusion | flops 133120 | bytes 532512 | tf_op jit(solution)/shard_map/concatenate | solution.py:298
  13.7 0.0 all-gather.3.cloned.1.call-update
  13.8 0.7 fusion.1
  14.5 1.9 %multiply_multiply_fusion = f32[3,256,128]{2,1,0:T(8,128)} fusion(f32[3,256,256]{2,1,0:T(8,128)} %y_ref.1, s32[]{:T(128)S(6)} %select_n.57, f32[3,256,256]{2,1,0:T(8,128)S(1)} %copy-done.2, f32[3,128]{1,0:T(4,128)S(1)} %constant_dynamic-slice_fusion.1, f32[3,256]{1,0:T(4,128)S(1)} %fusion.1), kind=kLoop, calls=%fused_computation | loop fusion | flops 294912 | bytes 1184260 | tf_op jit(solution)/shard_map/mul | solution.py:311
  16.4 1.5 %collective-permute-start.1 = (f32[3,256,128]{2,1,0:T(8,128)}, f32[3,256,128]{2,1,0:T(8,128)S(1)}, u32[]{:S(2)}, u32[]{:S(2)}) collective-permute-start(f32[3,256,128]{2,1,0:T(8,128)} %multiply_multiply_fusion), channel_id=1, source_target_pairs={{0,1},{1,0},{2,3},{3,2},{4,5},{5,4},{6,7},{7,6},{8,9},{9,8},{10,11... | collective-permute-start | bytes 1179656 | tf_op jit(solution)/shard_map/ppermute | solution.py:272
  17.9 0.2 constant_dynamic-slice_fusion.2
  18.1 0.1 copy.15
  18.2 0.7 slice_bitcast_fusion.3
  18.9 5.6 %collective-permute-start = (f32[136,128]{1,0:T(8,128)S(1)}, f32[136,128]{1,0:T(8,128)S(1)}, u32[]{:S(2)}, u32[]{:S(2)}) collective-permute-start(f32[136,128]{1,0:T(8,128)S(1)} %maximum_select_fusion), channel_id=1, source_target_pairs={{0,16},{1,17},{2,18},{3,19},{4,20},{5,21},{6,22},{7,23}} | collective-permute-start | bytes 208904 | tf_op jit(solution)/shard_map/ppermute | solution.py:284
  24.5 1.6 %collective-permute-done = f32[136,128]{1,0:T(8,128)S(1)} collective-permute-done((f32[136,128]{1,0:T(8,128)S(1)}, f32[136,128]{1,0:T(8,128)S(1)}, u32[]{:S(2)}, u32[]{:S(2)}) %collective-permute-start) | collective-permute-done | bytes 69664 | tf_op jit(solution)/shard_map/ppermute | solution.py:284
  26.1 1.3 collective-permute-start.2
  27.4 0.0 copy-start.8
  27.5 1.7 %copy.16 = f32[4,4,128,256]{3,2,1,0:T(8,128)} copy(f32[4,4,128,256]{3,0,2,1:T(4,128)S(1)} %bitcast.43) | data formatting | bytes 4194304 | tf_op jit(solution)/shard_map/transpose | solution.py:303
  29.2 0.7 concatenate.12.info
  29.8 1.4 broadcast_in_dim.34.s_ref.r_ref
  31.2 6.9 %partial.1 = f32[4,5,128,128]{3,2,1,0:T(8,128)} custom-call(s32[7]{0:T(128)} %concatenate.12.info, f32[4,512,256]{2,1,0:T(8,128)} %bitcast.42, f32[4,512,128]{2,1,0:T(8,128)} %broadcast_in_dim.34.s_ref.r_ref, f32[3,256,256]{2,1,0:T(8,128)} %x_ref.1, f32[3,256,256]{2,1,0:T(8,128)} %y_ref.1, f32[3,256,128]{2,1,0:T(8,128)} %copy-done.6), custom_call_target="tpu_custom_call" | custom-call | flops 603979776 | bytes 8388608 | tf_op jit(solution)/shard_map/partial/pallas_call | solution.py:87
  38.1 4.0 %all-to-all-start = ((f32[4,5,128,128]{3,2,1,0:T(8,128)}), f32[4,5,128,128]{3,2,1,0:T(8,128)S(1)}, u32[]{:S(2)}, u32[]{:S(2)}) async-start(f32[4,5,128,128]{3,2,1,0:T(8,128)} %partial.1), calls=%async_computation | async-start | bytes 2621440 | tf_op jit(solution)/shard_map/all_to_all | solution.py:276
  42.2 1.3 collective-permute-start.3
  43.5 1.3 collective-permute-done.3
  44.8 1.3 collective-permute-start.4
  46.1 0.7 fusion.2
  46.8 0.7 collective-permute-done.4
  47.5 11.6 %all-to-all-done = f32[4,5,128,128]{3,2,1,0:T(8,128)S(1)} async-done(((f32[4,5,128,128]{3,2,1,0:T(8,128)}), f32[4,5,128,128]{3,2,1,0:T(8,128)S(1)}, u32[]{:S(2)}, u32[]{:S(2)}) %all-to-all-start) | async-done | bytes 1310752 | tf_op jit(solution)/shard_map/all_to_all | solution.py:276
  59.1 0.1 reduce_sum.9
  59.2 2.0 %collective-permute-start.5 = (f32[128,128]{1,0:T(8,128)S(1)}, f32[128,128]{1,0:T(8,128)S(1)}, u32[]{:S(2)}, u32[]{:S(2)}) collective-permute-start(f32[128,128]{1,0:T(8,128)S(1)} %fusion), channel_id=1, source_target_pairs={{0,1},{1,0},{2,3},{3,2},{4,5},{5,4},{6,7},{7,6},{8,9},{9,8},{10,11... | collective-permute-start | bytes 196616 | tf_op jit(solution)/shard_map/ppermute | solution.py:272
  61.3 1.2 broadcast_in_dim.36
  62.5 3.5 %all-to-all-start.1 = ((f32[4,5,128,128]{3,2,1,0:T(8,128)}), f32[4,5,128,128]{3,2,1,0:T(8,128)S(1)}, u32[]{:S(2)}, u32[]{:S(2)}) async-start(f32[4,5,128,128]{3,2,1,0:T(8,128)} %broadcast_in_dim.36), calls=%async_computation.1 | async-start | bytes 2621440 | tf_op jit(solution)/shard_map/all_to_all | solution.py:276
  66.1 0.6 fusion.3.c_ref
  66.7 9.5 %inverse.1.f_ref = f32[128,128]{1,0:T(8,128)} custom-call(f32[128,128]{1,0:T(8,128)} %fusion.3.c_ref), custom_call_target="tpu_custom_call" | custom-call | flops 7247757312 | bytes 1048576 | tf_op jit(solution)/shard_map/inverse/pallas_call | solution.py:262
  76.2 1.3 collective-permute-start.6
  77.5 2.0 %collective-permute-done.6.n_ref = f32[128,128]{1,0:T(8,128)S(1)} collective-permute-done((f32[128,128]{1,0:T(8,128)}, f32[128,128]{1,0:T(8,128)S(1)}, u32[]{:S(2)}, u32[]{:S(2)}) %collective-permute-start.6) | collective-permute-done | bytes 65568 | tf_op jit(solution)/shard_map/ppermute | solution.py:284
  79.5 4.5 %all-to-all-done.1.v_ref.v0_ref = f32[4,5,128,128]{3,2,1,0:T(8,128)S(1)} async-done(((f32[4,5,128,128]{3,2,1,0:T(8,128)}), f32[4,5,128,128]{3,2,1,0:T(8,128)S(1)}, u32[]{:S(2)}, u32[]{:S(2)}) %all-to-all-start.1) | async-done | bytes 1310752 | tf_op jit(solution)/shard_map/all_to_all | solution.py:276
  84.1 0.8 collective-permute-start.7
  84.9 2.7 %collective-permute-done.7.v1_ref.v_ref = f32[4,5,128,128]{3,2,1,0:T(8,128)S(1)} collective-permute-done((f32[4,5,128,128]{3,2,1,0:T(8,128)S(1)}, f32[4,5,128,128]{3,2,1,0:T(8,128)S(1)}, u32[]{:S(2)}, u32[]{:S(2)}) %collective-permute-start.7) | collective-permute-done | bytes 1310752 | tf_op jit(solution)/shard_map/ppermute | solution.py:272
  87.6 0.4 collective-permute-start.8
  87.9 0.7 copy-done.3
  88.6 6.2 %lead.1 = f32[16,128,128]{2,1,0:T(8,128)} custom-call(s32[7]{0:T(128)} %concatenate.12.info, f32[4,5,128,128]{3,2,1,0:T(8,128)} %copy-done, f32[4,5,128,128]{3,2,1,0:T(8,128)} %copy-done.3, f32[4,512,128]{2,1,0:T(8,128)} %broadcast_in_dim.34.s_ref.r_ref, f32[136,128]{1,0:T(8,128)} %copy-done.5, f32[128,128]{1,0:T(8,128)} %inverse.1.f_ref, f32[128,128]{1,0:T(8,128)} %copy-done.7), custom_call_target="tpu_custom_call" | custom-call | flops 603979776 | bytes 6291456 | tf_op jit(solution)/shard_map/lead/pallas_call | solution.py:139
  94.8 5.1 %all-to-all-start.2 = ((f32[16,128,128]{2,1,0:T(8,128)}), f32[16,128,128]{2,1,0:T(8,128)S(1)}, u32[]{:S(2)}, u32[]{:S(2)}) async-start(f32[16,128,128]{2,1,0:T(8,128)} %lead.1), calls=%async_computation.2 | async-start | bytes 2097152 | tf_op jit(solution)/shard_map/all_to_all | solution.py:276
  99.9 18.4 %block.2 = (f32[512,1024]{1,0:T(8,128)}, f32[512,128]{1,0:T(8,128)}) custom-call(s32[7]{0:T(128)} %concatenate.12.info, f32[4,5,128,128]{3,2,1,0:T(8,128)} %copy-done, f32[4,512,128]{2,1,0:T(8,128)} %broadcast_in_dim.34.s_ref.r_ref, f32[16,520,128]{2,1,0:T(8,128)} %bitcast.47, f32[136,128]{1,0:T(8,128)} %copy-done.5), custom_call_target="tpu_custom_call" | custom-call | flops 10871635968 | bytes 10485760 | tf_op jit(solution)/shard_map/block/pallas_call | solution.py:221
  118.3 1.0 copy-done.4
  119.3 22.7 %block.3 = (f32[512,1024]{1,0:T(8,128)}, f32[512,128]{1,0:T(8,128)}, f32[4,4,128]{2,1,0:T(4,128)}) custom-call(s32[7]{0:T(128)} %concatenate.12.info, f32[4,5,128,128]{3,2,1,0:T(8,128)} %copy-done.3, f32[4,512,128]{2,1,0:T(8,128)} %broadcast_in_dim.34.s_ref.r_ref, f32[16,520,128]{2,1,0:T(8,128)} %collective-permute-done.8.c_ref, f32[136,128]{1,0:T(8,128)} %copy-done.5, ...), custom_call_target="tpu_custom_call" | custom-call | flops 10871635968 | bytes 10485760 | tf_op jit(solution)/shard_map/block/pallas_call | solution.py:221
  (33 shorter events, 0.2 us)
Async XLA Ops:
  7.2 7.3 %copy-start.2 = (f32[3,256,256]{2,1,0:T(8,128)S(1)}, f32[3,256,256]{2,1,0:T(8,128)}, u32[]{:S(2)}) copy-start(f32[3,256,256]{2,1,0:T(8,128)} %x_ref.1) | copy-start | bytes 2359300
  7.2 76.9 %all-gather.3.cloned.1.call-start = ((), (), s32[]{:S(2)}) async-start(), calls=%async_computation.3 | async-start | bytes 4526080 | tf_op jit(solution)/shard_map/all_gather | solution.py:301
  7.2 10.7 %slice-start = ((f32[4,128,4,256]{3,2,1,0:T(4,128)}), f32[1,128,4,256]{3,2,1,0:T(4,128)S(1)}, s32[]{:S(2)}) async-start(f32[4,128,4,256]{3,2,1,0:T(4,128)} %param.7), calls=%async_computation.4 | async-start | bytes 1048576 | tf_op jit(solution)/shard_map/slice | solution.py:313
  9.9 17.5 %copy-start.1 = (f32[4,128,4,256]{3,2,1,0:T(4,128)S(1)}, f32[4,128,4,256]{3,2,1,0:T(4,128)}, u32[]{:S(2)}) copy-start(f32[4,128,4,256]{3,2,1,0:T(4,128)} %param.7) | copy-start | bytes 6291460
  16.4 9.7 %collective-permute-start.1 = (f32[3,256,128]{2,1,0:T(8,128)}, f32[3,256,128]{2,1,0:T(8,128)S(1)}, u32[]{:S(2)}, u32[]{:S(2)}) collective-permute-start(f32[3,256,128]{2,1,0:T(8,128)} %multiply_multiply_fusion), channel_id=1, source_target_pairs={{0,1},{1,0},{2,3},{3,2},{4,5},{5,4},{6,7},{7,6},{8,9},{9,8},{10,11... | collective-permute-start | bytes 1179656 | tf_op jit(solution)/shard_map/ppermute | solution.py:272
  18.9 7.2 %collective-permute-start = (f32[136,128]{1,0:T(8,128)S(1)}, f32[136,128]{1,0:T(8,128)S(1)}, u32[]{:S(2)}, u32[]{:S(2)}) collective-permute-start(f32[136,128]{1,0:T(8,128)S(1)} %maximum_select_fusion), channel_id=1, source_target_pairs={{0,16},{1,17},{2,18},{3,19},{4,20},{5,21},{6,22},{7,23}} | collective-permute-start | bytes 208904 | tf_op jit(solution)/shard_map/ppermute | solution.py:284
  26.1 3.0 %copy-start.6 = (f32[3,256,128]{2,1,0:T(8,128)}, f32[3,256,128]{2,1,0:T(8,128)S(1)}, u32[]{:S(2)}) copy-start(f32[3,256,128]{2,1,0:T(8,128)S(1)} %collective-permute-done.1.z_ref) | copy-start | bytes 1179652
  26.1 12.0 %collective-permute-start.2 = (f32[136,128]{1,0:T(8,128)S(1)}, f32[136,128]{1,0:T(8,128)S(1)}, u32[]{:S(2)}, u32[]{:S(2)}) collective-permute-start(f32[136,128]{1,0:T(8,128)S(1)} %add.53), channel_id=1, source_target_pairs={{0,8},{16,24},{1,9},{17,25},{2,10},{18,26},{3,11},{19,27},{4,12},{... | collective-permute-start | bytes 208904 | tf_op jit(solution)/shard_map/ppermute | solution.py:284
  27.4 1.7 %copy-start.8 = (s32[3]{0:T(128)S(1)}, s32[3]{0:T(128)}, u32[]{:S(2)}) copy-start(s32[3]{0:T(128)} %param.11) | copy-start | bytes 40
  38.1 20.9 %all-to-all-start = ((f32[4,5,128,128]{3,2,1,0:T(8,128)}), f32[4,5,128,128]{3,2,1,0:T(8,128)S(1)}, u32[]{:S(2)}, u32[]{:S(2)}) async-start(f32[4,5,128,128]{3,2,1,0:T(8,128)} %partial.1), calls=%async_computation | async-start | bytes 2621440 | tf_op jit(solution)/shard_map/all_to_all | solution.py:276
  42.2 2.7 %collective-permute-start.3 = (f32[136,128]{1,0:T(8,128)S(1)}, f32[136,128]{1,0:T(8,128)S(1)}, u32[]{:S(2)}, u32[]{:S(2)}) collective-permute-start(f32[136,128]{1,0:T(8,128)S(1)} %add.54), channel_id=1, source_target_pairs={{0,64},{8,72},{16,80},{24,88},{1,65},{9,73},{17,81},{25,89},{2,66}... | collective-permute-start | bytes 208904 | tf_op jit(solution)/shard_map/ppermute | solution.py:284
  44.8 2.7 %collective-permute-start.4 = (f32[136,128]{1,0:T(8,128)S(1)}, f32[136,128]{1,0:T(8,128)S(1)}, u32[]{:S(2)}, u32[]{:S(2)}) collective-permute-start(f32[136,128]{1,0:T(8,128)S(1)} %add.55), channel_id=1, source_target_pairs={{0,32},{8,40},{16,48},{24,56},{64,96},{72,104},{80,112},{88,120},{... | collective-permute-start | bytes 208904 | tf_op jit(solution)/shard_map/ppermute | solution.py:284
  59.2 3.3 %copy-start.5 = (f32[136,128]{1,0:T(8,128)}, f32[136,128]{1,0:T(8,128)S(1)}, u32[]{:S(2)}) copy-start(f32[136,128]{1,0:T(8,128)S(1)} %add.56.z_ref) | copy-start | bytes 208900
  59.2 6.8 %collective-permute-start.5 = (f32[128,128]{1,0:T(8,128)S(1)}, f32[128,128]{1,0:T(8,128)S(1)}, u32[]{:S(2)}, u32[]{:S(2)}) collective-permute-start(f32[128,128]{1,0:T(8,128)S(1)} %fusion), channel_id=1, source_target_pairs={{0,1},{1,0},{2,3},{3,2},{4,5},{5,4},{6,7},{7,6},{8,9},{9,8},{10,11... | collective-permute-start | bytes 196616 | tf_op jit(solution)/shard_map/ppermute | solution.py:272
  62.5 21.5 %all-to-all-start.1 = ((f32[4,5,128,128]{3,2,1,0:T(8,128)}), f32[4,5,128,128]{3,2,1,0:T(8,128)S(1)}, u32[]{:S(2)}, u32[]{:S(2)}) async-start(f32[4,5,128,128]{3,2,1,0:T(8,128)} %broadcast_in_dim.36), calls=%async_computation.1 | async-start | bytes 2621440 | tf_op jit(solution)/shard_map/all_to_all | solution.py:276
  76.2 3.3 %collective-permute-start.6 = (f32[128,128]{1,0:T(8,128)}, f32[128,128]{1,0:T(8,128)S(1)}, u32[]{:S(2)}, u32[]{:S(2)}) collective-permute-start(f32[128,128]{1,0:T(8,128)} %inverse.1.f_ref), channel_id=1, source_target_pairs={{0,64},{1,65},{2,66},{3,67},{4,68},{5,69},{6,70},{7,71}} | collective-permute-start | bytes 196616 | tf_op jit(solution)/shard_map/ppermute | solution.py:284
  79.5 8.4 %copy-start.7 = (f32[128,128]{1,0:T(8,128)}, f32[128,128]{1,0:T(8,128)S(1)}, u32[]{:S(2)}) copy-start(f32[128,128]{1,0:T(8,128)S(1)} %collective-permute-done.6.n_ref) | copy-start | bytes 196612
  84.1 3.9 %copy-start = (f32[4,5,128,128]{3,2,1,0:T(8,128)}, f32[4,5,128,128]{3,2,1,0:T(8,128)S(1)}, u32[]{:S(2)}) copy-start(f32[4,5,128,128]{3,2,1,0:T(8,128)S(1)} %all-to-all-done.1.v_ref.v0_ref) | copy-start | bytes 3932164
  84.1 3.5 %collective-permute-start.7 = (f32[4,5,128,128]{3,2,1,0:T(8,128)S(1)}, f32[4,5,128,128]{3,2,1,0:T(8,128)S(1)}, u32[]{:S(2)}, u32[]{:S(2)}) collective-permute-start(f32[4,5,128,128]{3,2,1,0:T(8,128)S(1)} %all-to-all-done.1.v_ref.v0_ref), channel_id=1, source_target_pairs={{0,1},{1,0},{2,3},{3,2},{4,5},{5,4},{6,7},{7,6},{8,9},{9,8},{10,11... | collective-permute-start | bytes 3932168 | tf_op jit(solution)/shard_map/ppermute | solution.py:272
  87.5 1.0 copy-start.3
  87.6 30.7 %collective-permute-start.8 = (f32[16,520,128]{2,1,0:T(8,128)}, f32[16,520,128]{2,1,0:T(8,128)}, u32[]{:S(2)}, u32[]{:S(2)}) collective-permute-start(f32[16,520,128]{2,1,0:T(8,128)} %bitcast.46), channel_id=1, source_target_pairs={{0,1},{1,0},{2,3},{3,2},{4,5},{5,4},{6,7},{7,6},{8,9},{9,8},{10,11... | collective-permute-start | bytes 12779528 | tf_op jit(solution)/shard_map/ppermute | solution.py:272
  94.8 23.5 %all-to-all-start.2 = ((f32[16,128,128]{2,1,0:T(8,128)}), f32[16,128,128]{2,1,0:T(8,128)S(1)}, u32[]{:S(2)}, u32[]{:S(2)}) async-start(f32[16,128,128]{2,1,0:T(8,128)} %lead.1), calls=%async_computation.2 | async-start | bytes 2097152 | tf_op jit(solution)/shard_map/all_to_all | solution.py:276
  118.3 1.0 copy-start.4
Sparse Core Ops, SparseCore 0:
  13.9 55.2 all-gather.2

commit v9 on v8

--- a/solution.py
+++ b/solution.py
@@ -292,16 +292,15 @@
     info = jnp.concatenate([jnp.stack([r, col, p, x]).astype(jnp.int32), block_sizes])
     sup = support.astype(F32)
 
-    def message(t, extra):
-        tile = lax.dynamic_index_in_dim(coefficients, t, 0, keepdims=False)
-        tile = lax.dynamic_slice_in_dim(tile, p * 128, 128, 2)
-        return jnp.concatenate([jnp.transpose(tile, (1, 2, 0)).reshape(512, 128),
-                                lax.dynamic_index_in_dim(sup, t, 0, keepdims=False).T, extra], axis=0)
-
-    gathered = lax.all_gather(message(x, jnp.zeros((4, 128), F32)), "rows")
-
     own = jnp.transpose(coefficients, (2, 0, 1, 3)).reshape(4, 512, 256)
     own_sup = jnp.transpose(sup, (2, 0, 1)).reshape(4, 512)
+    tile = lax.dynamic_slice(own, (0, x * 128, p * 128), (4, 128, 128))
+    message = jnp.concatenate([jnp.swapaxes(tile, 1, 2).reshape(512, 128), lax.dynamic_slice_in_dim(own_sup, x * 128, 128, 1),
+                               jnp.zeros((4, 128), F32)], axis=0)
+    gathered = lax.all_gather(message, "rows")
+    head = lax.dynamic_slice(own, (x, 0, p * 128), (1, 128, 128))[0]
+    head = jnp.concatenate([head.T, own_sup[:, :128], right_sides[0]], axis=0)
+    head = jnp.where(r == 0, head, 0.0)
     own_sup = jnp.broadcast_to(own_sup[:, :, None], (4, 512, 128))
     eye = jnp.eye(128, dtype=F32)
 
@@ -310,18 +309,10 @@
     lent = lax.dynamic_slice_in_dim(primal, away, 128, 2) * lax.dynamic_slice_in_dim(dual_inverse, away, 128, 2)
     lent = swap(lent * active[:, :, None] * lax.dynamic_slice_in_dim(active, away, 128, 1)[:, None, :])
 
-    head = lax.dynamic_slice_in_dim(lax.dynamic_index_in_dim(coefficients[0], x, 1, keepdims=False), p * 128, 128, 1)
-    head = jnp.concatenate([head.T, sup[0].T, right_sides[0]], axis=0)
-    head = jnp.where(r == 0, head, 0.0)
-    head_next = over_rows(head, [(0, 2)])
-    head_next, lent = lax.optimization_barrier((head_next, lent))
-    head = head + head_next
-    head_next = over_rows(head, [(0, 1), (2, 3)])
     half = partial(info, own, own_sup, primal, dual_inverse, lent)
-    head_next, half = lax.optimization_barrier((head_next, half))
-    head = head + head_next
-    head_next = over_rows(head, [(z, 8 + z) for z in range(4)])
-    head = head + head_next
+    head, half = lax.optimization_barrier((head, half))
+    for pairs in ([(0, 2)], [(0, 1), (2, 3)], [(z, 8 + z) for z in range(4)]):
+        head = head + over_rows(head, pairs)
     head_next = over_rows(head, [(y + z, y + 4 + z) for y in (0, 8) for z in range(4)])
     terms = exchange(half, "cols", CHIPS)
     head_next, terms = lax.optimization_barrier((head_next, terms))

time: 150 us -> 143 us (0.953)
  waiting for transfers between devices: 24.4 us -> 12.1 us
  starting transfers between devices: 28.2 us -> 39.8 us
  local copies, waits for them, and re-layouts: 11.5 us -> 8.04 us
  other arithmetic: 6.73 us -> 4.54 us
    all_to_all x3, waiting for transfers between devices: 16.1 us -> 2.4 us  [exchange(): return lax.all_to_all(v, axis, 0, 0, axis_index_groups=groups, tiled=True)]
    all_to_all x3, starting transfers between devices: 12.6 us -> 19.3 us  [exchange(): return lax.all_to_all(v, axis, 0, 0, axis_index_groups=groups, tiled=True)]
    ppermute x5, starting transfers between devices: 10.7 us -> 15 us  [over_rows(): return lax.ppermute(v, 'rows', pairs)]
    dynamic_slice x3, local copies, waits for them, and re-layouts: 2.15 us -> 0.1 us  [the longest x2 0.09 us: local(): head = lax.dynamic_slice(own, (x, 0, p * 128), (1, 128, 128))[0]]
    transpose x2, local copies, waits for them, and re-layouts: 1.94 us -> 0.16 us  [local(): jnp.swapaxes(tile, 1, 2).reshape(512, 128)]
  transfers between devices with their start and end apart: 13 -> 13, of which waited for: 7 -> 8; matrix products, arithmetic and copies ran while one was open for 7% -> 5% of each run, Pallas kernels for 28% -> 29%
where the time goes in v9:
time: 143 us; the launch traced here: 142 us
  Pallas kernels  63.7 us (45%)
  starting transfers between devices  39.8 us (28%)
  between operations  14.3 us (10%)
  waiting for transfers between devices  12.1 us (8%)
  local copies, waits for them, and re-layouts  8.04 us (6%)
  other arithmetic  4.54 us (3%)
    pallas_call x2, Pallas kernels, block_product(): pl.pallas_call(functools.partial(block_body, last), grid_spec=grid, out_s...  41.1 us
    all_to_all x3, starting transfers between devices, exchange(): return lax.all_to_all(v, axis, 0, 0, axis_index_groups=groups, tiled=True)  19.3 us
    ppermute x5, starting transfers between devices, over_rows(): return lax.ppermute(v, 'rows', pairs)  15 us
    pallas_call x1, Pallas kernels, inverse_of(): pl.pallas_call(inverse_body, out_shape=jax.ShapeDtypeStruct((128, 128), F...  9.52 us
    ppermute x5, waiting for transfers between devices, over_rows(): return lax.ppermute(v, 'rows', pairs)  6.97 us
    pallas_call x1, Pallas kernels, partial(): pl.pallas_call(partial_body, grid_spec=grid, out_shape=out, compiler_para...  6.89 us
    pallas_call x1, Pallas kernels, lead(): pl.pallas_call(lead_body, grid_spec=grid, out_shape=jax.ShapeDtypeStruct(...  6.19 us
    ppermute x4, starting transfers between devices, swap(): return lax.ppermute(v, 'cols', SWAP)  5.46 us
  transfers between devices with their start and end apart: 13, of which 8 were waited for; matrix products, arithmetic and copies ran while one was open for 5% of the time, Pallas kernels for 29%

profile of v9, /device:TPU:1, one launch (start us, length us, event | category | flops | bytes accessed | tf_op | source)
XLA Modules:
  0.0 142.4 jit_solution(7152051271188218527)
XLA Ops:
  7.2 0.0 all-gather.3.cloned.1.call-start
  7.2 0.7 convert_bitcast_fusion
  7.9 2.1 %copy.12 = f32[4,4,128,256]{3,2,1,0:T(8,128)S(1)} copy(f32[4,4,128,256]{3,0,2,1:T(4,128)} %bitcast.34) | data formatting | bytes 4194304 | tf_op jit(solution)/shard_map/transpose | solution.py:295
  10.0 0.0 copy-start
  10.1 0.1 copy.14
  10.2 0.1 pad.2.clone
  10.3 1.1 maximum_maximum_fusion
  11.4 0.0 all-gather.3.cloned.1.call-update
  11.5 0.1 fusion.1
  11.5 1.2 multiply_multiply_fusion
  12.7 1.5 %collective-permute-start = (f32[3,256,128]{2,1,0:T(8,128)S(1)}, f32[3,256,128]{2,1,0:T(8,128)S(1)}, u32[]{:S(2)}, u32[]{:S(2)}) collective-permute-start(f32[3,256,128]{2,1,0:T(8,128)S(1)} %multiply_multiply_fusion), channel_id=1, source_target_pairs={{0,1},{1,0},{2,3},{3,2},{4,5},{5,4},{6,7},{7,6},{8,9},{9,8},{10,11... | collective-permute-start | bytes 1179656 | tf_op jit(solution)/shard_map/ppermute | solution.py:272
  14.2 0.1 copy.13
  14.3 0.7 concatenate.12.info
  15.0 0.7 slice_bitcast_fusion.2
  15.7 0.0 collective-permute-done.z_ref
  15.7 1.4 broadcast_in_dim.17.s_ref.r_ref
  17.1 6.9 %partial.1 = f32[4,5,128,128]{3,2,1,0:T(8,128)} custom-call(s32[7]{0:T(128)} %concatenate.12.info, f32[4,512,256]{2,1,0:T(8,128)} %bitcast.33, f32[4,512,128]{2,1,0:T(8,128)} %broadcast_in_dim.17.s_ref.r_ref, f32[3,256,256]{2,1,0:T(8,128)} %x_ref.1, f32[3,256,256]{2,1,0:T(8,128)} %y_ref.1, f32[3,256,128]{2,1,0:T(8,128)} %copy-done.6), custom_call_target="tpu_custom_call" | custom-call | flops 603979776 | bytes 8388608 | tf_op jit(solution)/shard_map/partial/pallas_call | solution.py:87
  24.0 4.1 %all-to-all-start = ((f32[4,5,128,128]{3,2,1,0:T(8,128)}), f32[4,5,128,128]{3,2,1,0:T(8,128)S(1)}, u32[]{:S(2)}, u32[]{:S(2)}) async-start(f32[4,5,128,128]{3,2,1,0:T(8,128)} %partial.1), calls=%async_computation | async-start | bytes 2621440 | tf_op jit(solution)/shard_map/all_to_all | solution.py:276
  28.1 5.5 %collective-permute-start.1 = (f32[136,128]{1,0:T(8,128)S(1)}, f32[136,128]{1,0:T(8,128)S(1)}, u32[]{:S(2)}, u32[]{:S(2)}) collective-permute-start(f32[136,128]{1,0:T(8,128)S(1)} %maximum_select_fusion), channel_id=1, source_target_pairs={{0,16},{1,17},{2,18},{3,19},{4,20},{5,21},{6,22},{7,23}} | collective-permute-start | bytes 208904 | tf_op jit(solution)/shard_map/ppermute | solution.py:284
  33.6 1.6 %collective-permute-done.1 = f32[136,128]{1,0:T(8,128)S(1)} collective-permute-done((f32[136,128]{1,0:T(8,128)S(1)}, f32[136,128]{1,0:T(8,128)S(1)}, u32[]{:S(2)}, u32[]{:S(2)}) %collective-permute-start.1) | collective-permute-done | bytes 69664 | tf_op jit(solution)/shard_map/ppermute | solution.py:284
  35.2 1.3 collective-permute-start.2
  36.5 1.3 collective-permute-done.2
  37.8 1.3 collective-permute-start.3
  39.2 1.3 collective-permute-done.3
  40.5 1.3 collective-permute-start.4
  41.8 0.7 fusion.2
  42.5 1.1 collective-permute-done.4
  43.6 2.1 %all-to-all-done = f32[4,5,128,128]{3,2,1,0:T(8,128)S(1)} async-done(((f32[4,5,128,128]{3,2,1,0:T(8,128)}), f32[4,5,128,128]{3,2,1,0:T(8,128)S(1)}, u32[]{:S(2)}, u32[]{:S(2)}) %all-to-all-start) | async-done | bytes 1310752 | tf_op jit(solution)/shard_map/all_to_all | solution.py:276
  45.6 0.1 reduce_sum.9
  45.8 2.5 %collective-permute-start.5 = (f32[128,128]{1,0:T(8,128)S(1)}, f32[128,128]{1,0:T(8,128)S(1)}, u32[]{:S(2)}, u32[]{:S(2)}) collective-permute-start(f32[128,128]{1,0:T(8,128)S(1)} %fusion), channel_id=1, source_target_pairs={{0,1},{1,0},{2,3},{3,2},{4,5},{5,4},{6,7},{7,6},{8,9},{9,8},{10,11... | collective-permute-start | bytes 196616 | tf_op jit(solution)/shard_map/ppermute | solution.py:272
  48.3 1.2 broadcast_in_dim.33
  49.5 4.9 %all-to-all-start.1 = ((f32[4,5,128,128]{3,2,1,0:T(8,128)}), f32[4,5,128,128]{3,2,1,0:T(8,128)S(1)}, u32[]{:S(2)}, u32[]{:S(2)}) async-start(f32[4,5,128,128]{3,2,1,0:T(8,128)} %broadcast_in_dim.33), calls=%async_computation.1 | async-start | bytes 2621440 | tf_op jit(solution)/shard_map/all_to_all | solution.py:276
  54.3 0.0 collective-permute-done.5
  54.3 0.6 fusion.3.c_ref
  55.0 9.5 %inverse.1.f_ref = f32[128,128]{1,0:T(8,128)} custom-call(f32[128,128]{1,0:T(8,128)} %fusion.3.c_ref), custom_call_target="tpu_custom_call" | custom-call | flops 7247757312 | bytes 1048576 | tf_op jit(solution)/shard_map/inverse/pallas_call | solution.py:262
  64.5 5.6 %collective-permute-start.6 = (f32[128,128]{1,0:T(8,128)}, f32[128,128]{1,0:T(8,128)S(1)}, u32[]{:S(2)}, u32[]{:S(2)}) collective-permute-start(f32[128,128]{1,0:T(8,128)} %inverse.1.f_ref), channel_id=1, source_target_pairs={{0,64},{1,65},{2,66},{3,67},{4,68},{5,69},{6,70},{7,71}} | collective-permute-start | bytes 196616 | tf_op jit(solution)/shard_map/ppermute | solution.py:284
  70.1 1.6 %collective-permute-done.6.n_ref = f32[128,128]{1,0:T(8,128)S(1)} collective-permute-done((f32[128,128]{1,0:T(8,128)}, f32[128,128]{1,0:T(8,128)S(1)}, u32[]{:S(2)}, u32[]{:S(2)}) %collective-permute-start.6) | collective-permute-done | bytes 65568 | tf_op jit(solution)/shard_map/ppermute | solution.py:284
  71.7 0.3 all-to-all-done.1.v_ref.v0_ref
  72.1 1.1 collective-permute-start.7
  73.2 2.7 %collective-permute-done.7.v1_ref.v_ref = f32[4,5,128,128]{3,2,1,0:T(8,128)S(1)} collective-permute-done((f32[4,5,128,128]{3,2,1,0:T(8,128)S(1)}, f32[4,5,128,128]{3,2,1,0:T(8,128)S(1)}, u32[]{:S(2)}, u32[]{:S(2)}) %collective-permute-start.7) | collective-permute-done | bytes 1310752 | tf_op jit(solution)/shard_map/ppermute | solution.py:272
  75.9 0.4 collective-permute-start.8
  76.3 0.7 copy-done.3
  76.9 6.2 %lead.1 = f32[16,128,128]{2,1,0:T(8,128)} custom-call(s32[7]{0:T(128)} %concatenate.12.info, f32[4,5,128,128]{3,2,1,0:T(8,128)} %copy-done.1, f32[4,5,128,128]{3,2,1,0:T(8,128)} %copy-done.3, f32[4,512,128]{2,1,0:T(8,128)} %broadcast_in_dim.17.s_ref.r_ref, f32[136,128]{1,0:T(8,128)} %copy-done.5, f32[128,128]{1,0:T(8,128)} %inverse.1.f_ref, f32[128,128]{1,0:T(8,128)} %copy-done.7), custom_call_target="tpu_custom_call" | custom-call | flops 603979776 | bytes 6291456 | tf_op jit(solution)/shard_map/lead/pallas_call | solution.py:139
  83.1 10.3 %all-to-all-start.2 = ((f32[16,128,128]{2,1,0:T(8,128)}), f32[16,128,128]{2,1,0:T(8,128)S(1)}, u32[]{:S(2)}, u32[]{:S(2)}) async-start(f32[16,128,128]{2,1,0:T(8,128)} %lead.1), calls=%async_computation.2 | async-start | bytes 2097152 | tf_op jit(solution)/shard_map/all_to_all | solution.py:276
  93.5 18.4 %block.2 = (f32[512,1024]{1,0:T(8,128)}, f32[512,128]{1,0:T(8,128)}) custom-call(s32[7]{0:T(128)} %concatenate.12.info, f32[4,5,128,128]{3,2,1,0:T(8,128)} %copy-done.1, f32[4,512,128]{2,1,0:T(8,128)} %broadcast_in_dim.17.s_ref.r_ref, f32[16,520,128]{2,1,0:T(8,128)} %bitcast.38, f32[136,128]{1,0:T(8,128)} %copy-done.5), custom_call_target="tpu_custom_call" | custom-call | flops 10871635968 | bytes 10485760 | tf_op jit(solution)/shard_map/block/pallas_call | solution.py:221
  111.8 0.0 all-to-all-done.2.rest_2_
  111.8 1.0 copy-done.4
  112.8 22.7 %block.3 = (f32[512,1024]{1,0:T(8,128)}, f32[512,128]{1,0:T(8,128)}, f32[4,4,128]{2,1,0:T(4,128)}) custom-call(s32[7]{0:T(128)} %concatenate.12.info, f32[4,5,128,128]{3,2,1,0:T(8,128)} %copy-done.3, f32[4,512,128]{2,1,0:T(8,128)} %broadcast_in_dim.17.s_ref.r_ref, f32[16,520,128]{2,1,0:T(8,128)} %collective-permute-done.8.c_ref, f32[136,128]{1,0:T(8,128)} %copy-done.5, ...), custom_call_target="tpu_custom_call" | custom-call | flops 10871635968 | bytes 10485760 | tf_op jit(solution)/shard_map/block/pallas_call | solution.py:221
  (31 shorter events, 0.2 us)
Async XLA Ops:
  7.2 64.9 %all-gather.3.cloned.1.call-start = ((), (), s32[]{:S(2)}) async-start(), calls=%async_computation.3 | async-start | bytes 4526080 | tf_op jit(solution)/shard_map/all_gather | solution.py:300
  7.9 3.5 %copy-start.8 = (s32[3]{0:T(128)S(1)}, s32[3]{0:T(128)}, u32[]{:S(2)}) copy-start(s32[3]{0:T(128)} %param.11) | copy-start | bytes 40
  7.9 3.6 %copy-start.2 = (f32[3,256,256]{2,1,0:T(8,128)S(1)}, f32[3,256,256]{2,1,0:T(8,128)}, u32[]{:S(2)}) copy-start(f32[3,256,256]{2,1,0:T(8,128)} %x_ref.1) | copy-start | bytes 2359300
  10.0 7.1 %copy-start = (f32[4,4,128,256]{3,2,1,0:T(8,128)}, f32[4,4,128,256]{3,2,1,0:T(8,128)S(1)}, u32[]{:S(2)}) copy-start(f32[4,4,128,256]{3,2,1,0:T(8,128)S(1)} %copy.12) | copy-start | bytes 6291460
  12.7 3.0 %collective-permute-start = (f32[3,256,128]{2,1,0:T(8,128)S(1)}, f32[3,256,128]{2,1,0:T(8,128)S(1)}, u32[]{:S(2)}, u32[]{:S(2)}) collective-permute-start(f32[3,256,128]{2,1,0:T(8,128)S(1)} %multiply_multiply_fusion), channel_id=1, source_target_pairs={{0,1},{1,0},{2,3},{3,2},{4,5},{5,4},{6,7},{7,6},{8,9},{9,8},{10,11... | collective-permute-start | bytes 1179656 | tf_op jit(solution)/shard_map/ppermute | solution.py:272
  15.7 1.4 copy-start.6
  24.0 21.6 %all-to-all-start = ((f32[4,5,128,128]{3,2,1,0:T(8,128)}), f32[4,5,128,128]{3,2,1,0:T(8,128)S(1)}, u32[]{:S(2)}, u32[]{:S(2)}) async-start(f32[4,5,128,128]{3,2,1,0:T(8,128)} %partial.1), calls=%async_computation | async-start | bytes 2621440 | tf_op jit(solution)/shard_map/all_to_all | solution.py:276
  28.1 7.1 %collective-permute-start.1 = (f32[136,128]{1,0:T(8,128)S(1)}, f32[136,128]{1,0:T(8,128)S(1)}, u32[]{:S(2)}, u32[]{:S(2)}) collective-permute-start(f32[136,128]{1,0:T(8,128)S(1)} %maximum_select_fusion), channel_id=1, source_target_pairs={{0,16},{1,17},{2,18},{3,19},{4,20},{5,21},{6,22},{7,23}} | collective-permute-start | bytes 208904 | tf_op jit(solution)/shard_map/ppermute | solution.py:284
  35.2 2.7 %collective-permute-start.2 = (f32[136,128]{1,0:T(8,128)S(1)}, f32[136,128]{1,0:T(8,128)S(1)}, u32[]{:S(2)}, u32[]{:S(2)}) collective-permute-start(f32[136,128]{1,0:T(8,128)S(1)} %add.44), channel_id=1, source_target_pairs={{0,8},{16,24},{1,9},{17,25},{2,10},{18,26},{3,11},{19,27},{4,12},{... | collective-permute-start | bytes 208904 | tf_op jit(solution)/shard_map/ppermute | solution.py:284
  37.8 2.7 %collective-permute-start.3 = (f32[136,128]{1,0:T(8,128)S(1)}, f32[136,128]{1,0:T(8,128)S(1)}, u32[]{:S(2)}, u32[]{:S(2)}) collective-permute-start(f32[136,128]{1,0:T(8,128)S(1)} %add.45), channel_id=1, source_target_pairs={{0,64},{8,72},{16,80},{24,88},{1,65},{9,73},{17,81},{25,89},{2,66}... | collective-permute-start | bytes 208904 | tf_op jit(solution)/shard_map/ppermute | solution.py:284
  40.5 3.1 %collective-permute-start.4 = (f32[136,128]{1,0:T(8,128)S(1)}, f32[136,128]{1,0:T(8,128)S(1)}, u32[]{:S(2)}, u32[]{:S(2)}) collective-permute-start(f32[136,128]{1,0:T(8,128)S(1)} %add.46), channel_id=1, source_target_pairs={{0,32},{8,40},{16,48},{24,56},{64,96},{72,104},{80,112},{88,120},{... | collective-permute-start | bytes 208904 | tf_op jit(solution)/shard_map/ppermute | solution.py:284
  45.7 3.7 %copy-start.5 = (f32[136,128]{1,0:T(8,128)}, f32[136,128]{1,0:T(8,128)S(1)}, u32[]{:S(2)}) copy-start(f32[136,128]{1,0:T(8,128)S(1)} %add.47.z_ref) | copy-start | bytes 208900
  45.8 8.6 %collective-permute-start.5 = (f32[128,128]{1,0:T(8,128)S(1)}, f32[128,128]{1,0:T(8,128)S(1)}, u32[]{:S(2)}, u32[]{:S(2)}) collective-permute-start(f32[128,128]{1,0:T(8,128)S(1)} %fusion), channel_id=1, source_target_pairs={{0,1},{1,0},{2,3},{3,2},{4,5},{5,4},{6,7},{7,6},{8,9},{9,8},{10,11... | collective-permute-start | bytes 196616 | tf_op jit(solution)/shard_map/ppermute | solution.py:272
  49.5 22.6 %all-to-all-start.1 = ((f32[4,5,128,128]{3,2,1,0:T(8,128)}), f32[4,5,128,128]{3,2,1,0:T(8,128)S(1)}, u32[]{:S(2)}, u32[]{:S(2)}) async-start(f32[4,5,128,128]{3,2,1,0:T(8,128)} %broadcast_in_dim.33), calls=%async_computation.1 | async-start | bytes 2621440 | tf_op jit(solution)/shard_map/all_to_all | solution.py:276
  64.5 7.2 %collective-permute-start.6 = (f32[128,128]{1,0:T(8,128)}, f32[128,128]{1,0:T(8,128)S(1)}, u32[]{:S(2)}, u32[]{:S(2)}) collective-permute-start(f32[128,128]{1,0:T(8,128)} %inverse.1.f_ref), channel_id=1, source_target_pairs={{0,64},{1,65},{2,66},{3,67},{4,68},{5,69},{6,70},{7,71}} | collective-permute-start | bytes 196616 | tf_op jit(solution)/shard_map/ppermute | solution.py:284
  71.7 4.5 %copy-start.7 = (f32[128,128]{1,0:T(8,128)}, f32[128,128]{1,0:T(8,128)S(1)}, u32[]{:S(2)}) copy-start(f32[128,128]{1,0:T(8,128)S(1)} %collective-permute-done.6.n_ref) | copy-start | bytes 196612
  72.1 4.2 %copy-start.1 = (f32[4,5,128,128]{3,2,1,0:T(8,128)}, f32[4,5,128,128]{3,2,1,0:T(8,128)S(1)}, u32[]{:S(2)}) copy-start(f32[4,5,128,128]{3,2,1,0:T(8,128)S(1)} %all-to-all-done.1.v_ref.v0_ref) | copy-start | bytes 3932164
  72.1 3.8 %collective-permute-start.7 = (f32[4,5,128,128]{3,2,1,0:T(8,128)S(1)}, f32[4,5,128,128]{3,2,1,0:T(8,128)S(1)}, u32[]{:S(2)}, u32[]{:S(2)}) collective-permute-start(f32[4,5,128,128]{3,2,1,0:T(8,128)S(1)} %all-to-all-done.1.v_ref.v0_ref), channel_id=1, source_target_pairs={{0,1},{1,0},{2,3},{3,2},{4,5},{5,4},{6,7},{7,6},{8,9},{9,8},{10,11... | collective-permute-start | bytes 3932168 | tf_op jit(solution)/shard_map/ppermute | solution.py:272
  75.9 1.0 copy-start.3
  75.9 36.0 %collective-permute-start.8 = (f32[16,520,128]{2,1,0:T(8,128)}, f32[16,520,128]{2,1,0:T(8,128)}, u32[]{:S(2)}, u32[]{:S(2)}) collective-permute-start(f32[16,520,128]{2,1,0:T(8,128)} %bitcast.37), channel_id=1, source_target_pairs={{0,1},{1,0},{2,3},{3,2},{4,5},{5,4},{6,7},{7,6},{8,9},{9,8},{10,11... | collective-permute-start | bytes 12779528 | tf_op jit(solution)/shard_map/ppermute | solution.py:272
  83.1 28.7 %all-to-all-start.2 = ((f32[16,128,128]{2,1,0:T(8,128)}), f32[16,128,128]{2,1,0:T(8,128)S(1)}, u32[]{:S(2)}, u32[]{:S(2)}) async-start(f32[16,128,128]{2,1,0:T(8,128)} %lead.1), calls=%async_computation.2 | async-start | bytes 2097152 | tf_op jit(solution)/shard_map/all_to_all | solution.py:276
  111.8 1.0 copy-start.4
Sparse Core Ops, SparseCore 0:
  11.6 55.2 all-gather.2

commit v10 on v9

--- a/solution.py
+++ b/solution.py
@@ -47,7 +47,7 @@
             wh[u], wl[u] = split(w)
             wh[3 + u], wl[3 + u] = split(z_ref[u])
 
-    parts = [jnp.zeros((128, 128), F32)] * 4
+    parts = [jnp.zeros((256, 128), F32)] * 4
     masks = []
     for u in range(6):
         block = ((col if u < 3 else col + 1 - 2 * p) * 3 + u % 3).astype(F32)
@@ -58,19 +58,22 @@
         v = product(dh, dl, wh[u], wl[u], NN)
         parts = [jnp.where(m[k], v, parts[k]) for k in range(4)]
     for k in range(4):
-        v_ref[0, k] = parts[k]
+        for h in range(2):
+            v_ref[h, k] = parts[k][h * 128:(h + 1) * 128]
 
     @pl.when(t == 0)
     def _():
         vs, es = [], []
         for m in masks:
-            vs.append(choose(m, parts))
-            es.append(choose(m, [c_ref[k, :, mine] for k in range(4)]))
+            top = [z[:128] for z in m]
+            vs.append(choose(top, [z[:128] for z in parts]))
+            es.append(choose(top, [c_ref[k, :128, mine] for k in range(4)]))
         vh, vl = split(jnp.concatenate(vs, axis=1))
         eh, el = split(jnp.concatenate(es, axis=1))
         total[...] = product(vh, vl, eh, el, NT)
 
-    v_ref[0, 4] = total[...]
+    for h in range(2):
+        v_ref[h, 4] = total[...]
 
 
 def whole(v):
@@ -80,18 +83,18 @@
 def partial(info, c, s, x, y, z):
     out = jax.ShapeDtypeStruct((4, 5, 128, 128), F32)
     grid = pltpu.PrefetchScalarGridSpec(
-        num_scalar_prefetch=1, grid=(4,),
-        in_specs=[pl.BlockSpec((4, 128, 256), lambda t, i: (0, t, 0)), pl.BlockSpec((4, 128, 128), lambda t, i: (0, t, 0)), whole(x), whole(y), whole(z)],
-        out_specs=pl.BlockSpec((1, 5, 128, 128), lambda t, i: (t, 0, 0, 0)),
+        num_scalar_prefetch=1, grid=(2,),
+        in_specs=[pl.BlockSpec((4, 256, 256), lambda t, i: (0, t, 0)), pl.BlockSpec((4, 256, 128), lambda t, i: (0, t, 0)), whole(x), whole(y), whole(z)],
+        out_specs=pl.BlockSpec((2, 5, 128, 128), lambda t, i: (t, 0, 0, 0)),
         scratch_shapes=[pltpu.VMEM((6, 256, 128), BF)] * 2 + [pltpu.VMEM((128, 128), F32)])
     return pl.pallas_call(partial_body, grid_spec=grid, out_shape=out,
                           compiler_params=pltpu.CompilerParams(vmem_limit_bytes=VMEM), name="partial",
                           cost_estimate=pl.CostEstimate(flops=2 * 3 * 512 * 768 * 256, bytes_accessed=8 << 20, transcendentals=0))(info, c, s, x, y, z)
 
 
-def gather_blocks(base, sup, high, low, axis):
+def gather_blocks(base, sup, high, low, axis, count=6):
     highs, lows = [], []
-    for u in range(6):
+    for u in range(count):
         block = (base + u).astype(F32).astype(BF)
         m = [s == block for s in sup]
         highs.append(choose(m, [high(k) for k in range(4)]))
@@ -103,42 +106,46 @@
     return jnp.broadcast_to(jnp.concatenate(rows, axis=1), (128, n)).astype(BF)
 
 
-def lead_body(info, v0_ref, v1_ref, s_ref, z_ref, f_ref, n_ref, o_ref, vh, vl, dh, dl, a_ref):
+def lead_body(last, info, v_ref, s_ref, z_ref, *rest):
+    if last:
+        b_ref, f_ref, n_ref, o_ref, a_ref = rest
+    else:
+        (a_ref,) = rest
     g = pl.program_id(0)
 
     @pl.when(g == 0)
     def _():
-        for j, v_ref in enumerate((v0_ref, v1_ref)):
-            for k in range(4):
-                vh[j, k], vl[j, k] = split(v_ref[info[3], k])
-                dh[j, k], dl[j, k] = split(v_ref[k, 4])
-        a_ref[...] = jnp.zeros_like(a_ref)
-
+        a_ref[...] = b_ref[...] if last else jnp.zeros_like(a_ref)
+
+    rows = [split(v_ref[info[3], k]) for k in range(4)]
+    tiles = [split(v_ref[k, 4]) for k in range(4)]
     sup = [s_ref[k].astype(BF) for k in range(4)]
     first = [column_labels([z_ref[128 + k:129 + k]], 128) for k in range(4)]
-    for j in range(2):
-        ah, al = gather_blocks(6 * g, sup, lambda k: vh[j, k], lambda k: vl[j, k], 1)
-        bh, bl = gather_blocks(6 * g, first, lambda k: dh[j, k], lambda k: dl[j, k], 0)
-        a_ref[...] += product(ah, al, bh, bl, NN)
-
-    @pl.when(g == 3)
-    def _():
-        r, p = info[0], info[2]
-        sent = jnp.where((r == 0) & (p == 1), f_ref[...], jnp.where((r == 8) & (p == 0), n_ref[...], a_ref[...]))
-        for j in range(16):
-            o_ref[j] = sent
-
-
-def lead(info, v0, v1, s, z, f, n):
-    args = [v0, v1, s, z, f, n]
-    specs = [whole(v) for v in args]
-    specs[2] = pl.BlockSpec((4, 128, 128), lambda g, i: (0, i[3], 0))
+    ah, al = gather_blocks(12 * g, sup, lambda k: rows[k][0], lambda k: rows[k][1], 1, 12)
+    bh, bl = gather_blocks(12 * g, first, lambda k: tiles[k][0], lambda k: tiles[k][1], 0, 12)
+    a_ref[...] += product(ah, al, bh, bl, NN)
+
+    if last:
+        @pl.when(g == 1)
+        def _():
+            r, p = info[0], info[2]
+            sent = jnp.where((r == 0) & (p == 1), f_ref[...], jnp.where((r == 8) & (p == 0), n_ref[...], a_ref[...]))
+            for j in range(16):
+                o_ref[j] = sent
+
+
+def lead(info, v, s, z, more=None):
+    last = more is not None
+    args = [v, s, z] + (list(more) if last else [])
+    specs = [whole(u) for u in args]
+    specs[1] = pl.BlockSpec((4, 128, 128), lambda g, i: (0, i[3], 0))
+    shape = (16, 128, 128) if last else (128, 128)
     grid = pltpu.PrefetchScalarGridSpec(
-        num_scalar_prefetch=1, grid=(4,), in_specs=specs, out_specs=pl.BlockSpec((16, 128, 128), lambda g, i: (0, 0, 0)),
-        scratch_shapes=[pltpu.VMEM((2, 4, 128, 128), BF)] * 4 + [pltpu.VMEM((128, 128), F32)])
-    return pl.pallas_call(lead_body, grid_spec=grid, out_shape=jax.ShapeDtypeStruct((16, 128, 128), F32),
+        num_scalar_prefetch=1, grid=(2,), in_specs=specs, out_specs=pl.BlockSpec(shape, lambda g, i: (0,) * len(shape)),
+        scratch_shapes=[pltpu.VMEM((128, 128), F32)] if last else [])
+    return pl.pallas_call(functools.partial(lead_body, last), grid_spec=grid, out_shape=jax.ShapeDtypeStruct(shape, F32),
                           compiler_params=pltpu.CompilerParams(vmem_limit_bytes=VMEM), name="lead",
-                          cost_estimate=pl.CostEstimate(flops=2 * 3 * 128 * 6144 * 128, bytes_accessed=6 << 20, transcendentals=0))(info, *args)
+                          cost_estimate=pl.CostEstimate(flops=2 * 3 * 128 * 6144 * 128, bytes_accessed=3 << 20, transcendentals=0))(info, *args)
 
 
 def block_body(last, info, v_ref, r_ref, c_ref, z_ref, *rest):
@@ -193,17 +200,17 @@
                 tile = slice(t * 128, (t + 1) * 128)
                 taken = product(xh, xl, ph[tile], plo[tile], NT)
                 x_ref[t] = jnp.where(t * 16 + row > 0, y_ref[t] - taken[4:], sides[4:])
-            for j in range(8):
-                span = slice(j * 128, (j + 1) * 128)
-                eh, el = split(e_ref[8 * p + j])
-                qh, ql = split(product(eh, el, ih, il, NT))
-                outer = product(ph, plo, qh, ql, NT)
-                across = col * 8 + j
-                for t in range(4):
-                    tile = slice(t * 128, (t + 1) * 128)
-                    down = t * 16 + row
+            eh, el = split(e_ref[pl.ds(8 * p, 8)].reshape(1024, 128))
+            qh, ql = split(product(eh, el, ih, il, NT))
+            for t in range(4):
+                tile = slice(t * 128, (t + 1) * 128)
+                down = t * 16 + row
+                outer = product(ph[tile], plo[tile], qh, ql, NT)
+                for j in range(8):
+                    span = slice(j * 128, (j + 1) * 128)
+                    across = col * 8 + j
                     diagonal = jnp.where(same & (down == across), jnp.broadcast_to(h_ref[t:t + 1], (128, 128)), 0.0)
-                    o_ref[tile, span] += diagonal - jnp.where((down > 0) & (across > 0), outer[tile], 0.0)
+                    o_ref[tile, span] += diagonal - jnp.where((down > 0) & (across > 0), outer[:, span], 0.0)
 
 
 def block_product(info, v, r, c, pick, z, tail=None):
@@ -324,9 +331,10 @@
     second = over_rows(inverse, [(0, 8)])
     v_own, inverse, second, gathered = lax.optimization_barrier((v_own, inverse, second, gathered))
     v_other = swap(v_own)
-    gathered, v_other = lax.optimization_barrier((gathered, v_other))
+    begun = lead(info, v_own, own_sup, head)
+    gathered, v_other, begun = lax.optimization_barrier((gathered, v_other, begun))
     swapped = swap(gathered)
-    every = exchange(lead(info, v_own, v_other, own_sup, head, inverse, second), "rows")
+    every = exchange(lead(info, v_other, own_sup, head, [begun, inverse, second]), "rows")
 
     start = block_product(info, v_own, own_sup, gathered, lambda g, i: (i[2], 0, 0), head)
     updated, panel, solved = block_product(info, v_other, own_sup, swapped, lambda g, i: (i[2], 0, 0), head,

time: 143 us -> 141 us (0.986)
  waiting for transfers between devices: 12.1 us -> 9.07 us
    ppermute x4, waiting for transfers between devices: 2.67 us -> 0.01 us  [swap(): return lax.ppermute(v, 'cols', SWAP)]
    pallas_call x1 -> x2, Pallas kernels: 6.19 us -> 8.41 us  [lead(): pl.pallas_call(functools.partial(lead_body, last), grid_spec=grid, out_sh...]
  transfers between devices with their start and end apart: 13 -> 13, of which waited for: 8 -> 6; matrix products, arithmetic and copies ran while one was open for 5% -> 5% of each run, Pallas kernels for 29% -> 30%
where the time goes in v10:
time: 141 us; the launch traced here: 140 us
  Pallas kernels  64.5 us (46%)
  starting transfers between devices  40.7 us (29%)
  between operations  14.3 us (10%)
  waiting for transfers between devices  9.07 us (6%)
  local copies, waits for them, and re-layouts  7.45 us (5%)
  other arithmetic  4.53 us (3%)
    pallas_call x2, Pallas kernels, block_product(): pl.pallas_call(functools.partial(block_body, last), grid_spec=grid, out_s...  40.1 us
    all_to_all x3, starting transfers between devices, exchange(): return lax.all_to_all(v, axis, 0, 0, axis_index_groups=groups, tiled=True)  19.4 us
    ppermute x5, starting transfers between devices, over_rows(): return lax.ppermute(v, 'rows', pairs)  16.1 us
    pallas_call x1, Pallas kernels, inverse_of(): pl.pallas_call(inverse_body, out_shape=jax.ShapeDtypeStruct((128, 128), F...  9.52 us
    pallas_call x2, Pallas kernels, lead(): pl.pallas_call(functools.partial(lead_body, last), grid_spec=grid, out_sh...  8.41 us
    ppermute x5, waiting for transfers between devices, over_rows(): return lax.ppermute(v, 'rows', pairs)  6.98 us
    pallas_call x1, Pallas kernels, partial(): pl.pallas_call(partial_body, grid_spec=grid, out_shape=out, compiler_para...  6.42 us
    ppermute x4, starting transfers between devices, swap(): return lax.ppermute(v, 'cols', SWAP)  5.12 us
  transfers between devices with their start and end apart: 13, of which 6 were waited for; matrix products, arithmetic and copies ran while one was open for 5% of the time, Pallas kernels for 30%

profile of v10, /device:TPU:1, one launch (start us, length us, event | category | flops | bytes accessed | tf_op | source)
XLA Modules:
  0.0 140.5 jit_solution(14368699065634571629)
XLA Ops:
  7.2 0.0 all-gather.3.cloned.1.call-start
  7.2 0.7 convert_bitcast_fusion
  7.9 2.1 %copy.12 = f32[4,4,128,256]{3,2,1,0:T(8,128)S(1)} copy(f32[4,4,128,256]{3,0,2,1:T(4,128)} %bitcast.34) | data formatting | bytes 4194304 | tf_op jit(solution)/shard_map/transpose | solution.py:302
  10.0 0.0 copy-start
  10.1 0.1 copy.14
  10.2 0.1 pad.2.clone
  10.3 1.1 maximum_maximum_fusion
  11.4 0.0 all-gather.3.cloned.1.call-update
  11.5 0.1 fusion.1
  11.5 1.2 multiply_multiply_fusion
  12.7 1.5 %collective-permute-start = (f32[3,256,128]{2,1,0:T(8,128)S(1)}, f32[3,256,128]{2,1,0:T(8,128)S(1)}, u32[]{:S(2)}, u32[]{:S(2)}) collective-permute-start(f32[3,256,128]{2,1,0:T(8,128)S(1)} %multiply_multiply_fusion), channel_id=1, source_target_pairs={{0,1},{1,0},{2,3},{3,2},{4,5},{5,4},{6,7},{7,6},{8,9},{9,8},{10,11... | collective-permute-start | bytes 1179656 | tf_op jit(solution)/shard_map/ppermute | solution.py:279
  14.2 0.1 copy.13
  14.3 0.7 concatenate.12.info
  15.0 0.7 slice_bitcast_fusion.2
  15.7 0.0 collective-permute-done.z_ref
  15.7 1.4 broadcast_in_dim.17.s_ref.r_ref
  17.1 6.4 %partial.1 = f32[4,5,128,128]{3,2,1,0:T(8,128)} custom-call(s32[7]{0:T(128)} %concatenate.12.info, f32[4,512,256]{2,1,0:T(8,128)} %bitcast.33, f32[4,512,128]{2,1,0:T(8,128)} %broadcast_in_dim.17.s_ref.r_ref, f32[3,256,256]{2,1,0:T(8,128)} %x_ref.1, f32[3,256,256]{2,1,0:T(8,128)} %y_ref.1, f32[3,256,128]{2,1,0:T(8,128)} %copy-done.6), custom_call_target="tpu_custom_call" | custom-call | flops 603979776 | bytes 8388608 | tf_op jit(solution)/shard_map/partial/pallas_call | solution.py:90
  23.5 4.1 %all-to-all-start = ((f32[4,5,128,128]{3,2,1,0:T(8,128)}), f32[4,5,128,128]{3,2,1,0:T(8,128)S(1)}, u32[]{:S(2)}, u32[]{:S(2)}) async-start(f32[4,5,128,128]{3,2,1,0:T(8,128)} %partial.1), calls=%async_computation | async-start | bytes 2621440 | tf_op jit(solution)/shard_map/all_to_all | solution.py:283
  27.6 5.5 %collective-permute-start.1 = (f32[136,128]{1,0:T(8,128)S(1)}, f32[136,128]{1,0:T(8,128)S(1)}, u32[]{:S(2)}, u32[]{:S(2)}) collective-permute-start(f32[136,128]{1,0:T(8,128)S(1)} %maximum_select_fusion), channel_id=1, source_target_pairs={{0,16},{1,17},{2,18},{3,19},{4,20},{5,21},{6,22},{7,23}} | collective-permute-start | bytes 208904 | tf_op jit(solution)/shard_map/ppermute | solution.py:291
  33.1 1.8 %collective-permute-done.1 = f32[136,128]{1,0:T(8,128)S(1)} collective-permute-done((f32[136,128]{1,0:T(8,128)S(1)}, f32[136,128]{1,0:T(8,128)S(1)}, u32[]{:S(2)}, u32[]{:S(2)}) %collective-permute-start.1) | collective-permute-done | bytes 69664 | tf_op jit(solution)/shard_map/ppermute | solution.py:291
  35.0 1.3 collective-permute-start.2
  36.3 1.5 %collective-permute-done.2 = f32[136,128]{1,0:T(8,128)S(1)} collective-permute-done((f32[136,128]{1,0:T(8,128)S(1)}, f32[136,128]{1,0:T(8,128)S(1)}, u32[]{:S(2)}, u32[]{:S(2)}) %collective-permute-start.2) | collective-permute-done | bytes 69664 | tf_op jit(solution)/shard_map/ppermute | solution.py:291
  37.8 1.3 collective-permute-start.3
  39.1 1.3 collective-permute-done.3
  40.4 1.3 collective-permute-start.4
  41.7 0.7 fusion.2
  42.4 0.7 collective-permute-done.4
  43.1 2.0 %all-to-all-done = f32[4,5,128,128]{3,2,1,0:T(8,128)S(1)} async-done(((f32[4,5,128,128]{3,2,1,0:T(8,128)}), f32[4,5,128,128]{3,2,1,0:T(8,128)S(1)}, u32[]{:S(2)}, u32[]{:S(2)}) %all-to-all-start) | async-done | bytes 1310752 | tf_op jit(solution)/shard_map/all_to_all | solution.py:283
  45.1 0.1 reduce_sum.9
  45.3 1.4 collective-permute-start.5
  46.7 1.2 broadcast_in_dim.33
  47.9 4.0 %all-to-all-start.1 = ((f32[4,5,128,128]{3,2,1,0:T(8,128)}), f32[4,5,128,128]{3,2,1,0:T(8,128)S(1)}, u32[]{:S(2)}, u32[]{:S(2)}) async-start(f32[4,5,128,128]{3,2,1,0:T(8,128)} %broadcast_in_dim.33), calls=%async_computation.1 | async-start | bytes 2621440 | tf_op jit(solution)/shard_map/all_to_all | solution.py:283
  52.0 0.0 collective-permute-done.5
  52.0 0.6 fusion.3.c_ref
  52.6 9.5 %inverse.1.rest_1_ = f32[128,128]{1,0:T(8,128)} custom-call(f32[128,128]{1,0:T(8,128)} %fusion.3.c_ref), custom_call_target="tpu_custom_call" | custom-call | flops 7247757312 | bytes 1048576 | tf_op jit(solution)/shard_map/inverse/pallas_call | solution.py:269
  62.1 6.8 %collective-permute-start.6 = (f32[128,128]{1,0:T(8,128)}, f32[128,128]{1,0:T(8,128)S(1)}, u32[]{:S(2)}, u32[]{:S(2)}) collective-permute-start(f32[128,128]{1,0:T(8,128)} %inverse.1.rest_1_), channel_id=1, source_target_pairs={{0,64},{1,65},{2,66},{3,67},{4,68},{5,69},{6,70},{7,71}} | collective-permute-start | bytes 196616 | tf_op jit(solution)/shard_map/ppermute | solution.py:291
  68.9 1.6 %collective-permute-done.6.rest_2_ = f32[128,128]{1,0:T(8,128)S(1)} collective-permute-done((f32[128,128]{1,0:T(8,128)}, f32[128,128]{1,0:T(8,128)S(1)}, u32[]{:S(2)}, u32[]{:S(2)}) %collective-permute-start.6) | collective-permute-done | bytes 65568 | tf_op jit(solution)/shard_map/ppermute | solution.py:291
  70.6 0.0 all-gather.3.cloned.1.call-done
  70.6 1.2 collective-permute-start.7
  71.8 4.0 %lead.2.rest_0_ = f32[128,128]{1,0:T(8,128)} custom-call(s32[7]{0:T(128)} %concatenate.12.info, f32[4,5,128,128]{3,2,1,0:T(8,128)} %copy-done.1, f32[4,512,128]{2,1,0:T(8,128)} %broadcast_in_dim.17.s_ref.r_ref, f32[136,128]{1,0:T(8,128)} %copy-done.4), custom_call_target="tpu_custom_call" | custom-call | flops 603979776 | bytes 3145728 | tf_op jit(solution)/shard_map/lead/pallas_call | solution.py:146
  75.8 0.0 collective-permute-done.7.v_ref
  75.8 1.0 collective-permute-start.8
  76.8 0.1 copy-done.3
  76.8 4.5 %lead.3 = f32[16,128,128]{2,1,0:T(8,128)} custom-call(s32[7]{0:T(128)} %concatenate.12.info, f32[4,5,128,128]{3,2,1,0:T(8,128)} %copy-done.3, f32[4,512,128]{2,1,0:T(8,128)} %broadcast_in_dim.17.s_ref.r_ref, f32[136,128]{1,0:T(8,128)} %copy-done.4, f32[128,128]{1,0:T(8,128)} %lead.2.rest_0_, f32[128,128]{1,0:T(8,128)} %inverse.1.rest_1_, f32[128,128]{1,0:T(8,128)} %copy-done.7), custom_call_target="tpu_custom_call" | custom-call | flops 603979776 | bytes 3145728 | tf_op jit(solution)/shard_map/lead/pallas_call | solution.py:146
  81.3 11.3 %all-to-all-start.2 = ((f32[16,128,128]{2,1,0:T(8,128)}), f32[16,128,128]{2,1,0:T(8,128)S(1)}, u32[]{:S(2)}, u32[]{:S(2)}) async-start(f32[16,128,128]{2,1,0:T(8,128)} %lead.3), calls=%async_computation.2 | async-start | bytes 2097152 | tf_op jit(solution)/shard_map/all_to_all | solution.py:283
  92.6 18.4 %block.2 = (f32[512,1024]{1,0:T(8,128)}, f32[512,128]{1,0:T(8,128)}) custom-call(s32[7]{0:T(128)} %concatenate.12.info, f32[4,5,128,128]{3,2,1,0:T(8,128)} %copy-done.1, f32[4,512,128]{2,1,0:T(8,128)} %broadcast_in_dim.17.s_ref.r_ref, f32[16,520,128]{2,1,0:T(8,128)} %bitcast.38, f32[136,128]{1,0:T(8,128)} %copy-done.4), custom_call_target="tpu_custom_call" | custom-call | flops 10871635968 | bytes 10485760 | tf_op jit(solution)/shard_map/block/pallas_call | solution.py:228
  110.9 1.0 copy-done.5
  111.9 21.7 %block.3 = (f32[512,1024]{1,0:T(8,128)}, f32[512,128]{1,0:T(8,128)}, f32[4,4,128]{2,1,0:T(4,128)}) custom-call(s32[7]{0:T(128)} %concatenate.12.info, f32[4,5,128,128]{3,2,1,0:T(8,128)} %copy-done.3, f32[4,512,128]{2,1,0:T(8,128)} %broadcast_in_dim.17.s_ref.r_ref, f32[16,520,128]{2,1,0:T(8,128)} %collective-permute-done.8.c_ref, f32[136,128]{1,0:T(8,128)} %copy-done.4, ...), custom_call_target="tpu_custom_call" | custom-call | flops 10871635968 | bytes 10485760 | tf_op jit(solution)/shard_map/block/pallas_call | solution.py:228
  (32 shorter events, 0.2 us)
Async XLA Ops:
  7.2 63.4 %all-gather.3.cloned.1.call-start = ((), (), s32[]{:S(2)}) async-start(), calls=%async_computation.3 | async-start | bytes 4526080 | tf_op jit(solution)/shard_map/all_gather | solution.py:307
  7.9 3.5 %copy-start.8 = (s32[3]{0:T(128)S(1)}, s32[3]{0:T(128)}, u32[]{:S(2)}) copy-start(s32[3]{0:T(128)} %param.11) | copy-start | bytes 40
  7.9 3.6 %copy-start.2 = (f32[3,256,256]{2,1,0:T(8,128)S(1)}, f32[3,256,256]{2,1,0:T(8,128)}, u32[]{:S(2)}) copy-start(f32[3,256,256]{2,1,0:T(8,128)} %x_ref.1) | copy-start | bytes 2359300
  10.0 7.1 %copy-start = (f32[4,4,128,256]{3,2,1,0:T(8,128)}, f32[4,4,128,256]{3,2,1,0:T(8,128)S(1)}, u32[]{:S(2)}) copy-start(f32[4,4,128,256]{3,2,1,0:T(8,128)S(1)} %copy.12) | copy-start | bytes 6291460
  12.7 3.0 %collective-permute-start = (f32[3,256,128]{2,1,0:T(8,128)S(1)}, f32[3,256,128]{2,1,0:T(8,128)S(1)}, u32[]{:S(2)}, u32[]{:S(2)}) collective-permute-start(f32[3,256,128]{2,1,0:T(8,128)S(1)} %multiply_multiply_fusion), channel_id=1, source_target_pairs={{0,1},{1,0},{2,3},{3,2},{4,5},{5,4},{6,7},{7,6},{8,9},{9,8},{10,11... | collective-permute-start | bytes 1179656 | tf_op jit(solution)/shard_map/ppermute | solution.py:279
  15.7 1.4 copy-start.6
  23.5 21.6 %all-to-all-start = ((f32[4,5,128,128]{3,2,1,0:T(8,128)}), f32[4,5,128,128]{3,2,1,0:T(8,128)S(1)}, u32[]{:S(2)}, u32[]{:S(2)}) async-start(f32[4,5,128,128]{3,2,1,0:T(8,128)} %partial.1), calls=%async_computation | async-start | bytes 2621440 | tf_op jit(solution)/shard_map/all_to_all | solution.py:283
  27.6 7.3 %collective-permute-start.1 = (f32[136,128]{1,0:T(8,128)S(1)}, f32[136,128]{1,0:T(8,128)S(1)}, u32[]{:S(2)}, u32[]{:S(2)}) collective-permute-start(f32[136,128]{1,0:T(8,128)S(1)} %maximum_select_fusion), channel_id=1, source_target_pairs={{0,16},{1,17},{2,18},{3,19},{4,20},{5,21},{6,22},{7,23}} | collective-permute-start | bytes 208904 | tf_op jit(solution)/shard_map/ppermute | solution.py:291
  35.0 2.8 %collective-permute-start.2 = (f32[136,128]{1,0:T(8,128)S(1)}, f32[136,128]{1,0:T(8,128)S(1)}, u32[]{:S(2)}, u32[]{:S(2)}) collective-permute-start(f32[136,128]{1,0:T(8,128)S(1)} %add.44), channel_id=1, source_target_pairs={{0,8},{16,24},{1,9},{17,25},{2,10},{18,26},{3,11},{19,27},{4,12},{... | collective-permute-start | bytes 208904 | tf_op jit(solution)/shard_map/ppermute | solution.py:291
  37.8 2.7 %collective-permute-start.3 = (f32[136,128]{1,0:T(8,128)S(1)}, f32[136,128]{1,0:T(8,128)S(1)}, u32[]{:S(2)}, u32[]{:S(2)}) collective-permute-start(f32[136,128]{1,0:T(8,128)S(1)} %add.45), channel_id=1, source_target_pairs={{0,64},{8,72},{16,80},{24,88},{1,65},{9,73},{17,81},{25,89},{2,66}... | collective-permute-start | bytes 208904 | tf_op jit(solution)/shard_map/ppermute | solution.py:291
  40.4 2.7 %collective-permute-start.4 = (f32[136,128]{1,0:T(8,128)S(1)}, f32[136,128]{1,0:T(8,128)S(1)}, u32[]{:S(2)}, u32[]{:S(2)}) collective-permute-start(f32[136,128]{1,0:T(8,128)S(1)} %add.46), channel_id=1, source_target_pairs={{0,32},{8,40},{16,48},{24,56},{64,96},{72,104},{80,112},{88,120},{... | collective-permute-start | bytes 208904 | tf_op jit(solution)/shard_map/ppermute | solution.py:291
  45.3 2.7 %copy-start.4 = (f32[136,128]{1,0:T(8,128)}, f32[136,128]{1,0:T(8,128)S(1)}, u32[]{:S(2)}) copy-start(f32[136,128]{1,0:T(8,128)S(1)} %add.47.z_ref) | copy-start | bytes 208900
  45.3 6.7 %collective-permute-start.5 = (f32[128,128]{1,0:T(8,128)S(1)}, f32[128,128]{1,0:T(8,128)S(1)}, u32[]{:S(2)}, u32[]{:S(2)}) collective-permute-start(f32[128,128]{1,0:T(8,128)S(1)} %fusion), channel_id=1, source_target_pairs={{0,1},{1,0},{2,3},{3,2},{4,5},{5,4},{6,7},{7,6},{8,9},{9,8},{10,11... | collective-permute-start | bytes 196616 | tf_op jit(solution)/shard_map/ppermute | solution.py:279
  47.9 22.6 %all-to-all-start.1 = ((f32[4,5,128,128]{3,2,1,0:T(8,128)}), f32[4,5,128,128]{3,2,1,0:T(8,128)S(1)}, u32[]{:S(2)}, u32[]{:S(2)}) async-start(f32[4,5,128,128]{3,2,1,0:T(8,128)} %broadcast_in_dim.33), calls=%async_computation.1 | async-start | bytes 2621440 | tf_op jit(solution)/shard_map/all_to_all | solution.py:283
  62.1 8.4 %collective-permute-start.6 = (f32[128,128]{1,0:T(8,128)}, f32[128,128]{1,0:T(8,128)S(1)}, u32[]{:S(2)}, u32[]{:S(2)}) collective-permute-start(f32[128,128]{1,0:T(8,128)} %inverse.1.rest_1_), channel_id=1, source_target_pairs={{0,64},{1,65},{2,66},{3,67},{4,68},{5,69},{6,70},{7,71}} | collective-permute-start | bytes 196616 | tf_op jit(solution)/shard_map/ppermute | solution.py:291
  70.6 6.2 %copy-start.7 = (f32[128,128]{1,0:T(8,128)}, f32[128,128]{1,0:T(8,128)S(1)}, u32[]{:S(2)}) copy-start(f32[128,128]{1,0:T(8,128)S(1)} %collective-permute-done.6.rest_2_) | copy-start | bytes 196612
  70.6 1.3 copy-start.1
  70.6 5.2 %collective-permute-start.7 = (f32[4,5,128,128]{3,2,1,0:T(8,128)S(1)}, f32[4,5,128,128]{3,2,1,0:T(8,128)S(1)}, u32[]{:S(2)}, u32[]{:S(2)}) collective-permute-start(f32[4,5,128,128]{3,2,1,0:T(8,128)S(1)} %all-to-all-done.1.v_ref), channel_id=1, source_target_pairs={{0,1},{1,0},{2,3},{3,2},{4,5},{5,4},{6,7},{7,6},{8,9},{9,8},{10,11... | collective-permute-start | bytes 3932168 | tf_op jit(solution)/shard_map/ppermute | solution.py:279
  75.8 1.0 copy-start.3
  75.8 35.1 %collective-permute-start.8 = (f32[16,520,128]{2,1,0:T(8,128)}, f32[16,520,128]{2,1,0:T(8,128)}, u32[]{:S(2)}, u32[]{:S(2)}) collective-permute-start(f32[16,520,128]{2,1,0:T(8,128)} %bitcast.37), channel_id=1, source_target_pairs={{0,1},{1,0},{2,3},{3,2},{4,5},{5,4},{6,7},{7,6},{8,9},{9,8},{10,11... | collective-permute-start | bytes 12779528 | tf_op jit(solution)/shard_map/ppermute | solution.py:279
  81.3 29.6 %all-to-all-start.2 = ((f32[16,128,128]{2,1,0:T(8,128)}), f32[16,128,128]{2,1,0:T(8,128)S(1)}, u32[]{:S(2)}, u32[]{:S(2)}) async-start(f32[16,128,128]{2,1,0:T(8,128)} %lead.3), calls=%async_computation.2 | async-start | bytes 2097152 | tf_op jit(solution)/shard_map/all_to_all | solution.py:283
  110.9 1.0 copy-start.5
Sparse Core Ops, SparseCore 0:
  11.6 55.2 all-gather.2

commit v11 on v10

--- a/solution.py
+++ b/solution.py
@@ -10,7 +10,7 @@
 F32 = jnp.float32
 NT = (((1,), (1,)), ((), ()))
 NN = (((1,), (0,)), ((), ()))
-VMEM = 56 << 20
+VMEM = 32 << 20
 
 
 def split(v):
@@ -77,7 +77,7 @@
 
 
 def whole(v):
-    return pl.BlockSpec(v.shape, lambda g, i: (0,) * v.ndim)
+    return pl.BlockSpec(v.shape, lambda g, i: (0,) * v.ndim, pipeline_mode=pl.Buffered(1))
 
 
 def partial(info, c, s, x, y, z):
@@ -217,7 +217,7 @@
     last = tail is not None
     args = [v, r, c, z] + (list(tail) if last else [])
     specs = [whole(u) for u in args]
-    specs[2] = pl.BlockSpec((8, 520, 128), pick)
+    specs[2] = pl.BlockSpec((8, 520, 128), pick, pipeline_mode=pl.Buffered(1))
     shapes = [(512, 1024), (512, 128)] + ([(4, 4, 128)] if last else [])
     outs = [pl.BlockSpec((512, 1024), lambda g, i: (0, 0)), pl.BlockSpec((512, 128), lambda g, i: (0, 0)),
             pl.BlockSpec((4, 4, 128), lambda g, i: (0, 0, 0))]

time: 141 us -> 143 us (1.014)
  Pallas kernels: 64.5 us -> 53.6 us
  local copies, waits for them, and re-layouts: 7.45 us -> 17.9 us
    unnamed x18 -> x34, local copies, waits for them, and re-layouts: 1.07 us -> 12.5 us
    pallas_call x2, Pallas kernels: 40.1 us -> 35.4 us  [block_product(): pl.pallas_call(functools.partial(block_body, last), grid_spec=grid, out_s...]
    pallas_call x2, Pallas kernels: 8.41 us -> 4.91 us  [lead(): pl.pallas_call(functools.partial(lead_body, last), grid_spec=grid, out_sh...]
    pallas_call x1, Pallas kernels: 6.42 us -> 3.7 us  [partial(): pl.pallas_call(partial_body, grid_spec=grid, out_shape=out, compiler_para...]
  transfers between devices with their start and end apart: 13 -> 13, of which waited for: 6 -> 8; matrix products, arithmetic and copies ran while one was open for 5% -> 5% of each run, Pallas kernels for 30% -> 24%
where the time goes in v11:
time: 143 us; the launch traced here: 142 us
  Pallas kernels  53.6 us (37%)
  starting transfers between devices  40.9 us (29%)
  local copies, waits for them, and re-layouts  17.9 us (13%)
  between operations  14.3 us (10%)
  waiting for transfers between devices  10.3 us (7%)
  other arithmetic  5.02 us (4%)
    pallas_call x2, Pallas kernels, block_product(): pl.pallas_call(functools.partial(block_body, last), grid_spec=grid, out_s...  35.4 us
    all_to_all x3, starting transfers between devices, exchange(): return lax.all_to_all(v, axis, 0, 0, axis_index_groups=groups, tiled=True)  19.7 us
    ppermute x5, starting transfers between devices, over_rows(): return lax.ppermute(v, 'rows', pairs)  15.4 us
    unnamed x34, local copies, waits for them, and re-layouts  12.5 us
    pallas_call x1, Pallas kernels, inverse_of(): pl.pallas_call(inverse_body, out_shape=jax.ShapeDtypeStruct((128, 128), F...  9.52 us
    ppermute x5, waiting for transfers between devices, over_rows(): return lax.ppermute(v, 'rows', pairs)  7.48 us
    ppermute x4, starting transfers between devices, swap(): return lax.ppermute(v, 'cols', SWAP)  5.78 us
    pallas_call x2, Pallas kernels, lead(): pl.pallas_call(functools.partial(lead_body, last), grid_spec=grid, out_sh...  4.91 us
  transfers between devices with their start and end apart: 13, of which 8 were waited for; matrix products, arithmetic and copies ran while one was open for 5% of the time, Pallas kernels for 24%

profile of v11, /device:TPU:1, one launch (start us, length us, event | category | flops | bytes accessed | tf_op | source)
XLA Modules:
  0.0 142.0 jit_solution(4229316564219332255)
XLA Ops:
  7.2 0.7 convert_bitcast_fusion
  7.9 2.1 %copy.12 = f32[4,4,128,256]{3,2,1,0:T(8,128)S(1)} copy(f32[4,4,128,256]{3,0,2,1:T(4,128)} %bitcast.36) | data formatting | bytes 4194304 | tf_op jit(solution)/shard_map/transpose | solution.py:302
  10.1 0.1 copy.14
  10.3 0.1 pad.2.clone
  10.3 0.9 maximum_maximum_fusion
  11.3 1.9 %multiply_multiply_fusion = f32[3,256,128]{2,1,0:T(8,128)} fusion(f32[3,256,256]{2,1,0:T(8,128)} %y_ref.1, s32[]{:T(128)S(6)} %select_n.50, f32[3,256,256]{2,1,0:T(8,128)S(1)} %copy-done.1, f32[3,128]{1,0:T(4,128)S(1)} %constant_dynamic-slice_fusion, f32[3,256]{1,0:T(4,128)S(1)} %fusion.1), kind=kLoop, calls=%fused_computation | loop fusion | flops 294912 | bytes 1184260 | tf_op jit(solution)/shard_map/mul | solution.py:317
  13.2 1.4 %collective-permute-start = (f32[3,256,128]{2,1,0:T(8,128)}, f32[3,256,128]{2,1,0:T(8,128)S(1)}, u32[]{:S(2)}, u32[]{:S(2)}) collective-permute-start(f32[3,256,128]{2,1,0:T(8,128)} %multiply_multiply_fusion), channel_id=1, source_target_pairs={{0,1},{1,0},{2,3},{3,2},{4,5},{5,4},{6,7},{7,6},{8,9},{9,8},{10,11... | collective-permute-start | bytes 1179656 | tf_op jit(solution)/shard_map/ppermute | solution.py:279
  14.7 0.1 copy.13
  14.8 0.7 concatenate.12.info
  15.5 0.6 maximum_select_fusion
  16.2 1.0 broadcast_in_dim.17.s_ref.r_ref
  17.3 1.1 copy-done.2
  18.4 1.1 copy-done.3
  19.5 3.7 %partial.1 = f32[4,5,128,128]{3,2,1,0:T(8,128)S(1)} custom-call(s32[7]{0:T(128)S(1)} %concatenate.12.info, f32[4,512,256]{2,1,0:T(8,128)S(1)} %bitcast.33, f32[4,512,128]{2,1,0:T(8,128)S(1)} %broadcast_in_dim.17.s_ref.r_ref, f32[3,256,256]{2,1,0:T(8,128)S(1)} %copy-done.2, f32[3,256,256]{2,1,0:T(8,128)S(1)} %copy-done.3, ...), custom_call_target="tpu_custom_call" | custom-call | flops 603979776 | bytes 8388608 | tf_op jit(solution)/shard_map/partial/pallas_call | solution.py:90
  23.2 1.0 copy-done
  24.3 4.2 %all-to-all-start = ((f32[4,5,128,128]{3,2,1,0:T(8,128)}), f32[4,5,128,128]{3,2,1,0:T(8,128)S(1)}, u32[]{:S(2)}, u32[]{:S(2)}) async-start(f32[4,5,128,128]{3,2,1,0:T(8,128)} %copy-done), calls=%async_computation | async-start | bytes 2621440 | tf_op jit(solution)/shard_map/all_to_all | solution.py:283
  28.5 5.5 %collective-permute-start.1 = (f32[136,128]{1,0:T(8,128)S(1)}, f32[136,128]{1,0:T(8,128)S(1)}, u32[]{:S(2)}, u32[]{:S(2)}) collective-permute-start(f32[136,128]{1,0:T(8,128)S(1)} %copy-done.14), channel_id=1, source_target_pairs={{0,16},{1,17},{2,18},{3,19},{4,20},{5,21},{6,22},{7,23}} | collective-permute-start | bytes 208904 | tf_op jit(solution)/shard_map/ppermute | solution.py:291
  34.0 1.3 collective-permute-done.1
  35.4 1.3 collective-permute-start.2
  36.7 1.3 collective-permute-done.2
  38.0 1.3 collective-permute-start.3
  39.4 1.3 collective-permute-done.3
  40.7 1.3 collective-permute-start.4
  42.0 1.8 %collective-permute-done.4 = f32[136,128]{1,0:T(8,128)S(1)} collective-permute-done((f32[136,128]{1,0:T(8,128)S(1)}, f32[136,128]{1,0:T(8,128)S(1)}, u32[]{:S(2)}, u32[]{:S(2)}) %collective-permute-start.4) | collective-permute-done | bytes 69664 | tf_op jit(solution)/shard_map/ppermute | solution.py:291
  43.8 2.0 %all-to-all-done = f32[4,5,128,128]{3,2,1,0:T(8,128)S(1)} async-done(((f32[4,5,128,128]{3,2,1,0:T(8,128)}), f32[4,5,128,128]{3,2,1,0:T(8,128)S(1)}, u32[]{:S(2)}, u32[]{:S(2)}) %all-to-all-start) | async-done | bytes 1310752 | tf_op jit(solution)/shard_map/all_to_all | solution.py:283
  45.9 0.1 reduce_sum.9
  46.0 2.8 %collective-permute-start.5 = (f32[128,128]{1,0:T(8,128)S(1)}, f32[128,128]{1,0:T(8,128)S(1)}, u32[]{:S(2)}, u32[]{:S(2)}) collective-permute-start(f32[128,128]{1,0:T(8,128)S(1)} %fusion), channel_id=1, source_target_pairs={{0,1},{1,0},{2,3},{3,2},{4,5},{5,4},{6,7},{7,6},{8,9},{9,8},{10,11... | collective-permute-start | bytes 196616 | tf_op jit(solution)/shard_map/ppermute | solution.py:279
  48.9 1.2 broadcast_in_dim.33
  50.1 4.3 %all-to-all-start.1 = ((f32[4,5,128,128]{3,2,1,0:T(8,128)}), f32[4,5,128,128]{3,2,1,0:T(8,128)S(1)}, u32[]{:S(2)}, u32[]{:S(2)}) async-start(f32[4,5,128,128]{3,2,1,0:T(8,128)} %broadcast_in_dim.33), calls=%async_computation.1 | async-start | bytes 2621440 | tf_op jit(solution)/shard_map/all_to_all | solution.py:283
  54.3 0.6 fusion.3.c_ref
  55.0 9.5 %inverse.1.rest_1_ = f32[128,128]{1,0:T(8,128)} custom-call(f32[128,128]{1,0:T(8,128)} %fusion.3.c_ref), custom_call_target="tpu_custom_call" | custom-call | flops 7247757312 | bytes 1048576 | tf_op jit(solution)/shard_map/inverse/pallas_call | solution.py:269
  64.5 6.0 %collective-permute-start.6 = (f32[128,128]{1,0:T(8,128)}, f32[128,128]{1,0:T(8,128)S(1)}, u32[]{:S(2)}, u32[]{:S(2)}) collective-permute-start(f32[128,128]{1,0:T(8,128)} %inverse.1.rest_1_), channel_id=1, source_target_pairs={{0,64},{1,65},{2,66},{3,67},{4,68},{5,69},{6,70},{7,71}} | collective-permute-start | bytes 196616 | tf_op jit(solution)/shard_map/ppermute | solution.py:291
  70.5 1.6 %collective-permute-done.6.rest_2_ = f32[128,128]{1,0:T(8,128)S(1)} collective-permute-done((f32[128,128]{1,0:T(8,128)}, f32[128,128]{1,0:T(8,128)S(1)}, u32[]{:S(2)}, u32[]{:S(2)}) %collective-permute-start.6) | collective-permute-done | bytes 65568 | tf_op jit(solution)/shard_map/ppermute | solution.py:291
  72.2 1.2 collective-permute-start.7
  73.3 1.9 %lead.2.rest_0_ = f32[128,128]{1,0:T(8,128)S(1)} custom-call(s32[7]{0:T(128)S(1)} %concatenate.12.info, f32[4,5,128,128]{3,2,1,0:T(8,128)S(1)} %all-to-all-done.1.v_ref, f32[4,512,128]{2,1,0:T(8,128)S(1)} %broadcast_in_dim.17.s_ref.r_ref, f32[136,128]{1,0:T(8,128)S(1)} %add.47.z_ref), custom_call_target="tpu_custom_call" | custom-call | flops 603979776 | bytes 3145728 | tf_op jit(solution)/shard_map/lead/pallas_call | solution.py:146
  75.2 0.7 collective-permute-done.7.v_ref
  76.0 0.4 collective-permute-start.8
  76.4 3.0 %lead.3 = f32[16,128,128]{2,1,0:T(8,128)} custom-call(s32[7]{0:T(128)S(1)} %concatenate.12.info, f32[4,5,128,128]{3,2,1,0:T(8,128)S(1)} %collective-permute-done.7.v_ref, f32[4,512,128]{2,1,0:T(8,128)S(1)} %broadcast_in_dim.17.s_ref.r_ref, f32[136,128]{1,0:T(8,128)S(1)} %add.47.z_ref, f32[128,128]{1,0:T(8,128)S(1)} %lead.2.rest_0_, ...), custom_call_target="tpu_custom_call" | custom-call | flops 603979776 | bytes 3145728 | tf_op jit(solution)/shard_map/lead/pallas_call | solution.py:146
  79.3 1.1 copy-done.4
  80.4 11.2 %all-to-all-start.2 = ((f32[16,128,128]{2,1,0:T(8,128)}), f32[16,128,128]{2,1,0:T(8,128)S(1)}, u32[]{:S(2)}, u32[]{:S(2)}) async-start(f32[16,128,128]{2,1,0:T(8,128)} %lead.3), calls=%async_computation.2 | async-start | bytes 2097152 | tf_op jit(solution)/shard_map/all_to_all | solution.py:283
  91.6 2.2 %copy-done.8 = f32[8320,128]{1,0:T(8,128)S(1)} copy-done((f32[8320,128]{1,0:T(8,128)S(1)}, f32[8320,128]{1,0:T(8,128)}, u32[]{:S(2)}) %copy-start.8) | copy-done | bytes 4259864
  93.8 15.4 %block.2 = (f32[512,1024]{1,0:T(8,128)S(1)}, f32[512,128]{1,0:T(8,128)S(1)}) custom-call(s32[7]{0:T(128)S(1)} %concatenate.12.info, f32[4,5,128,128]{3,2,1,0:T(8,128)S(1)} %all-to-all-done.1.v_ref, f32[4,512,128]{2,1,0:T(8,128)S(1)} %broadcast_in_dim.17.s_ref.r_ref, f32[16,520,128]{2,1,0:T(8,128)S(1)} %bitcast.35, f32[136,128]{1,0:T(8,128)S(1)} %add.47.z_ref), custom_call_target="tpu_custom_call" | custom-call | flops 10871635968 | bytes 10485760 | tf_op jit(solution)/shard_map/block/pallas_call | solution.py:228
  109.2 1.3 copy-done.10
  110.6 0.7 copy-done.12
  111.3 1.3 copy-done.5
  112.6 1.6 %copy-done.11 = f32[512,1024]{1,0:T(8,128)S(1)} copy-done((f32[512,1024]{1,0:T(8,128)S(1)}, f32[512,1024]{1,0:T(8,128)}, u32[]{:S(2)}) %copy-start.11) | copy-done | bytes 2097176
  114.2 0.9 copy-done.13
  115.1 20.0 %block.3 = (f32[512,1024]{1,0:T(8,128)}, f32[512,128]{1,0:T(8,128)}, f32[4,4,128]{2,1,0:T(4,128)}) custom-call(s32[7]{0:T(128)S(1)} %concatenate.12.info, f32[4,5,128,128]{3,2,1,0:T(8,128)S(1)} %copy-done.5, f32[4,512,128]{2,1,0:T(8,128)S(1)} %broadcast_in_dim.17.s_ref.r_ref, f32[16,520,128]{2,1,0:T(8,128)} %collective-permute-done.8.c_ref, ...), custom_call_target="tpu_custom_call" | custom-call | flops 10871635968 | bytes 10485760 | tf_op jit(solution)/shard_map/block/pallas_call | solution.py:228
  (48 shorter events, 0.4 us)
Async XLA Ops:
  7.2 65.0 %all-gather.3.cloned.1.call-start = ((), (), s32[]{:S(2)}) async-start(), calls=%async_computation.3 | async-start | bytes 4526080 | tf_op jit(solution)/shard_map/all_gather | solution.py:307
  7.9 2.1 %copy-start.15 = (f32[4,512]{1,0:T(4,128)}, f32[4,512]{1,0:T(4,128)S(1)}, u32[]{:S(2)}) copy-start(f32[4,512]{1,0:T(4,128)S(1)} %convert_bitcast_fusion) | copy-start | bytes 24580
  7.9 3.3 %copy-start.16 = (s32[3]{0:T(128)S(1)}, s32[3]{0:T(128)}, u32[]{:S(2)}) copy-start(s32[3]{0:T(128)} %param.11) | copy-start | bytes 40
  7.9 3.4 %copy-start.1 = (f32[3,256,256]{2,1,0:T(8,128)S(1)}, f32[3,256,256]{2,1,0:T(8,128)}, u32[]{:S(2)}) copy-start(f32[3,256,256]{2,1,0:T(8,128)} %x_ref.1) | copy-start | bytes 2359300
  10.0 5.5 %copy-start.7 = (f32[4,4,128]{2,1,0:T(4,128)S(1)}, f32[4,4,128]{2,1,0:T(4,128)}, u32[]{:S(2)}) copy-start(f32[4,4,128]{2,1,0:T(4,128)} %rest_4_.1) | copy-start | bytes 24580
  13.2 3.0 %collective-permute-start = (f32[3,256,128]{2,1,0:T(8,128)}, f32[3,256,128]{2,1,0:T(8,128)S(1)}, u32[]{:S(2)}, u32[]{:S(2)}) collective-permute-start(f32[3,256,128]{2,1,0:T(8,128)} %multiply_multiply_fusion), channel_id=1, source_target_pairs={{0,1},{1,0},{2,3},{3,2},{4,5},{5,4},{6,7},{7,6},{8,9},{9,8},{10,11... | collective-permute-start | bytes 1179656 | tf_op jit(solution)/shard_map/ppermute | solution.py:279
  17.3 1.1 copy-start.2
  18.4 1.1 copy-start.3
  23.2 1.1 copy-start
  24.3 4.2 %copy-start.14 = (f32[136,128]{1,0:T(8,128)S(1)}, f32[136,128]{1,0:T(8,128)}, u32[]{:S(2)}) copy-start(f32[136,128]{1,0:T(8,128)} %maximum_select_fusion) | copy-start | bytes 208900
  24.3 17.7 %copy-start.9 = (f32[4,128]{1,0:T(4,128)S(1)}, f32[4,128]{1,0:T(4,128)}, u32[]{:S(2)}) copy-start(f32[4,128]{1,0:T(4,128)} %rest_3_.1) | copy-start | bytes 6148
  24.3 21.6 %all-to-all-start = ((f32[4,5,128,128]{3,2,1,0:T(8,128)}), f32[4,5,128,128]{3,2,1,0:T(8,128)S(1)}, u32[]{:S(2)}, u32[]{:S(2)}) async-start(f32[4,5,128,128]{3,2,1,0:T(8,128)} %copy-done), calls=%async_computation | async-start | bytes 2621440 | tf_op jit(solution)/shard_map/all_to_all | solution.py:283
  28.5 6.9 %collective-permute-start.1 = (f32[136,128]{1,0:T(8,128)S(1)}, f32[136,128]{1,0:T(8,128)S(1)}, u32[]{:S(2)}, u32[]{:S(2)}) collective-permute-start(f32[136,128]{1,0:T(8,128)S(1)} %copy-done.14), channel_id=1, source_target_pairs={{0,16},{1,17},{2,18},{3,19},{4,20},{5,21},{6,22},{7,23}} | collective-permute-start | bytes 208904 | tf_op jit(solution)/shard_map/ppermute | solution.py:291
  35.4 2.7 %collective-permute-start.2 = (f32[136,128]{1,0:T(8,128)S(1)}, f32[136,128]{1,0:T(8,128)S(1)}, u32[]{:S(2)}, u32[]{:S(2)}) collective-permute-start(f32[136,128]{1,0:T(8,128)S(1)} %add.44), channel_id=1, source_target_pairs={{0,8},{16,24},{1,9},{17,25},{2,10},{18,26},{3,11},{19,27},{4,12},{... | collective-permute-start | bytes 208904 | tf_op jit(solution)/shard_map/ppermute | solution.py:291
  38.0 2.7 %collective-permute-start.3 = (f32[136,128]{1,0:T(8,128)S(1)}, f32[136,128]{1,0:T(8,128)S(1)}, u32[]{:S(2)}, u32[]{:S(2)}) collective-permute-start(f32[136,128]{1,0:T(8,128)S(1)} %add.45), channel_id=1, source_target_pairs={{0,64},{8,72},{16,80},{24,88},{1,65},{9,73},{17,81},{25,89},{2,66}... | collective-permute-start | bytes 208904 | tf_op jit(solution)/shard_map/ppermute | solution.py:291
  40.7 3.1 %collective-permute-start.4 = (f32[136,128]{1,0:T(8,128)S(1)}, f32[136,128]{1,0:T(8,128)S(1)}, u32[]{:S(2)}, u32[]{:S(2)}) collective-permute-start(f32[136,128]{1,0:T(8,128)S(1)} %add.46), channel_id=1, source_target_pairs={{0,32},{8,40},{16,48},{24,56},{64,96},{72,104},{80,112},{88,120},{... | collective-permute-start | bytes 208904 | tf_op jit(solution)/shard_map/ppermute | solution.py:291
  46.0 8.3 %collective-permute-start.5 = (f32[128,128]{1,0:T(8,128)S(1)}, f32[128,128]{1,0:T(8,128)S(1)}, u32[]{:S(2)}, u32[]{:S(2)}) collective-permute-start(f32[128,128]{1,0:T(8,128)S(1)} %fusion), channel_id=1, source_target_pairs={{0,1},{1,0},{2,3},{3,2},{4,5},{5,4},{6,7},{7,6},{8,9},{9,8},{10,11... | collective-permute-start | bytes 196616 | tf_op jit(solution)/shard_map/ppermute | solution.py:279
  50.1 22.1 %all-to-all-start.1 = ((f32[4,5,128,128]{3,2,1,0:T(8,128)}), f32[4,5,128,128]{3,2,1,0:T(8,128)S(1)}, u32[]{:S(2)}, u32[]{:S(2)}) async-start(f32[4,5,128,128]{3,2,1,0:T(8,128)} %broadcast_in_dim.33), calls=%async_computation.1 | async-start | bytes 2621440 | tf_op jit(solution)/shard_map/all_to_all | solution.py:283
  64.5 11.9 %copy-start.6 = (f32[128,128]{1,0:T(8,128)S(1)}, f32[128,128]{1,0:T(8,128)}, u32[]{:S(2)}) copy-start(f32[128,128]{1,0:T(8,128)} %inverse.1.rest_1_) | copy-start | bytes 196612
  64.5 7.6 %collective-permute-start.6 = (f32[128,128]{1,0:T(8,128)}, f32[128,128]{1,0:T(8,128)S(1)}, u32[]{:S(2)}, u32[]{:S(2)}) collective-permute-start(f32[128,128]{1,0:T(8,128)} %inverse.1.rest_1_), channel_id=1, source_target_pairs={{0,64},{1,65},{2,66},{3,67},{4,68},{5,69},{6,70},{7,71}} | collective-permute-start | bytes 196616 | tf_op jit(solution)/shard_map/ppermute | solution.py:291
  72.2 3.8 %collective-permute-start.7 = (f32[4,5,128,128]{3,2,1,0:T(8,128)S(1)}, f32[4,5,128,128]{3,2,1,0:T(8,128)S(1)}, u32[]{:S(2)}, u32[]{:S(2)}) collective-permute-start(f32[4,5,128,128]{3,2,1,0:T(8,128)S(1)} %all-to-all-done.1.v_ref), channel_id=1, source_target_pairs={{0,1},{1,0},{2,3},{3,2},{4,5},{5,4},{6,7},{7,6},{8,9},{9,8},{10,11... | collective-permute-start | bytes 3932168 | tf_op jit(solution)/shard_map/ppermute | solution.py:279
  76.0 35.3 %collective-permute-start.8 = (f32[16,520,128]{2,1,0:T(8,128)}, f32[16,520,128]{2,1,0:T(8,128)}, u32[]{:S(2)}, u32[]{:S(2)}) collective-permute-start(f32[16,520,128]{2,1,0:T(8,128)} %bitcast.34), channel_id=1, source_target_pairs={{0,1},{1,0},{2,3},{3,2},{4,5},{5,4},{6,7},{7,6},{8,9},{9,8},{10,11... | collective-permute-start | bytes 12779528 | tf_op jit(solution)/shard_map/ppermute | solution.py:279
  79.3 1.1 copy-start.4
  80.4 30.9 %all-to-all-start.2 = ((f32[16,128,128]{2,1,0:T(8,128)}), f32[16,128,128]{2,1,0:T(8,128)S(1)}, u32[]{:S(2)}, u32[]{:S(2)}) async-start(f32[16,128,128]{2,1,0:T(8,128)} %lead.3), calls=%async_computation.2 | async-start | bytes 2097152 | tf_op jit(solution)/shard_map/all_to_all | solution.py:283
  91.6 2.2 %copy-start.8 = (f32[8320,128]{1,0:T(8,128)S(1)}, f32[8320,128]{1,0:T(8,128)}, u32[]{:S(2)}) copy-start(f32[8320,128]{1,0:T(8,128)} %all-gather.3.cloned.1.call-done) | copy-start | bytes 12779524
  109.2 1.3 copy-start.10
  110.6 0.7 copy-start.12
  111.3 1.3 copy-start.5
  112.6 1.6 %copy-start.11 = (f32[512,1024]{1,0:T(8,128)S(1)}, f32[512,1024]{1,0:T(8,128)}, u32[]{:S(2)}) copy-start(f32[512,1024]{1,0:T(8,128)} %copy-done.10) | copy-start | bytes 6291460
  114.2 0.9 copy-start.13
Sparse Core Ops, SparseCore 0:
  11.3 55.1 all-gather.2

commit v12 on v11

--- a/solution.py
+++ b/solution.py
@@ -11,6 +11,7 @@
 NT = (((1,), (1,)), ((), ()))
 NN = (((1,), (0,)), ((), ()))
 VMEM = 32 << 20
+LARGE = 52 << 20
 
 
 def split(v):
@@ -227,7 +228,7 @@
         + ([pltpu.VMEM((512, 128), F32)] if last else []))
     return pl.pallas_call(functools.partial(block_body, last), grid_spec=grid,
                           out_shape=[jax.ShapeDtypeStruct(u, F32) for u in shapes],
-                          compiler_params=pltpu.CompilerParams(vmem_limit_bytes=VMEM), name="block",
+                          compiler_params=pltpu.CompilerParams(vmem_limit_bytes=LARGE), name="block",
                           cost_estimate=pl.CostEstimate(flops=2 * 3 * 512 * 3072 * 1152, bytes_accessed=10 << 20, transcendentals=0))(info, *args)
 
 

time: 143 us -> 140 us (0.979)
  local copies, waits for them, and re-layouts: 17.9 us -> 10.8 us
  Pallas kernels: 53.6 us -> 57.5 us
    unnamed x34 -> x26, local copies, waits for them, and re-layouts: 12.5 us -> 5.43 us
    pallas_call x2, Pallas kernels: 35.4 us -> 39.3 us  [block_product(): pl.pallas_call(functools.partial(block_body, last), grid_spec=grid, out_s...]
  transfers between devices with their start and end apart: 13 -> 13, of which waited for: 8 -> 8; matrix products, arithmetic and copies ran while one was open for 5% -> 5% of each run, Pallas kernels for 24% -> 26%
where the time goes in v12:
time: 140 us; the launch traced here: 139 us
  Pallas kernels  57.5 us (41%)
  starting transfers between devices  40.8 us (29%)
  between operations  14.3 us (10%)
  local copies, waits for them, and re-layouts  10.8 us (8%)
  waiting for transfers between devices  10.3 us (7%)
  other arithmetic  5.03 us (4%)
    pallas_call x2, Pallas kernels, block_product(): pl.pallas_call(functools.partial(block_body, last), grid_spec=grid, out_s...  39.3 us
    all_to_all x3, starting transfers between devices, exchange(): return lax.all_to_all(v, axis, 0, 0, axis_index_groups=groups, tiled=True)  19.6 us
    ppermute x5, starting transfers between devices, over_rows(): return lax.ppermute(v, 'rows', pairs)  15.4 us
    pallas_call x1, Pallas kernels, inverse_of(): pl.pallas_call(inverse_body, out_shape=jax.ShapeDtypeStruct((128, 128), F...  9.52 us
    ppermute x5, waiting for transfers between devices, over_rows(): return lax.ppermute(v, 'rows', pairs)  7.47 us
    ppermute x4, starting transfers between devices, swap(): return lax.ppermute(v, 'cols', SWAP)  5.78 us
    unnamed x26, local copies, waits for them, and re-layouts  5.43 us
    pallas_call x2, Pallas kernels, lead(): pl.pallas_call(functools.partial(lead_body, last), grid_spec=grid, out_sh...  4.98 us
  transfers between devices with their start and end apart: 13, of which 8 were waited for; matrix products, arithmetic and copies ran while one was open for 5% of the time, Pallas kernels for 26%

profile of v12, /device:TPU:1, one launch (start us, length us, event | category | flops | bytes accessed | tf_op | source)
XLA Modules:
  0.0 138.8 jit_solution(9899356638558304995)
XLA Ops:
  7.2 0.0 all-gather.3.cloned.1.call-start
  7.2 0.7 convert_bitcast_fusion
  7.9 2.1 %copy.12 = f32[4,4,128,256]{3,2,1,0:T(8,128)S(1)} copy(f32[4,4,128,256]{3,0,2,1:T(4,128)} %bitcast.34) | data formatting | bytes 4194304 | tf_op jit(solution)/shard_map/transpose | solution.py:303
  10.1 0.1 copy.14
  10.3 0.1 pad.2.clone
  10.3 0.9 maximum_maximum_fusion
  11.2 0.0 all-gather.3.cloned.1.call-update
  11.2 0.1 fusion.1
  11.3 1.9 %multiply_multiply_fusion = f32[3,256,128]{2,1,0:T(8,128)} fusion(f32[3,256,256]{2,1,0:T(8,128)} %y_ref.1, s32[]{:T(128)S(6)} %select_n.50, f32[3,256,256]{2,1,0:T(8,128)S(1)} %copy-done.2, f32[3,128]{1,0:T(4,128)S(1)} %constant_dynamic-slice_fusion, f32[3,256]{1,0:T(4,128)S(1)} %fusion.1), kind=kLoop, calls=%fused_computation | loop fusion | flops 294912 | bytes 1184260 | tf_op jit(solution)/shard_map/mul | solution.py:318
  13.2 1.4 %collective-permute-start = (f32[3,256,128]{2,1,0:T(8,128)}, f32[3,256,128]{2,1,0:T(8,128)S(1)}, u32[]{:S(2)}, u32[]{:S(2)}) collective-permute-start(f32[3,256,128]{2,1,0:T(8,128)} %multiply_multiply_fusion), channel_id=1, source_target_pairs={{0,1},{1,0},{2,3},{3,2},{4,5},{5,4},{6,7},{7,6},{8,9},{9,8},{10,11... | collective-permute-start | bytes 1179656 | tf_op jit(solution)/shard_map/ppermute | solution.py:280
  14.7 0.1 copy.13
  14.8 0.7 concatenate.12.info
  15.5 0.6 maximum_select_fusion
  16.2 0.1 collective-permute-done.z_ref
  16.2 1.0 broadcast_in_dim.17.s_ref.r_ref
  17.3 0.0 copy-start.3
  17.3 1.1 copy-done.3
  18.4 1.1 copy-done.4
  19.5 3.7 %partial.1 = f32[4,5,128,128]{3,2,1,0:T(8,128)S(1)} custom-call(s32[7]{0:T(128)S(1)} %concatenate.12.info, f32[4,512,256]{2,1,0:T(8,128)S(1)} %bitcast.33, f32[4,512,128]{2,1,0:T(8,128)S(1)} %broadcast_in_dim.17.s_ref.r_ref, f32[3,256,256]{2,1,0:T(8,128)S(1)} %copy-done.3, f32[3,256,256]{2,1,0:T(8,128)S(1)} %copy-done.4, ...), custom_call_target="tpu_custom_call" | custom-call | flops 603979776 | bytes 8388608 | tf_op jit(solution)/shard_map/partial/pallas_call | solution.py:91
  23.2 1.0 copy-done
  24.3 4.2 %all-to-all-start = ((f32[4,5,128,128]{3,2,1,0:T(8,128)}), f32[4,5,128,128]{3,2,1,0:T(8,128)S(1)}, u32[]{:S(2)}, u32[]{:S(2)}) async-start(f32[4,5,128,128]{3,2,1,0:T(8,128)} %copy-done), calls=%async_computation | async-start | bytes 2621440 | tf_op jit(solution)/shard_map/all_to_all | solution.py:284
  28.5 5.5 %collective-permute-start.1 = (f32[136,128]{1,0:T(8,128)S(1)}, f32[136,128]{1,0:T(8,128)S(1)}, u32[]{:S(2)}, u32[]{:S(2)}) collective-permute-start(f32[136,128]{1,0:T(8,128)S(1)} %copy-done.10), channel_id=1, source_target_pairs={{0,16},{1,17},{2,18},{3,19},{4,20},{5,21},{6,22},{7,23}} | collective-permute-start | bytes 208904 | tf_op jit(solution)/shard_map/ppermute | solution.py:292
  34.0 1.3 collective-permute-done.1
  35.4 1.3 collective-permute-start.2
  36.7 1.3 collective-permute-done.2
  38.0 1.3 collective-permute-start.3
  39.4 1.3 collective-permute-done.3
  40.7 1.3 collective-permute-start.4
  42.0 1.8 %collective-permute-done.4 = f32[136,128]{1,0:T(8,128)S(1)} collective-permute-done((f32[136,128]{1,0:T(8,128)S(1)}, f32[136,128]{1,0:T(8,128)S(1)}, u32[]{:S(2)}, u32[]{:S(2)}) %collective-permute-start.4) | collective-permute-done | bytes 69664 | tf_op jit(solution)/shard_map/ppermute | solution.py:292
  43.8 2.0 %all-to-all-done = f32[4,5,128,128]{3,2,1,0:T(8,128)S(1)} async-done(((f32[4,5,128,128]{3,2,1,0:T(8,128)}), f32[4,5,128,128]{3,2,1,0:T(8,128)S(1)}, u32[]{:S(2)}, u32[]{:S(2)}) %all-to-all-start) | async-done | bytes 1310752 | tf_op jit(solution)/shard_map/all_to_all | solution.py:284
  45.9 0.1 reduce_sum.9
  46.0 2.8 %collective-permute-start.5 = (f32[128,128]{1,0:T(8,128)S(1)}, f32[128,128]{1,0:T(8,128)S(1)}, u32[]{:S(2)}, u32[]{:S(2)}) collective-permute-start(f32[128,128]{1,0:T(8,128)S(1)} %fusion), channel_id=1, source_target_pairs={{0,1},{1,0},{2,3},{3,2},{4,5},{5,4},{6,7},{7,6},{8,9},{9,8},{10,11... | collective-permute-start | bytes 196616 | tf_op jit(solution)/shard_map/ppermute | solution.py:280
  48.9 1.2 broadcast_in_dim.33
  50.1 4.3 %all-to-all-start.1 = ((f32[4,5,128,128]{3,2,1,0:T(8,128)}), f32[4,5,128,128]{3,2,1,0:T(8,128)S(1)}, u32[]{:S(2)}, u32[]{:S(2)}) async-start(f32[4,5,128,128]{3,2,1,0:T(8,128)} %broadcast_in_dim.33), calls=%async_computation.1 | async-start | bytes 2621440 | tf_op jit(solution)/shard_map/all_to_all | solution.py:284
  54.3 0.6 fusion.3.c_ref
  55.0 9.5 %inverse.1.rest_1_ = f32[128,128]{1,0:T(8,128)} custom-call(f32[128,128]{1,0:T(8,128)} %fusion.3.c_ref), custom_call_target="tpu_custom_call" | custom-call | flops 7247757312 | bytes 1048576 | tf_op jit(solution)/shard_map/inverse/pallas_call | solution.py:270
  64.5 6.0 %collective-permute-start.6 = (f32[128,128]{1,0:T(8,128)}, f32[128,128]{1,0:T(8,128)S(1)}, u32[]{:S(2)}, u32[]{:S(2)}) collective-permute-start(f32[128,128]{1,0:T(8,128)} %inverse.1.rest_1_), channel_id=1, source_target_pairs={{0,64},{1,65},{2,66},{3,67},{4,68},{5,69},{6,70},{7,71}} | collective-permute-start | bytes 196616 | tf_op jit(solution)/shard_map/ppermute | solution.py:292
  70.5 1.6 %collective-permute-done.6.rest_2_ = f32[128,128]{1,0:T(8,128)S(1)} collective-permute-done((f32[128,128]{1,0:T(8,128)}, f32[128,128]{1,0:T(8,128)S(1)}, u32[]{:S(2)}, u32[]{:S(2)}) %collective-permute-start.6) | collective-permute-done | bytes 65568 | tf_op jit(solution)/shard_map/ppermute | solution.py:292
  72.2 1.2 collective-permute-start.7
  73.3 1.9 %lead.2.rest_0_ = f32[128,128]{1,0:T(8,128)S(1)} custom-call(s32[7]{0:T(128)S(1)} %concatenate.12.info, f32[4,5,128,128]{3,2,1,0:T(8,128)S(1)} %all-to-all-done.1.v_ref, f32[4,512,128]{2,1,0:T(8,128)S(1)} %broadcast_in_dim.17.s_ref.r_ref, f32[136,128]{1,0:T(8,128)S(1)} %add.47.z_ref), custom_call_target="tpu_custom_call" | custom-call | flops 603979776 | bytes 3145728 | tf_op jit(solution)/shard_map/lead/pallas_call | solution.py:147
  75.3 0.7 collective-permute-done.7.v_ref
  76.0 0.4 collective-permute-start.8
  76.4 3.1 %lead.3 = f32[16,128,128]{2,1,0:T(8,128)} custom-call(s32[7]{0:T(128)S(1)} %concatenate.12.info, f32[4,5,128,128]{3,2,1,0:T(8,128)S(1)} %collective-permute-done.7.v_ref, f32[4,512,128]{2,1,0:T(8,128)S(1)} %broadcast_in_dim.17.s_ref.r_ref, f32[136,128]{1,0:T(8,128)S(1)} %add.47.z_ref, f32[128,128]{1,0:T(8,128)S(1)} %lead.2.rest_0_, ...), custom_call_target="tpu_custom_call" | custom-call | flops 603979776 | bytes 3145728 | tf_op jit(solution)/shard_map/lead/pallas_call | solution.py:147
  79.4 1.0 copy-done.5
  80.5 11.1 %all-to-all-start.2 = ((f32[16,128,128]{2,1,0:T(8,128)}), f32[16,128,128]{2,1,0:T(8,128)S(1)}, u32[]{:S(2)}, u32[]{:S(2)}) async-start(f32[16,128,128]{2,1,0:T(8,128)} %lead.3), calls=%async_computation.2 | async-start | bytes 2097152 | tf_op jit(solution)/shard_map/all_to_all | solution.py:284
  91.6 18.0 %block.2 = (f32[512,1024]{1,0:T(8,128)}, f32[512,128]{1,0:T(8,128)S(1)}) custom-call(s32[7]{0:T(128)S(1)} %concatenate.12.info, f32[4,5,128,128]{3,2,1,0:T(8,128)} %copy-done.1, f32[4,512,128]{2,1,0:T(8,128)S(1)} %broadcast_in_dim.17.s_ref.r_ref, f32[16,520,128]{2,1,0:T(8,128)} %bitcast.38, f32[136,128]{1,0:T(8,128)S(1)} %add.47.z_ref), custom_call_target="tpu_custom_call" | custom-call | flops 10871635968 | bytes 10485760 | tf_op jit(solution)/shard_map/block/pallas_call | solution.py:229
  109.7 1.0 copy-done.9
  110.7 21.3 %block.3 = (f32[512,1024]{1,0:T(8,128)}, f32[512,128]{1,0:T(8,128)}, f32[4,4,128]{2,1,0:T(4,128)}) custom-call(s32[7]{0:T(128)S(1)} %concatenate.12.info, f32[4,5,128,128]{3,2,1,0:T(8,128)} %copy-done.5, f32[4,512,128]{2,1,0:T(8,128)S(1)} %broadcast_in_dim.17.s_ref.r_ref, f32[16,520,128]{2,1,0:T(8,128)} %collective-permute-done.8.c_ref, ...), custom_call_target="tpu_custom_call" | custom-call | flops 10871635968 | bytes 10485760 | tf_op jit(solution)/shard_map/block/pallas_call | solution.py:229
  (40 shorter events, 0.2 us)
Async XLA Ops:
  7.2 65.0 %all-gather.3.cloned.1.call-start = ((), (), s32[]{:S(2)}) async-start(), calls=%async_computation.3 | async-start | bytes 4526080 | tf_op jit(solution)/shard_map/all_gather | solution.py:308
  7.9 2.1 %copy-start.11 = (f32[4,512]{1,0:T(4,128)}, f32[4,512]{1,0:T(4,128)S(1)}, u32[]{:S(2)}) copy-start(f32[4,512]{1,0:T(4,128)S(1)} %convert_bitcast_fusion) | copy-start | bytes 24580
  7.9 3.3 %copy-start.12 = (s32[3]{0:T(128)S(1)}, s32[3]{0:T(128)}, u32[]{:S(2)}) copy-start(s32[3]{0:T(128)} %param.11) | copy-start | bytes 40
  7.9 3.4 %copy-start.2 = (f32[3,256,256]{2,1,0:T(8,128)S(1)}, f32[3,256,256]{2,1,0:T(8,128)}, u32[]{:S(2)}) copy-start(f32[3,256,256]{2,1,0:T(8,128)} %x_ref.1) | copy-start | bytes 2359300
  10.0 5.5 %copy-start.7 = (f32[4,4,128]{2,1,0:T(4,128)S(1)}, f32[4,4,128]{2,1,0:T(4,128)}, u32[]{:S(2)}) copy-start(f32[4,4,128]{2,1,0:T(4,128)} %rest_4_.1) | copy-start | bytes 24580
  13.2 3.0 %collective-permute-start = (f32[3,256,128]{2,1,0:T(8,128)}, f32[3,256,128]{2,1,0:T(8,128)S(1)}, u32[]{:S(2)}, u32[]{:S(2)}) collective-permute-start(f32[3,256,128]{2,1,0:T(8,128)} %multiply_multiply_fusion), channel_id=1, source_target_pairs={{0,1},{1,0},{2,3},{3,2},{4,5},{5,4},{6,7},{7,6},{8,9},{9,8},{10,11... | collective-permute-start | bytes 1179656 | tf_op jit(solution)/shard_map/ppermute | solution.py:280
  17.3 1.1 copy-start.3
  18.4 1.1 copy-start.4
  23.2 1.1 copy-start
  24.3 4.2 %copy-start.10 = (f32[136,128]{1,0:T(8,128)S(1)}, f32[136,128]{1,0:T(8,128)}, u32[]{:S(2)}) copy-start(f32[136,128]{1,0:T(8,128)} %maximum_select_fusion) | copy-start | bytes 208900
  24.3 17.7 %copy-start.8 = (f32[4,128]{1,0:T(4,128)S(1)}, f32[4,128]{1,0:T(4,128)}, u32[]{:S(2)}) copy-start(f32[4,128]{1,0:T(4,128)} %rest_3_.1) | copy-start | bytes 6148
  24.3 21.6 %all-to-all-start = ((f32[4,5,128,128]{3,2,1,0:T(8,128)}), f32[4,5,128,128]{3,2,1,0:T(8,128)S(1)}, u32[]{:S(2)}, u32[]{:S(2)}) async-start(f32[4,5,128,128]{3,2,1,0:T(8,128)} %copy-done), calls=%async_computation | async-start | bytes 2621440 | tf_op jit(solution)/shard_map/all_to_all | solution.py:284
  28.5 6.8 %collective-permute-start.1 = (f32[136,128]{1,0:T(8,128)S(1)}, f32[136,128]{1,0:T(8,128)S(1)}, u32[]{:S(2)}, u32[]{:S(2)}) collective-permute-start(f32[136,128]{1,0:T(8,128)S(1)} %copy-done.10), channel_id=1, source_target_pairs={{0,16},{1,17},{2,18},{3,19},{4,20},{5,21},{6,22},{7,23}} | collective-permute-start | bytes 208904 | tf_op jit(solution)/shard_map/ppermute | solution.py:292
  35.4 2.7 %collective-permute-start.2 = (f32[136,128]{1,0:T(8,128)S(1)}, f32[136,128]{1,0:T(8,128)S(1)}, u32[]{:S(2)}, u32[]{:S(2)}) collective-permute-start(f32[136,128]{1,0:T(8,128)S(1)} %add.44), channel_id=1, source_target_pairs={{0,8},{16,24},{1,9},{17,25},{2,10},{18,26},{3,11},{19,27},{4,12},{... | collective-permute-start | bytes 208904 | tf_op jit(solution)/shard_map/ppermute | solution.py:292
  38.0 2.7 %collective-permute-start.3 = (f32[136,128]{1,0:T(8,128)S(1)}, f32[136,128]{1,0:T(8,128)S(1)}, u32[]{:S(2)}, u32[]{:S(2)}) collective-permute-start(f32[136,128]{1,0:T(8,128)S(1)} %add.45), channel_id=1, source_target_pairs={{0,64},{8,72},{16,80},{24,88},{1,65},{9,73},{17,81},{25,89},{2,66}... | collective-permute-start | bytes 208904 | tf_op jit(solution)/shard_map/ppermute | solution.py:292
  40.7 3.1 %collective-permute-start.4 = (f32[136,128]{1,0:T(8,128)S(1)}, f32[136,128]{1,0:T(8,128)S(1)}, u32[]{:S(2)}, u32[]{:S(2)}) collective-permute-start(f32[136,128]{1,0:T(8,128)S(1)} %add.46), channel_id=1, source_target_pairs={{0,32},{8,40},{16,48},{24,56},{64,96},{72,104},{80,112},{88,120},{... | collective-permute-start | bytes 208904 | tf_op jit(solution)/shard_map/ppermute | solution.py:292
  46.0 8.3 %collective-permute-start.5 = (f32[128,128]{1,0:T(8,128)S(1)}, f32[128,128]{1,0:T(8,128)S(1)}, u32[]{:S(2)}, u32[]{:S(2)}) collective-permute-start(f32[128,128]{1,0:T(8,128)S(1)} %fusion), channel_id=1, source_target_pairs={{0,1},{1,0},{2,3},{3,2},{4,5},{5,4},{6,7},{7,6},{8,9},{9,8},{10,11... | collective-permute-start | bytes 196616 | tf_op jit(solution)/shard_map/ppermute | solution.py:280
  50.1 22.1 %all-to-all-start.1 = ((f32[4,5,128,128]{3,2,1,0:T(8,128)}), f32[4,5,128,128]{3,2,1,0:T(8,128)S(1)}, u32[]{:S(2)}, u32[]{:S(2)}) async-start(f32[4,5,128,128]{3,2,1,0:T(8,128)} %broadcast_in_dim.33), calls=%async_computation.1 | async-start | bytes 2621440 | tf_op jit(solution)/shard_map/all_to_all | solution.py:284
  64.5 11.9 %copy-start.6 = (f32[128,128]{1,0:T(8,128)S(1)}, f32[128,128]{1,0:T(8,128)}, u32[]{:S(2)}) copy-start(f32[128,128]{1,0:T(8,128)} %inverse.1.rest_1_) | copy-start | bytes 196612
  64.5 7.6 %collective-permute-start.6 = (f32[128,128]{1,0:T(8,128)}, f32[128,128]{1,0:T(8,128)S(1)}, u32[]{:S(2)}, u32[]{:S(2)}) collective-permute-start(f32[128,128]{1,0:T(8,128)} %inverse.1.rest_1_), channel_id=1, source_target_pairs={{0,64},{1,65},{2,66},{3,67},{4,68},{5,69},{6,70},{7,71}} | collective-permute-start | bytes 196616 | tf_op jit(solution)/shard_map/ppermute | solution.py:292
  72.2 7.3 %copy-start.1 = (f32[4,5,128,128]{3,2,1,0:T(8,128)}, f32[4,5,128,128]{3,2,1,0:T(8,128)S(1)}, u32[]{:S(2)}) copy-start(f32[4,5,128,128]{3,2,1,0:T(8,128)S(1)} %all-to-all-done.1.v_ref) | copy-start | bytes 3932164
  72.2 3.8 %collective-permute-start.7 = (f32[4,5,128,128]{3,2,1,0:T(8,128)S(1)}, f32[4,5,128,128]{3,2,1,0:T(8,128)S(1)}, u32[]{:S(2)}, u32[]{:S(2)}) collective-permute-start(f32[4,5,128,128]{3,2,1,0:T(8,128)S(1)} %all-to-all-done.1.v_ref), channel_id=1, source_target_pairs={{0,1},{1,0},{2,3},{3,2},{4,5},{5,4},{6,7},{7,6},{8,9},{9,8},{10,11... | collective-permute-start | bytes 3932168 | tf_op jit(solution)/shard_map/ppermute | solution.py:280
  76.0 33.7 %collective-permute-start.8 = (f32[16,520,128]{2,1,0:T(8,128)}, f32[16,520,128]{2,1,0:T(8,128)}, u32[]{:S(2)}, u32[]{:S(2)}) collective-permute-start(f32[16,520,128]{2,1,0:T(8,128)} %bitcast.37), channel_id=1, source_target_pairs={{0,1},{1,0},{2,3},{3,2},{4,5},{5,4},{6,7},{7,6},{8,9},{9,8},{10,11... | collective-permute-start | bytes 12779528 | tf_op jit(solution)/shard_map/ppermute | solution.py:280
  79.4 1.0 copy-start.5
  80.5 29.2 %all-to-all-start.2 = ((f32[16,128,128]{2,1,0:T(8,128)}), f32[16,128,128]{2,1,0:T(8,128)S(1)}, u32[]{:S(2)}, u32[]{:S(2)}) async-start(f32[16,128,128]{2,1,0:T(8,128)} %lead.3), calls=%async_computation.2 | async-start | bytes 2097152 | tf_op jit(solution)/shard_map/all_to_all | solution.py:284
  109.7 1.0 copy-start.9
Sparse Core Ops, SparseCore 0:
  11.3 55.1 all-gather.2

commit v13 on v12

--- a/solution.py
+++ b/solution.py
@@ -130,7 +130,7 @@
         @pl.when(g == 1)
         def _():
             r, p = info[0], info[2]
-            sent = jnp.where((r == 0) & (p == 1), f_ref[...], jnp.where((r == 8) & (p == 0), n_ref[...], a_ref[...]))
+            sent = jnp.where((r == 0) & (p == 1), f_ref[...], jnp.where((r == 12) & (p == 0), n_ref[...], a_ref[...]))
             for j in range(16):
                 o_ref[j] = sent
 
@@ -188,7 +188,7 @@
         def _():
             row, col, p = info[0], info[1], info[2]
             same = lax.broadcasted_iota(jnp.int32, (128, 128), 0) == lax.broadcasted_iota(jnp.int32, (128, 128), 1)
-            ih, il = split(e_ref[8 * (1 - p)])
+            ih, il = split(e_ref[12 * (1 - p)])
             total[:128] += jnp.where(same & (row == 0), jnp.broadcast_to(h_ref[:1], (128, 128)), 0.0)
             th, tl = split(total[...])
             panel = product(th, tl, ih, il, NT)
@@ -319,9 +319,9 @@
 
     half = partial(info, own, own_sup, primal, dual_inverse, lent)
     head, half = lax.optimization_barrier((head, half))
-    for pairs in ([(0, 2)], [(0, 1), (2, 3)], [(z, 8 + z) for z in range(4)]):
+    for pairs in ([(0, 1)], [(0, 3), (1, 2)], [(z, 4 + z) for z in range(4)]):
         head = head + over_rows(head, pairs)
-    head_next = over_rows(head, [(y + z, y + 4 + z) for y in (0, 8) for z in range(4)])
+    head_next = over_rows(head, [(y + z, (12 if y == 0 else 8) + z) for y in (0, 4) for z in range(4)])
     terms = exchange(half, "cols", CHIPS)
     head_next, terms = lax.optimization_barrier((head_next, terms))
     head = head + head_next
@@ -329,7 +329,7 @@
     v_own = exchange(repeat(jnp.concatenate([total[:4], head[None, :128]], axis=0), 4), "cols", CHIPS)
     corner = total[4] + eye * jnp.where(p == 0, damping[0], 0.0)
     inverse = inverse_of(corner + swap(corner))
-    second = over_rows(inverse, [(0, 8)])
+    second = over_rows(inverse, [(0, 12)])
     v_own, inverse, second, gathered = lax.optimization_barrier((v_own, inverse, second, gathered))
     v_other = swap(v_own)
     begun = lead(info, v_own, own_sup, head)

time: 140 us -> 136 us (0.971)
  starting transfers between devices: 40.8 us -> 33.8 us
  waiting for transfers between devices: 10.3 us -> 13.6 us
    ppermute x5, starting transfers between devices: 15.4 us -> 12.3 us  [over_rows(): return lax.ppermute(v, 'rows', pairs)]
    all_to_all x3, waiting for transfers between devices: 2.03 us -> 4.82 us  [exchange(): return lax.all_to_all(v, axis, 0, 0, axis_index_groups=groups, tiled=True)]
    all_to_all x3, starting transfers between devices: 19.6 us -> 17.2 us  [exchange(): return lax.all_to_all(v, axis, 0, 0, axis_index_groups=groups, tiled=True)]
    ppermute x4, starting transfers between devices: 5.78 us -> 4.2 us  [swap(): return lax.ppermute(v, 'cols', SWAP)]
  transfers between devices with their start and end apart: 13 -> 13, of which waited for: 8 -> 9; matrix products, arithmetic and copies ran while one was open for 5% -> 5% of each run, Pallas kernels for 26% -> 27%
where the time goes in v13:
time: 136 us; the launch traced here: 135 us
  Pallas kernels  57.5 us (42%)
  starting transfers between devices  33.8 us (25%)
  between operations  14.3 us (11%)
  waiting for transfers between devices  13.6 us (10%)
  local copies, waits for them, and re-layouts  10.8 us (8%)
  other arithmetic  5.03 us (4%)
    pallas_call x2, Pallas kernels, block_product(): pl.pallas_call(functools.partial(block_body, last), grid_spec=grid, out_s...  39.3 us
    all_to_all x3, starting transfers between devices, exchange(): return lax.all_to_all(v, axis, 0, 0, axis_index_groups=groups, tiled=True)  17.2 us
    ppermute x5, starting transfers between devices, over_rows(): return lax.ppermute(v, 'rows', pairs)  12.3 us
    pallas_call x1, Pallas kernels, inverse_of(): pl.pallas_call(inverse_body, out_shape=jax.ShapeDtypeStruct((128, 128), F...  9.52 us
    ppermute x5, waiting for transfers between devices, over_rows(): return lax.ppermute(v, 'rows', pairs)  7.93 us
    unnamed x26, local copies, waits for them, and re-layouts  5.43 us
    pallas_call x2, Pallas kernels, lead(): pl.pallas_call(functools.partial(lead_body, last), grid_spec=grid, out_sh...  4.99 us
    all_to_all x3, waiting for transfers between devices, exchange(): return lax.all_to_all(v, axis, 0, 0, axis_index_groups=groups, tiled=True)  4.82 us
  transfers between devices with their start and end apart: 13, of which 9 were waited for; matrix products, arithmetic and copies ran while one was open for 5% of the time, Pallas kernels for 27%

profile of v13, /device:TPU:1, one launch (start us, length us, event | category | flops | bytes accessed | tf_op | source)
XLA Modules:
  0.0 135.1 jit_solution(12581589818093112993)
XLA Ops:
  7.2 0.0 all-gather.3.cloned.1.call-start
  7.2 0.7 convert_bitcast_fusion
  7.9 2.1 %copy.12 = f32[4,4,128,256]{3,2,1,0:T(8,128)S(1)} copy(f32[4,4,128,256]{3,0,2,1:T(4,128)} %bitcast.34) | data formatting | bytes 4194304 | tf_op jit(solution)/shard_map/transpose | solution.py:303
  10.1 0.1 copy.14
  10.3 0.1 pad.2.clone
  10.3 0.9 maximum_maximum_fusion
  11.2 0.0 all-gather.3.cloned.1.call-update
  11.2 0.1 fusion.1
  11.3 1.9 %multiply_multiply_fusion = f32[3,256,128]{2,1,0:T(8,128)} fusion(f32[3,256,256]{2,1,0:T(8,128)} %y_ref.1, s32[]{:T(128)S(6)} %select_n.50, f32[3,256,256]{2,1,0:T(8,128)S(1)} %copy-done.2, f32[3,128]{1,0:T(4,128)S(1)} %constant_dynamic-slice_fusion, f32[3,256]{1,0:T(4,128)S(1)} %fusion.1), kind=kLoop, calls=%fused_computation | loop fusion | flops 294912 | bytes 1184260 | tf_op jit(solution)/shard_map/mul | solution.py:318
  13.2 1.4 %collective-permute-start = (f32[3,256,128]{2,1,0:T(8,128)}, f32[3,256,128]{2,1,0:T(8,128)S(1)}, u32[]{:S(2)}, u32[]{:S(2)}) collective-permute-start(f32[3,256,128]{2,1,0:T(8,128)} %multiply_multiply_fusion), channel_id=1, source_target_pairs={{0,1},{1,0},{2,3},{3,2},{4,5},{5,4},{6,7},{7,6},{8,9},{9,8},{10,11... | collective-permute-start | bytes 1179656 | tf_op jit(solution)/shard_map/ppermute | solution.py:280
  14.7 0.1 copy.13
  14.8 0.7 concatenate.12.info
  15.5 0.6 maximum_select_fusion
  16.2 0.1 collective-permute-done.z_ref
  16.2 1.0 broadcast_in_dim.17.s_ref.r_ref
  17.3 1.1 copy-done.3
  18.4 1.1 copy-done.4
  19.5 3.7 %partial.1 = f32[4,5,128,128]{3,2,1,0:T(8,128)S(1)} custom-call(s32[7]{0:T(128)S(1)} %concatenate.12.info, f32[4,512,256]{2,1,0:T(8,128)S(1)} %bitcast.33, f32[4,512,128]{2,1,0:T(8,128)S(1)} %broadcast_in_dim.17.s_ref.r_ref, f32[3,256,256]{2,1,0:T(8,128)S(1)} %copy-done.3, f32[3,256,256]{2,1,0:T(8,128)S(1)} %copy-done.4, ...), custom_call_target="tpu_custom_call" | custom-call | flops 603979776 | bytes 8388608 | tf_op jit(solution)/shard_map/partial/pallas_call | solution.py:91
  23.2 1.0 copy-done
  24.3 4.2 %all-to-all-start = ((f32[4,5,128,128]{3,2,1,0:T(8,128)}), f32[4,5,128,128]{3,2,1,0:T(8,128)S(1)}, u32[]{:S(2)}, u32[]{:S(2)}) async-start(f32[4,5,128,128]{3,2,1,0:T(8,128)} %copy-done), calls=%async_computation | async-start | bytes 2621440 | tf_op jit(solution)/shard_map/all_to_all | solution.py:284
  28.5 3.5 %collective-permute-start.1 = (f32[136,128]{1,0:T(8,128)S(1)}, f32[136,128]{1,0:T(8,128)S(1)}, u32[]{:S(2)}, u32[]{:S(2)}) collective-permute-start(f32[136,128]{1,0:T(8,128)S(1)} %copy-done.10), channel_id=1, source_target_pairs={{0,8},{1,9},{2,10},{3,11},{4,12},{5,13},{6,14},{7,15}} | collective-permute-start | bytes 208904 | tf_op jit(solution)/shard_map/ppermute | solution.py:292
  32.1 1.3 collective-permute-done.1
  33.4 1.4 %collective-permute-start.2 = (f32[136,128]{1,0:T(8,128)S(1)}, f32[136,128]{1,0:T(8,128)S(1)}, u32[]{:S(2)}, u32[]{:S(2)}) collective-permute-start(f32[136,128]{1,0:T(8,128)S(1)} %add.44), channel_id=1, source_target_pairs={{0,24},{8,16},{1,25},{9,17},{2,26},{10,18},{3,27},{11,19},{4,28},{... | collective-permute-start | bytes 208904 | tf_op jit(solution)/shard_map/ppermute | solution.py:292
  34.9 2.1 %collective-permute-done.2 = f32[136,128]{1,0:T(8,128)S(1)} collective-permute-done((f32[136,128]{1,0:T(8,128)S(1)}, f32[136,128]{1,0:T(8,128)S(1)}, u32[]{:S(2)}, u32[]{:S(2)}) %collective-permute-start.2) | collective-permute-done | bytes 69664 | tf_op jit(solution)/shard_map/ppermute | solution.py:292
  37.0 1.3 collective-permute-start.3
  38.3 1.3 collective-permute-done.3
  39.7 1.3 collective-permute-start.4
  41.0 1.3 collective-permute-done.4
  42.3 3.5 %all-to-all-done = f32[4,5,128,128]{3,2,1,0:T(8,128)S(1)} async-done(((f32[4,5,128,128]{3,2,1,0:T(8,128)}), f32[4,5,128,128]{3,2,1,0:T(8,128)S(1)}, u32[]{:S(2)}, u32[]{:S(2)}) %all-to-all-start) | async-done | bytes 1310752 | tf_op jit(solution)/shard_map/all_to_all | solution.py:284
  45.9 0.1 reduce_sum.9
  46.0 1.6 %collective-permute-start.5 = (f32[128,128]{1,0:T(8,128)S(1)}, f32[128,128]{1,0:T(8,128)S(1)}, u32[]{:S(2)}, u32[]{:S(2)}) collective-permute-start(f32[128,128]{1,0:T(8,128)S(1)} %fusion), channel_id=1, source_target_pairs={{0,1},{1,0},{2,3},{3,2},{4,5},{5,4},{6,7},{7,6},{8,9},{9,8},{10,11... | collective-permute-start | bytes 196616 | tf_op jit(solution)/shard_map/ppermute | solution.py:280
  47.7 1.2 broadcast_in_dim.33
  48.9 3.5 %all-to-all-start.1 = ((f32[4,5,128,128]{3,2,1,0:T(8,128)}), f32[4,5,128,128]{3,2,1,0:T(8,128)S(1)}, u32[]{:S(2)}, u32[]{:S(2)}) async-start(f32[4,5,128,128]{3,2,1,0:T(8,128)} %broadcast_in_dim.33), calls=%async_computation.1 | async-start | bytes 2621440 | tf_op jit(solution)/shard_map/all_to_all | solution.py:284
  52.4 0.6 fusion.3.c_ref
  53.1 9.5 %inverse.1.rest_1_ = f32[128,128]{1,0:T(8,128)} custom-call(f32[128,128]{1,0:T(8,128)} %fusion.3.c_ref), custom_call_target="tpu_custom_call" | custom-call | flops 7247757312 | bytes 1048576 | tf_op jit(solution)/shard_map/inverse/pallas_call | solution.py:270
  62.6 4.8 %collective-permute-start.6 = (f32[128,128]{1,0:T(8,128)}, f32[128,128]{1,0:T(8,128)S(1)}, u32[]{:S(2)}, u32[]{:S(2)}) collective-permute-start(f32[128,128]{1,0:T(8,128)} %inverse.1.rest_1_), channel_id=1, source_target_pairs={{0,96},{1,97},{2,98},{3,99},{4,100},{5,101},{6,102},{7,103}} | collective-permute-start | bytes 196616 | tf_op jit(solution)/shard_map/ppermute | solution.py:292
  67.4 1.8 %collective-permute-done.6.rest_2_ = f32[128,128]{1,0:T(8,128)S(1)} collective-permute-done((f32[128,128]{1,0:T(8,128)}, f32[128,128]{1,0:T(8,128)S(1)}, u32[]{:S(2)}, u32[]{:S(2)}) %collective-permute-start.6) | collective-permute-done | bytes 65568 | tf_op jit(solution)/shard_map/ppermute | solution.py:292
  69.2 1.3 all-to-all-done.1.v_ref
  70.4 0.8 collective-permute-start.7
  71.2 1.9 %lead.2.rest_0_ = f32[128,128]{1,0:T(8,128)S(1)} custom-call(s32[7]{0:T(128)S(1)} %concatenate.12.info, f32[4,5,128,128]{3,2,1,0:T(8,128)S(1)} %all-to-all-done.1.v_ref, f32[4,512,128]{2,1,0:T(8,128)S(1)} %broadcast_in_dim.17.s_ref.r_ref, f32[136,128]{1,0:T(8,128)S(1)} %add.47.z_ref), custom_call_target="tpu_custom_call" | custom-call | flops 603979776 | bytes 3145728 | tf_op jit(solution)/shard_map/lead/pallas_call | solution.py:147
  73.2 0.7 collective-permute-done.7.v_ref
  73.9 0.4 collective-permute-start.8
  74.3 3.1 %lead.3 = f32[16,128,128]{2,1,0:T(8,128)} custom-call(s32[7]{0:T(128)S(1)} %concatenate.12.info, f32[4,5,128,128]{3,2,1,0:T(8,128)S(1)} %collective-permute-done.7.v_ref, f32[4,512,128]{2,1,0:T(8,128)S(1)} %broadcast_in_dim.17.s_ref.r_ref, f32[136,128]{1,0:T(8,128)S(1)} %add.47.z_ref, f32[128,128]{1,0:T(8,128)S(1)} %lead.2.rest_0_, ...), custom_call_target="tpu_custom_call" | custom-call | flops 603979776 | bytes 3145728 | tf_op jit(solution)/shard_map/lead/pallas_call | solution.py:147
  77.3 1.0 copy-done.5
  78.4 9.4 %all-to-all-start.2 = ((f32[16,128,128]{2,1,0:T(8,128)}), f32[16,128,128]{2,1,0:T(8,128)S(1)}, u32[]{:S(2)}, u32[]{:S(2)}) async-start(f32[16,128,128]{2,1,0:T(8,128)} %lead.3), calls=%async_computation.2 | async-start | bytes 2097152 | tf_op jit(solution)/shard_map/all_to_all | solution.py:284
  87.8 18.0 %block.2 = (f32[512,1024]{1,0:T(8,128)}, f32[512,128]{1,0:T(8,128)S(1)}) custom-call(s32[7]{0:T(128)S(1)} %concatenate.12.info, f32[4,5,128,128]{3,2,1,0:T(8,128)} %copy-done.1, f32[4,512,128]{2,1,0:T(8,128)S(1)} %broadcast_in_dim.17.s_ref.r_ref, f32[16,520,128]{2,1,0:T(8,128)} %bitcast.38, f32[136,128]{1,0:T(8,128)S(1)} %add.47.z_ref), custom_call_target="tpu_custom_call" | custom-call | flops 10871635968 | bytes 10485760 | tf_op jit(solution)/shard_map/block/pallas_call | solution.py:229
  105.9 1.0 copy-done.9
  106.9 21.3 %block.3 = (f32[512,1024]{1,0:T(8,128)}, f32[512,128]{1,0:T(8,128)}, f32[4,4,128]{2,1,0:T(4,128)}) custom-call(s32[7]{0:T(128)S(1)} %concatenate.12.info, f32[4,5,128,128]{3,2,1,0:T(8,128)} %copy-done.5, f32[4,512,128]{2,1,0:T(8,128)S(1)} %broadcast_in_dim.17.s_ref.r_ref, f32[16,520,128]{2,1,0:T(8,128)} %collective-permute-done.8.c_ref, ...), custom_call_target="tpu_custom_call" | custom-call | flops 10871635968 | bytes 10485760 | tf_op jit(solution)/shard_map/block/pallas_call | solution.py:229
  (40 shorter events, 0.2 us)
Async XLA Ops:
  7.2 63.3 %all-gather.3.cloned.1.call-start = ((), (), s32[]{:S(2)}) async-start(), calls=%async_computation.3 | async-start | bytes 4526080 | tf_op jit(solution)/shard_map/all_gather | solution.py:308
  7.9 2.1 %copy-start.11 = (f32[4,512]{1,0:T(4,128)}, f32[4,512]{1,0:T(4,128)S(1)}, u32[]{:S(2)}) copy-start(f32[4,512]{1,0:T(4,128)S(1)} %convert_bitcast_fusion) | copy-start | bytes 24580
  7.9 3.3 %copy-start.12 = (s32[3]{0:T(128)S(1)}, s32[3]{0:T(128)}, u32[]{:S(2)}) copy-start(s32[3]{0:T(128)} %param.11) | copy-start | bytes 40
  7.9 3.4 %copy-start.2 = (f32[3,256,256]{2,1,0:T(8,128)S(1)}, f32[3,256,256]{2,1,0:T(8,128)}, u32[]{:S(2)}) copy-start(f32[3,256,256]{2,1,0:T(8,128)} %x_ref.1) | copy-start | bytes 2359300
  10.0 5.5 %copy-start.7 = (f32[4,4,128]{2,1,0:T(4,128)S(1)}, f32[4,4,128]{2,1,0:T(4,128)}, u32[]{:S(2)}) copy-start(f32[4,4,128]{2,1,0:T(4,128)} %rest_4_.1) | copy-start | bytes 24580
  13.2 3.0 %collective-permute-start = (f32[3,256,128]{2,1,0:T(8,128)}, f32[3,256,128]{2,1,0:T(8,128)S(1)}, u32[]{:S(2)}, u32[]{:S(2)}) collective-permute-start(f32[3,256,128]{2,1,0:T(8,128)} %multiply_multiply_fusion), channel_id=1, source_target_pairs={{0,1},{1,0},{2,3},{3,2},{4,5},{5,4},{6,7},{7,6},{8,9},{9,8},{10,11... | collective-permute-start | bytes 1179656 | tf_op jit(solution)/shard_map/ppermute | solution.py:280
  17.3 1.1 copy-start.3
  18.4 1.1 copy-start.4
  23.2 1.1 copy-start
  24.3 4.2 %copy-start.10 = (f32[136,128]{1,0:T(8,128)S(1)}, f32[136,128]{1,0:T(8,128)}, u32[]{:S(2)}) copy-start(f32[136,128]{1,0:T(8,128)} %maximum_select_fusion) | copy-start | bytes 208900
  24.3 16.7 %copy-start.8 = (f32[4,128]{1,0:T(4,128)S(1)}, f32[4,128]{1,0:T(4,128)}, u32[]{:S(2)}) copy-start(f32[4,128]{1,0:T(4,128)} %rest_3_.1) | copy-start | bytes 6148
  24.3 21.6 %all-to-all-start = ((f32[4,5,128,128]{3,2,1,0:T(8,128)}), f32[4,5,128,128]{3,2,1,0:T(8,128)S(1)}, u32[]{:S(2)}, u32[]{:S(2)}) async-start(f32[4,5,128,128]{3,2,1,0:T(8,128)} %copy-done), calls=%async_computation | async-start | bytes 2621440 | tf_op jit(solution)/shard_map/all_to_all | solution.py:284
  28.5 4.9 %collective-permute-start.1 = (f32[136,128]{1,0:T(8,128)S(1)}, f32[136,128]{1,0:T(8,128)S(1)}, u32[]{:S(2)}, u32[]{:S(2)}) collective-permute-start(f32[136,128]{1,0:T(8,128)S(1)} %copy-done.10), channel_id=1, source_target_pairs={{0,8},{1,9},{2,10},{3,11},{4,12},{5,13},{6,14},{7,15}} | collective-permute-start | bytes 208904 | tf_op jit(solution)/shard_map/ppermute | solution.py:292
  33.4 3.6 %collective-permute-start.2 = (f32[136,128]{1,0:T(8,128)S(1)}, f32[136,128]{1,0:T(8,128)S(1)}, u32[]{:S(2)}, u32[]{:S(2)}) collective-permute-start(f32[136,128]{1,0:T(8,128)S(1)} %add.44), channel_id=1, source_target_pairs={{0,24},{8,16},{1,25},{9,17},{2,26},{10,18},{3,27},{11,19},{4,28},{... | collective-permute-start | bytes 208904 | tf_op jit(solution)/shard_map/ppermute | solution.py:292
  37.0 2.7 %collective-permute-start.3 = (f32[136,128]{1,0:T(8,128)S(1)}, f32[136,128]{1,0:T(8,128)S(1)}, u32[]{:S(2)}, u32[]{:S(2)}) collective-permute-start(f32[136,128]{1,0:T(8,128)S(1)} %add.45), channel_id=1, source_target_pairs={{0,32},{8,40},{16,48},{24,56},{1,33},{9,41},{17,49},{25,57},{2,34}... | collective-permute-start | bytes 208904 | tf_op jit(solution)/shard_map/ppermute | solution.py:292
  39.7 2.7 %collective-permute-start.4 = (f32[136,128]{1,0:T(8,128)S(1)}, f32[136,128]{1,0:T(8,128)S(1)}, u32[]{:S(2)}, u32[]{:S(2)}) collective-permute-start(f32[136,128]{1,0:T(8,128)S(1)} %add.46), channel_id=1, source_target_pairs={{0,96},{8,104},{16,112},{24,120},{32,64},{40,72},{48,80},{56,88},{... | collective-permute-start | bytes 208904 | tf_op jit(solution)/shard_map/ppermute | solution.py:292
  46.0 6.4 %collective-permute-start.5 = (f32[128,128]{1,0:T(8,128)S(1)}, f32[128,128]{1,0:T(8,128)S(1)}, u32[]{:S(2)}, u32[]{:S(2)}) collective-permute-start(f32[128,128]{1,0:T(8,128)S(1)} %fusion), channel_id=1, source_target_pairs={{0,1},{1,0},{2,3},{3,2},{4,5},{5,4},{6,7},{7,6},{8,9},{9,8},{10,11... | collective-permute-start | bytes 196616 | tf_op jit(solution)/shard_map/ppermute | solution.py:280
  48.9 21.6 %all-to-all-start.1 = ((f32[4,5,128,128]{3,2,1,0:T(8,128)}), f32[4,5,128,128]{3,2,1,0:T(8,128)S(1)}, u32[]{:S(2)}, u32[]{:S(2)}) async-start(f32[4,5,128,128]{3,2,1,0:T(8,128)} %broadcast_in_dim.33), calls=%async_computation.1 | async-start | bytes 2621440 | tf_op jit(solution)/shard_map/all_to_all | solution.py:284
  62.6 11.7 %copy-start.6 = (f32[128,128]{1,0:T(8,128)S(1)}, f32[128,128]{1,0:T(8,128)}, u32[]{:S(2)}) copy-start(f32[128,128]{1,0:T(8,128)} %inverse.1.rest_1_) | copy-start | bytes 196612
  62.6 6.6 %collective-permute-start.6 = (f32[128,128]{1,0:T(8,128)}, f32[128,128]{1,0:T(8,128)S(1)}, u32[]{:S(2)}, u32[]{:S(2)}) collective-permute-start(f32[128,128]{1,0:T(8,128)} %inverse.1.rest_1_), channel_id=1, source_target_pairs={{0,96},{1,97},{2,98},{3,99},{4,100},{5,101},{6,102},{7,103}} | collective-permute-start | bytes 196616 | tf_op jit(solution)/shard_map/ppermute | solution.py:292
  70.4 6.9 %copy-start.1 = (f32[4,5,128,128]{3,2,1,0:T(8,128)}, f32[4,5,128,128]{3,2,1,0:T(8,128)S(1)}, u32[]{:S(2)}) copy-start(f32[4,5,128,128]{3,2,1,0:T(8,128)S(1)} %all-to-all-done.1.v_ref) | copy-start | bytes 3932164
  70.4 3.5 %collective-permute-start.7 = (f32[4,5,128,128]{3,2,1,0:T(8,128)S(1)}, f32[4,5,128,128]{3,2,1,0:T(8,128)S(1)}, u32[]{:S(2)}, u32[]{:S(2)}) collective-permute-start(f32[4,5,128,128]{3,2,1,0:T(8,128)S(1)} %all-to-all-done.1.v_ref), channel_id=1, source_target_pairs={{0,1},{1,0},{2,3},{3,2},{4,5},{5,4},{6,7},{7,6},{8,9},{9,8},{10,11... | collective-permute-start | bytes 3932168 | tf_op jit(solution)/shard_map/ppermute | solution.py:280
  73.9 32.0 %collective-permute-start.8 = (f32[16,520,128]{2,1,0:T(8,128)}, f32[16,520,128]{2,1,0:T(8,128)}, u32[]{:S(2)}, u32[]{:S(2)}) collective-permute-start(f32[16,520,128]{2,1,0:T(8,128)} %bitcast.37), channel_id=1, source_target_pairs={{0,1},{1,0},{2,3},{3,2},{4,5},{5,4},{6,7},{7,6},{8,9},{9,8},{10,11... | collective-permute-start | bytes 12779528 | tf_op jit(solution)/shard_map/ppermute | solution.py:280
  77.3 1.0 copy-start.5
  78.4 27.5 %all-to-all-start.2 = ((f32[16,128,128]{2,1,0:T(8,128)}), f32[16,128,128]{2,1,0:T(8,128)S(1)}, u32[]{:S(2)}, u32[]{:S(2)}) async-start(f32[16,128,128]{2,1,0:T(8,128)} %lead.3), calls=%async_computation.2 | async-start | bytes 2097152 | tf_op jit(solution)/shard_map/all_to_all | solution.py:284
  105.9 1.0 copy-start.9
Sparse Core Ops, SparseCore 0:
  11.3 55.1 all-gather.2

commit v14 on v13

--- a/solution.py
+++ b/solution.py
@@ -11,7 +11,7 @@
 NT = (((1,), (1,)), ((), ()))
 NN = (((1,), (0,)), ((), ()))
 VMEM = 32 << 20
-LARGE = 52 << 20
+LARGE = 51 << 20
 
 
 def split(v):
@@ -105,6 +105,21 @@
 
 def column_labels(rows, n):
     return jnp.broadcast_to(jnp.concatenate(rows, axis=1), (128, n)).astype(BF)
+
+
+def assemble_body(t_ref, h_ref, o_ref, c_ref):
+    for k in range(5):
+        total = t_ref[0, k] + t_ref[1, k] + t_ref[2, k] + t_ref[3, k]
+        if k == 4:
+            c_ref[...] = total
+        for j in range(4):
+            o_ref[j, k] = h_ref[:128] if k == 4 else total
+
+
+def assemble(terms, head):
+    return pl.pallas_call(assemble_body, out_shape=[jax.ShapeDtypeStruct((4, 5, 128, 128), F32), jax.ShapeDtypeStruct((128, 128), F32)],
+                          compiler_params=pltpu.CompilerParams(vmem_limit_bytes=VMEM), name="assemble",
+                          cost_estimate=pl.CostEstimate(flops=1 << 20, bytes_accessed=3 << 20, transcendentals=0))(terms, head)
 
 
 def lead_body(last, info, v_ref, s_ref, z_ref, *rest):
@@ -325,9 +340,9 @@
     terms = exchange(half, "cols", CHIPS)
     head_next, terms = lax.optimization_barrier((head_next, terms))
     head = head + head_next
-    total = jnp.sum(terms, axis=0)
-    v_own = exchange(repeat(jnp.concatenate([total[:4], head[None, :128]], axis=0), 4), "cols", CHIPS)
-    corner = total[4] + eye * jnp.where(p == 0, damping[0], 0.0)
+    mixed, corner = assemble(terms, head)
+    v_own = exchange(mixed, "cols", CHIPS)
+    corner = corner + eye * jnp.where(p == 0, damping[0], 0.0)
     inverse = inverse_of(corner + swap(corner))
     second = over_rows(inverse, [(0, 12)])
     v_own, inverse, second, gathered = lax.optimization_barrier((v_own, inverse, second, gathered))

time: 136 us -> 134 us (0.985)
  Pallas kernels: 57.5 us -> 55.8 us
  transfers between devices with their start and end apart: 13 -> 13, of which waited for: 9 -> 9; matrix products, arithmetic and copies ran while one was open for 5% -> 4% of each run, Pallas kernels for 27% -> 26%
where the time goes in v14:
time: 134 us; the launch traced here: 133 us
  Pallas kernels  55.8 us (42%)
  starting transfers between devices  33.8 us (25%)
  between operations  14.3 us (11%)
  waiting for transfers between devices  13.6 us (10%)
  local copies, waits for them, and re-layouts  10.6 us (8%)
  other arithmetic  4.9 us (4%)
    pallas_call x2, Pallas kernels, block_product(): pl.pallas_call(functools.partial(block_body, last), grid_spec=grid, out_s...  38.5 us
    all_to_all x3, starting transfers between devices, exchange(): return lax.all_to_all(v, axis, 0, 0, axis_index_groups=groups, tiled=True)  17.3 us
    ppermute x5, starting transfers between devices, over_rows(): return lax.ppermute(v, 'rows', pairs)  12.3 us
    pallas_call x1, Pallas kernels, inverse_of(): pl.pallas_call(inverse_body, out_shape=jax.ShapeDtypeStruct((128, 128), F...  9.54 us
    ppermute x5, waiting for transfers between devices, over_rows(): return lax.ppermute(v, 'rows', pairs)  7.79 us
    unnamed x26, local copies, waits for them, and re-layouts  6.4 us
    all_to_all x3, waiting for transfers between devices, exchange(): return lax.all_to_all(v, axis, 0, 0, axis_index_groups=groups, tiled=True)  4.95 us
    ppermute x4, starting transfers between devices, swap(): return lax.ppermute(v, 'cols', SWAP)  4.19 us
  transfers between devices with their start and end apart: 13, of which 9 were waited for; matrix products, arithmetic and copies ran while one was open for 4% of the time, Pallas kernels for 26%

profile of v14, /device:TPU:1, one launch (start us, length us, event | category | flops | bytes accessed | tf_op | source)
XLA Modules:
  0.0 133.0 jit_solution(173922539146205969)
XLA Ops:
  7.2 0.0 all-gather.3.cloned.1.call-start
  7.2 0.7 convert_bitcast_fusion
  7.9 2.1 %copy.12 = f32[4,4,128,256]{3,2,1,0:T(8,128)S(1)} copy(f32[4,4,128,256]{3,0,2,1:T(4,128)} %bitcast.26) | data formatting | bytes 4194304 | tf_op jit(solution)/shard_map/transpose | solution.py:318
  10.1 0.1 copy.14
  10.3 0.1 pad.2.clone
  10.3 0.9 maximum_maximum_fusion
  11.2 0.0 all-gather.3.cloned.1.call-update
  11.2 0.1 fusion
  11.3 1.9 %multiply_multiply_fusion = f32[3,256,128]{2,1,0:T(8,128)} fusion(f32[3,256,256]{2,1,0:T(8,128)} %y_ref.1, s32[]{:T(128)S(6)} %select_n.50, f32[3,256,256]{2,1,0:T(8,128)S(1)} %copy-done.2, f32[3,128]{1,0:T(4,128)S(1)} %constant_dynamic-slice_fusion, f32[3,256]{1,0:T(4,128)S(1)} %fusion), kind=kLoop, calls=%fused_computation | loop fusion | flops 294912 | bytes 1184260 | tf_op jit(solution)/shard_map/mul | solution.py:333
  13.2 1.4 %collective-permute-start = (f32[3,256,128]{2,1,0:T(8,128)}, f32[3,256,128]{2,1,0:T(8,128)S(1)}, u32[]{:S(2)}, u32[]{:S(2)}) collective-permute-start(f32[3,256,128]{2,1,0:T(8,128)} %multiply_multiply_fusion), channel_id=1, source_target_pairs={{0,1},{1,0},{2,3},{3,2},{4,5},{5,4},{6,7},{7,6},{8,9},{9,8},{10,11... | collective-permute-start | bytes 1179656 | tf_op jit(solution)/shard_map/ppermute | solution.py:295
  14.7 0.1 copy.13
  14.8 0.7 concatenate.9.info
  15.5 0.6 maximum_select_fusion
  16.2 0.1 collective-permute-done.z_ref
  16.2 1.0 broadcast_in_dim.22.s_ref.r_ref
  17.3 1.1 copy-done.3
  18.4 1.1 copy-done.4
  19.5 3.7 %partial.1 = f32[4,5,128,128]{3,2,1,0:T(8,128)S(1)} custom-call(s32[7]{0:T(128)S(1)} %concatenate.9.info, f32[4,512,256]{2,1,0:T(8,128)S(1)} %bitcast.25, f32[4,512,128]{2,1,0:T(8,128)S(1)} %broadcast_in_dim.22.s_ref.r_ref, f32[3,256,256]{2,1,0:T(8,128)S(1)} %copy-done.3, f32[3,256,256]{2,1,0:T(8,128)S(1)} %copy-done.4, ...), custom_call_target="tpu_custom_call" | custom-call | flops 603979776 | bytes 8388608 | tf_op jit(solution)/shard_map/partial/pallas_call | solution.py:91
  23.2 1.0 copy-done
  24.3 4.2 %all-to-all-start = ((f32[4,5,128,128]{3,2,1,0:T(8,128)}), f32[4,5,128,128]{3,2,1,0:T(8,128)S(1)}, u32[]{:S(2)}, u32[]{:S(2)}) async-start(f32[4,5,128,128]{3,2,1,0:T(8,128)} %copy-done), calls=%async_computation | async-start | bytes 2621440 | tf_op jit(solution)/shard_map/all_to_all | solution.py:299
  28.5 3.5 %collective-permute-start.1 = (f32[136,128]{1,0:T(8,128)S(1)}, f32[136,128]{1,0:T(8,128)S(1)}, u32[]{:S(2)}, u32[]{:S(2)}) collective-permute-start(f32[136,128]{1,0:T(8,128)S(1)} %copy-done.10), channel_id=1, source_target_pairs={{0,8},{1,9},{2,10},{3,11},{4,12},{5,13},{6,14},{7,15}} | collective-permute-start | bytes 208904 | tf_op jit(solution)/shard_map/ppermute | solution.py:307
  32.1 1.3 %collective-permute-done.1 = f32[136,128]{1,0:T(8,128)S(1)} collective-permute-done((f32[136,128]{1,0:T(8,128)S(1)}, f32[136,128]{1,0:T(8,128)S(1)}, u32[]{:S(2)}, u32[]{:S(2)}) %collective-permute-start.1) | collective-permute-done | bytes 69664 | tf_op jit(solution)/shard_map/ppermute | solution.py:307
  33.4 1.4 %collective-permute-start.2 = (f32[136,128]{1,0:T(8,128)S(1)}, f32[136,128]{1,0:T(8,128)S(1)}, u32[]{:S(2)}, u32[]{:S(2)}) collective-permute-start(f32[136,128]{1,0:T(8,128)S(1)} %add.44), channel_id=1, source_target_pairs={{0,24},{8,16},{1,25},{9,17},{2,26},{10,18},{3,27},{11,19},{4,28},{... | collective-permute-start | bytes 208904 | tf_op jit(solution)/shard_map/ppermute | solution.py:307
  34.9 2.0 %collective-permute-done.2 = f32[136,128]{1,0:T(8,128)S(1)} collective-permute-done((f32[136,128]{1,0:T(8,128)S(1)}, f32[136,128]{1,0:T(8,128)S(1)}, u32[]{:S(2)}, u32[]{:S(2)}) %collective-permute-start.2) | collective-permute-done | bytes 69664 | tf_op jit(solution)/shard_map/ppermute | solution.py:307
  36.9 1.3 collective-permute-start.3
  38.2 1.3 %collective-permute-done.3 = f32[136,128]{1,0:T(8,128)S(1)} collective-permute-done((f32[136,128]{1,0:T(8,128)S(1)}, f32[136,128]{1,0:T(8,128)S(1)}, u32[]{:S(2)}, u32[]{:S(2)}) %collective-permute-start.3) | collective-permute-done | bytes 69664 | tf_op jit(solution)/shard_map/ppermute | solution.py:307
  39.5 1.3 collective-permute-start.4
  40.8 1.3 collective-permute-done.4
  42.2 3.7 %all-to-all-done.t_ref = f32[4,5,128,128]{3,2,1,0:T(8,128)S(1)} async-done(((f32[4,5,128,128]{3,2,1,0:T(8,128)}), f32[4,5,128,128]{3,2,1,0:T(8,128)S(1)}, u32[]{:S(2)}, u32[]{:S(2)}) %all-to-all-start) | async-done | bytes 1310752 | tf_op jit(solution)/shard_map/all_to_all | solution.py:299
  45.9 0.1 assemble.1
  46.0 1.0 copy-done.6
  47.1 1.6 %collective-permute-start.5 = (f32[128,128]{1,0:T(8,128)S(1)}, f32[128,128]{1,0:T(8,128)S(1)}, u32[]{:S(2)}, u32[]{:S(2)}) collective-permute-start(f32[128,128]{1,0:T(8,128)S(1)} %select_add_fusion), channel_id=1, source_target_pairs={{0,1},{1,0},{2,3},{3,2},{4,5},{5,4},{6,7},{7,6},{8,9},{9,8},{10,11... | collective-permute-start | bytes 196616 | tf_op jit(solution)/shard_map/ppermute | solution.py:295
  48.7 3.5 %all-to-all-start.1 = ((f32[4,5,128,128]{3,2,1,0:T(8,128)}), f32[4,5,128,128]{3,2,1,0:T(8,128)S(1)}, u32[]{:S(2)}, u32[]{:S(2)}) async-start(f32[4,5,128,128]{3,2,1,0:T(8,128)} %copy-done.6), calls=%async_computation.1 | async-start | bytes 2621440 | tf_op jit(solution)/shard_map/all_to_all | solution.py:299
  52.2 0.6 fusion.2.c_ref
  52.9 9.5 %inverse.1.rest_1_ = f32[128,128]{1,0:T(8,128)} custom-call(f32[128,128]{1,0:T(8,128)} %fusion.2.c_ref), custom_call_target="tpu_custom_call" | custom-call | flops 7247757312 | bytes 1048576 | tf_op jit(solution)/shard_map/inverse/pallas_call | solution.py:285
  62.4 4.8 %collective-permute-start.6 = (f32[128,128]{1,0:T(8,128)}, f32[128,128]{1,0:T(8,128)S(1)}, u32[]{:S(2)}, u32[]{:S(2)}) collective-permute-start(f32[128,128]{1,0:T(8,128)} %inverse.1.rest_1_), channel_id=1, source_target_pairs={{0,96},{1,97},{2,98},{3,99},{4,100},{5,101},{6,102},{7,103}} | collective-permute-start | bytes 196616 | tf_op jit(solution)/shard_map/ppermute | solution.py:307
  67.2 1.8 %collective-permute-done.6.rest_2_ = f32[128,128]{1,0:T(8,128)S(1)} collective-permute-done((f32[128,128]{1,0:T(8,128)}, f32[128,128]{1,0:T(8,128)S(1)}, u32[]{:S(2)}, u32[]{:S(2)}) %collective-permute-start.6) | collective-permute-done | bytes 65568 | tf_op jit(solution)/shard_map/ppermute | solution.py:307
  69.0 1.2 all-to-all-done.1.v_ref
  70.2 0.8 collective-permute-start.7
  71.0 1.9 %lead.2.rest_0_ = f32[128,128]{1,0:T(8,128)S(1)} custom-call(s32[7]{0:T(128)S(1)} %concatenate.9.info, f32[4,5,128,128]{3,2,1,0:T(8,128)S(1)} %all-to-all-done.1.v_ref, f32[4,512,128]{2,1,0:T(8,128)S(1)} %broadcast_in_dim.22.s_ref.r_ref, f32[136,128]{1,0:T(8,128)S(1)} %add.47.h_ref.z_ref), custom_call_target="tpu_custom_call" | custom-call | flops 603979776 | bytes 3145728 | tf_op jit(solution)/shard_map/lead/pallas_call | solution.py:162
  73.0 0.7 collective-permute-done.7.v_ref
  73.7 0.4 collective-permute-start.8
  74.1 2.0 %lead.3 = f32[16,128,128]{2,1,0:T(8,128)S(1)} custom-call(s32[7]{0:T(128)S(1)} %concatenate.9.info, f32[4,5,128,128]{3,2,1,0:T(8,128)S(1)} %collective-permute-done.7.v_ref, f32[4,512,128]{2,1,0:T(8,128)S(1)} %broadcast_in_dim.22.s_ref.r_ref, f32[136,128]{1,0:T(8,128)S(1)} %add.47.h_ref.z_ref, f32[128,128]{1,0:T(8,128)S(1)} %lead.2.rest_0_, ...), custom_call_target="tpu_custom_call" | custom-call | flops 603979776 | bytes 3145728 | tf_op jit(solution)/shard_map/lead/pallas_call | solution.py:162
  76.1 1.0 copy-done.1
  77.1 1.0 copy-done.5
  78.1 9.5 %all-to-all-start.2 = ((f32[16,128,128]{2,1,0:T(8,128)}), f32[16,128,128]{2,1,0:T(8,128)}, u32[]{:S(2)}, u32[]{:S(2)}) async-start(f32[16,128,128]{2,1,0:T(8,128)} %copy-done.1), calls=%async_computation.2 | async-start | bytes 2097152 | tf_op jit(solution)/shard_map/all_to_all | solution.py:299
  87.6 17.4 %block.2 = (f32[512,1024]{1,0:T(8,128)}, f32[512,128]{1,0:T(8,128)S(1)}) custom-call(s32[7]{0:T(128)S(1)} %concatenate.9.info, f32[4,5,128,128]{3,2,1,0:T(8,128)S(1)} %all-to-all-done.1.v_ref, f32[4,512,128]{2,1,0:T(8,128)S(1)} %broadcast_in_dim.22.s_ref.r_ref, f32[16,520,128]{2,1,0:T(8,128)} %bitcast.30, f32[136,128]{1,0:T(8,128)S(1)} %add.47.h_ref.z_ref), custom_call_target="tpu_custom_call" | custom-call | flops 10871635968 | bytes 10485760 | tf_op jit(solution)/shard_map/block/pallas_call | solution.py:244
  105.1 21.1 %block.3 = (f32[512,1024]{1,0:T(8,128)}, f32[512,128]{1,0:T(8,128)}, f32[4,4,128]{2,1,0:T(4,128)}) custom-call(s32[7]{0:T(128)S(1)} %concatenate.9.info, f32[4,5,128,128]{3,2,1,0:T(8,128)} %copy-done.5, f32[4,512,128]{2,1,0:T(8,128)S(1)} %broadcast_in_dim.22.s_ref.r_ref, f32[16,520,128]{2,1,0:T(8,128)} %collective-permute-done.8.c_ref, ...), custom_call_target="tpu_custom_call" | custom-call | flops 10871635968 | bytes 10485760 | tf_op jit(solution)/shard_map/block/pallas_call | solution.py:244
  (36 shorter events, 0.2 us)
Async XLA Ops:
  7.2 63.1 %all-gather.3.cloned.1.call-start = ((), (), s32[]{:S(2)}) async-start(), calls=%async_computation.3 | async-start | bytes 4526080 | tf_op jit(solution)/shard_map/all_gather | solution.py:323
  7.9 2.1 %copy-start.11 = (f32[4,512]{1,0:T(4,128)}, f32[4,512]{1,0:T(4,128)S(1)}, u32[]{:S(2)}) copy-start(f32[4,512]{1,0:T(4,128)S(1)} %convert_bitcast_fusion) | copy-start | bytes 24580
  7.9 3.3 %copy-start.12 = (s32[3]{0:T(128)S(1)}, s32[3]{0:T(128)}, u32[]{:S(2)}) copy-start(s32[3]{0:T(128)} %param.11) | copy-start | bytes 40
  7.9 3.4 %copy-start.2 = (f32[3,256,256]{2,1,0:T(8,128)S(1)}, f32[3,256,256]{2,1,0:T(8,128)}, u32[]{:S(2)}) copy-start(f32[3,256,256]{2,1,0:T(8,128)} %x_ref.1) | copy-start | bytes 2359300
  10.0 5.5 %copy-start.8 = (f32[4,4,128]{2,1,0:T(4,128)S(1)}, f32[4,4,128]{2,1,0:T(4,128)}, u32[]{:S(2)}) copy-start(f32[4,4,128]{2,1,0:T(4,128)} %rest_4_.1) | copy-start | bytes 24580
  13.2 3.0 %collective-permute-start = (f32[3,256,128]{2,1,0:T(8,128)}, f32[3,256,128]{2,1,0:T(8,128)S(1)}, u32[]{:S(2)}, u32[]{:S(2)}) collective-permute-start(f32[3,256,128]{2,1,0:T(8,128)} %multiply_multiply_fusion), channel_id=1, source_target_pairs={{0,1},{1,0},{2,3},{3,2},{4,5},{5,4},{6,7},{7,6},{8,9},{9,8},{10,11... | collective-permute-start | bytes 1179656 | tf_op jit(solution)/shard_map/ppermute | solution.py:295
  17.3 1.1 copy-start.3
  18.4 1.1 copy-start.4
  23.2 1.1 copy-start
  24.3 4.2 %copy-start.10 = (f32[136,128]{1,0:T(8,128)S(1)}, f32[136,128]{1,0:T(8,128)}, u32[]{:S(2)}) copy-start(f32[136,128]{1,0:T(8,128)} %maximum_select_fusion) | copy-start | bytes 208900
  24.3 16.5 %copy-start.9 = (f32[4,128]{1,0:T(4,128)S(1)}, f32[4,128]{1,0:T(4,128)}, u32[]{:S(2)}) copy-start(f32[4,128]{1,0:T(4,128)} %rest_3_.1) | copy-start | bytes 6148
  24.3 21.6 %all-to-all-start = ((f32[4,5,128,128]{3,2,1,0:T(8,128)}), f32[4,5,128,128]{3,2,1,0:T(8,128)S(1)}, u32[]{:S(2)}, u32[]{:S(2)}) async-start(f32[4,5,128,128]{3,2,1,0:T(8,128)} %copy-done), calls=%async_computation | async-start | bytes 2621440 | tf_op jit(solution)/shard_map/all_to_all | solution.py:299
  28.5 4.9 %collective-permute-start.1 = (f32[136,128]{1,0:T(8,128)S(1)}, f32[136,128]{1,0:T(8,128)S(1)}, u32[]{:S(2)}, u32[]{:S(2)}) collective-permute-start(f32[136,128]{1,0:T(8,128)S(1)} %copy-done.10), channel_id=1, source_target_pairs={{0,8},{1,9},{2,10},{3,11},{4,12},{5,13},{6,14},{7,15}} | collective-permute-start | bytes 208904 | tf_op jit(solution)/shard_map/ppermute | solution.py:307
  33.4 3.4 %collective-permute-start.2 = (f32[136,128]{1,0:T(8,128)S(1)}, f32[136,128]{1,0:T(8,128)S(1)}, u32[]{:S(2)}, u32[]{:S(2)}) collective-permute-start(f32[136,128]{1,0:T(8,128)S(1)} %add.44), channel_id=1, source_target_pairs={{0,24},{8,16},{1,25},{9,17},{2,26},{10,18},{3,27},{11,19},{4,28},{... | collective-permute-start | bytes 208904 | tf_op jit(solution)/shard_map/ppermute | solution.py:307
  36.9 2.7 %collective-permute-start.3 = (f32[136,128]{1,0:T(8,128)S(1)}, f32[136,128]{1,0:T(8,128)S(1)}, u32[]{:S(2)}, u32[]{:S(2)}) collective-permute-start(f32[136,128]{1,0:T(8,128)S(1)} %add.45), channel_id=1, source_target_pairs={{0,32},{8,40},{16,48},{24,56},{1,33},{9,41},{17,49},{25,57},{2,34}... | collective-permute-start | bytes 208904 | tf_op jit(solution)/shard_map/ppermute | solution.py:307
  39.5 2.7 %collective-permute-start.4 = (f32[136,128]{1,0:T(8,128)S(1)}, f32[136,128]{1,0:T(8,128)S(1)}, u32[]{:S(2)}, u32[]{:S(2)}) collective-permute-start(f32[136,128]{1,0:T(8,128)S(1)} %add.46), channel_id=1, source_target_pairs={{0,96},{8,104},{16,112},{24,120},{32,64},{40,72},{48,80},{56,88},{... | collective-permute-start | bytes 208904 | tf_op jit(solution)/shard_map/ppermute | solution.py:307
  46.0 1.1 copy-start.6
  47.1 5.1 %collective-permute-start.5 = (f32[128,128]{1,0:T(8,128)S(1)}, f32[128,128]{1,0:T(8,128)S(1)}, u32[]{:S(2)}, u32[]{:S(2)}) collective-permute-start(f32[128,128]{1,0:T(8,128)S(1)} %select_add_fusion), channel_id=1, source_target_pairs={{0,1},{1,0},{2,3},{3,2},{4,5},{5,4},{6,7},{7,6},{8,9},{9,8},{10,11... | collective-permute-start | bytes 196616 | tf_op jit(solution)/shard_map/ppermute | solution.py:295
  48.7 21.6 %all-to-all-start.1 = ((f32[4,5,128,128]{3,2,1,0:T(8,128)}), f32[4,5,128,128]{3,2,1,0:T(8,128)S(1)}, u32[]{:S(2)}, u32[]{:S(2)}) async-start(f32[4,5,128,128]{3,2,1,0:T(8,128)} %copy-done.6), calls=%async_computation.1 | async-start | bytes 2621440 | tf_op jit(solution)/shard_map/all_to_all | solution.py:299
  62.4 11.7 %copy-start.7 = (f32[128,128]{1,0:T(8,128)S(1)}, f32[128,128]{1,0:T(8,128)}, u32[]{:S(2)}) copy-start(f32[128,128]{1,0:T(8,128)} %inverse.1.rest_1_) | copy-start | bytes 196612
  62.4 6.6 %collective-permute-start.6 = (f32[128,128]{1,0:T(8,128)}, f32[128,128]{1,0:T(8,128)S(1)}, u32[]{:S(2)}, u32[]{:S(2)}) collective-permute-start(f32[128,128]{1,0:T(8,128)} %inverse.1.rest_1_), channel_id=1, source_target_pairs={{0,96},{1,97},{2,98},{3,99},{4,100},{5,101},{6,102},{7,103}} | collective-permute-start | bytes 196616 | tf_op jit(solution)/shard_map/ppermute | solution.py:307
  70.2 3.5 %collective-permute-start.7 = (f32[4,5,128,128]{3,2,1,0:T(8,128)S(1)}, f32[4,5,128,128]{3,2,1,0:T(8,128)S(1)}, u32[]{:S(2)}, u32[]{:S(2)}) collective-permute-start(f32[4,5,128,128]{3,2,1,0:T(8,128)S(1)} %all-to-all-done.1.v_ref), channel_id=1, source_target_pairs={{0,1},{1,0},{2,3},{3,2},{4,5},{5,4},{6,7},{7,6},{8,9},{9,8},{10,11... | collective-permute-start | bytes 3932168 | tf_op jit(solution)/shard_map/ppermute | solution.py:295
  73.7 31.4 %collective-permute-start.8 = (f32[16,520,128]{2,1,0:T(8,128)}, f32[16,520,128]{2,1,0:T(8,128)}, u32[]{:S(2)}, u32[]{:S(2)}) collective-permute-start(f32[16,520,128]{2,1,0:T(8,128)} %bitcast.29), channel_id=1, source_target_pairs={{0,1},{1,0},{2,3},{3,2},{4,5},{5,4},{6,7},{7,6},{8,9},{9,8},{10,11... | collective-permute-start | bytes 12779528 | tf_op jit(solution)/shard_map/ppermute | solution.py:295
  76.1 1.0 copy-start.1
  77.1 1.0 copy-start.5
  78.1 26.9 %all-to-all-start.2 = ((f32[16,128,128]{2,1,0:T(8,128)}), f32[16,128,128]{2,1,0:T(8,128)}, u32[]{:S(2)}, u32[]{:S(2)}) async-start(f32[16,128,128]{2,1,0:T(8,128)} %copy-done.1), calls=%async_computation.2 | async-start | bytes 2097152 | tf_op jit(solution)/shard_map/all_to_all | solution.py:299
Sparse Core Ops, SparseCore 0:
  11.3 55.1 all-gather.2

commit v15 on v14

--- a/solution.py
+++ b/solution.py
@@ -183,7 +183,8 @@
         total[...] = b_ref[...] if last else jnp.zeros_like(total)
 
     rows = [r_ref[k].astype(BF) for k in range(4)]
-    ah, al = gather_blocks(6 * g, rows, lambda k: vh[k], lambda k: vl[k], 1)
+    ah, al = gather_blocks(12 * g, rows, lambda k: vh[k], lambda k: vl[k], 1, 12)
+    both = jnp.concatenate([ah, al], axis=0)
     for q in range(3):
         n = 512 if q < 2 else 128
         r = slice(q * 512, q * 512 + n)
@@ -191,15 +192,16 @@
             sup = [column_labels([c_ref[4 * q + t, 512 + k:513 + k] for t in range(4)], n) for k in range(4)]
         else:
             sup = [column_labels([z_ref[128 + k:129 + k]], n) for k in range(4)]
-        bh, bl = gather_blocks(6 * g, sup, lambda k: ch[k, :, r], lambda k: cl[k, :, r], 0)
-        value = product(ah, al, bh, bl, NN)
+        bh, bl = gather_blocks(12 * g, sup, lambda k: ch[k, :, r], lambda k: cl[k, :, r], 0, 12)
+        pair = lax.dot_general(both, bh, NN, preferred_element_type=F32)
+        value = pair[:512] + pair[512:] + lax.dot_general(ah, bl, NN, preferred_element_type=F32)
         if q < 2:
             o_ref[:, r] += value
         else:
             total[...] += value
 
     if last:
-        @pl.when(g == 3)
+        @pl.when(g == 1)
         def _():
             row, col, p = info[0], info[1], info[2]
             same = lax.broadcasted_iota(jnp.int32, (128, 128), 0) == lax.broadcasted_iota(jnp.int32, (128, 128), 1)
@@ -238,7 +240,7 @@
     outs = [pl.BlockSpec((512, 1024), lambda g, i: (0, 0)), pl.BlockSpec((512, 128), lambda g, i: (0, 0)),
             pl.BlockSpec((4, 4, 128), lambda g, i: (0, 0, 0))]
     grid = pltpu.PrefetchScalarGridSpec(
-        num_scalar_prefetch=1, grid=(4,), in_specs=specs, out_specs=outs[:len(shapes)],
+        num_scalar_prefetch=1, grid=(2,), in_specs=specs, out_specs=outs[:len(shapes)],
         scratch_shapes=[pltpu.VMEM((4, 512, 128), BF)] * 2 + [pltpu.VMEM((4, 128, 1152), BF)] * 2
         + ([pltpu.VMEM((512, 128), F32)] if last else []))
     return pl.pallas_call(functools.partial(block_body, last), grid_spec=grid,

time: 134 us -> 133 us (level)
  Pallas kernels: 55.8 us -> 53.7 us
    pallas_call x2, Pallas kernels: 38.5 us -> 36.4 us  [block_product(): pl.pallas_call(functools.partial(block_body, last), grid_spec=grid, out_s...]
  transfers between devices with their start and end apart: 13 -> 13, of which waited for: 9 -> 10; matrix products, arithmetic and copies ran while one was open for 4% -> 4% of each run, Pallas kernels for 26% -> 25%
where the time goes in v15:
time: 133 us; the launch traced here: 131 us
  Pallas kernels  53.7 us (40%)
  starting transfers between devices  33.8 us (25%)
  between operations  14.3 us (11%)
  waiting for transfers between devices  13.7 us (10%)
  local copies, waits for them, and re-layouts  10.6 us (8%)
  other arithmetic  4.9 us (4%)
    pallas_call x2, Pallas kernels, block_product(): pl.pallas_call(functools.partial(block_body, last), grid_spec=grid, out_s...  36.4 us
    all_to_all x3, starting transfers between devices, exchange(): return lax.all_to_all(v, axis, 0, 0, axis_index_groups=groups, tiled=True)  17.3 us
    ppermute x5, starting transfers between devices, over_rows(): return lax.ppermute(v, 'rows', pairs)  12.3 us
    pallas_call x1, Pallas kernels, inverse_of(): pl.pallas_call(inverse_body, out_shape=jax.ShapeDtypeStruct((128, 128), F...  9.54 us
    ppermute x5, waiting for transfers between devices, over_rows(): return lax.ppermute(v, 'rows', pairs)  7.79 us
    unnamed x26, local copies, waits for them, and re-layouts  6.4 us
    all_to_all x3, waiting for transfers between devices, exchange(): return lax.all_to_all(v, axis, 0, 0, axis_index_groups=groups, tiled=True)  5.1 us
    ppermute x4, starting transfers between devices, swap(): return lax.ppermute(v, 'cols', SWAP)  4.19 us
  transfers between devices with their start and end apart: 13, of which 10 were waited for; matrix products, arithmetic and copies ran while one was open for 4% of the time, Pallas kernels for 25%

profile of v15, /device:TPU:1, one launch (start us, length us, event | category | flops | bytes accessed | tf_op | source)
XLA Modules:
  0.0 131.1 jit_solution(18208645966983423253)
XLA Ops:
  7.2 0.0 all-gather.3.cloned.1.call-start
  7.2 0.7 convert_bitcast_fusion
  7.9 2.1 %copy.12 = f32[4,4,128,256]{3,2,1,0:T(8,128)S(1)} copy(f32[4,4,128,256]{3,0,2,1:T(4,128)} %bitcast.26) | data formatting | bytes 4194304 | tf_op jit(solution)/shard_map/transpose | solution.py:320
  10.1 0.1 copy.14
  10.3 0.1 pad.2.clone
  10.3 0.9 maximum_maximum_fusion
  11.2 0.1 fusion
  11.3 1.9 %multiply_multiply_fusion = f32[3,256,128]{2,1,0:T(8,128)} fusion(f32[3,256,256]{2,1,0:T(8,128)} %y_ref.1, s32[]{:T(128)S(6)} %select_n.50, f32[3,256,256]{2,1,0:T(8,128)S(1)} %copy-done.2, f32[3,128]{1,0:T(4,128)S(1)} %constant_dynamic-slice_fusion, f32[3,256]{1,0:T(4,128)S(1)} %fusion), kind=kLoop, calls=%fused_computation | loop fusion | flops 294912 | bytes 1184260 | tf_op jit(solution)/shard_map/mul | solution.py:335
  13.2 1.4 %collective-permute-start = (f32[3,256,128]{2,1,0:T(8,128)}, f32[3,256,128]{2,1,0:T(8,128)S(1)}, u32[]{:S(2)}, u32[]{:S(2)}) collective-permute-start(f32[3,256,128]{2,1,0:T(8,128)} %multiply_multiply_fusion), channel_id=1, source_target_pairs={{0,1},{1,0},{2,3},{3,2},{4,5},{5,4},{6,7},{7,6},{8,9},{9,8},{10,11... | collective-permute-start | bytes 1179656 | tf_op jit(solution)/shard_map/ppermute | solution.py:297
  14.7 0.1 copy.13
  14.8 0.7 concatenate.9.info
  15.5 0.6 maximum_select_fusion
  16.2 0.1 collective-permute-done.z_ref
  16.2 1.0 broadcast_in_dim.22.s_ref.r_ref
  17.3 1.1 copy-done.3
  18.4 1.1 copy-done.4
  19.5 3.7 %partial.1 = f32[4,5,128,128]{3,2,1,0:T(8,128)S(1)} custom-call(s32[7]{0:T(128)S(1)} %concatenate.9.info, f32[4,512,256]{2,1,0:T(8,128)S(1)} %bitcast.25, f32[4,512,128]{2,1,0:T(8,128)S(1)} %broadcast_in_dim.22.s_ref.r_ref, f32[3,256,256]{2,1,0:T(8,128)S(1)} %copy-done.3, f32[3,256,256]{2,1,0:T(8,128)S(1)} %copy-done.4, ...), custom_call_target="tpu_custom_call" | custom-call | flops 603979776 | bytes 8388608 | tf_op jit(solution)/shard_map/partial/pallas_call | solution.py:91
  23.2 1.0 copy-done
  24.3 4.2 %all-to-all-start = ((f32[4,5,128,128]{3,2,1,0:T(8,128)}), f32[4,5,128,128]{3,2,1,0:T(8,128)S(1)}, u32[]{:S(2)}, u32[]{:S(2)}) async-start(f32[4,5,128,128]{3,2,1,0:T(8,128)} %copy-done), calls=%async_computation | async-start | bytes 2621440 | tf_op jit(solution)/shard_map/all_to_all | solution.py:301
  28.5 3.5 %collective-permute-start.1 = (f32[136,128]{1,0:T(8,128)S(1)}, f32[136,128]{1,0:T(8,128)S(1)}, u32[]{:S(2)}, u32[]{:S(2)}) collective-permute-start(f32[136,128]{1,0:T(8,128)S(1)} %copy-done.10), channel_id=1, source_target_pairs={{0,8},{1,9},{2,10},{3,11},{4,12},{5,13},{6,14},{7,15}} | collective-permute-start | bytes 208904 | tf_op jit(solution)/shard_map/ppermute | solution.py:309
  32.1 1.3 %collective-permute-done.1 = f32[136,128]{1,0:T(8,128)S(1)} collective-permute-done((f32[136,128]{1,0:T(8,128)S(1)}, f32[136,128]{1,0:T(8,128)S(1)}, u32[]{:S(2)}, u32[]{:S(2)}) %collective-permute-start.1) | collective-permute-done | bytes 69664 | tf_op jit(solution)/shard_map/ppermute | solution.py:309
  33.4 1.4 %collective-permute-start.2 = (f32[136,128]{1,0:T(8,128)S(1)}, f32[136,128]{1,0:T(8,128)S(1)}, u32[]{:S(2)}, u32[]{:S(2)}) collective-permute-start(f32[136,128]{1,0:T(8,128)S(1)} %add.44), channel_id=1, source_target_pairs={{0,24},{8,16},{1,25},{9,17},{2,26},{10,18},{3,27},{11,19},{4,28},{... | collective-permute-start | bytes 208904 | tf_op jit(solution)/shard_map/ppermute | solution.py:309
  34.9 2.0 %collective-permute-done.2 = f32[136,128]{1,0:T(8,128)S(1)} collective-permute-done((f32[136,128]{1,0:T(8,128)S(1)}, f32[136,128]{1,0:T(8,128)S(1)}, u32[]{:S(2)}, u32[]{:S(2)}) %collective-permute-start.2) | collective-permute-done | bytes 69664 | tf_op jit(solution)/shard_map/ppermute | solution.py:309
  36.9 1.3 collective-permute-start.3
  38.2 1.3 %collective-permute-done.3 = f32[136,128]{1,0:T(8,128)S(1)} collective-permute-done((f32[136,128]{1,0:T(8,128)S(1)}, f32[136,128]{1,0:T(8,128)S(1)}, u32[]{:S(2)}, u32[]{:S(2)}) %collective-permute-start.3) | collective-permute-done | bytes 69664 | tf_op jit(solution)/shard_map/ppermute | solution.py:309
  39.5 1.3 collective-permute-start.4
  40.8 1.3 %collective-permute-done.4 = f32[136,128]{1,0:T(8,128)S(1)} collective-permute-done((f32[136,128]{1,0:T(8,128)S(1)}, f32[136,128]{1,0:T(8,128)S(1)}, u32[]{:S(2)}, u32[]{:S(2)}) %collective-permute-start.4) | collective-permute-done | bytes 69664 | tf_op jit(solution)/shard_map/ppermute | solution.py:309
  42.2 3.7 %all-to-all-done.t_ref = f32[4,5,128,128]{3,2,1,0:T(8,128)S(1)} async-done(((f32[4,5,128,128]{3,2,1,0:T(8,128)}), f32[4,5,128,128]{3,2,1,0:T(8,128)S(1)}, u32[]{:S(2)}, u32[]{:S(2)}) %all-to-all-start) | async-done | bytes 1310752 | tf_op jit(solution)/shard_map/all_to_all | solution.py:301
  45.9 0.1 assemble.1
  46.0 1.0 copy-done.6
  47.1 1.6 %collective-permute-start.5 = (f32[128,128]{1,0:T(8,128)S(1)}, f32[128,128]{1,0:T(8,128)S(1)}, u32[]{:S(2)}, u32[]{:S(2)}) collective-permute-start(f32[128,128]{1,0:T(8,128)S(1)} %select_add_fusion), channel_id=1, source_target_pairs={{0,1},{1,0},{2,3},{3,2},{4,5},{5,4},{6,7},{7,6},{8,9},{9,8},{10,11... | collective-permute-start | bytes 196616 | tf_op jit(solution)/shard_map/ppermute | solution.py:297
  48.7 3.5 %all-to-all-start.1 = ((f32[4,5,128,128]{3,2,1,0:T(8,128)}), f32[4,5,128,128]{3,2,1,0:T(8,128)S(1)}, u32[]{:S(2)}, u32[]{:S(2)}) async-start(f32[4,5,128,128]{3,2,1,0:T(8,128)} %copy-done.6), calls=%async_computation.1 | async-start | bytes 2621440 | tf_op jit(solution)/shard_map/all_to_all | solution.py:301
  52.2 0.6 fusion.2.c_ref
  52.9 9.5 %inverse.1.rest_1_ = f32[128,128]{1,0:T(8,128)} custom-call(f32[128,128]{1,0:T(8,128)} %fusion.2.c_ref), custom_call_target="tpu_custom_call" | custom-call | flops 7247757312 | bytes 1048576 | tf_op jit(solution)/shard_map/inverse/pallas_call | solution.py:287
  62.4 4.8 %collective-permute-start.6 = (f32[128,128]{1,0:T(8,128)}, f32[128,128]{1,0:T(8,128)S(1)}, u32[]{:S(2)}, u32[]{:S(2)}) collective-permute-start(f32[128,128]{1,0:T(8,128)} %inverse.1.rest_1_), channel_id=1, source_target_pairs={{0,96},{1,97},{2,98},{3,99},{4,100},{5,101},{6,102},{7,103}} | collective-permute-start | bytes 196616 | tf_op jit(solution)/shard_map/ppermute | solution.py:309
  67.2 1.8 %collective-permute-done.6.rest_2_ = f32[128,128]{1,0:T(8,128)S(1)} collective-permute-done((f32[128,128]{1,0:T(8,128)}, f32[128,128]{1,0:T(8,128)S(1)}, u32[]{:S(2)}, u32[]{:S(2)}) %collective-permute-start.6) | collective-permute-done | bytes 65568 | tf_op jit(solution)/shard_map/ppermute | solution.py:309
  69.0 1.2 all-to-all-done.1.v_ref
  70.2 0.8 collective-permute-start.7
  71.0 1.9 %lead.2.rest_0_ = f32[128,128]{1,0:T(8,128)S(1)} custom-call(s32[7]{0:T(128)S(1)} %concatenate.9.info, f32[4,5,128,128]{3,2,1,0:T(8,128)S(1)} %all-to-all-done.1.v_ref, f32[4,512,128]{2,1,0:T(8,128)S(1)} %broadcast_in_dim.22.s_ref.r_ref, f32[136,128]{1,0:T(8,128)S(1)} %add.47.h_ref.z_ref), custom_call_target="tpu_custom_call" | custom-call | flops 603979776 | bytes 3145728 | tf_op jit(solution)/shard_map/lead/pallas_call | solution.py:162
  73.0 0.7 collective-permute-done.7.v_ref
  73.7 0.4 collective-permute-start.8
  74.1 2.0 %lead.3 = f32[16,128,128]{2,1,0:T(8,128)S(1)} custom-call(s32[7]{0:T(128)S(1)} %concatenate.9.info, f32[4,5,128,128]{3,2,1,0:T(8,128)S(1)} %collective-permute-done.7.v_ref, f32[4,512,128]{2,1,0:T(8,128)S(1)} %broadcast_in_dim.22.s_ref.r_ref, f32[136,128]{1,0:T(8,128)S(1)} %add.47.h_ref.z_ref, f32[128,128]{1,0:T(8,128)S(1)} %lead.2.rest_0_, ...), custom_call_target="tpu_custom_call" | custom-call | flops 603979776 | bytes 3145728 | tf_op jit(solution)/shard_map/lead/pallas_call | solution.py:162
  76.1 1.0 copy-done.1
  77.1 1.0 copy-done.5
  78.1 9.5 %all-to-all-start.2 = ((f32[16,128,128]{2,1,0:T(8,128)}), f32[16,128,128]{2,1,0:T(8,128)}, u32[]{:S(2)}, u32[]{:S(2)}) async-start(f32[16,128,128]{2,1,0:T(8,128)} %copy-done.1), calls=%async_computation.2 | async-start | bytes 2097152 | tf_op jit(solution)/shard_map/all_to_all | solution.py:301
  87.6 15.9 %block.2 = (f32[512,1024]{1,0:T(8,128)}, f32[512,128]{1,0:T(8,128)S(1)}) custom-call(s32[7]{0:T(128)S(1)} %concatenate.9.info, f32[4,5,128,128]{3,2,1,0:T(8,128)S(1)} %all-to-all-done.1.v_ref, f32[4,512,128]{2,1,0:T(8,128)S(1)} %broadcast_in_dim.22.s_ref.r_ref, f32[16,520,128]{2,1,0:T(8,128)} %bitcast.30, f32[136,128]{1,0:T(8,128)S(1)} %add.47.h_ref.z_ref), custom_call_target="tpu_custom_call" | custom-call | flops 10871635968 | bytes 10485760 | tf_op jit(solution)/shard_map/block/pallas_call | solution.py:246
  103.6 0.1 all-to-all-done.2.rest_2_
  103.7 20.5 %block.3 = (f32[512,1024]{1,0:T(8,128)}, f32[512,128]{1,0:T(8,128)}, f32[4,4,128]{2,1,0:T(4,128)}) custom-call(s32[7]{0:T(128)S(1)} %concatenate.9.info, f32[4,5,128,128]{3,2,1,0:T(8,128)} %copy-done.5, f32[4,512,128]{2,1,0:T(8,128)S(1)} %broadcast_in_dim.22.s_ref.r_ref, f32[16,520,128]{2,1,0:T(8,128)} %collective-permute-done.8.c_ref, ...), custom_call_target="tpu_custom_call" | custom-call | flops 10871635968 | bytes 10485760 | tf_op jit(solution)/shard_map/block/pallas_call | solution.py:246
  (36 shorter events, 0.2 us)
Async XLA Ops:
  7.2 63.1 %all-gather.3.cloned.1.call-start = ((), (), s32[]{:S(2)}) async-start(), calls=%async_computation.3 | async-start | bytes 4526080 | tf_op jit(solution)/shard_map/all_gather | solution.py:325
  7.9 2.1 %copy-start.11 = (f32[4,512]{1,0:T(4,128)}, f32[4,512]{1,0:T(4,128)S(1)}, u32[]{:S(2)}) copy-start(f32[4,512]{1,0:T(4,128)S(1)} %convert_bitcast_fusion) | copy-start | bytes 24580
  7.9 3.3 %copy-start.12 = (s32[3]{0:T(128)S(1)}, s32[3]{0:T(128)}, u32[]{:S(2)}) copy-start(s32[3]{0:T(128)} %param.11) | copy-start | bytes 40
  7.9 3.4 %copy-start.2 = (f32[3,256,256]{2,1,0:T(8,128)S(1)}, f32[3,256,256]{2,1,0:T(8,128)}, u32[]{:S(2)}) copy-start(f32[3,256,256]{2,1,0:T(8,128)} %x_ref.1) | copy-start | bytes 2359300
  10.0 5.5 %copy-start.8 = (f32[4,4,128]{2,1,0:T(4,128)S(1)}, f32[4,4,128]{2,1,0:T(4,128)}, u32[]{:S(2)}) copy-start(f32[4,4,128]{2,1,0:T(4,128)} %rest_4_.1) | copy-start | bytes 24580
  13.2 3.0 %collective-permute-start = (f32[3,256,128]{2,1,0:T(8,128)}, f32[3,256,128]{2,1,0:T(8,128)S(1)}, u32[]{:S(2)}, u32[]{:S(2)}) collective-permute-start(f32[3,256,128]{2,1,0:T(8,128)} %multiply_multiply_fusion), channel_id=1, source_target_pairs={{0,1},{1,0},{2,3},{3,2},{4,5},{5,4},{6,7},{7,6},{8,9},{9,8},{10,11... | collective-permute-start | bytes 1179656 | tf_op jit(solution)/shard_map/ppermute | solution.py:297
  17.3 1.1 copy-start.3
  18.4 1.1 copy-start.4
  23.2 1.1 copy-start
  24.3 4.2 %copy-start.10 = (f32[136,128]{1,0:T(8,128)S(1)}, f32[136,128]{1,0:T(8,128)}, u32[]{:S(2)}) copy-start(f32[136,128]{1,0:T(8,128)} %maximum_select_fusion) | copy-start | bytes 208900
  24.3 16.5 %copy-start.9 = (f32[4,128]{1,0:T(4,128)S(1)}, f32[4,128]{1,0:T(4,128)}, u32[]{:S(2)}) copy-start(f32[4,128]{1,0:T(4,128)} %rest_3_.1) | copy-start | bytes 6148
  24.3 21.6 %all-to-all-start = ((f32[4,5,128,128]{3,2,1,0:T(8,128)}), f32[4,5,128,128]{3,2,1,0:T(8,128)S(1)}, u32[]{:S(2)}, u32[]{:S(2)}) async-start(f32[4,5,128,128]{3,2,1,0:T(8,128)} %copy-done), calls=%async_computation | async-start | bytes 2621440 | tf_op jit(solution)/shard_map/all_to_all | solution.py:301
  28.5 4.9 %collective-permute-start.1 = (f32[136,128]{1,0:T(8,128)S(1)}, f32[136,128]{1,0:T(8,128)S(1)}, u32[]{:S(2)}, u32[]{:S(2)}) collective-permute-start(f32[136,128]{1,0:T(8,128)S(1)} %copy-done.10), channel_id=1, source_target_pairs={{0,8},{1,9},{2,10},{3,11},{4,12},{5,13},{6,14},{7,15}} | collective-permute-start | bytes 208904 | tf_op jit(solution)/shard_map/ppermute | solution.py:309
  33.4 3.4 %collective-permute-start.2 = (f32[136,128]{1,0:T(8,128)S(1)}, f32[136,128]{1,0:T(8,128)S(1)}, u32[]{:S(2)}, u32[]{:S(2)}) collective-permute-start(f32[136,128]{1,0:T(8,128)S(1)} %add.44), channel_id=1, source_target_pairs={{0,24},{8,16},{1,25},{9,17},{2,26},{10,18},{3,27},{11,19},{4,28},{... | collective-permute-start | bytes 208904 | tf_op jit(solution)/shard_map/ppermute | solution.py:309
  36.9 2.7 %collective-permute-start.3 = (f32[136,128]{1,0:T(8,128)S(1)}, f32[136,128]{1,0:T(8,128)S(1)}, u32[]{:S(2)}, u32[]{:S(2)}) collective-permute-start(f32[136,128]{1,0:T(8,128)S(1)} %add.45), channel_id=1, source_target_pairs={{0,32},{8,40},{16,48},{24,56},{1,33},{9,41},{17,49},{25,57},{2,34}... | collective-permute-start | bytes 208904 | tf_op jit(solution)/shard_map/ppermute | solution.py:309
  39.5 2.7 %collective-permute-start.4 = (f32[136,128]{1,0:T(8,128)S(1)}, f32[136,128]{1,0:T(8,128)S(1)}, u32[]{:S(2)}, u32[]{:S(2)}) collective-permute-start(f32[136,128]{1,0:T(8,128)S(1)} %add.46), channel_id=1, source_target_pairs={{0,96},{8,104},{16,112},{24,120},{32,64},{40,72},{48,80},{56,88},{... | collective-permute-start | bytes 208904 | tf_op jit(solution)/shard_map/ppermute | solution.py:309
  46.0 1.1 copy-start.6
  47.1 5.1 %collective-permute-start.5 = (f32[128,128]{1,0:T(8,128)S(1)}, f32[128,128]{1,0:T(8,128)S(1)}, u32[]{:S(2)}, u32[]{:S(2)}) collective-permute-start(f32[128,128]{1,0:T(8,128)S(1)} %select_add_fusion), channel_id=1, source_target_pairs={{0,1},{1,0},{2,3},{3,2},{4,5},{5,4},{6,7},{7,6},{8,9},{9,8},{10,11... | collective-permute-start | bytes 196616 | tf_op jit(solution)/shard_map/ppermute | solution.py:297
  48.7 21.6 %all-to-all-start.1 = ((f32[4,5,128,128]{3,2,1,0:T(8,128)}), f32[4,5,128,128]{3,2,1,0:T(8,128)S(1)}, u32[]{:S(2)}, u32[]{:S(2)}) async-start(f32[4,5,128,128]{3,2,1,0:T(8,128)} %copy-done.6), calls=%async_computation.1 | async-start | bytes 2621440 | tf_op jit(solution)/shard_map/all_to_all | solution.py:301
  62.4 11.7 %copy-start.7 = (f32[128,128]{1,0:T(8,128)S(1)}, f32[128,128]{1,0:T(8,128)}, u32[]{:S(2)}) copy-start(f32[128,128]{1,0:T(8,128)} %inverse.1.rest_1_) | copy-start | bytes 196612
  62.4 6.6 %collective-permute-start.6 = (f32[128,128]{1,0:T(8,128)}, f32[128,128]{1,0:T(8,128)S(1)}, u32[]{:S(2)}, u32[]{:S(2)}) collective-permute-start(f32[128,128]{1,0:T(8,128)} %inverse.1.rest_1_), channel_id=1, source_target_pairs={{0,96},{1,97},{2,98},{3,99},{4,100},{5,101},{6,102},{7,103}} | collective-permute-start | bytes 196616 | tf_op jit(solution)/shard_map/ppermute | solution.py:309
  70.2 3.5 %collective-permute-start.7 = (f32[4,5,128,128]{3,2,1,0:T(8,128)S(1)}, f32[4,5,128,128]{3,2,1,0:T(8,128)S(1)}, u32[]{:S(2)}, u32[]{:S(2)}) collective-permute-start(f32[4,5,128,128]{3,2,1,0:T(8,128)S(1)} %all-to-all-done.1.v_ref), channel_id=1, source_target_pairs={{0,1},{1,0},{2,3},{3,2},{4,5},{5,4},{6,7},{7,6},{8,9},{9,8},{10,11... | collective-permute-start | bytes 3932168 | tf_op jit(solution)/shard_map/ppermute | solution.py:297
  73.7 30.0 %collective-permute-start.8 = (f32[16,520,128]{2,1,0:T(8,128)}, f32[16,520,128]{2,1,0:T(8,128)}, u32[]{:S(2)}, u32[]{:S(2)}) collective-permute-start(f32[16,520,128]{2,1,0:T(8,128)} %bitcast.29), channel_id=1, source_target_pairs={{0,1},{1,0},{2,3},{3,2},{4,5},{5,4},{6,7},{7,6},{8,9},{9,8},{10,11... | collective-permute-start | bytes 12779528 | tf_op jit(solution)/shard_map/ppermute | solution.py:297
  76.1 1.0 copy-start.1
  77.1 1.0 copy-start.5
  78.1 25.6 %all-to-all-start.2 = ((f32[16,128,128]{2,1,0:T(8,128)}), f32[16,128,128]{2,1,0:T(8,128)}, u32[]{:S(2)}, u32[]{:S(2)}) async-start(f32[16,128,128]{2,1,0:T(8,128)} %copy-done.1), calls=%async_computation.2 | async-start | bytes 2097152 | tf_op jit(solution)/shard_map/all_to_all | solution.py:301
Sparse Core Ops, SparseCore 0:
  11.3 55.1 all-gather.2
